TPU v7x, 32 devices: a whole 2x2x4 slice. The times are simulated.
32 devices in a mesh: gx: 4 (over z), gy: 8 (over y, x, core).
Axes of the slice: x: 2, y: 2, z: 4, core: 2. Of those that a mesh axis runs over, the one named last changes fastest.
Arguments:
- embeddings: bfloat16 [65536, 4096], P(('gx', 'gy'))
- signs: int32 [4096, 256], replicated, may hold values from -1 to 1, as said below
Outputs:
- triangle: float32 [256, 256], replicated
- basis: bfloat16 [65536, 256], P(('gx', 'gy'))
- projected: float32 [256, 4096], replicated
Inputs may be any that keep to these rules, and one draw needn't show every extreme that they name: Every entry of signs is -1 or 1.
All inputs are finite; a program needn't handle non-finite values.
Results may differ from a plain program's by a relative error of at most 0.0024.
Values sent between devices are 32-bit elements; how exact they have to be, the bound alone decides.
No kernel may reach another device: no remote copies, remote signals or barrier semaphores. Data moves between devices by JAX's collectives and lax.ppermute only.
A program may use at most 128 MiB of HBM per device.

v0:
```python
import math

import jax
import jax.numpy as jnp
from jax import lax
from jax.sharding import PartitionSpec as P


def shards(embeddings, signs):
    in_scale = 1.0 / math.sqrt(embeddings.shape[1])
    sketch = (
        jnp.dot(embeddings, signs.astype(jnp.bfloat16), preferred_element_type=jnp.float32)
        * in_scale
    )
    rows_all = sketch.shape[0] * lax.axis_size(("gx", "gy"))
    gram = jnp.dot(sketch.T, sketch, precision=lax.Precision.HIGHEST) / rows_all
    sketch_half = sketch.astype(jnp.bfloat16)
    term = jnp.einsum("rk,rd->kd", sketch_half, embeddings, preferred_element_type=jnp.float32)
    term = term * (1.0 / math.sqrt(rows_all))
    cross = lax.psum(term, ("gx", "gy"))
    lower = jnp.linalg.cholesky(lax.psum(gram, ("gx", "gy")))
    basis = lax.linalg.triangular_solve(
        lower, sketch, left_side=False, lower=True, transpose_a=True
    ).astype(jnp.bfloat16)
    projected = lax.linalg.triangular_solve(lower, cross, left_side=True, lower=True)
    return (lower.T, basis, projected)


def solution(mesh):
    return jax.shard_map(
        shards,
        mesh=mesh,
        in_specs=(P(("gx", "gy"), None), P()),
        out_specs=(P(), P(("gx", "gy"), None), P()),
        check_vma=False,
    )
```

profile of v0, /device:TPU:0, one launch (start us, length us, event | category | flops | bytes accessed | tf_op | source)
XLA Modules:
  0.0 258.7 jit_solution(15293520967876725187)
XLA Ops:
  7.2 0.0 all-reduce.4.cloned.1.call-start
  7.2 0.0 copy-start
  7.2 9.9 %convolution_multiply_fusion.1 = f32[2048,256]{1,0:T(8,128)S(1)} fusion(bf16[2048,4096]{1,0:T(8,128)(2,1)} %param.2, s32[4096,256]{1,0:T(8,128)} %param.3), kind=kOutput, calls=%fused_computation.5 | convolution fusion | flops 4296540160 | bytes 23068672 | tf_op jit(solution)/shard_map/dot_general | solution.py:12
  17.1 4.2 %convolution_multiply_fusion.2 = f32[256,256]{0,1:T(8,128)} fusion(f32[2048,256]{1,0:T(8,128)S(1)} %convolution_multiply_fusion.1), kind=kOutput, calls=%fused_computation.11 | convolution fusion | flops 1610678272 | bytes 2359296 | tf_op jit(solution)/shard_map/dot_general | solution.py:16
  21.3 0.0 copy-done
  21.3 6.0 %convolution_multiply_fusion = f32[256,4096]{1,0:T(8,128)} fusion(bf16[2048,4096]{1,0:T(8,128)(2,1)S(1)} %copy-done, f32[2048,256]{1,0:T(8,128)S(1)} %convolution_multiply_fusion.1), kind=kOutput, calls=%fused_computation.2 | convolution fusion | flops 4296540160 | bytes 23068672 | tf_op jit(solution)/shard_map/rk,rd->kd/dot_general | solution.py:18
  27.3 0.0 all-reduce.4.cloned.1.call-update
  27.4 146.4 %all-reduce.4.cloned.1.call-done = (f32[256,256]{0,1:T(8,128)}, f32[256,4096]{1,0:T(8,128)}) async-done(((f32[256,256]{0,1:T(8,128)}, f32[256,4096]{1,0:T(8,128)}), (f32[256,256]{0,1:T(8,128)}, f32[256,4096]{1,0:T(8,128)})) %all-reduce.4.cloned.1.call-update) | async-done | bytes 4456464 | tf_op jit(solution)/shard_map/psum | solution.py:21
  173.8 1.1 copy.6
  174.9 1.0 fusion.6
  175.9 11.7 %cholesky.50 = f32[128,128]{1,0:T(8,128)S(1)} custom-call(f32[128,128]{1,0:T(8,128)S(1)} %cholesky.118), custom_call_target="Cholesky" | custom-call | tf_op jit(solution)/shard_map/jit(cholesky)/cholesky | solution.py:21
  187.6 9.8 %custom-call.16 = f32[1,128,128]{1,2,0:T(8,128)S(1)} custom-call(f32[1,128,128]{2,1,0:T(8,128)S(1)} %get-tuple-element.31), custom_call_target="InvertDiagBlocksLowerTriangular" | custom-call | tf_op jit(solution)/shard_map/jit(cholesky)/cholesky | solution.py:21
  197.5 0.2 constant_dynamic-update-slice_fusion.1
  197.7 0.3 convolution_subtract_fusion.2
  197.9 11.7 %cholesky.105 = f32[128,128]{1,0:T(8,128)S(1)} custom-call(f32[128,128]{1,0:T(8,128)S(1)} %convolution_subtract_fusion.2), custom_call_target="Cholesky" | custom-call | tf_op jit(solution)/shard_map/jit(cholesky)/cholesky | solution.py:21
  209.7 0.6 compare_reduce_fusion
  211.7 0.8 copy.7
  212.5 0.1 triangular_solve.58
  212.6 4.0 %while.1 = (s32[]{:T(128)}, f32[256,256]{1,0:T(8,128)S(1)}, s32[2,2]{1,0:T(2,128)S(1)}, f32[2,128,128]{2,1,0:T(8,128)S(1)}, s32[]{:T(128)}) while((s32[]{:T(128)}, f32[256,256]{1,0:T(8,128)S(1)}, s32[2,2]{1,0:T(2,128)S(1)}, f32[2,128,128]{2,1,0:T(8,128)S(1)}, s32[]{:T(128)}) %tuple.30), condition=%wide.while_cond, body=%wide.while_body.sunk | while | flops 2 | bytes 131189 | solution.py:22
  212.6 0.6 fusion.28
  213.2 1.4 bitcast_dynamic-update-slice_fusion.2
  214.6 0.6 fusion.28
  215.2 1.4 bitcast_dynamic-update-slice_fusion.2
  216.6 19.9 %custom-call.17 = f32[2,128,128]{1,2,0:T(8,128)S(1)} custom-call(f32[2,128,128]{2,1,0:T(8,128)S(1)} %get-tuple-element.10), custom_call_target="InvertDiagBlocksLowerTriangular" | custom-call | tf_op jit(solution)/shard_map/triangular_solve | solution.py:22
  236.5 1.1 fusion.16
  237.6 1.8 convolution_subtract_fusion.1
  239.4 1.1 convolution_convert_fusion
  240.5 0.1 pad_maximum_fusion.1
  240.6 1.3 copy.8
  241.9 0.0 copy-start.1
  241.9 3.6 %fusion = f32[128,4096]{1,0:T(8,128)S(1)} fusion(f32[256,4096]{1,0:T(8,128)} %get-tuple-element.23, f32[2,128,128]{1,2,0:T(8,128)S(1)} %custom-call.17), kind=kOutput, calls=%fused_computation.8 | convolution fusion | flops 805306368 | bytes 4259840 | tf_op jit(solution)/shard_map/triangular_solve | solution.py:25
  245.5 0.0 copy-done.1
  245.6 1.9 convolution_subtract_fusion
  247.5 1.9 fusion.12
  249.4 2.4 pad_maximum_fusion
  (9 shorter events, 0.2 us)
Async XLA Ops:
  7.2 166.6 %all-reduce.4.cloned.1.call-start = ((), (), s32[]{:S(2)}) async-start(), calls=%async_computation | async-start | bytes 8912896 | tf_op jit(solution)/shard_map/psum | solution.py:21
  7.2 14.1 %copy-start = (bf16[2048,4096]{1,0:T(8,128)(2,1)S(1)}, bf16[2048,4096]{1,0:T(8,128)(2,1)}, u32[]{:S(2)}) copy-start(bf16[2048,4096]{1,0:T(8,128)(2,1)} %param.2) | copy-start | bytes 50331652
  241.9 3.6 %copy-start.1 = (f32[256,4096]{1,0:T(8,128)S(1)}, f32[256,4096]{1,0:T(8,128)}, u32[]{:S(2)}) copy-start(f32[256,4096]{1,0:T(8,128)} %get-tuple-element.23) | copy-start | bytes 12582916
Sparse Core Ops, SparseCore 0:
  27.5 146.2 all-reduce.3
where the time goes:
time: 259 us
  waiting for transfers between devices  146 us (56%)
  other arithmetic  57.4 us (22%)
  matrix products  32 us (12%)
  between operations  15.5 us (6%)
  local copies, waits for them, and re-layouts  7.28 us (3%)
    psum x1, waiting for transfers between devices, shards(): lower = jnp.linalg.cholesky(lax.psum(gram, ('gx', 'gy')))  146 us
    another operation x6, other arithmetic, shards(): lower = jnp.linalg.cholesky(lax.psum(gram, ('gx', 'gy')))  33.9 us
    another operation x4, other arithmetic, shards(): lax.linalg.triangular_solve(lower, sketch, left_side=False, lower=True, t...  20 us
    dot_general x1, matrix products, shards(): jnp.dot(embeddings, signs.astype(jnp.bfloat16), preferred_element_type=jn...  9.9 us
    another operation x3, matrix products, shards(): lax.linalg.triangular_solve(lower, cross, left_side=True, lower=True)  7.49 us
    dot_general x1, matrix products, shards(): jnp.einsum('rk,rd->kd', sketch_half, embeddings, preferred_element_type=j...  6.03 us
  transfers between devices with their start and end apart: 1, of which 1 were waited for; matrix products, arithmetic and copies ran while one was open for 0% of the time, Pallas kernels for 0%

commit v1 on v0

v1 whole, which is shorter than its diff:
```python
import functools
import math

import jax
import jax.numpy as jnp
from jax import lax
from jax.experimental import pallas as pl
from jax.experimental.pallas import tpu as pltpu
from jax.sharding import PartitionSpec as P

AXES = ("gx", "gy")
CHUNKS = 1
MIB = 1 << 20


def dot(a, b, dims=((1,), (0,))):
    return lax.dot_general(a, b, (dims, ((), ())), preferred_element_type=jnp.float32)


def split(a):
    high = a.astype(jnp.bfloat16)
    return high, (a - high.astype(jnp.float32)).astype(jnp.bfloat16)


def orders_of(n_devices):
    bits = list(range(1, n_devices.bit_length() - 1))
    swapped = bits[:]
    for i in range(0, len(bits) - 1, 2):
        swapped[i], swapped[i + 1] = bits[i + 1], bits[i]
    return bits, swapped


def bits_of(me, order):
    value = jnp.int32(0)
    for b in order:
        value = value * 2 + ((me >> b) & 1)
    return value


def sketch_kernel(in_scale, gram_scale, me, e, signs, sketch, rounded_t, gram_sent, gram_kept, s16, acc, mixed):
    step = pl.program_id(0)

    @pl.when(step == 0)
    def _():
        s16[...] = signs[...].astype(jnp.bfloat16)
        acc[...] = jnp.zeros_like(acc)
        mixed[...] = jnp.zeros_like(mixed)

    sk = dot(e[...], s16[...]) * in_scale
    sketch[...] = sk
    high, low = split(sk)
    high_t = high.T
    rounded_t[...] = high_t
    acc[...] += dot(high_t, high)
    mixed[...] += dot(high_t, low)

    @pl.when(step == pl.num_programs(0) - 1)
    def _():
        cross = mixed[...]
        acc[...] = (acc[...] + cross + cross.T) * gram_scale
        half = acc.shape[0] // 2
        own = me[0] & 1
        gram_kept[...] = acc[pl.ds(pl.multiple_of(own * half, half), half), :]
        gram_sent[...] = acc[pl.ds(pl.multiple_of((1 - own) * half, half), half), :]


def sketch_call(me, e, signs, rows_all):
    rows, d = e.shape
    k = signs.shape[1]
    block = 256
    return pl.pallas_call(
        functools.partial(sketch_kernel, 1.0 / math.sqrt(d), 1.0 / rows_all),
        grid_spec=pltpu.PrefetchScalarGridSpec(
            num_scalar_prefetch=1,
            grid=(rows // block,),
            in_specs=[
                pl.BlockSpec((block, d), lambda i, me: (i, 0)),
                pl.BlockSpec((d, k), lambda i, me: (0, 0), pipeline_mode=pl.Buffered(1)),
            ],
            out_specs=[
                pl.BlockSpec((block, k), lambda i, me: (i, 0)),
                pl.BlockSpec((k, block), lambda i, me: (0, i)),
                pl.BlockSpec((k // 2, k), lambda i, me: (0, 0)),
                pl.BlockSpec((k // 2, k), lambda i, me: (0, 0)),
            ],
            scratch_shapes=[
                pltpu.VMEM((d, k), jnp.bfloat16),
                pltpu.VMEM((k, k), jnp.float32),
                pltpu.VMEM((k, k), jnp.float32),
            ],
        ),
        out_shape=[
            jax.ShapeDtypeStruct((rows, k), jnp.float32),
            jax.ShapeDtypeStruct((k, rows), jnp.bfloat16),
            jax.ShapeDtypeStruct((k // 2, k), jnp.float32),
            jax.ShapeDtypeStruct((k // 2, k), jnp.float32),
        ],
        compiler_params=pltpu.CompilerParams(vmem_limit_bytes=40 * MIB),
        cost_estimate=pl.CostEstimate(flops=2 * rows * d * k, bytes_accessed=rows * d * 2 + d * k * 4, transcendentals=0),
        name="sketch",
    )(me, e, signs)


def cross_kernel(scale, groups, info, e, rounded_t, *outs):
    step = pl.program_id(0)
    value = dot(rounded_t[...], e[...]) * scale
    size = value.shape[0] // groups
    per = 4 // len(outs)
    for o, out in enumerate(outs):

        @pl.when(step // per == o)
        def _(out=out):
            for g in range(groups):
                at = pl.multiple_of((info[4] ^ g) * size, size)
                out[0, pl.ds(at, size), :] = value[g * size : (g + 1) * size]


def cross_call(info, e, rounded_t, scale, groups, width, n_outs):
    rows, d = e.shape
    k = rounded_t.shape[0]
    per = 4 // n_outs
    return pl.pallas_call(
        functools.partial(cross_kernel, scale, groups),
        grid_spec=pltpu.PrefetchScalarGridSpec(
            num_scalar_prefetch=1,
            grid=(4,),
            in_specs=[
                pl.BlockSpec((rows, width), lambda i, info: (0, info[i])),
                pl.BlockSpec((k, rows), lambda i, info: (0, 0), pipeline_mode=pl.Buffered(1)),
            ],
            out_specs=[
                pl.BlockSpec((1, k, width), lambda i, info, o=o: (jnp.clip(i - o * per, 0, per - 1), 0, 0))
                for o in range(n_outs)
            ],
        ),
        out_shape=[jax.ShapeDtypeStruct((per, k, width), jnp.float32)] * n_outs,
        compiler_params=pltpu.CompilerParams(vmem_limit_bytes=40 * MIB),
        cost_estimate=pl.CostEstimate(flops=2 * rows * k * width * 4, bytes_accessed=rows * width * 8, transcendentals=0),
        name="cross",
    )(info, e, rounded_t)


def factor_kernel(me, kept, got, triangle, high, low, work):
    k = triangle.shape[0]
    half = k // 2
    own = me[0] & 1
    work[pl.ds(pl.multiple_of(own * half, half), half), :k] = kept[...]
    work[pl.ds(pl.multiple_of((1 - own) * half, half), half), :k] = got[...]
    b = 64
    rows_k = lax.broadcasted_iota(jnp.int32, (k, k), 0)
    cols_k = lax.broadcasted_iota(jnp.int32, (k, k), 1)
    work[:, k:] = jnp.where(rows_k == cols_k, 1.0, 0.0)
    lane = lax.broadcasted_iota(jnp.int32, (8, 2 * b), 1)
    sub = lax.broadcasted_iota(jnp.int32, (8, 2 * b), 0)
    for n in range(k // b):
        first = (n % 2) * b
        pair = (n // 2) * 2 * b
        own_lanes = (lane >= first) & (lane < first + b)
        w = []
        for v in range(b // 8):
            a = work[n * b + 8 * v : n * b + 8 * v + 8, pair : pair + 2 * b]
            ident = jnp.where(lane == (b - first) + 8 * v + sub, 1.0, 0.0)
            w.append(jnp.where(own_lanes, a, ident))
        for j in range(b):
            v0, r = divmod(j, 8)
            row = jnp.broadcast_to(w[v0][r : r + 1, :], (8, 2 * b))
            pivot = jnp.broadcast_to(row[:, first + j : first + j + 1], (8, 2 * b))
            row = row * (1.0 / pivot)
            for v in range(v0, b // 8):
                col = jnp.broadcast_to(w[v][:, first + j : first + j + 1], (8, 2 * b))
                if v == v0:
                    if r == 7:
                        continue
                    col = jnp.where(sub > r, col, 0.0)
                w[v] = w[v] - col * row
        inv = []
        for v in range(b // 8):
            diag = jnp.sum(jnp.where(lane == first + 8 * v + sub, w[v], 0.0), axis=1, keepdims=True)
            moved = pltpu.roll(w[v], b, 1)
            inv.append(jnp.where(own_lanes, moved * (1.0 / jnp.sqrt(diag)), 0.0))
        inv = jnp.concatenate(inv, axis=0)
        y = lax.dot_general(
            inv, work[pair : pair + 2 * b, :], (((1,), (0,)), ((), ())),
            precision=lax.Precision.HIGHEST, preferred_element_type=jnp.float32,
        )
        r_rows, i_rows = y[:, :k], y[:, k:]
        at = lax.broadcasted_iota(jnp.int32, (b, k), 0) + n * b
        to = lax.broadcasted_iota(jnp.int32, (b, k), 1)
        triangle[n * b : (n + 1) * b, :] = jnp.where(to >= at, r_rows, 0.0)
        i_rows = jnp.where(to <= at, i_rows, 0.0)
        i_high, i_low = split(i_rows)
        high[n * b : (n + 1) * b, :] = i_high
        low[n * b : (n + 1) * b, :] = i_low
        if (n + 1) * b < k:
            later = jnp.where(to >= (n + 1) * b, r_rows, 0.0)
            work[...] -= lax.dot_general(
                later, y, (((0,), (0,)), ((), ())),
                precision=lax.Precision.HIGHEST, preferred_element_type=jnp.float32,
            )


def factor_call(me, kept, got):
    k = kept.shape[1]
    whole = lambda shape: pl.BlockSpec(shape, lambda i, me: (0, 0))
    return pl.pallas_call(
        factor_kernel,
        grid_spec=pltpu.PrefetchScalarGridSpec(
            num_scalar_prefetch=1,
            grid=(1,),
            in_specs=[whole((k // 2, k))] * 2,
            out_specs=[whole((k, k))] * 3,
            scratch_shapes=[pltpu.VMEM((k, 2 * k), jnp.float32)],
        ),
        out_shape=[
            jax.ShapeDtypeStruct((k, k), jnp.float32),
            jax.ShapeDtypeStruct((k, k), jnp.bfloat16),
            jax.ShapeDtypeStruct((k, k), jnp.bfloat16),
        ],
        compiler_params=pltpu.CompilerParams(vmem_limit_bytes=24 * MIB),
        cost_estimate=pl.CostEstimate(flops=10**10, bytes_accessed=k * k * 8, transcendentals=0),
        name="factor",
    )(me, kept, got)


def basis_kernel(sketch, high, low, out):
    s_high, s_low = split(sketch[...])
    right = ((1,), (1,))
    out[...] = (
        dot(s_high, high[...], right) + (dot(s_high, low[...], right) + dot(s_low, high[...], right))
    ).astype(out.dtype)


def basis_call(sketch, high, low):
    rows, k = sketch.shape
    block = 512
    whole = pl.BlockSpec((k, k), lambda i: (0, 0))
    return pl.pallas_call(
        basis_kernel,
        grid=(rows // block,),
        in_specs=[pl.BlockSpec((block, k), lambda i: (i, 0)), whole, whole],
        out_specs=pl.BlockSpec((block, k), lambda i: (i, 0)),
        out_shape=jax.ShapeDtypeStruct((rows, k), jnp.bfloat16),
        compiler_params=pltpu.CompilerParams(vmem_limit_bytes=24 * MIB),
        cost_estimate=pl.CostEstimate(flops=6 * rows * k * k, bytes_accessed=rows * k * 6, transcendentals=0),
        name="basis",
    )(sketch, high, low)


def project_kernel(groups, info, high, low, *refs):
    *blocks, out = refs[-5:]
    which = pl.program_id(0)
    for n, block in enumerate(blocks):

        @pl.when(which == n)
        def _(n=n, block=block):
            size = block.shape[1] // groups
            order = info[8 + n // 2]
            value = jnp.concatenate(
                [block[0, pl.ds(pl.multiple_of((order ^ g) * size, size), size), :] for g in range(groups)], axis=0
            )
            c_high, c_low = split(value)
            out[...] = dot(high[...], c_high) + (dot(high[...], c_low) + dot(low[...], c_high))


def project_call(info, high, low, blocks, groups, d, before):
    per, k, width = blocks[0].shape
    whole = pl.BlockSpec((k, k), lambda i, j, info: (0, 0))
    pick = lambda n: lambda i, j, info: (jnp.where(i < n, 0, jnp.where(i > n, per - 1, j)), 0, 0)
    extra = [] if before is None else [before]
    return pl.pallas_call(
        functools.partial(project_kernel, groups),
        grid_spec=pltpu.PrefetchScalarGridSpec(
            num_scalar_prefetch=1,
            grid=(4, per),
            in_specs=[whole, whole]
            + [pl.BlockSpec(memory_space=pl.ANY)] * len(extra)
            + [pl.BlockSpec((1, k, width), pick(n)) for n in range(4)],
            out_specs=pl.BlockSpec((k, width), lambda i, j, info: (0, info[i * per + j])),
        ),
        out_shape=jax.ShapeDtypeStruct((k, d), jnp.float32),
        input_output_aliases={3: 0} if extra else {},
        compiler_params=pltpu.CompilerParams(vmem_limit_bytes=24 * MIB),
        cost_estimate=pl.CostEstimate(flops=6 * k * k * width * 8, bytes_accessed=k * width * 64, transcendentals=0),
        name="project",
    )(info, high, low, *extra, *blocks)


def solution(mesh):
    n_devices = math.prod(mesh.shape.values())
    orders = orders_of(n_devices)
    steps = len(orders[0])
    groups = 1 << (steps - 2)
    pairs = [(i, i ^ 1) for i in range(n_devices)]
    swaps = [[(i, i ^ (1 << orders[i & 1][s])) for i in range(n_devices)] for s in range(steps)]

    def with_pair(a):
        return lax.ppermute(a, AXES, pairs)

    def swap(a, s):
        return lax.ppermute(a, AXES, swaps[s])

    def shards(e, signs):
        rows_all = e.shape[0] * n_devices
        d = e.shape[1]
        width = d // (8 * CHUNKS)
        me = lax.axis_index(AXES).astype(jnp.int32)
        own = me & 1
        place = [bits_of(me, o[:2]) for o in orders]
        rest = [bits_of(me, o[2:]) for o in orders]
        mine = lambda pair: jnp.where(own == 0, pair[0], pair[1])
        other = lambda pair: jnp.where(own == 0, pair[1], pair[0])

        def blocks_at(chunk, region, at):
            return [(chunk * 2 + region) * 4 + (at ^ n) for n in range(4)]

        def vector(*values):
            return jnp.stack([jnp.asarray(v, jnp.int32) for v in values])

        me1 = me[None]
        sketch, rounded_t, gram_sent, gram = sketch_call(me1, e, signs, rows_all)

        gram = gram + with_pair(gram_sent)
        for s in range(steps):
            gram = gram + swap(gram, s)
        triangle, high, low = factor_call(me1, gram, with_pair(gram))

        projected = None
        for chunk in range(CHUNKS):
            own_at = blocks_at(chunk, own, mine(place))
            other_at = blocks_at(chunk, 1 - own, other(place))
            scale = 1.0 / math.sqrt(rows_all)
            (sent,) = cross_call(vector(*other_at, other(rest)), e, rounded_t, scale, groups, width, 1)
            kept, first = cross_call(vector(*own_at, mine(rest)), e, rounded_t, scale, groups, width, 2)
            got = with_pair(sent)
            r = swap(first + got[2:], 0)
            kept = kept + got[:2]
            r2 = swap(kept[1] + r[1], 1)
            a = kept[0] + r[0] + r2
            for s in range(2, steps):
                half = a.shape[0] // 2
                a = a[:half] + swap(a[half:], s)
            for s in range(steps - 1, 1, -1):
                a = jnp.concatenate([a, swap(a, s)], axis=0)
            a = jnp.stack([a, swap(a, 1)])
            a2 = swap(a, 0)
            b = with_pair(a)
            b2 = with_pair(a2)
            info = vector(*own_at, *other_at, mine(rest), other(rest))
            projected = project_call(info, high, low, [a, a2, b, b2], groups, d, projected)
        basis = basis_call(sketch, high, low)
        return triangle, basis, projected

    return jax.shard_map(
        shards,
        mesh=mesh,
        in_specs=(P(AXES, None), P()),
        out_specs=(P(), P(AXES, None), P()),
        check_vma=False,
    )
```

time: 259 us -> 188 us (0.73)
  Pallas kernels: 0 us -> 74 us
  waiting for transfers between devices: 146 us -> 78.7 us
  other arithmetic: 57.4 us -> 2.61 us
  matrix products: 32 us -> 0 us
  starting transfers between devices: 0.04 us -> 29.3 us
  between operations: 15.5 us -> 0.78 us
  local copies, waits for them, and re-layouts: 7.28 us -> 2.47 us
    psum x1 -> x0, waiting for transfers between devices: 146 us -> none  [shards(): lower = jnp.linalg.cholesky(lax.psum(gram, ('gx', 'gy')))]
    ppermute x0 -> x17, waiting for transfers between devices: none -> 78.7 us  [the longest x12 76.7 us: swap(): return lax.ppermute(a, AXES, swaps[s])]
    pallas_call x0 -> x6, Pallas kernels: none -> 74 us  [the longest x1 36.8 us: factor_call(): pl.pallas_call(factor_kernel, grid_spec=pltpu.PrefetchScalarGridSpec(num_...]
    another operation x11 -> x2, other arithmetic: 56.4 us -> 0.2 us  [shards(): a = jnp.stack([a, swap(a, 1)])]
    ppermute x0 -> x17, starting transfers between devices: none -> 29.3 us  [the longest x12 28.2 us: swap(): return lax.ppermute(a, AXES, swaps[s])]
    dot_general x3 -> x0, matrix products: 20.1 us -> none  [the longest x1 9.9 us: shards(): jnp.dot(embeddings, signs.astype(jnp.bfloat16), preferred_element_type=jn...]
    another operation x8 -> x0, matrix products: 11.9 us -> none  [the longest x3 7.49 us: shards(): lax.linalg.triangular_solve(lower, cross, left_side=True, lower=True)]
    another operation x9 -> x3, local copies, waits for them, and re-layouts: 4.05 us -> 0.25 us  [vector(): return jnp.stack([jnp.asarray(v, jnp.int32) for v in values])]
  transfers between devices with their start and end apart: 1 -> 17, of which waited for: 1 -> 13; matrix products, arithmetic and copies ran while one was open for 0% -> 0% of each run, Pallas kernels for 0% -> 24%
where the time goes in v1:
time: 188 us
  waiting for transfers between devices  78.7 us (42%)
  Pallas kernels  74 us (39%)
  starting transfers between devices  29.3 us (16%)
  other arithmetic  2.61 us (1%)
  local copies, waits for them, and re-layouts  2.47 us (1%)
    ppermute x12, waiting for transfers between devices, swap(): return lax.ppermute(a, AXES, swaps[s])  76.7 us
    pallas_call x1, Pallas kernels, factor_call(): pl.pallas_call(factor_kernel, grid_spec=pltpu.PrefetchScalarGridSpec(num_...  36.8 us
    ppermute x12, starting transfers between devices, swap(): return lax.ppermute(a, AXES, swaps[s])  28.2 us
    pallas_call x2, Pallas kernels, cross_call(): pl.pallas_call(functools.partial(cross_kernel, scale, groups), grid_spec=...  13.3 us
    pallas_call x1, Pallas kernels, sketch_call(): pl.pallas_call(functools.partial(sketch_kernel, 1.0 / math.sqrt(d), 1.0 /...  12.6 us
    pallas_call x1, Pallas kernels, project_call(): pl.pallas_call(functools.partial(project_kernel, groups), grid_spec=pltpu...  8.68 us
  transfers between devices with their start and end apart: 17, of which 13 were waited for; matrix products, arithmetic and copies ran while one was open for 0% of the time, Pallas kernels for 24%

profile of v1, /device:TPU:0, one launch (start us, length us, event | category | flops | bytes accessed | tf_op | source)
XLA Modules:
  0.0 187.9 jit_solution(16603671850888048033)
XLA Ops:
  0.7 2.2 %copy-done = s32[4096,256]{1,0:T(8,128)S(1)} copy-done((s32[4096,256]{1,0:T(8,128)S(1)}, s32[4096,256]{1,0:T(8,128)}, u32[]{:S(2)}) %copy-start) | copy-done | bytes 4194328
  2.9 12.6 %sketch.1 = (f32[2048,256]{1,0:T(8,128)S(1)}, bf16[256,2048]{1,0:T(8,128)(2,1)S(1)}, f32[128,256]{1,0:T(8,128)S(1)}, f32[128,256]{1,0:T(8,128)S(1)}) custom-call(s32[1]{0:T(128)} %bitcast.me, bf16[2048,4096]{1,0:T(8,128)(2,1)} %e.5, s32[4096,256]{1,0:T(8,128)S(1)} %copy-done), custom_call_target="tpu_custom_call" | custom-call | flops 4294967296 | bytes 20971520 | tf_op jit(solution)/shard_map/sketch/pallas_call | solution.py:71
  15.4 0.1 stack.70.info
  15.5 7.2 %cross.3 = f32[4,256,512]{2,1,0:T(8,128)} custom-call(s32[5]{0:T(128)S(1)} %stack.70.info, bf16[2048,4096]{1,0:T(8,128)(2,1)} %e.5, bf16[256,2048]{1,0:T(8,128)(2,1)S(1)} %get-tuple-element.18.rounded_t), custom_call_target="tpu_custom_call" | custom-call | flops 2147483648 | bytes 8388608 | tf_op jit(solution)/shard_map/cross/pallas_call | solution.py:122
  22.7 0.4 collective-permute-start.6
  23.1 0.1 stack.69.info
  23.2 6.2 %cross.2 = (f32[2,256,512]{2,1,0:T(8,128)S(1)}, f32[2,256,512]{2,1,0:T(8,128)S(1)}) custom-call(s32[5]{0:T(128)S(1)} %stack.69.info, bf16[2048,4096]{1,0:T(8,128)(2,1)} %e.5, bf16[256,2048]{1,0:T(8,128)(2,1)S(1)} %get-tuple-element.18.rounded_t), custom_call_target="tpu_custom_call" | custom-call | flops 2147483648 | bytes 8388608 | tf_op jit(solution)/shard_map/cross/pallas_call | solution.py:122
  29.4 0.0 collective-permute-done.6
  29.4 2.0 %slice_add_fusion.1 = (f32[2,256,512]{2,1,0:T(8,128)S(1)}, f32[2,256,512]{2,1,0:T(8,128)S(1)}) fusion(f32[2,256,512]{2,1,0:T(8,128)S(1)} %get-tuple-element.19, f32[4,256,512]{2,1,0:T(8,128)} %collective-permute-done.6, f32[2,256,512]{2,1,0:T(8,128)S(1)} %get-tuple-element.20), kind=kLoop, calls=%fused_computation.1 | loop fusion | flops 524288 | bytes 6291456 | tf_op jit(solution)/shard_map/add | solution.py:336
  31.4 2.6 %collective-permute-start.7 = (f32[2,256,512]{2,1,0:T(8,128)S(1)}, f32[2,256,512]{2,1,0:T(8,128)S(1)}, u32[]{:S(2)}, u32[]{:S(2)}) collective-permute-start(f32[2,256,512]{2,1,0:T(8,128)S(1)} %get-tuple-element.22), channel_id=1, source_target_pairs={{0,2},{1,5},{2,0},{3,7},{4,6},{5,1},{6,4},{7,3},{8,10},{9,13},{10,... | collective-permute-start | bytes 3145736 | tf_op jit(solution)/shard_map/ppermute | solution.py:300
  34.0 12.8 %collective-permute-done.7 = f32[2,256,512]{2,1,0:T(8,128)S(1)} collective-permute-done((f32[2,256,512]{2,1,0:T(8,128)S(1)}, f32[2,256,512]{2,1,0:T(8,128)S(1)}, u32[]{:S(2)}, u32[]{:S(2)}) %collective-permute-start.7) | collective-permute-done | bytes 1048608 | tf_op jit(solution)/shard_map/ppermute | solution.py:300
  46.8 0.1 fusion
  46.9 2.1 %collective-permute-start.8 = (f32[256,512]{1,0:T(8,128)S(1)}, f32[256,512]{1,0:T(8,128)S(1)}, u32[]{:S(2)}, u32[]{:S(2)}) collective-permute-start(f32[256,512]{1,0:T(8,128)S(1)} %fusion), channel_id=1, source_target_pairs={{0,4},{1,3},{2,6},{3,1},{4,0},{5,7},{6,2},{7,5},{8,12},{9,11},{10,... | collective-permute-start | bytes 1572872 | tf_op jit(solution)/shard_map/ppermute | solution.py:300
  49.0 7.2 %collective-permute-done.8 = f32[256,512]{1,0:T(8,128)S(1)} collective-permute-done((f32[256,512]{1,0:T(8,128)S(1)}, f32[256,512]{1,0:T(8,128)S(1)}, u32[]{:S(2)}, u32[]{:S(2)}) %collective-permute-start.8) | collective-permute-done | bytes 524320 | tf_op jit(solution)/shard_map/ppermute | solution.py:300
  56.1 0.1 fusion.2
  56.3 2.1 %collective-permute-start.9 = (f32[128,512]{1,0:T(8,128)S(1)}, f32[128,512]{1,0:T(8,128)S(1)}, u32[]{:S(2)}, u32[]{:S(2)}) collective-permute-start(f32[128,512]{1,0:T(8,128)S(1)} %slice.47), channel_id=1, source_target_pairs={{0,8},{1,17},{2,10},{3,19},{4,12},{5,21},{6,14},{7,23},{8,0},{9,25... | collective-permute-start | bytes 786440 | tf_op jit(solution)/shard_map/ppermute | solution.py:300
  58.4 5.5 %collective-permute-done.9 = f32[128,512]{1,0:T(8,128)S(1)} collective-permute-done((f32[128,512]{1,0:T(8,128)S(1)}, f32[128,512]{1,0:T(8,128)S(1)}, u32[]{:S(2)}, u32[]{:S(2)}) %collective-permute-start.9) | collective-permute-done | bytes 262176 | tf_op jit(solution)/shard_map/ppermute | solution.py:300
  64.0 3.7 %collective-permute-start.10 = (f32[64,512]{1,0:T(8,128)S(1)}, f32[64,512]{1,0:T(8,128)S(1)}, u32[]{:S(2)}, u32[]{:S(2)}) collective-permute-start(f32[64,512]{1,0:T(8,128)S(1)} %slice.49), channel_id=1, source_target_pairs={{0,16},{1,9},{2,18},{3,11},{4,20},{5,13},{6,22},{7,15},{8,24},{9,1... | collective-permute-start | bytes 393224 | tf_op jit(solution)/shard_map/ppermute | solution.py:300
  67.8 3.0 %collective-permute-done.10 = f32[64,512]{1,0:T(8,128)S(1)} collective-permute-done((f32[64,512]{1,0:T(8,128)S(1)}, f32[64,512]{1,0:T(8,128)S(1)}, u32[]{:S(2)}, u32[]{:S(2)}) %collective-permute-start.10) | collective-permute-done | bytes 131104 | tf_op jit(solution)/shard_map/ppermute | solution.py:300
  70.8 3.5 %collective-permute-start.11 = (f32[64,512]{1,0:T(8,128)S(1)}, f32[64,512]{1,0:T(8,128)S(1)}, u32[]{:S(2)}, u32[]{:S(2)}) collective-permute-start(f32[64,512]{1,0:T(8,128)S(1)} %slice_add_fusion.5), channel_id=1, source_target_pairs={{0,16},{1,9},{2,18},{3,11},{4,20},{5,13},{6,22},{7,15},{8,24},{9,1... | collective-permute-start | bytes 393224 | tf_op jit(solution)/shard_map/ppermute | solution.py:300
  74.2 8.0 %collective-permute-done.11 = f32[64,512]{1,0:T(8,128)S(1)} collective-permute-done((f32[64,512]{1,0:T(8,128)S(1)}, f32[64,512]{1,0:T(8,128)S(1)}, u32[]{:S(2)}, u32[]{:S(2)}) %collective-permute-start.11) | collective-permute-done | bytes 131104 | tf_op jit(solution)/shard_map/ppermute | solution.py:300
  82.2 1.6 collective-permute-start.12
  83.9 4.8 %collective-permute-done.12 = f32[128,512]{1,0:T(8,128)S(1)} collective-permute-done((f32[128,512]{1,0:T(8,128)S(1)}, f32[128,512]{1,0:T(8,128)S(1)}, u32[]{:S(2)}, u32[]{:S(2)}) %collective-permute-start.12) | collective-permute-done | bytes 262176 | tf_op jit(solution)/shard_map/ppermute | solution.py:300
  88.7 0.1 fusion.3
  88.8 1.5 collective-permute-start.13
  90.4 10.6 %collective-permute-done.13 = f32[256,512]{1,0:T(8,128)S(1)} collective-permute-done((f32[256,512]{1,0:T(8,128)S(1)}, f32[256,512]{1,0:T(8,128)S(1)}, u32[]{:S(2)}, u32[]{:S(2)}) %collective-permute-start.13) | collective-permute-done | bytes 524320 | tf_op jit(solution)/shard_map/ppermute | solution.py:300
  101.0 0.1 pad_maximum_fusion.refs_0_
  101.1 1.6 collective-permute-start.14
  102.7 1.3 collective-permute-done
  104.0 0.6 collective-permute-start.1
  104.6 14.1 %collective-permute-done.1 = f32[128,256]{1,0:T(8,128)S(1)} collective-permute-done((f32[128,256]{1,0:T(8,128)S(1)}, f32[128,256]{1,0:T(8,128)S(1)}, u32[]{:S(2)}, u32[]{:S(2)}) %collective-permute-start.1) | collective-permute-done | bytes 131104 | tf_op jit(solution)/shard_map/ppermute | solution.py:300
  118.8 1.3 collective-permute-start.2
  120.1 3.7 %collective-permute-done.2 = f32[128,256]{1,0:T(8,128)S(1)} collective-permute-done((f32[128,256]{1,0:T(8,128)S(1)}, f32[128,256]{1,0:T(8,128)S(1)}, u32[]{:S(2)}, u32[]{:S(2)}) %collective-permute-start.2) | collective-permute-done | bytes 131104 | tf_op jit(solution)/shard_map/ppermute | solution.py:300
  123.8 2.0 %collective-permute-start.3 = (f32[128,256]{1,0:T(8,128)S(1)}, f32[128,256]{1,0:T(8,128)S(1)}, u32[]{:S(2)}, u32[]{:S(2)}) collective-permute-start(f32[128,256]{1,0:T(8,128)S(1)} %add.84), channel_id=1, source_target_pairs={{0,8},{1,17},{2,10},{3,19},{4,12},{5,21},{6,14},{7,23},{8,0},{9,25... | collective-permute-start | bytes 393224 | tf_op jit(solution)/shard_map/ppermute | solution.py:300
  125.8 3.1 %collective-permute-done.3 = f32[128,256]{1,0:T(8,128)S(1)} collective-permute-done((f32[128,256]{1,0:T(8,128)S(1)}, f32[128,256]{1,0:T(8,128)S(1)}, u32[]{:S(2)}, u32[]{:S(2)}) %collective-permute-start.3) | collective-permute-done | bytes 131104 | tf_op jit(solution)/shard_map/ppermute | solution.py:300
  128.9 5.6 %collective-permute-start.4 = (f32[128,256]{1,0:T(8,128)S(1)}, f32[128,256]{1,0:T(8,128)S(1)}, u32[]{:S(2)}, u32[]{:S(2)}) collective-permute-start(f32[128,256]{1,0:T(8,128)S(1)} %add.85), channel_id=1, source_target_pairs={{0,16},{1,9},{2,18},{3,11},{4,20},{5,13},{6,22},{7,15},{8,24},{9,1... | collective-permute-start | bytes 393224 | tf_op jit(solution)/shard_map/ppermute | solution.py:300
  134.5 3.8 %collective-permute-done.4 = f32[128,256]{1,0:T(8,128)S(1)} collective-permute-done((f32[128,256]{1,0:T(8,128)S(1)}, f32[128,256]{1,0:T(8,128)S(1)}, u32[]{:S(2)}, u32[]{:S(2)}) %collective-permute-start.4) | collective-permute-done | bytes 131104 | tf_op jit(solution)/shard_map/ppermute | solution.py:300
  138.3 0.1 collective-permute-start.5
  138.4 0.5 collective-permute-start.15
  138.9 0.0 collective-permute-done.14.refs_1_
  138.9 0.1 collective-permute-start.16
  139.0 0.1 stack.68.info
  139.1 0.7 collective-permute-done.5.got
  139.8 36.8 %factor.1 = (f32[256,256]{1,0:T(8,128)}, bf16[256,256]{1,0:T(8,128)(2,1)S(1)}, bf16[256,256]{1,0:T(8,128)(2,1)S(1)}) custom-call(s32[1]{0:T(128)} %bitcast.me, f32[128,256]{1,0:T(8,128)S(1)} %add.86.kept, f32[128,256]{1,0:T(8,128)S(1)} %collective-permute-done.5.got), custom_call_target="tpu_custom_call" | custom-call | flops 10000000000 | bytes 524288 | tf_op jit(solution)/shard_map/factor/pallas_call | solution.py:205
  176.6 2.6 %basis.1 = bf16[2048,256]{1,0:T(8,128)(2,1)} custom-call(f32[2048,256]{1,0:T(8,128)S(1)} %get-tuple-element.15.sketch, bf16[256,256]{1,0:T(8,128)(2,1)S(1)} %get-tuple-element.16.high, bf16[256,256]{1,0:T(8,128)(2,1)S(1)} %get-tuple-element.17.low), custom_call_target="tpu_custom_call" | custom-call | flops 805306368 | bytes 3145728 | tf_op jit(solution)/shard_map/basis/pallas_call | solution.py:237
  179.2 0.0 collective-permute-done.15.refs_2_
  179.2 0.0 collective-permute-done.16.refs_3_
  179.2 8.7 %project.1 = f32[256,4096]{1,0:T(8,128)} custom-call(s32[10]{0:T(128)S(1)} %stack.68.info, bf16[256,256]{1,0:T(8,128)(2,1)S(1)} %get-tuple-element.16.high, bf16[256,256]{1,0:T(8,128)(2,1)S(1)} %get-tuple-element.17.low, f32[2,256,512]{2,1,0:T(8,128)S(1)} %pad_maximum_fusion.refs_0_, f32[2,256,512]{2,1,0:T(8,128)} %collective-permute-done.14.refs_1_, ...), custom_call_target="tpu_custom_call" | custom-call | flops 1610612736 | bytes 8388608 | tf_op jit(solution)/shard_map/project/pallas_call | solution.py:270
  (12 shorter events, 0.2 us)
Async XLA Ops:
  0.7 2.2 %copy-start = (s32[4096,256]{1,0:T(8,128)S(1)}, s32[4096,256]{1,0:T(8,128)}, u32[]{:S(2)}) copy-start(s32[4096,256]{1,0:T(8,128)} %signs.1) | copy-start | bytes 12582916
  22.7 6.7 %collective-permute-start.6 = (f32[4,256,512]{2,1,0:T(8,128)}, f32[4,256,512]{2,1,0:T(8,128)}, u32[]{:S(2)}, u32[]{:S(2)}) collective-permute-start(f32[4,256,512]{2,1,0:T(8,128)} %cross.3), channel_id=1, source_target_pairs={{0,1},{1,0},{2,3},{3,2},{4,5},{5,4},{6,7},{7,6},{8,9},{9,8},{10,11... | collective-permute-start | bytes 6291464 | tf_op jit(solution)/shard_map/ppermute | solution.py:297
  31.4 15.3 %collective-permute-start.7 = (f32[2,256,512]{2,1,0:T(8,128)S(1)}, f32[2,256,512]{2,1,0:T(8,128)S(1)}, u32[]{:S(2)}, u32[]{:S(2)}) collective-permute-start(f32[2,256,512]{2,1,0:T(8,128)S(1)} %get-tuple-element.22), channel_id=1, source_target_pairs={{0,2},{1,5},{2,0},{3,7},{4,6},{5,1},{6,4},{7,3},{8,10},{9,13},{10,... | collective-permute-start | bytes 3145736 | tf_op jit(solution)/shard_map/ppermute | solution.py:300
  46.9 9.3 %collective-permute-start.8 = (f32[256,512]{1,0:T(8,128)S(1)}, f32[256,512]{1,0:T(8,128)S(1)}, u32[]{:S(2)}, u32[]{:S(2)}) collective-permute-start(f32[256,512]{1,0:T(8,128)S(1)} %fusion), channel_id=1, source_target_pairs={{0,4},{1,3},{2,6},{3,1},{4,0},{5,7},{6,2},{7,5},{8,12},{9,11},{10,... | collective-permute-start | bytes 1572872 | tf_op jit(solution)/shard_map/ppermute | solution.py:300
  56.3 7.7 %collective-permute-start.9 = (f32[128,512]{1,0:T(8,128)S(1)}, f32[128,512]{1,0:T(8,128)S(1)}, u32[]{:S(2)}, u32[]{:S(2)}) collective-permute-start(f32[128,512]{1,0:T(8,128)S(1)} %slice.47), channel_id=1, source_target_pairs={{0,8},{1,17},{2,10},{3,19},{4,12},{5,21},{6,14},{7,23},{8,0},{9,25... | collective-permute-start | bytes 786440 | tf_op jit(solution)/shard_map/ppermute | solution.py:300
  64.0 6.7 %collective-permute-start.10 = (f32[64,512]{1,0:T(8,128)S(1)}, f32[64,512]{1,0:T(8,128)S(1)}, u32[]{:S(2)}, u32[]{:S(2)}) collective-permute-start(f32[64,512]{1,0:T(8,128)S(1)} %slice.49), channel_id=1, source_target_pairs={{0,16},{1,9},{2,18},{3,11},{4,20},{5,13},{6,22},{7,15},{8,24},{9,1... | collective-permute-start | bytes 393224 | tf_op jit(solution)/shard_map/ppermute | solution.py:300
  70.8 11.4 %collective-permute-start.11 = (f32[64,512]{1,0:T(8,128)S(1)}, f32[64,512]{1,0:T(8,128)S(1)}, u32[]{:S(2)}, u32[]{:S(2)}) collective-permute-start(f32[64,512]{1,0:T(8,128)S(1)} %slice_add_fusion.5), channel_id=1, source_target_pairs={{0,16},{1,9},{2,18},{3,11},{4,20},{5,13},{6,22},{7,15},{8,24},{9,1... | collective-permute-start | bytes 393224 | tf_op jit(solution)/shard_map/ppermute | solution.py:300
  82.2 6.4 %collective-permute-start.12 = (f32[128,512]{1,0:T(8,128)S(1)}, f32[128,512]{1,0:T(8,128)S(1)}, u32[]{:S(2)}, u32[]{:S(2)}) collective-permute-start(f32[128,512]{1,0:T(8,128)S(1)} %pad_maximum_fusion.2), channel_id=1, source_target_pairs={{0,8},{1,17},{2,10},{3,19},{4,12},{5,21},{6,14},{7,23},{8,0},{9,25... | collective-permute-start | bytes 786440 | tf_op jit(solution)/shard_map/ppermute | solution.py:300
  88.8 12.2 %collective-permute-start.13 = (f32[256,512]{1,0:T(8,128)S(1)}, f32[256,512]{1,0:T(8,128)S(1)}, u32[]{:S(2)}, u32[]{:S(2)}) collective-permute-start(f32[256,512]{1,0:T(8,128)S(1)} %get-tuple-element.24), channel_id=1, source_target_pairs={{0,4},{1,3},{2,6},{3,1},{4,0},{5,7},{6,2},{7,5},{8,12},{9,11},{10,... | collective-permute-start | bytes 1572872 | tf_op jit(solution)/shard_map/ppermute | solution.py:300
  101.1 37.8 %collective-permute-start.14 = (f32[2,256,512]{2,1,0:T(8,128)S(1)}, f32[2,256,512]{2,1,0:T(8,128)}, u32[]{:S(2)}, u32[]{:S(2)}) collective-permute-start(f32[2,256,512]{2,1,0:T(8,128)S(1)} %pad_maximum_fusion.refs_0_), channel_id=1, source_target_pairs={{0,2},{1,5},{2,0},{3,7},{4,6},{5,1},{6,4},{7,3},{8,10},{9,13},{10,... | collective-permute-start | bytes 3145736 | tf_op jit(solution)/shard_map/ppermute | solution.py:300
  102.7 1.3 collective-permute-start
  104.0 14.7 %collective-permute-start.1 = (f32[128,256]{1,0:T(8,128)S(1)}, f32[128,256]{1,0:T(8,128)S(1)}, u32[]{:S(2)}, u32[]{:S(2)}) collective-permute-start(f32[128,256]{1,0:T(8,128)S(1)} %add.82), channel_id=1, source_target_pairs={{0,2},{1,5},{2,0},{3,7},{4,6},{5,1},{6,4},{7,3},{8,10},{9,13},{10,... | collective-permute-start | bytes 393224 | tf_op jit(solution)/shard_map/ppermute | solution.py:300
  118.8 5.0 %collective-permute-start.2 = (f32[128,256]{1,0:T(8,128)S(1)}, f32[128,256]{1,0:T(8,128)S(1)}, u32[]{:S(2)}, u32[]{:S(2)}) collective-permute-start(f32[128,256]{1,0:T(8,128)S(1)} %add.83), channel_id=1, source_target_pairs={{0,4},{1,3},{2,6},{3,1},{4,0},{5,7},{6,2},{7,5},{8,12},{9,11},{10,... | collective-permute-start | bytes 393224 | tf_op jit(solution)/shard_map/ppermute | solution.py:300
  123.8 5.0 %collective-permute-start.3 = (f32[128,256]{1,0:T(8,128)S(1)}, f32[128,256]{1,0:T(8,128)S(1)}, u32[]{:S(2)}, u32[]{:S(2)}) collective-permute-start(f32[128,256]{1,0:T(8,128)S(1)} %add.84), channel_id=1, source_target_pairs={{0,8},{1,17},{2,10},{3,19},{4,12},{5,21},{6,14},{7,23},{8,0},{9,25... | collective-permute-start | bytes 393224 | tf_op jit(solution)/shard_map/ppermute | solution.py:300
  128.9 9.4 %collective-permute-start.4 = (f32[128,256]{1,0:T(8,128)S(1)}, f32[128,256]{1,0:T(8,128)S(1)}, u32[]{:S(2)}, u32[]{:S(2)}) collective-permute-start(f32[128,256]{1,0:T(8,128)S(1)} %add.85), channel_id=1, source_target_pairs={{0,16},{1,9},{2,18},{3,11},{4,20},{5,13},{6,22},{7,15},{8,24},{9,1... | collective-permute-start | bytes 393224 | tf_op jit(solution)/shard_map/ppermute | solution.py:300
  138.3 1.4 collective-permute-start.5
  138.4 40.8 %collective-permute-start.15 = (f32[2,256,512]{2,1,0:T(8,128)S(1)}, f32[2,256,512]{2,1,0:T(8,128)}, u32[]{:S(2)}, u32[]{:S(2)}) collective-permute-start(f32[2,256,512]{2,1,0:T(8,128)S(1)} %pad_maximum_fusion.refs_0_), channel_id=1, source_target_pairs={{0,1},{1,0},{2,3},{3,2},{4,5},{5,4},{6,7},{7,6},{8,9},{9,8},{10,11... | collective-permute-start | bytes 3145736 | tf_op jit(solution)/shard_map/ppermute | solution.py:297
  138.9 40.3 %collective-permute-start.16 = (f32[2,256,512]{2,1,0:T(8,128)}, f32[2,256,512]{2,1,0:T(8,128)}, u32[]{:S(2)}, u32[]{:S(2)}) collective-permute-start(f32[2,256,512]{2,1,0:T(8,128)} %collective-permute-done.14.refs_1_), channel_id=1, source_target_pairs={{0,1},{1,0},{2,3},{3,2},{4,5},{5,4},{6,7},{7,6},{8,9},{9,8},{10,11... | collective-permute-start | bytes 3145736 | tf_op jit(solution)/shard_map/ppermute | solution.py:297

commit v2 on v0

v2 whole, which is shorter than its diff:
```python
import functools
import math

import jax
import jax.numpy as jnp
from jax import lax
from jax.experimental import pallas as pl
from jax.experimental.pallas import tpu as pltpu
from jax.sharding import PartitionSpec as P

AXES = ("gx", "gy")
CHUNKS = 2
MIB = 1 << 20


def dot(a, b, dims=((1,), (0,))):
    return lax.dot_general(a, b, (dims, ((), ())), preferred_element_type=jnp.float32)


def split(a):
    high = a.astype(jnp.bfloat16)
    return high, (a - high.astype(jnp.float32)).astype(jnp.bfloat16)


def orders_of(n_devices):
    bits = list(range(1, n_devices.bit_length() - 1))
    swapped = bits[:]
    for i in range(0, len(bits) - 1, 2):
        swapped[i], swapped[i + 1] = bits[i + 1], bits[i]
    return bits, swapped


def bits_of(me, order):
    value = jnp.int32(0)
    for b in order:
        value = value * 2 + ((me >> b) & 1)
    return value


def in_vmem(*shape_dtype):
    return pltpu.VMEM(*shape_dtype)


def pinned(*arrays):
    return [pltpu.with_memory_space_constraint(a, pltpu.VMEM) for a in arrays]


VMEM_SPEC = pl.BlockSpec(memory_space=pltpu.VMEM)
SMEM_SPEC = pl.BlockSpec(memory_space=pltpu.SMEM)
ANY_SPEC = pl.BlockSpec(memory_space=pl.ANY)


def front_kernel(in_scale, gram_scale, me, e, signs, e_kept, sketch, rounded_t, gram_sent, gram_kept, s32, s16, acc, sem):
    rows = e.shape[0]
    n = sem.shape[0] - 1
    block = rows // n
    signs_copy = pltpu.make_async_copy(signs, s32, sem.at[n])
    signs_copy.start()

    def rows_copy(i):
        at = pl.ds(pl.multiple_of(i * block, block), block)
        return pltpu.make_async_copy(e.at[at], e_kept.at[at], sem.at[i])

    for i in range(n):
        rows_copy(i).start()
    signs_copy.wait()
    s16[...] = s32[...].astype(jnp.bfloat16)

    def step(i, carry):
        rows_copy(i).wait()
        at = pl.ds(pl.multiple_of(i * block, block), block)
        sk = dot(e_kept[at, :], s16[...]) * in_scale
        sketch[at, :] = sk
        rounded_t[:, at] = sk.astype(jnp.bfloat16).T
        return carry

    lax.fori_loop(0, n, step, 0)
    high, low = split(sketch[...])
    acc[...] = dot(rounded_t[...], low)
    acc[...] = (dot(rounded_t[...], high) + (acc[...] + acc[...].T)) * gram_scale
    half = acc.shape[0] // 2
    own = me[0] & 1
    gram_kept[...] = acc[pl.ds(pl.multiple_of(own * half, half), half), :]
    gram_sent[...] = acc[pl.ds(pl.multiple_of((1 - own) * half, half), half), :]


def front_call(me, e, signs, rows_all):
    rows, d = e.shape
    k = signs.shape[1]
    copies = 4
    return pl.pallas_call(
        functools.partial(front_kernel, 1.0 / math.sqrt(d), 1.0 / rows_all),
        in_specs=[SMEM_SPEC, ANY_SPEC, ANY_SPEC],
        out_specs=[VMEM_SPEC] * 5,
        out_shape=[
            in_vmem((rows, d), e.dtype),
            in_vmem((rows, k), jnp.float32),
            in_vmem((k, rows), jnp.bfloat16),
            in_vmem((k // 2, k), jnp.float32),
            in_vmem((k // 2, k), jnp.float32),
        ],
        scratch_shapes=[
            pltpu.VMEM((d, k), jnp.int32),
            pltpu.VMEM((d, k), jnp.bfloat16),
            pltpu.VMEM((k, k), jnp.float32),
            pltpu.SemaphoreType.DMA((copies + 1,)),
        ],
        compiler_params=pltpu.CompilerParams(vmem_limit_bytes=24 * MIB),
        cost_estimate=pl.CostEstimate(flops=2 * rows * d * k, bytes_accessed=rows * d * 2 + d * k * 4, transcendentals=0),
        name="front",
    )(me, e, pltpu.with_memory_space_constraint(signs, pltpu.HBM))


def cross_kernel(scale, groups, width, info, e, rounded_t, *outs):
    k = rounded_t.shape[0]
    size = k // groups
    per = 4 // len(outs)
    for n in range(4):
        at = pl.ds(pl.multiple_of(info[n] * width, width), width)
        value = dot(rounded_t[...], e[:, at]) * scale
        for g in range(groups):
            to = pl.multiple_of((n % per) * k + (info[4] ^ g) * size, size)
            outs[n // per][pl.ds(to, size), :] = value[g * size : (g + 1) * size]


def cross_call(info, e, rounded_t, scale, groups, width, n_outs):
    rows, d = e.shape
    k = rounded_t.shape[0]
    return pl.pallas_call(
        functools.partial(cross_kernel, scale, groups, width),
        in_specs=[SMEM_SPEC, VMEM_SPEC, VMEM_SPEC],
        out_specs=[VMEM_SPEC] * n_outs,
        out_shape=[in_vmem((4 // n_outs * k, width), jnp.float32)] * n_outs,
        compiler_params=pltpu.CompilerParams(vmem_limit_bytes=16 * MIB),
        cost_estimate=pl.CostEstimate(flops=2 * rows * k * width * 4, bytes_accessed=0, transcendentals=0),
        name="cross",
    )(info, *pinned(e, rounded_t))


def factor_kernel(me, kept, got, triangle, high, low, work):
    k = triangle.shape[0]
    half = k // 2
    own = me[0] & 1
    work[pl.ds(pl.multiple_of(own * half, half), half), :k] = kept[...]
    work[pl.ds(pl.multiple_of((1 - own) * half, half), half), :k] = got[...]
    b = 64
    rows_k = lax.broadcasted_iota(jnp.int32, (k, k), 0)
    cols_k = lax.broadcasted_iota(jnp.int32, (k, k), 1)
    work[:, k:] = jnp.where(rows_k == cols_k, 1.0, 0.0)
    lane = lax.broadcasted_iota(jnp.int32, (8, 2 * b), 1)
    sub = lax.broadcasted_iota(jnp.int32, (8, 2 * b), 0)

    def over_lanes(a, at):
        return jnp.broadcast_to(a[:, at : at + 1], (8, 2 * b))

    for n in range(k // b):
        first = (n % 2) * b
        pair = (n // 2) * 2 * b
        own_lanes = (lane >= first) & (lane < first + b)
        w = []
        for v in range(b // 8):
            a = work[n * b + 8 * v : n * b + 8 * v + 8, pair : pair + 2 * b]
            ident = jnp.where(lane == (b - first) + 8 * v + sub, 1.0, 0.0)
            w.append(jnp.where(own_lanes, a, ident))
        inv = []
        for q in range(b // 8):
            at = first + 8 * q
            row = [jnp.broadcast_to(w[q][i : i + 1, :], (8, 2 * b)) for i in range(8)]
            s = {(i, j): over_lanes(row[i], at + j) for i in range(8) for j in range(i, 8)}
            factor = {}
            scaled = []
            for j in range(8):
                r = 1.0 / s[j, j]
                for i in range(j + 1, 8):
                    factor[i, j] = s[j, i] * r
                    for m in range(i, 8):
                        s[i, m] = s[i, m] - factor[i, j] * s[j, m]
                    row[i] = row[i] - factor[i, j] * row[j]
                scaled.append(row[j] * r)
            new, pivots = row[0], s[0, 0]
            for i in range(1, 8):
                new = jnp.where(sub == i, row[i], new)
                pivots = jnp.where(sub == i, s[i, i], pivots)
            for v in range(q + 1, b // 8):
                col = [over_lanes(w[v], at + j) for j in range(8)]
                for j in range(8):
                    for m in range(j + 1, 8):
                        col[m] = col[m] - col[j] * factor[m, j]
                t = [col[j] * scaled[j] for j in range(8)]
                w[v] = w[v] - (((t[0] + t[1]) + (t[2] + t[3])) + ((t[4] + t[5]) + (t[6] + t[7])))
            moved = pltpu.roll(new * (1.0 / jnp.sqrt(pivots)), b, 1)
            inv.append(jnp.where(own_lanes, moved, 0.0))
        inv = jnp.concatenate(inv, axis=0)
        y = lax.dot_general(
            inv, work[pair : pair + 2 * b, :], (((1,), (0,)), ((), ())),
            precision=lax.Precision.HIGHEST, preferred_element_type=jnp.float32,
        )
        r_rows, i_rows = y[:, :k], y[:, k:]
        at = lax.broadcasted_iota(jnp.int32, (b, k), 0) + n * b
        to = lax.broadcasted_iota(jnp.int32, (b, k), 1)
        triangle[n * b : (n + 1) * b, :] = jnp.where(to >= at, r_rows, 0.0)
        i_rows = jnp.where(to <= at, i_rows, 0.0)
        i_high, i_low = split(i_rows)
        high[n * b : (n + 1) * b, :] = i_high
        low[n * b : (n + 1) * b, :] = i_low
        if (n + 1) * b < k:
            later = jnp.where(to >= (n + 1) * b, r_rows, 0.0)
            work[...] -= lax.dot_general(
                later, y, (((0,), (0,)), ((), ())),
                precision=lax.Precision.HIGHEST, preferred_element_type=jnp.float32,
            )


def factor_call(me, kept, got):
    k = kept.shape[1]
    return pl.pallas_call(
        factor_kernel,
        in_specs=[SMEM_SPEC, VMEM_SPEC, VMEM_SPEC],
        out_specs=[VMEM_SPEC] * 3,
        out_shape=[
            jax.ShapeDtypeStruct((k, k), jnp.float32),
            in_vmem((k, k), jnp.bfloat16),
            in_vmem((k, k), jnp.bfloat16),
        ],
        scratch_shapes=[pltpu.VMEM((k, 2 * k), jnp.float32)],
        compiler_params=pltpu.CompilerParams(vmem_limit_bytes=16 * MIB),
        cost_estimate=pl.CostEstimate(flops=10**10, bytes_accessed=k * k * 8, transcendentals=0),
        name="factor",
    )(me, kept, got)


def basis_kernel(sketch, high, low, out):
    s_high, s_low = split(sketch[...])
    right = ((1,), (1,))
    out[...] = (
        dot(s_high, high[...], right) + (dot(s_high, low[...], right) + dot(s_low, high[...], right))
    ).astype(out.dtype)


def basis_call(sketch, high, low):
    rows, k = sketch.shape
    block = rows // 4
    return pl.pallas_call(
        basis_kernel,
        grid=(rows // block,),
        in_specs=[pl.BlockSpec((block, k), lambda i: (i, 0))] + [pl.BlockSpec((k, k), lambda i: (0, 0))] * 2,
        out_specs=pl.BlockSpec((block, k), lambda i: (i, 0)),
        out_shape=jax.ShapeDtypeStruct((rows, k), jnp.bfloat16),
        compiler_params=pltpu.CompilerParams(vmem_limit_bytes=16 * MIB),
        cost_estimate=pl.CostEstimate(flops=6 * rows * k * k, bytes_accessed=rows * k * 6, transcendentals=0),
        name="basis",
    )(sketch, high, low)


def project_kernel(groups, width, info, high, low, *refs):
    *blocks, out, value, sem = refs
    blocks = blocks[-4:]
    k = high.shape[0]
    size = k // groups
    copies = []
    for n in range(8):
        block, order = blocks[n // 2], info[8 + n // 4]
        c_high, c_low = split(
            jnp.concatenate(
                [
                    block[pl.ds(pl.multiple_of((n % 2) * k + (order ^ g) * size, size), size), :]
                    for g in range(groups)
                ],
                axis=0,
            )
        )
        value[n] = dot(high[...], c_high) + (dot(high[...], c_low) + dot(low[...], c_high))
        at = pl.ds(pl.multiple_of(info[n] * width, width), width)
        copies.append(pltpu.make_async_copy(value.at[n], out.at[:, at], sem.at[n]))
        copies[-1].start()
    for copy in copies:
        copy.wait()


def project_call(info, high, low, blocks, groups, d, before):
    k, width = high.shape[0], blocks[0].shape[1]
    extra = [] if before is None else [before]
    return pl.pallas_call(
        functools.partial(project_kernel, groups, width),
        in_specs=[SMEM_SPEC, VMEM_SPEC, VMEM_SPEC] + [ANY_SPEC] * len(extra) + [VMEM_SPEC] * 4,
        out_specs=ANY_SPEC,
        out_shape=jax.ShapeDtypeStruct((k, d), jnp.float32),
        input_output_aliases={3: 0} if extra else {},
        scratch_shapes=[pltpu.VMEM((8, k, width), jnp.float32), pltpu.SemaphoreType.DMA((8,))],
        compiler_params=pltpu.CompilerParams(vmem_limit_bytes=16 * MIB),
        cost_estimate=pl.CostEstimate(flops=6 * k * k * width * 8, bytes_accessed=k * width * 32, transcendentals=0),
        name="project",
    )(info, *pinned(high, low), *extra, *pinned(*blocks))


def solution(mesh):
    n_devices = math.prod(mesh.shape.values())
    orders = orders_of(n_devices)
    steps = len(orders[0])
    groups = 1 << (steps - 2)
    pairs = [(i, i ^ 1) for i in range(n_devices)]
    swaps = [[(i, i ^ (1 << orders[i & 1][s])) for i in range(n_devices)] for s in range(steps)]

    def with_pair(a):
        return lax.ppermute(a, AXES, pairs)

    def swap(a, s):
        return lax.ppermute(a, AXES, swaps[s])

    def join(*arrays):
        return arrays[0] if len(arrays) == 1 else jnp.concatenate(arrays, axis=0)

    def shards(e, signs):
        rows_all = e.shape[0] * n_devices
        d = e.shape[1]
        k = signs.shape[1]
        width = d // (8 * CHUNKS)
        scale = 1.0 / math.sqrt(rows_all)
        me = lax.axis_index(AXES).astype(jnp.int32)
        own = me & 1
        place = [bits_of(me, o[:2]) for o in orders]
        rest = [bits_of(me, o[2:]) for o in orders]
        mine = lambda pair: jnp.where(own == 0, pair[0], pair[1])
        other = lambda pair: jnp.where(own == 0, pair[1], pair[0])

        def blocks_at(chunk, region, at):
            return [(chunk * 2 + region) * 4 + (at ^ n) for n in range(4)]

        def vector(*values):
            return jnp.stack([jnp.asarray(v, jnp.int32) for v in values])

        me1 = me[None]
        e_kept, sketch, rounded_t, gram_sent, gram = front_call(me1, e, signs, rows_all)
        gram = gram + with_pair(gram_sent)

        stay, go, whole = [], [], []
        for chunk in range(CHUNKS):
            (sent,) = cross_call(
                vector(*blocks_at(chunk, 1 - own, other(place)), other(rest)), e_kept, rounded_t, scale, groups, width, 1
            )
            kept, first = cross_call(
                vector(*blocks_at(chunk, own, mine(place)), mine(rest)), e_kept, rounded_t, scale, groups, width, 2
            )
            got = with_pair(sent)
            stay.append(kept + got[: 2 * k])
            go.append(first + got[2 * k :])
            whole.append([gram] if chunk == 0 else [])
        for s in range(steps):
            for chunk in range(CHUNKS):
                r = swap(join(go[chunk], *whole[chunk]), s)
                n = stay[chunk].shape[0]
                a = stay[chunk] + r[:n]
                whole[chunk] = [g + r[n:] for g in whole[chunk]]
                stay[chunk], go[chunk] = a[: n // 2], a[n // 2 :]
                if s == steps - 1:
                    stay[chunk] = a
        triangle, high, low = factor_call(me1, whole[0][0], with_pair(whole[0][0]))
        last = []
        for s in range(steps - 1, -1, -1):
            for chunk in range(CHUNKS):
                r = swap(stay[chunk], s)
                if s:
                    stay[chunk] = join(stay[chunk], r)
                else:
                    last.append(r)
        basis = basis_call(sketch, high, low)
        projected = None
        for chunk in range(CHUNKS):
            blocks = [stay[chunk], last[chunk], with_pair(stay[chunk]), with_pair(last[chunk])]
            info = vector(
                *blocks_at(chunk, own, mine(place)), *blocks_at(chunk, 1 - own, other(place)), mine(rest), other(rest)
            )
            projected = project_call(info, high, low, blocks, groups, d, projected)
        return triangle, basis, projected

    return jax.shard_map(
        shards,
        mesh=mesh,
        in_specs=(P(AXES, None), P()),
        out_specs=(P(), P(AXES, None), P()),
        check_vma=False,
    )
```

time: 259 us -> 158 us (0.61)
  waiting for transfers between devices: 146 us -> 47.3 us
  other arithmetic: 57.4 us -> 5 us
  Pallas kernels: 0 us -> 39.1 us
  starting transfers between devices: 0.04 us -> 34 us
  matrix products: 32 us -> 0 us
  local copies, waits for them, and re-layouts: 7.28 us -> 31 us
  between operations: 15.5 us -> 1.13 us
    psum x1 -> x0, waiting for transfers between devices: 146 us -> none  [shards(): lower = jnp.linalg.cholesky(lax.psum(gram, ('gx', 'gy')))]
    another operation x11 -> x0, other arithmetic: 56.4 us -> none  [the longest x6 33.9 us: shards(): lower = jnp.linalg.cholesky(lax.psum(gram, ('gx', 'gy')))]
    ppermute x0 -> x24, waiting for transfers between devices: none -> 47.3 us  [the longest x16 47.3 us: swap(): return lax.ppermute(a, AXES, swaps[s])]
    pallas_call x0 -> x9, Pallas kernels: none -> 39.1 us  [the longest x1 11.6 us: factor_call(): pl.pallas_call(factor_kernel, in_specs=[SMEM_SPEC, VMEM_SPEC, VMEM_SPEC],...]
    ppermute x0 -> x24, starting transfers between devices: none -> 34 us  [the longest x16 32.4 us: swap(): return lax.ppermute(a, AXES, swaps[s])]
    unnamed x6 -> x18, local copies, waits for them, and re-layouts: 2.15 us -> 30.4 us
    dot_general x3 -> x0, matrix products: 20.1 us -> none  [the longest x1 9.9 us: shards(): jnp.dot(embeddings, signs.astype(jnp.bfloat16), preferred_element_type=jn...]
    another operation x8 -> x0, matrix products: 11.9 us -> none  [the longest x3 7.49 us: shards(): lax.linalg.triangular_solve(lower, cross, left_side=True, lower=True)]
  transfers between devices with their start and end apart: 1 -> 24, of which waited for: 1 -> 12; matrix products, arithmetic and copies ran while one was open for 0% -> 3% of each run, Pallas kernels for 0% -> 15%
where the time goes in v2:
time: 158 us
  waiting for transfers between devices  47.3 us (30%)
  Pallas kernels  39.1 us (25%)
  starting transfers between devices  34 us (22%)
  local copies, waits for them, and re-layouts  31 us (20%)
  other arithmetic  5 us (3%)
    ppermute x16, waiting for transfers between devices, swap(): return lax.ppermute(a, AXES, swaps[s])  47.3 us
    ppermute x16, starting transfers between devices, swap(): return lax.ppermute(a, AXES, swaps[s])  32.4 us
    unnamed x18, local copies, waits for them, and re-layouts  30.4 us
    pallas_call x1, Pallas kernels, factor_call(): pl.pallas_call(factor_kernel, in_specs=[SMEM_SPEC, VMEM_SPEC, VMEM_SPEC],...  11.6 us
    pallas_call x1, Pallas kernels, front_call(): pl.pallas_call(functools.partial(front_kernel, 1.0 / math.sqrt(d), 1.0 /...  9.66 us
    pallas_call x4, Pallas kernels, cross_call(): pl.pallas_call(functools.partial(cross_kernel, scale, groups, width), in_...  9.4 us
    pallas_call x2, Pallas kernels, project_call(): pl.pallas_call(functools.partial(project_kernel, groups, width), in_specs...  5.88 us
  transfers between devices with their start and end apart: 24, of which 12 were waited for; matrix products, arithmetic and copies ran while one was open for 3% of the time, Pallas kernels for 15%

profile of v2, /device:TPU:0, one launch (start us, length us, event | category | flops | bytes accessed | tf_op | source)
XLA Modules:
  0.0 157.6 jit_solution(1400404201963348118)
XLA Ops:
  0.7 9.7 %front.1 = (bf16[2048,4096]{1,0:T(8,128)(2,1)S(1)}, f32[2048,256]{1,0:T(8,128)S(1)}, bf16[256,2048]{1,0:T(8,128)(2,1)S(1)}, f32[128,256]{1,0:T(8,128)S(1)}, f32[128,256]{1,0:T(8,128)S(1)}) custom-call(s32[1]{0:T(128)} %bitcast.me, bf16[2048,4096]{1,0:T(8,128)(2,1)} %e.1, s32[4096,256]{1,0:T(8,128)} %signs.1), custom_call_target="tpu_custom_call" | custom-call | flops 4294967296 | bytes 20971520 | tf_op jit(solution)/shard_map/front/pallas_call | solution.py:91
  10.3 5.7 %copy-done = bf16[2048,4096]{1,0:T(8,128)(2,1)} copy-done((bf16[2048,4096]{1,0:T(8,128)(2,1)}, bf16[2048,4096]{1,0:T(8,128)(2,1)S(1)}, u32[]{:S(2)}) %copy-start) | copy-done | bytes 16777240
  16.2 5.8 %copy-done.1 = bf16[2048,4096]{1,0:T(8,128)(2,1)S(1)} copy-done((bf16[2048,4096]{1,0:T(8,128)(2,1)S(1)}, bf16[2048,4096]{1,0:T(8,128)(2,1)}, u32[]{:S(2)}) %copy-start.1) | copy-done | bytes 16777240
  21.9 2.8 %cross.7 = f32[1024,256]{1,0:T(8,128)} custom-call(s32[5]{0:T(128)S(1)} %stack.117.info, bf16[2048,4096]{1,0:T(8,128)(2,1)S(1)} %copy-done.1, bf16[256,2048]{1,0:T(8,128)(2,1)S(1)} %get-tuple-element.18.rounded_t), custom_call_target="tpu_custom_call" | custom-call | flops 1073741824 | tf_op jit(solution)/shard_map/cross/pallas_call | solution.py:129
  24.8 0.5 collective-permute-start.13
  25.3 5.8 %copy-done.2 = bf16[2048,4096]{1,0:T(8,128)(2,1)S(1)} copy-done((bf16[2048,4096]{1,0:T(8,128)(2,1)S(1)}, bf16[2048,4096]{1,0:T(8,128)(2,1)}, u32[]{:S(2)}) %copy-start.2) | copy-done | bytes 16777240
  31.1 2.8 %cross.5 = f32[1024,256]{1,0:T(8,128)} custom-call(s32[5]{0:T(128)S(1)} %stack.105.info, bf16[2048,4096]{1,0:T(8,128)(2,1)S(1)} %copy-done.2, bf16[256,2048]{1,0:T(8,128)(2,1)S(1)} %get-tuple-element.18.rounded_t), custom_call_target="tpu_custom_call" | custom-call | flops 1073741824 | tf_op jit(solution)/shard_map/cross/pallas_call | solution.py:129
  34.6 5.8 %copy-done.3 = bf16[2048,4096]{1,0:T(8,128)(2,1)S(1)} copy-done((bf16[2048,4096]{1,0:T(8,128)(2,1)S(1)}, bf16[2048,4096]{1,0:T(8,128)(2,1)}, u32[]{:S(2)}) %copy-start.3) | copy-done | bytes 16777240
  40.3 1.9 %cross.6 = (f32[512,256]{1,0:T(8,128)S(1)}, f32[512,256]{1,0:T(8,128)S(1)}) custom-call(s32[5]{0:T(128)S(1)} %stack.116.info, bf16[2048,4096]{1,0:T(8,128)(2,1)S(1)} %copy-done.3, bf16[256,2048]{1,0:T(8,128)(2,1)S(1)} %get-tuple-element.18.rounded_t), custom_call_target="tpu_custom_call" | custom-call | flops 1073741824 | tf_op jit(solution)/shard_map/cross/pallas_call | solution.py:129
  42.2 0.8 copy-done.5
  43.0 0.8 copy-done.7
  43.9 5.8 %copy-done.4 = bf16[2048,4096]{1,0:T(8,128)(2,1)S(1)} copy-done((bf16[2048,4096]{1,0:T(8,128)(2,1)S(1)}, bf16[2048,4096]{1,0:T(8,128)(2,1)}, u32[]{:S(2)}) %copy-start.4) | copy-done | bytes 16777240
  49.6 1.9 %cross.4 = (f32[512,256]{1,0:T(8,128)S(1)}, f32[512,256]{1,0:T(8,128)S(1)}) custom-call(s32[5]{0:T(128)S(1)} %stack.99.info, bf16[2048,4096]{1,0:T(8,128)(2,1)S(1)} %copy-done.4, bf16[256,2048]{1,0:T(8,128)(2,1)S(1)} %get-tuple-element.18.rounded_t), custom_call_target="tpu_custom_call" | custom-call | flops 1073741824 | tf_op jit(solution)/shard_map/cross/pallas_call | solution.py:129
  51.6 1.2 slice_add_fusion
  52.7 2.5 %collective-permute-start.14 = (f32[512,256]{1,0:T(8,128)S(1)}, f32[512,256]{1,0:T(8,128)S(1)}, u32[]{:S(2)}, u32[]{:S(2)}) collective-permute-start(f32[512,256]{1,0:T(8,128)S(1)} %slice_add_fusion), channel_id=1, source_target_pairs={{0,2},{1,5},{2,0},{3,7},{4,6},{5,1},{6,4},{7,3},{8,10},{9,13},{10,... | collective-permute-start | bytes 1572872 | tf_op jit(solution)/shard_map/ppermute | solution.py:308
  55.3 1.1 slice_add_fusion.4
  56.5 5.9 %collective-permute-done.14 = f32[512,256]{1,0:T(8,128)S(1)} collective-permute-done((f32[512,256]{1,0:T(8,128)S(1)}, f32[512,256]{1,0:T(8,128)S(1)}, u32[]{:S(2)}, u32[]{:S(2)}) %collective-permute-start.14) | collective-permute-done | bytes 524320 | tf_op jit(solution)/shard_map/ppermute | solution.py:308
  62.4 1.1 fusion
  63.6 2.1 %collective-permute-start.15 = (f32[256,256]{1,0:T(8,128)S(1)}, f32[256,256]{1,0:T(8,128)S(1)}, u32[]{:S(2)}, u32[]{:S(2)}) collective-permute-start(f32[256,256]{1,0:T(8,128)S(1)} %slice.115), channel_id=1, source_target_pairs={{0,4},{1,3},{2,6},{3,1},{4,0},{5,7},{6,2},{7,5},{8,12},{9,11},{10,... | collective-permute-start | bytes 786440 | tf_op jit(solution)/shard_map/ppermute | solution.py:308
  65.7 6.5 %collective-permute-done.2 = f32[640,256]{1,0:T(8,128)S(1)} collective-permute-done((f32[640,256]{1,0:T(8,128)S(1)}, f32[640,256]{1,0:T(8,128)S(1)}, u32[]{:S(2)}, u32[]{:S(2)}) %collective-permute-start.2) | collective-permute-done | bytes 655392 | tf_op jit(solution)/shard_map/ppermute | solution.py:308
  72.3 1.1 slice_add_fusion.2
  73.5 2.1 %collective-permute-start.3 = (f32[384,256]{1,0:T(8,128)S(1)}, f32[384,256]{1,0:T(8,128)S(1)}, u32[]{:S(2)}, u32[]{:S(2)}) collective-permute-start(f32[384,256]{1,0:T(8,128)S(1)} %pad_maximum_fusion.3), channel_id=1, source_target_pairs={{0,4},{1,3},{2,6},{3,1},{4,0},{5,7},{6,2},{7,5},{8,12},{9,11},{10,... | collective-permute-start | bytes 1179656 | tf_op jit(solution)/shard_map/ppermute | solution.py:308
  75.7 1.6 %collective-permute-start.16 = (f32[128,256]{1,0:T(8,128)S(1)}, f32[128,256]{1,0:T(8,128)S(1)}, u32[]{:S(2)}, u32[]{:S(2)}) collective-permute-start(f32[128,256]{1,0:T(8,128)S(1)} %slice.117), channel_id=1, source_target_pairs={{0,8},{1,17},{2,10},{3,19},{4,12},{5,21},{6,14},{7,23},{8,0},{9,25... | collective-permute-start | bytes 393224 | tf_op jit(solution)/shard_map/ppermute | solution.py:308
  77.3 4.1 %collective-permute-done.3 = f32[384,256]{1,0:T(8,128)S(1)} collective-permute-done((f32[384,256]{1,0:T(8,128)S(1)}, f32[384,256]{1,0:T(8,128)S(1)}, u32[]{:S(2)}, u32[]{:S(2)}) %collective-permute-start.3) | collective-permute-done | bytes 393248 | tf_op jit(solution)/shard_map/ppermute | solution.py:308
  81.5 2.2 %collective-permute-start.4 = (f32[256,256]{1,0:T(8,128)S(1)}, f32[256,256]{1,0:T(8,128)S(1)}, u32[]{:S(2)}, u32[]{:S(2)}) collective-permute-start(f32[256,256]{1,0:T(8,128)S(1)} %pad_maximum_fusion.4), channel_id=1, source_target_pairs={{0,8},{1,17},{2,10},{3,19},{4,12},{5,21},{6,14},{7,23},{8,0},{9,25... | collective-permute-start | bytes 786440 | tf_op jit(solution)/shard_map/ppermute | solution.py:308
  83.7 2.6 %collective-permute-start.17 = (f32[64,256]{1,0:T(8,128)S(1)}, f32[64,256]{1,0:T(8,128)S(1)}, u32[]{:S(2)}, u32[]{:S(2)}) collective-permute-start(f32[64,256]{1,0:T(8,128)S(1)} %slice.119), channel_id=1, source_target_pairs={{0,16},{1,9},{2,18},{3,11},{4,20},{5,13},{6,22},{7,15},{8,24},{9,1... | collective-permute-start | bytes 196616 | tf_op jit(solution)/shard_map/ppermute | solution.py:308
  86.3 4.3 %collective-permute-done.4 = f32[256,256]{1,0:T(8,128)S(1)} collective-permute-done((f32[256,256]{1,0:T(8,128)S(1)}, f32[256,256]{1,0:T(8,128)S(1)}, u32[]{:S(2)}, u32[]{:S(2)}) %collective-permute-start.4) | collective-permute-done | bytes 262176 | tf_op jit(solution)/shard_map/ppermute | solution.py:308
  90.7 2.9 %collective-permute-start.5 = (f32[192,256]{1,0:T(8,128)S(1)}, f32[192,256]{1,0:T(8,128)S(1)}, u32[]{:S(2)}, u32[]{:S(2)}) collective-permute-start(f32[192,256]{1,0:T(8,128)S(1)} %pad_maximum_fusion.7), channel_id=1, source_target_pairs={{0,16},{1,9},{2,18},{3,11},{4,20},{5,13},{6,22},{7,15},{8,24},{9,1... | collective-permute-start | bytes 589832 | tf_op jit(solution)/shard_map/ppermute | solution.py:308
  93.8 5.2 %collective-permute-done.5 = f32[192,256]{1,0:T(8,128)S(1)} collective-permute-done((f32[192,256]{1,0:T(8,128)S(1)}, f32[192,256]{1,0:T(8,128)S(1)}, u32[]{:S(2)}, u32[]{:S(2)}) %collective-permute-start.5) | collective-permute-done | bytes 196640 | tf_op jit(solution)/shard_map/ppermute | solution.py:308
  99.0 2.1 %collective-permute-start.7 = (f32[64,256]{1,0:T(8,128)S(1)}, f32[64,256]{1,0:T(8,128)S(1)}, u32[]{:S(2)}, u32[]{:S(2)}) collective-permute-start(f32[64,256]{1,0:T(8,128)S(1)} %slice_add_fusion.14), channel_id=1, source_target_pairs={{0,16},{1,9},{2,18},{3,11},{4,20},{5,13},{6,22},{7,15},{8,24},{9,1... | collective-permute-start | bytes 196616 | tf_op jit(solution)/shard_map/ppermute | solution.py:308
  101.1 3.3 %collective-permute-done.18 = f32[64,256]{1,0:T(8,128)S(1)} collective-permute-done((f32[64,256]{1,0:T(8,128)S(1)}, f32[64,256]{1,0:T(8,128)S(1)}, u32[]{:S(2)}, u32[]{:S(2)}) %collective-permute-start.18) | collective-permute-done | bytes 65568 | tf_op jit(solution)/shard_map/ppermute | solution.py:308
  104.4 5.6 %collective-permute-start.19 = (f32[128,256]{1,0:T(8,128)S(1)}, f32[128,256]{1,0:T(8,128)S(1)}, u32[]{:S(2)}, u32[]{:S(2)}) collective-permute-start(f32[128,256]{1,0:T(8,128)S(1)} %pad_maximum_fusion.9), channel_id=1, source_target_pairs={{0,8},{1,17},{2,10},{3,19},{4,12},{5,21},{6,14},{7,23},{8,0},{9,25... | collective-permute-start | bytes 393224 | tf_op jit(solution)/shard_map/ppermute | solution.py:308
  110.0 2.2 %collective-permute-start.8 = (f32[128,256]{1,0:T(8,128)S(1)}, f32[128,256]{1,0:T(8,128)S(1)}, u32[]{:S(2)}, u32[]{:S(2)}) collective-permute-start(f32[128,256]{1,0:T(8,128)S(1)} %pad_maximum_fusion.8), channel_id=1, source_target_pairs={{0,8},{1,17},{2,10},{3,19},{4,12},{5,21},{6,14},{7,23},{8,0},{9,25... | collective-permute-start | bytes 393224 | tf_op jit(solution)/shard_map/ppermute | solution.py:308
  112.3 0.7 collective-permute-done.19
  113.0 1.6 collective-permute-start.20
  114.6 0.7 collective-permute-done.8
  115.2 1.6 collective-permute-start.9
  116.8 5.5 %collective-permute-done.20 = f32[256,256]{1,0:T(8,128)S(1)} collective-permute-done((f32[256,256]{1,0:T(8,128)S(1)}, f32[256,256]{1,0:T(8,128)S(1)}, u32[]{:S(2)}, u32[]{:S(2)}) %collective-permute-start.20) | collective-permute-done | bytes 262176 | tf_op jit(solution)/shard_map/ppermute | solution.py:308
  122.3 1.5 collective-permute-start.21
  123.8 4.1 %collective-permute-done.9 = f32[256,256]{1,0:T(8,128)S(1)} collective-permute-done((f32[256,256]{1,0:T(8,128)S(1)}, f32[256,256]{1,0:T(8,128)S(1)}, u32[]{:S(2)}, u32[]{:S(2)}) %collective-permute-start.9) | collective-permute-done | bytes 262176 | tf_op jit(solution)/shard_map/ppermute | solution.py:308
  128.0 1.5 collective-permute-start.10
  129.7 0.5 collective-permute-start.22
  130.3 1.4 collective-permute-done.21.refs_2_
  131.7 5.6 %collective-permute-done.10.refs_1_ = f32[512,256]{1,0:T(8,128)} collective-permute-done((f32[512,256]{1,0:T(8,128)S(1)}, f32[512,256]{1,0:T(8,128)}, u32[]{:S(2)}, u32[]{:S(2)}) %collective-permute-start.10) | collective-permute-done | bytes 524320 | tf_op jit(solution)/shard_map/ppermute | solution.py:308
  137.3 11.6 %factor.1 = (f32[256,256]{1,0:T(8,128)}, bf16[256,256]{1,0:T(8,128)(2,1)S(1)}, bf16[256,256]{1,0:T(8,128)(2,1)S(1)}) custom-call(s32[1]{0:T(128)} %bitcast.me, f32[128,256]{1,0:T(8,128)S(1)} %slice_add_fusion.8.kept, f32[128,256]{1,0:T(8,128)S(1)} %collective-permute-done.6.got), custom_call_target="tpu_custom_call" | custom-call | flops 10000000000 | bytes 524288 | tf_op jit(solution)/shard_map/factor/pallas_call | solution.py:216
  148.9 2.6 %basis.1 = bf16[2048,256]{1,0:T(8,128)(2,1)} custom-call(f32[2048,256]{1,0:T(8,128)S(1)} %get-tuple-element.22.sketch, bf16[256,256]{1,0:T(8,128)(2,1)S(1)} %get-tuple-element.23.high, bf16[256,256]{1,0:T(8,128)(2,1)S(1)} %get-tuple-element.24.low), custom_call_target="tpu_custom_call" | custom-call | flops 805306368 | bytes 3145728 | tf_op jit(solution)/shard_map/basis/pallas_call | solution.py:243
  151.5 2.9 %project.2.refs_0_ = f32[256,4096]{1,0:T(8,128)} custom-call(s32[10]{0:T(128)S(1)} %stack.115.info, bf16[256,256]{1,0:T(8,128)(2,1)S(1)} %get-tuple-element.23.high, bf16[256,256]{1,0:T(8,128)(2,1)S(1)} %get-tuple-element.24.low, f32[512,256]{1,0:T(8,128)S(1)} %pad_maximum_fusion.1.refs_0_, f32[512,256]{1,0:T(8,128)} %collective-permute-done.10.refs_1_, ...), custom_call_target="tpu_custom_call" | custom-call | flops 805306368 | bytes 2097152 | tf_op jit(solution)/shard_map/project/pallas_call | solution.py:283
  154.5 2.9 %project.3 = f32[256,4096]{1,0:T(8,128)} custom-call(s32[10]{0:T(128)S(1)} %stack.114.info, bf16[256,256]{1,0:T(8,128)(2,1)S(1)} %get-tuple-element.23.high, bf16[256,256]{1,0:T(8,128)(2,1)S(1)} %get-tuple-element.24.low, f32[256,4096]{1,0:T(8,128)} %project.2.refs_0_, f32[512,256]{1,0:T(8,128)S(1)} %pad_maximum_fusion.2.refs_1_, ...), custom_call_target="tpu_custom_call", output_to_operand_aliasing={{}: (3, {})} | custom-call | flops 805306368 | bytes 2097152 | tf_op jit(solution)/shard_map/project/pallas_call | solution.py:283
  (63 shorter events, 2.0 us)
Async XLA Ops:
  10.3 5.8 %copy-start = (bf16[2048,4096]{1,0:T(8,128)(2,1)}, bf16[2048,4096]{1,0:T(8,128)(2,1)S(1)}, u32[]{:S(2)}) copy-start(bf16[2048,4096]{1,0:T(8,128)(2,1)S(1)} %get-tuple-element.17.e) | copy-start | bytes 50331652
  16.2 5.8 %copy-start.1 = (bf16[2048,4096]{1,0:T(8,128)(2,1)S(1)}, bf16[2048,4096]{1,0:T(8,128)(2,1)}, u32[]{:S(2)}) copy-start(bf16[2048,4096]{1,0:T(8,128)(2,1)} %copy-done) | copy-start | bytes 50331652
  24.8 26.8 %collective-permute-start.13 = (f32[1024,256]{1,0:T(8,128)}, f32[1024,256]{1,0:T(8,128)}, u32[]{:S(2)}, u32[]{:S(2)}) collective-permute-start(f32[1024,256]{1,0:T(8,128)} %cross.7), channel_id=1, source_target_pairs={{0,1},{1,0},{2,3},{3,2},{4,5},{5,4},{6,7},{7,6},{8,9},{9,8},{10,11... | collective-permute-start | bytes 3145736 | tf_op jit(solution)/shard_map/ppermute | solution.py:305
  25.3 5.8 %copy-start.2 = (bf16[2048,4096]{1,0:T(8,128)(2,1)S(1)}, bf16[2048,4096]{1,0:T(8,128)(2,1)}, u32[]{:S(2)}) copy-start(bf16[2048,4096]{1,0:T(8,128)(2,1)} %copy-done) | copy-start | bytes 50331652
  34.0 21.3 %collective-permute-start.1 = (f32[1024,256]{1,0:T(8,128)}, f32[1024,256]{1,0:T(8,128)}, u32[]{:S(2)}, u32[]{:S(2)}) collective-permute-start(f32[1024,256]{1,0:T(8,128)} %cross.5), channel_id=1, source_target_pairs={{0,1},{1,0},{2,3},{3,2},{4,5},{5,4},{6,7},{7,6},{8,9},{9,8},{10,11... | collective-permute-start | bytes 3145736 | tf_op jit(solution)/shard_map/ppermute | solution.py:305
  34.0 17.5 %collective-permute-start = (f32[128,256]{1,0:T(8,128)S(1)}, f32[128,256]{1,0:T(8,128)S(1)}, u32[]{:S(2)}, u32[]{:S(2)}) collective-permute-start(f32[128,256]{1,0:T(8,128)S(1)} %get-tuple-element.16), channel_id=1, source_target_pairs={{0,1},{1,0},{2,3},{3,2},{4,5},{5,4},{6,7},{7,6},{8,9},{9,8},{10,11... | collective-permute-start | bytes 393224 | tf_op jit(solution)/shard_map/ppermute | solution.py:305
  34.6 5.8 %copy-start.3 = (bf16[2048,4096]{1,0:T(8,128)(2,1)S(1)}, bf16[2048,4096]{1,0:T(8,128)(2,1)}, u32[]{:S(2)}) copy-start(bf16[2048,4096]{1,0:T(8,128)(2,1)} %copy-done) | copy-start | bytes 50331652
  42.2 0.8 copy-start.5
  43.0 0.8 copy-start.7
  43.9 5.8 %copy-start.4 = (bf16[2048,4096]{1,0:T(8,128)(2,1)S(1)}, bf16[2048,4096]{1,0:T(8,128)(2,1)}, u32[]{:S(2)}) copy-start(bf16[2048,4096]{1,0:T(8,128)(2,1)} %copy-done) | copy-start | bytes 50331652
  49.6 1.9 %copy-start.6 = (f32[512,256]{1,0:T(8,128)S(1)}, f32[512,256]{1,0:T(8,128)}, u32[]{:S(2)}) copy-start(f32[512,256]{1,0:T(8,128)} %copy-done.5) | copy-start | bytes 1572868
  51.5 10.9 %copy-start.8 = (f32[512,256]{1,0:T(8,128)S(1)}, f32[512,256]{1,0:T(8,128)}, u32[]{:S(2)}) copy-start(f32[512,256]{1,0:T(8,128)} %copy-done.7) | copy-start | bytes 1572868
  52.7 9.7 %collective-permute-start.14 = (f32[512,256]{1,0:T(8,128)S(1)}, f32[512,256]{1,0:T(8,128)S(1)}, u32[]{:S(2)}, u32[]{:S(2)}) collective-permute-start(f32[512,256]{1,0:T(8,128)S(1)} %slice_add_fusion), channel_id=1, source_target_pairs={{0,2},{1,5},{2,0},{3,7},{4,6},{5,1},{6,4},{7,3},{8,10},{9,13},{10,... | collective-permute-start | bytes 1572872 | tf_op jit(solution)/shard_map/ppermute | solution.py:308
  56.4 15.8 %collective-permute-start.2 = (f32[640,256]{1,0:T(8,128)S(1)}, f32[640,256]{1,0:T(8,128)S(1)}, u32[]{:S(2)}, u32[]{:S(2)}) collective-permute-start(f32[640,256]{1,0:T(8,128)S(1)} %pad_maximum_fusion), channel_id=1, source_target_pairs={{0,2},{1,5},{2,0},{3,7},{4,6},{5,1},{6,4},{7,3},{8,10},{9,13},{10,... | collective-permute-start | bytes 1966088 | tf_op jit(solution)/shard_map/ppermute | solution.py:308
  63.6 12.0 %collective-permute-start.15 = (f32[256,256]{1,0:T(8,128)S(1)}, f32[256,256]{1,0:T(8,128)S(1)}, u32[]{:S(2)}, u32[]{:S(2)}) collective-permute-start(f32[256,256]{1,0:T(8,128)S(1)} %slice.115), channel_id=1, source_target_pairs={{0,4},{1,3},{2,6},{3,1},{4,0},{5,7},{6,2},{7,5},{8,12},{9,11},{10,... | collective-permute-start | bytes 786440 | tf_op jit(solution)/shard_map/ppermute | solution.py:308
  73.5 7.9 %collective-permute-start.3 = (f32[384,256]{1,0:T(8,128)S(1)}, f32[384,256]{1,0:T(8,128)S(1)}, u32[]{:S(2)}, u32[]{:S(2)}) collective-permute-start(f32[384,256]{1,0:T(8,128)S(1)} %pad_maximum_fusion.3), channel_id=1, source_target_pairs={{0,4},{1,3},{2,6},{3,1},{4,0},{5,7},{6,2},{7,5},{8,12},{9,11},{10,... | collective-permute-start | bytes 1179656 | tf_op jit(solution)/shard_map/ppermute | solution.py:308
  75.7 8.0 %collective-permute-start.16 = (f32[128,256]{1,0:T(8,128)S(1)}, f32[128,256]{1,0:T(8,128)S(1)}, u32[]{:S(2)}, u32[]{:S(2)}) collective-permute-start(f32[128,256]{1,0:T(8,128)S(1)} %slice.117), channel_id=1, source_target_pairs={{0,8},{1,17},{2,10},{3,19},{4,12},{5,21},{6,14},{7,23},{8,0},{9,25... | collective-permute-start | bytes 393224 | tf_op jit(solution)/shard_map/ppermute | solution.py:308
  81.5 9.2 %collective-permute-start.4 = (f32[256,256]{1,0:T(8,128)S(1)}, f32[256,256]{1,0:T(8,128)S(1)}, u32[]{:S(2)}, u32[]{:S(2)}) collective-permute-start(f32[256,256]{1,0:T(8,128)S(1)} %pad_maximum_fusion.4), channel_id=1, source_target_pairs={{0,8},{1,17},{2,10},{3,19},{4,12},{5,21},{6,14},{7,23},{8,0},{9,25... | collective-permute-start | bytes 786440 | tf_op jit(solution)/shard_map/ppermute | solution.py:308
  83.7 10.0 %collective-permute-start.17 = (f32[64,256]{1,0:T(8,128)S(1)}, f32[64,256]{1,0:T(8,128)S(1)}, u32[]{:S(2)}, u32[]{:S(2)}) collective-permute-start(f32[64,256]{1,0:T(8,128)S(1)} %slice.119), channel_id=1, source_target_pairs={{0,16},{1,9},{2,18},{3,11},{4,20},{5,13},{6,22},{7,15},{8,24},{9,1... | collective-permute-start | bytes 196616 | tf_op jit(solution)/shard_map/ppermute | solution.py:308
  90.7 8.3 %collective-permute-start.5 = (f32[192,256]{1,0:T(8,128)S(1)}, f32[192,256]{1,0:T(8,128)S(1)}, u32[]{:S(2)}, u32[]{:S(2)}) collective-permute-start(f32[192,256]{1,0:T(8,128)S(1)} %pad_maximum_fusion.7), channel_id=1, source_target_pairs={{0,16},{1,9},{2,18},{3,11},{4,20},{5,13},{6,22},{7,15},{8,24},{9,1... | collective-permute-start | bytes 589832 | tf_op jit(solution)/shard_map/ppermute | solution.py:308
  93.7 10.7 %collective-permute-start.18 = (f32[64,256]{1,0:T(8,128)S(1)}, f32[64,256]{1,0:T(8,128)S(1)}, u32[]{:S(2)}, u32[]{:S(2)}) collective-permute-start(f32[64,256]{1,0:T(8,128)S(1)} %slice_add_fusion.13), channel_id=1, source_target_pairs={{0,16},{1,9},{2,18},{3,11},{4,20},{5,13},{6,22},{7,15},{8,24},{9,1... | collective-permute-start | bytes 196616 | tf_op jit(solution)/shard_map/ppermute | solution.py:308
  99.0 11.0 %collective-permute-start.7 = (f32[64,256]{1,0:T(8,128)S(1)}, f32[64,256]{1,0:T(8,128)S(1)}, u32[]{:S(2)}, u32[]{:S(2)}) collective-permute-start(f32[64,256]{1,0:T(8,128)S(1)} %slice_add_fusion.14), channel_id=1, source_target_pairs={{0,16},{1,9},{2,18},{3,11},{4,20},{5,13},{6,22},{7,15},{8,24},{9,1... | collective-permute-start | bytes 196616 | tf_op jit(solution)/shard_map/ppermute | solution.py:308
  104.4 8.6 %collective-permute-start.19 = (f32[128,256]{1,0:T(8,128)S(1)}, f32[128,256]{1,0:T(8,128)S(1)}, u32[]{:S(2)}, u32[]{:S(2)}) collective-permute-start(f32[128,256]{1,0:T(8,128)S(1)} %pad_maximum_fusion.9), channel_id=1, source_target_pairs={{0,8},{1,17},{2,10},{3,19},{4,12},{5,21},{6,14},{7,23},{8,0},{9,25... | collective-permute-start | bytes 393224 | tf_op jit(solution)/shard_map/ppermute | solution.py:308
  110.0 5.2 %collective-permute-start.8 = (f32[128,256]{1,0:T(8,128)S(1)}, f32[128,256]{1,0:T(8,128)S(1)}, u32[]{:S(2)}, u32[]{:S(2)}) collective-permute-start(f32[128,256]{1,0:T(8,128)S(1)} %pad_maximum_fusion.8), channel_id=1, source_target_pairs={{0,8},{1,17},{2,10},{3,19},{4,12},{5,21},{6,14},{7,23},{8,0},{9,25... | collective-permute-start | bytes 393224 | tf_op jit(solution)/shard_map/ppermute | solution.py:308
  113.0 9.3 %collective-permute-start.20 = (f32[256,256]{1,0:T(8,128)S(1)}, f32[256,256]{1,0:T(8,128)S(1)}, u32[]{:S(2)}, u32[]{:S(2)}) collective-permute-start(f32[256,256]{1,0:T(8,128)S(1)} %pad_maximum_fusion.6), channel_id=1, source_target_pairs={{0,4},{1,3},{2,6},{3,1},{4,0},{5,7},{6,2},{7,5},{8,12},{9,11},{10,... | collective-permute-start | bytes 786440 | tf_op jit(solution)/shard_map/ppermute | solution.py:308
  115.2 12.7 %collective-permute-start.9 = (f32[256,256]{1,0:T(8,128)S(1)}, f32[256,256]{1,0:T(8,128)S(1)}, u32[]{:S(2)}, u32[]{:S(2)}) collective-permute-start(f32[256,256]{1,0:T(8,128)S(1)} %pad_maximum_fusion.5), channel_id=1, source_target_pairs={{0,4},{1,3},{2,6},{3,1},{4,0},{5,7},{6,2},{7,5},{8,12},{9,11},{10,... | collective-permute-start | bytes 786440 | tf_op jit(solution)/shard_map/ppermute | solution.py:308
  122.3 9.4 %collective-permute-start.21 = (f32[512,256]{1,0:T(8,128)S(1)}, f32[512,256]{1,0:T(8,128)}, u32[]{:S(2)}, u32[]{:S(2)}) collective-permute-start(f32[512,256]{1,0:T(8,128)S(1)} %pad_maximum_fusion.2.refs_1_), channel_id=1, source_target_pairs={{0,2},{1,5},{2,0},{3,7},{4,6},{5,1},{6,4},{7,3},{8,10},{9,13},{10,... | collective-permute-start | bytes 1572872 | tf_op jit(solution)/shard_map/ppermute | solution.py:308
  128.0 9.4 %collective-permute-start.10 = (f32[512,256]{1,0:T(8,128)S(1)}, f32[512,256]{1,0:T(8,128)}, u32[]{:S(2)}, u32[]{:S(2)}) collective-permute-start(f32[512,256]{1,0:T(8,128)S(1)} %pad_maximum_fusion.1.refs_0_), channel_id=1, source_target_pairs={{0,2},{1,5},{2,0},{3,7},{4,6},{5,1},{6,4},{7,3},{8,10},{9,13},{10,... | collective-permute-start | bytes 1572872 | tf_op jit(solution)/shard_map/ppermute | solution.py:308
  129.4 7.9 %collective-permute-start.6 = (f32[128,256]{1,0:T(8,128)S(1)}, f32[128,256]{1,0:T(8,128)S(1)}, u32[]{:S(2)}, u32[]{:S(2)}) collective-permute-start(f32[128,256]{1,0:T(8,128)S(1)} %slice_add_fusion.8.kept), channel_id=1, source_target_pairs={{0,1},{1,0},{2,3},{3,2},{4,5},{5,4},{6,7},{7,6},{8,9},{9,8},{10,11... | collective-permute-start | bytes 393224 | tf_op jit(solution)/shard_map/ppermute | solution.py:305
  129.7 24.8 %collective-permute-start.22 = (f32[512,256]{1,0:T(8,128)S(1)}, f32[512,256]{1,0:T(8,128)S(1)}, u32[]{:S(2)}, u32[]{:S(2)}) collective-permute-start(f32[512,256]{1,0:T(8,128)S(1)} %pad_maximum_fusion.2.refs_1_), channel_id=1, source_target_pairs={{0,1},{1,0},{2,3},{3,2},{4,5},{5,4},{6,7},{7,6},{8,9},{9,8},{10,11... | collective-permute-start | bytes 1572872 | tf_op jit(solution)/shard_map/ppermute | solution.py:305
  130.2 21.3 %collective-permute-start.11 = (f32[512,256]{1,0:T(8,128)S(1)}, f32[512,256]{1,0:T(8,128)S(1)}, u32[]{:S(2)}, u32[]{:S(2)}) collective-permute-start(f32[512,256]{1,0:T(8,128)S(1)} %pad_maximum_fusion.1.refs_0_), channel_id=1, source_target_pairs={{0,1},{1,0},{2,3},{3,2},{4,5},{5,4},{6,7},{7,6},{8,9},{9,8},{10,11... | collective-permute-start | bytes 1572872 | tf_op jit(solution)/shard_map/ppermute | solution.py:305
  131.7 22.8 %collective-permute-start.23 = (f32[512,256]{1,0:T(8,128)}, f32[512,256]{1,0:T(8,128)S(1)}, u32[]{:S(2)}, u32[]{:S(2)}) collective-permute-start(f32[512,256]{1,0:T(8,128)} %collective-permute-done.21.refs_2_), channel_id=1, source_target_pairs={{0,1},{1,0},{2,3},{3,2},{4,5},{5,4},{6,7},{7,6},{8,9},{9,8},{10,11... | collective-permute-start | bytes 1572872 | tf_op jit(solution)/shard_map/ppermute | solution.py:305
  137.3 14.2 %collective-permute-start.12 = (f32[512,256]{1,0:T(8,128)}, f32[512,256]{1,0:T(8,128)S(1)}, u32[]{:S(2)}, u32[]{:S(2)}) collective-permute-start(f32[512,256]{1,0:T(8,128)} %collective-permute-done.10.refs_1_), channel_id=1, source_target_pairs={{0,1},{1,0},{2,3},{3,2},{4,5},{5,4},{6,7},{7,6},{8,9},{9,8},{10,11... | collective-permute-start | bytes 1572872 | tf_op jit(solution)/shard_map/ppermute | solution.py:305

commit v3 on v2

--- a/solution.py
+++ b/solution.py
@@ -36,22 +36,22 @@
         value = value * 2 + ((me >> b) & 1)
     return value
 
-
-def in_vmem(*shape_dtype):
-    return pltpu.VMEM(*shape_dtype)
-
-
-def pinned(*arrays):
-    return [pltpu.with_memory_space_constraint(a, pltpu.VMEM) for a in arrays]
-
-
 VMEM_SPEC = pl.BlockSpec(memory_space=pltpu.VMEM)
 SMEM_SPEC = pl.BlockSpec(memory_space=pltpu.SMEM)
 ANY_SPEC = pl.BlockSpec(memory_space=pl.ANY)
 
 
-def front_kernel(in_scale, gram_scale, me, e, signs, e_kept, sketch, rounded_t, gram_sent, gram_kept, s32, s16, acc, sem):
+def pinned(*arrays):
+    return [pltpu.with_memory_space_constraint(a, pltpu.VMEM) for a in arrays]
+
+
+def front_kernel(
+    in_scale, gram_scale, scale, groups, width,
+    info, e, signs, sketch_out, rounded_out, gram_sent, gram_kept, sent, kept, first,
+    e_kept, sketch, rounded_t, s32, s16, acc, pieces, sem, out_sem,
+):
     rows = e.shape[0]
+    k = rounded_t.shape[0]
     n = sem.shape[0] - 1
     block = rows // n
     signs_copy = pltpu.make_async_copy(signs, s32, sem.at[n])
@@ -75,85 +75,134 @@
         return carry
 
     lax.fori_loop(0, n, step, 0)
+    outs = [
+        pltpu.make_async_copy(sketch, sketch_out, out_sem.at[0]),
+        pltpu.make_async_copy(rounded_t, rounded_out, out_sem.at[1]),
+    ]
+    for copy in outs:
+        copy.start()
     high, low = split(sketch[...])
     acc[...] = dot(rounded_t[...], low)
     acc[...] = (dot(rounded_t[...], high) + (acc[...] + acc[...].T)) * gram_scale
-    half = acc.shape[0] // 2
-    own = me[0] & 1
+    half = k // 2
+    own = info[10] & 1
     gram_kept[...] = acc[pl.ds(pl.multiple_of(own * half, half), half), :]
     gram_sent[...] = acc[pl.ds(pl.multiple_of((1 - own) * half, half), half), :]
-
-
-def front_call(me, e, signs, rows_all):
+    size = k // groups
+    for piece in range(8):
+        at = pl.ds(pl.multiple_of(info[piece] * width, width), width)
+        value = dot(rounded_t[...], e_kept[:, at]) * scale
+        for g in range(groups):
+            to = pl.multiple_of((info[8 + piece // 4] ^ g) * size, size)
+            pieces[piece, pl.ds(to, size), :] = value[g * size : (g + 1) * size]
+        if piece < 4:
+            to = sent.at[pl.ds(piece * k, k)]
+        else:
+            to = (kept if piece < 6 else first).at[pl.ds(piece % 2 * k, k)]
+        outs.append(pltpu.make_async_copy(pieces.at[piece], to, out_sem.at[2 + piece]))
+        outs[-1].start()
+    for copy in outs:
+        copy.wait()
+
+
+def front_call(info, e, signs, rows_all, groups, width):
     rows, d = e.shape
     k = signs.shape[1]
     copies = 4
     return pl.pallas_call(
-        functools.partial(front_kernel, 1.0 / math.sqrt(d), 1.0 / rows_all),
+        functools.partial(
+            front_kernel, 1.0 / math.sqrt(d), 1.0 / rows_all, 1.0 / math.sqrt(rows_all), groups, width
+        ),
         in_specs=[SMEM_SPEC, ANY_SPEC, ANY_SPEC],
-        out_specs=[VMEM_SPEC] * 5,
+        out_specs=[ANY_SPEC] * 2 + [VMEM_SPEC] * 2 + [ANY_SPEC] * 3,
         out_shape=[
-            in_vmem((rows, d), e.dtype),
-            in_vmem((rows, k), jnp.float32),
-            in_vmem((k, rows), jnp.bfloat16),
-            in_vmem((k // 2, k), jnp.float32),
-            in_vmem((k // 2, k), jnp.float32),
+            jax.ShapeDtypeStruct((rows, k), jnp.float32),
+            jax.ShapeDtypeStruct((k, rows), jnp.bfloat16),
+            jax.ShapeDtypeStruct((k // 2, k), jnp.float32),
+            jax.ShapeDtypeStruct((k // 2, k), jnp.float32),
+            jax.ShapeDtypeStruct((4 * k, width), jnp.float32),
+            jax.ShapeDtypeStruct((2 * k, width), jnp.float32),
+            jax.ShapeDtypeStruct((2 * k, width), jnp.float32),
         ],
         scratch_shapes=[
+            pltpu.VMEM((rows, d), e.dtype),
+            pltpu.VMEM((rows, k), jnp.float32),
+            pltpu.VMEM((k, rows), jnp.bfloat16),
             pltpu.VMEM((d, k), jnp.int32),
             pltpu.VMEM((d, k), jnp.bfloat16),
             pltpu.VMEM((k, k), jnp.float32),
+            pltpu.VMEM((8, k, width), jnp.float32),
             pltpu.SemaphoreType.DMA((copies + 1,)),
+            pltpu.SemaphoreType.DMA((10,)),
         ],
-        compiler_params=pltpu.CompilerParams(vmem_limit_bytes=24 * MIB),
-        cost_estimate=pl.CostEstimate(flops=2 * rows * d * k, bytes_accessed=rows * d * 2 + d * k * 4, transcendentals=0),
+        compiler_params=pltpu.CompilerParams(vmem_limit_bytes=56 * MIB),
+        cost_estimate=pl.CostEstimate(flops=3 * rows * d * k, bytes_accessed=rows * d * 2 + d * k * 4, transcendentals=0),
         name="front",
-    )(me, e, pltpu.with_memory_space_constraint(signs, pltpu.HBM))
-
-
-def cross_kernel(scale, groups, width, info, e, rounded_t, *outs):
-    k = rounded_t.shape[0]
-    size = k // groups
-    per = 4 // len(outs)
-    for n in range(4):
-        at = pl.ds(pl.multiple_of(info[n] * width, width), width)
-        value = dot(rounded_t[...], e[:, at]) * scale
+    )(info, e, pltpu.with_memory_space_constraint(signs, pltpu.HBM))
+
+
+def cross_kernel(scale, groups, info, e, rounded_t, sent, kept, first):
+    step = pl.program_id(0)
+    value = dot(rounded_t[...], e[...]) * scale
+    size = value.shape[0] // groups
+    order = info[8 + step // 4]
+
+    def put(out):
         for g in range(groups):
-            to = pl.multiple_of((n % per) * k + (info[4] ^ g) * size, size)
-            outs[n // per][pl.ds(to, size), :] = value[g * size : (g + 1) * size]
-
-
-def cross_call(info, e, rounded_t, scale, groups, width, n_outs):
-    rows, d = e.shape
+            to = pl.multiple_of((order ^ g) * size, size)
+            out[pl.ds(to, size), :] = value[g * size : (g + 1) * size]
+
+    pl.when(step < 4)(lambda: put(sent))
+    pl.when(step // 2 == 2)(lambda: put(kept))
+    pl.when(step // 2 == 3)(lambda: put(first))
+
+
+def cross_call(info, e, rounded_t, rows_all, groups, width):
+    rows = e.shape[0]
     k = rounded_t.shape[0]
     return pl.pallas_call(
-        functools.partial(cross_kernel, scale, groups, width),
-        in_specs=[SMEM_SPEC, VMEM_SPEC, VMEM_SPEC],
-        out_specs=[VMEM_SPEC] * n_outs,
-        out_shape=[in_vmem((4 // n_outs * k, width), jnp.float32)] * n_outs,
+        functools.partial(cross_kernel, 1.0 / math.sqrt(rows_all), groups),
+        grid_spec=pltpu.PrefetchScalarGridSpec(
+            num_scalar_prefetch=1,
+            grid=(8,),
+            in_specs=[
+                pl.BlockSpec((rows, width), lambda i, info: (0, info[i])),
+                pl.BlockSpec((k, rows), lambda i, info: (0, 0), pipeline_mode=pl.Buffered(1)),
+            ],
+            out_specs=[
+                pl.BlockSpec((k, width), lambda i, info, o=o, n=n: (jnp.clip(i - o, 0, n - 1), 0))
+                for o, n in ((0, 4), (4, 2), (6, 2))
+            ],
+        ),
+        out_shape=[jax.ShapeDtypeStruct((n * k, width), jnp.float32) for n in (4, 2, 2)],
         compiler_params=pltpu.CompilerParams(vmem_limit_bytes=16 * MIB),
-        cost_estimate=pl.CostEstimate(flops=2 * rows * k * width * 4, bytes_accessed=0, transcendentals=0),
+        cost_estimate=pl.CostEstimate(flops=16 * rows * k * width, bytes_accessed=rows * width * 16, transcendentals=0),
         name="cross",
-    )(info, *pinned(e, rounded_t))
-
-
-def factor_kernel(me, kept, got, triangle, high, low, work):
-    k = triangle.shape[0]
-    half = k // 2
-    own = me[0] & 1
-    work[pl.ds(pl.multiple_of(own * half, half), half), :k] = kept[...]
-    work[pl.ds(pl.multiple_of((1 - own) * half, half), half), :k] = got[...]
+    )(info, pltpu.with_memory_space_constraint(e, pltpu.HBM), rounded_t)
+
+
+def factor_kernel(part, info, *refs):
+    triangle, high, low, work = refs[-4:]
+    half, k = triangle.shape
     b = 64
-    rows_k = lax.broadcasted_iota(jnp.int32, (k, k), 0)
-    cols_k = lax.broadcasted_iota(jnp.int32, (k, k), 1)
-    work[:, k:] = jnp.where(rows_k == cols_k, 1.0, 0.0)
+    if part == 0:
+        kept, got = refs[:2]
+        own = info[10] & 1
+        work[pl.ds(pl.multiple_of(own * half, half), half), :k] = kept[...]
+        work[pl.ds(pl.multiple_of((1 - own) * half, half), half), :k] = got[...]
+        rows_k = lax.broadcasted_iota(jnp.int32, (k, k), 0)
+        cols_k = lax.broadcasted_iota(jnp.int32, (k, k), 1)
+        work[:, k:] = jnp.where(rows_k == cols_k, 1.0, 0.0)
+    else:
+        work[...] = refs[0][...]
     lane = lax.broadcasted_iota(jnp.int32, (8, 2 * b), 1)
     sub = lax.broadcasted_iota(jnp.int32, (8, 2 * b), 0)
 
     def over_lanes(a, at):
         return jnp.broadcast_to(a[:, at : at + 1], (8, 2 * b))
 
-    for n in range(k // b):
+    for n in range(part * (half // b), (part + 1) * (half // b)):
+        put = slice(n * b - part * half, (n + 1) * b - part * half)
         first = (n % 2) * b
         pair = (n // 2) * 2 * b
         own_lanes = (lane >= first) & (lane < first + b)
@@ -198,11 +247,11 @@
         r_rows, i_rows = y[:, :k], y[:, k:]
         at = lax.broadcasted_iota(jnp.int32, (b, k), 0) + n * b
         to = lax.broadcasted_iota(jnp.int32, (b, k), 1)
-        triangle[n * b : (n + 1) * b, :] = jnp.where(to >= at, r_rows, 0.0)
+        triangle[put, :] = jnp.where(to >= at, r_rows, 0.0)
         i_rows = jnp.where(to <= at, i_rows, 0.0)
         i_high, i_low = split(i_rows)
-        high[n * b : (n + 1) * b, :] = i_high
-        low[n * b : (n + 1) * b, :] = i_low
+        high[put, :] = i_high
+        low[put, :] = i_low
         if (n + 1) * b < k:
             later = jnp.where(to >= (n + 1) * b, r_rows, 0.0)
             work[...] -= lax.dot_general(
@@ -211,22 +260,22 @@
             )
 
 
-def factor_call(me, kept, got):
-    k = kept.shape[1]
+def factor_call(part, info, *inputs):
+    k = inputs[0].shape[0] * (2 - part)
     return pl.pallas_call(
-        factor_kernel,
-        in_specs=[SMEM_SPEC, VMEM_SPEC, VMEM_SPEC],
-        out_specs=[VMEM_SPEC] * 3,
+        functools.partial(factor_kernel, part),
+        in_specs=[SMEM_SPEC] + [VMEM_SPEC] * len(inputs),
+        out_specs=[VMEM_SPEC] * 4,
         out_shape=[
-            jax.ShapeDtypeStruct((k, k), jnp.float32),
-            in_vmem((k, k), jnp.bfloat16),
-            in_vmem((k, k), jnp.bfloat16),
+            jax.ShapeDtypeStruct((k // 2, k), jnp.float32),
+            jax.ShapeDtypeStruct((k // 2, k), jnp.bfloat16),
+            jax.ShapeDtypeStruct((k // 2, k), jnp.bfloat16),
+            jax.ShapeDtypeStruct((k, 2 * k), jnp.float32),
         ],
-        scratch_shapes=[pltpu.VMEM((k, 2 * k), jnp.float32)],
         compiler_params=pltpu.CompilerParams(vmem_limit_bytes=16 * MIB),
-        cost_estimate=pl.CostEstimate(flops=10**10, bytes_accessed=k * k * 8, transcendentals=0),
+        cost_estimate=pl.CostEstimate(flops=5 * 10**9, bytes_accessed=k * k * 8, transcendentals=0),
         name="factor",
-    )(me, kept, got)
+    )(info, *inputs)
 
 
 def basis_kernel(sketch, high, low, out):
@@ -315,7 +364,6 @@
         d = e.shape[1]
         k = signs.shape[1]
         width = d // (8 * CHUNKS)
-        scale = 1.0 / math.sqrt(rows_all)
         me = lax.axis_index(AXES).astype(jnp.int32)
         own = me & 1
         place = [bits_of(me, o[:2]) for o in orders]
@@ -323,54 +371,81 @@
         mine = lambda pair: jnp.where(own == 0, pair[0], pair[1])
         other = lambda pair: jnp.where(own == 0, pair[1], pair[0])
 
-        def blocks_at(chunk, region, at):
-            return [(chunk * 2 + region) * 4 + (at ^ n) for n in range(4)]
-
-        def vector(*values):
-            return jnp.stack([jnp.asarray(v, jnp.int32) for v in values])
-
-        me1 = me[None]
-        e_kept, sketch, rounded_t, gram_sent, gram = front_call(me1, e, signs, rows_all)
-        gram = gram + with_pair(gram_sent)
-
-        stay, go, whole = [], [], []
-        for chunk in range(CHUNKS):
-            (sent,) = cross_call(
-                vector(*blocks_at(chunk, 1 - own, other(place)), other(rest)), e_kept, rounded_t, scale, groups, width, 1
-            )
-            kept, first = cross_call(
-                vector(*blocks_at(chunk, own, mine(place)), mine(rest)), e_kept, rounded_t, scale, groups, width, 2
-            )
-            got = with_pair(sent)
-            stay.append(kept + got[: 2 * k])
-            go.append(first + got[2 * k :])
-            whole.append([gram] if chunk == 0 else [])
-        for s in range(steps):
-            for chunk in range(CHUNKS):
-                r = swap(join(go[chunk], *whole[chunk]), s)
-                n = stay[chunk].shape[0]
-                a = stay[chunk] + r[:n]
-                whole[chunk] = [g + r[n:] for g in whole[chunk]]
-                stay[chunk], go[chunk] = a[: n // 2], a[n // 2 :]
-                if s == steps - 1:
-                    stay[chunk] = a
-        triangle, high, low = factor_call(me1, whole[0][0], with_pair(whole[0][0]))
-        last = []
-        for s in range(steps - 1, -1, -1):
-            for chunk in range(CHUNKS):
-                r = swap(stay[chunk], s)
-                if s:
-                    stay[chunk] = join(stay[chunk], r)
-                else:
-                    last.append(r)
-        basis = basis_call(sketch, high, low)
-        projected = None
-        for chunk in range(CHUNKS):
-            blocks = [stay[chunk], last[chunk], with_pair(stay[chunk]), with_pair(last[chunk])]
-            info = vector(
-                *blocks_at(chunk, own, mine(place)), *blocks_at(chunk, 1 - own, other(place)), mine(rest), other(rest)
-            )
-            projected = project_call(info, high, low, blocks, groups, d, projected)
+        def info_of(chunk):
+            at = [(chunk * 2 + 1 - own) * 4 + (other(place) ^ n) for n in range(4)]
+            at += [(chunk * 2 + own) * 4 + (mine(place) ^ n) for n in range(4)]
+            return jnp.stack(at + [other(rest), mine(rest), me])
+
+        infos = [info_of(chunk) for chunk in range(CHUNKS)]
+        last = [me]
+
+        def in_turn(a):
+            a, _ = lax.optimization_barrier((a, last[0]))
+            last[0] = a
+            return a
+
+        sketch, rounded_t, gram_sent, gram, sent, kept, first = front_call(infos[0], e, signs, rows_all, groups, width)
+        got, gram_got = with_pair(sent), with_pair(gram_sent)
+        gram = gram + gram_got
+        stay, go = [kept + got[: 2 * k], None], [in_turn(join(first + got[2 * k :], gram)), None]
+        part = {0: swap(go[0], 0)}
+        sent, kept, first = cross_call(infos[1], e, in_turn(rounded_t), rows_all, groups, width)
+        got = with_pair(in_turn(sent))
+        stay[1], go[1] = kept + got[: 2 * k], first + got[2 * k :]
+
+        def halve(chunk, s):
+            nonlocal gram
+            r = part[chunk]
+            n = stay[chunk].shape[0]
+            a = stay[chunk] + r[:n]
+            if chunk == 0:
+                gram = gram + r[n:]
+            if s == steps - 1:
+                stay[chunk] = in_turn(a)
+                return
+            stay[chunk] = a[: n // 2]
+            send = a[n // 2 :]
+            part[chunk] = swap(in_turn(join(send, gram) if chunk == 0 else send), s + 1)
+
+        def double(chunk, s):
+            part[chunk] = swap(stay[chunk], s)
+
+        def joined(chunk):
+            stay[chunk] = in_turn(join(stay[chunk], part[chunk]))
+
+        S = steps
+        halve(0, 0)
+        part[1] = swap(in_turn(go[1]), 0)
+        for s in range(1, S):
+            halve(0, s)
+        double(0, S - 1)
+        gram_got = with_pair(gram)
+        down = list(range(S - 1, 0, -1))
+        for i in range(max(S, len(down))):
+            if i < S:
+                halve(1, i)
+            if i < len(down):
+                joined(0)
+                double(0, down[i] - 1)
+        double(1, S - 1)
+        triangle_a, high_a, low_a, work = factor_call(0, infos[0], in_turn(gram), gram_got)
+        for s in down[:-1]:
+            joined(1)
+            double(1, s - 1)
+        far = [None, None]
+        far[0] = in_turn(part[0])
+        from_pair = [[with_pair(stay[0]), with_pair(far[0])], None]
+        joined(1)
+        double(1, 0)
+        pair_stay = with_pair(stay[1])
+        triangle_b, high_b, low_b, _ = factor_call(1, infos[0], in_turn(work))
+        triangle = join(triangle_a, triangle_b)
+        high, low = in_turn(join(high_a, high_b)), join(low_a, low_b)
+        basis = in_turn(basis_call(sketch, high, low))
+        projected = in_turn(project_call(infos[0], high, low, [*from_pair[0], stay[0], far[0]], groups, d, None))
+        far[1], projected = lax.optimization_barrier((part[1], projected))
+        blocks = [pair_stay, with_pair(far[1]), stay[1], far[1]]
+        projected = project_call(infos[1], high, low, blocks, groups, d, projected)
         return triangle, basis, projected
 
     return jax.shard_map(

time: 158 us -> 120 us (0.76)
  local copies, waits for them, and re-layouts: 31 us -> 2.02 us
  starting transfers between devices: 34 us -> 28.5 us
  waiting for transfers between devices: 47.3 us -> 42.9 us
  Pallas kernels: 39.1 us -> 42 us
    unnamed x18 -> x9, local copies, waits for them, and re-layouts: 30.4 us -> 1.24 us
    ppermute x16, waiting for transfers between devices: 47.3 us -> 39.4 us  [swap(): return lax.ppermute(a, AXES, swaps[s])]
    ppermute x16, starting transfers between devices: 32.4 us -> 26.8 us  [swap(): return lax.ppermute(a, AXES, swaps[s])]
    pallas_call x1, Pallas kernels: 9.66 us -> 14 us  [front_call(): pl.pallas_call(functools.partial(front_kernel, 1.0 / math.sqrt(d), 1.0 /...]
    ppermute x8, waiting for transfers between devices: 0.02 us -> 3.44 us  [with_pair(): return lax.ppermute(a, AXES, pairs)]
    add x14, other arithmetic: 4.77 us -> 2.51 us  [the longest x1 1.11 us: shards(): first + got[2 * k:]]
    pallas_call x5 -> x3, Pallas kernels: 21 us -> 20.5 us  [the longest x2 12.2 us: factor_call(): pl.pallas_call(functools.partial(factor_kernel, part), in_specs=[SMEM_SPE...]
  transfers between devices with their start and end apart: 24 -> 24, of which waited for: 12 -> 14; matrix products, arithmetic and copies ran while one was open for 3% -> 2% of each run, Pallas kernels for 15% -> 21%
where the time goes in v3:
time: 120 us
  waiting for transfers between devices  42.9 us (36%)
  Pallas kernels  42 us (35%)
  starting transfers between devices  28.5 us (24%)
  other arithmetic  3.47 us (3%)
  local copies, waits for them, and re-layouts  2.02 us (2%)
    ppermute x16, waiting for transfers between devices, swap(): return lax.ppermute(a, AXES, swaps[s])  39.4 us
    ppermute x16, starting transfers between devices, swap(): return lax.ppermute(a, AXES, swaps[s])  26.8 us
    pallas_call x1, Pallas kernels, front_call(): pl.pallas_call(functools.partial(front_kernel, 1.0 / math.sqrt(d), 1.0 /...  14 us
    pallas_call x2, Pallas kernels, factor_call(): pl.pallas_call(functools.partial(factor_kernel, part), in_specs=[SMEM_SPE...  12.2 us
    pallas_call x1, Pallas kernels, cross_call(): pl.pallas_call(functools.partial(cross_kernel, 1.0 / math.sqrt(rows_all),...  8.27 us
    pallas_call x2, Pallas kernels, project_call(): pl.pallas_call(functools.partial(project_kernel, groups, width), in_specs...  4.84 us
    ppermute x8, waiting for transfers between devices, with_pair(): return lax.ppermute(a, AXES, pairs)  3.44 us
    pallas_call x1, Pallas kernels, basis_call(): pl.pallas_call(basis_kernel, grid=(rows // block,), in_specs=[pl.BlockSpe...  2.67 us
  transfers between devices with their start and end apart: 24, of which 14 were waited for; matrix products, arithmetic and copies ran while one was open for 2% of the time, Pallas kernels for 21%

profile of v3, /device:TPU:0, one launch (start us, length us, event | category | flops | bytes accessed | tf_op | source)
XLA Modules:
  0.0 120.0 jit_solution(8008320030223859983)
XLA Ops:
  0.7 0.6 stack.77.info
  1.3 14.0 %front.1 = (f32[2048,256]{1,0:T(8,128)}, bf16[256,2048]{1,0:T(8,128)(2,1)}, f32[128,256]{1,0:T(8,128)}, f32[128,256]{1,0:T(8,128)}, f32[1024,256]{1,0:T(8,128)}, /*index=5*/f32[512,256]{1,0:T(8,128)}, f32[512,256]{1,0:T(8,128)}) custom-call(s32[11]{0:T(128)} %stack.77.info, bf16[2048,4096]{1,0:T(8,128)(2,1)} %e.3, s32[4096,256]{1,0:T(8,128)} %signs.1), custom_call_target="tpu_custom_call" | custom-call | flops 6442450944 | bytes 20971520 | tf_op jit(solution)/shard_map/front/pallas_call | solution.py:112
  15.3 0.5 collective-permute-start.1
  15.9 2.6 %collective-permute-done = f32[128,256]{1,0:T(8,128)S(1)} collective-permute-done((f32[128,256]{1,0:T(8,128)}, f32[128,256]{1,0:T(8,128)S(1)}, u32[]{:S(2)}, u32[]{:S(2)}) %collective-permute-start) | collective-permute-done | bytes 131104 | tf_op jit(solution)/shard_map/ppermute | solution.py:354
  18.5 0.9 add.133
  19.5 1.1 slice_add_fusion.4
  20.6 2.9 %collective-permute-start.2 = (f32[640,256]{1,0:T(8,128)S(1)}, f32[640,256]{1,0:T(8,128)S(1)}, u32[]{:S(2)}, u32[]{:S(2)}) collective-permute-start(f32[640,256]{1,0:T(8,128)S(1)} %pad_maximum_fusion), channel_id=1, source_target_pairs={{0,2},{1,5},{2,0},{3,7},{4,6},{5,1},{6,4},{7,3},{8,10},{9,13},{10,... | collective-permute-start | bytes 1966088 | tf_op jit(solution)/shard_map/ppermute | solution.py:357
  23.6 0.1 stack.86.info
  23.7 1.2 %copy-done.1 = bf16[256,2048]{1,0:T(8,128)(2,1)S(1)} copy-done((bf16[256,2048]{1,0:T(8,128)(2,1)S(1)}, bf16[256,2048]{1,0:T(8,128)(2,1)}, u32[]{:S(2)}) %copy-start.1) | copy-done | bytes 1048600
  24.9 8.3 %cross.1 = (f32[1024,256]{1,0:T(8,128)S(1)}, f32[512,256]{1,0:T(8,128)S(1)}, f32[512,256]{1,0:T(8,128)S(1)}) custom-call(s32[11]{0:T(128)S(1)} %stack.86.info, bf16[2048,4096]{1,0:T(8,128)(2,1)} %e.3, bf16[256,2048]{1,0:T(8,128)(2,1)S(1)} %copy-done.1), custom_call_target="tpu_custom_call" | custom-call | flops 2147483648 | bytes 8388608 | tf_op jit(solution)/shard_map/cross/pallas_call | solution.py:163
  33.3 0.1 slice_add_fusion.2
  33.5 1.6 %collective-permute-start.3 = (f32[384,256]{1,0:T(8,128)S(1)}, f32[384,256]{1,0:T(8,128)S(1)}, u32[]{:S(2)}, u32[]{:S(2)}) collective-permute-start(f32[384,256]{1,0:T(8,128)S(1)} %pad_maximum_fusion.3), channel_id=1, source_target_pairs={{0,4},{1,3},{2,6},{3,1},{4,0},{5,7},{6,2},{7,5},{8,12},{9,11},{10,... | collective-permute-start | bytes 1179656 | tf_op jit(solution)/shard_map/ppermute | solution.py:357
  35.1 6.2 %collective-permute-done.3 = f32[384,256]{1,0:T(8,128)S(1)} collective-permute-done((f32[384,256]{1,0:T(8,128)S(1)}, f32[384,256]{1,0:T(8,128)S(1)}, u32[]{:S(2)}, u32[]{:S(2)}) %collective-permute-start.3) | collective-permute-done | bytes 393248 | tf_op jit(solution)/shard_map/ppermute | solution.py:357
  41.5 1.6 %collective-permute-start.5 = (f32[256,256]{1,0:T(8,128)S(1)}, f32[256,256]{1,0:T(8,128)S(1)}, u32[]{:S(2)}, u32[]{:S(2)}) collective-permute-start(f32[256,256]{1,0:T(8,128)S(1)} %pad_maximum_fusion.4), channel_id=1, source_target_pairs={{0,8},{1,17},{2,10},{3,19},{4,12},{5,21},{6,14},{7,23},{8,0},{9,25... | collective-permute-start | bytes 786440 | tf_op jit(solution)/shard_map/ppermute | solution.py:357
  43.1 1.4 %collective-permute-start.7 = (f32[512,256]{1,0:T(8,128)S(1)}, f32[512,256]{1,0:T(8,128)S(1)}, u32[]{:S(2)}, u32[]{:S(2)}) collective-permute-start(f32[512,256]{1,0:T(8,128)S(1)} %slice_add_fusion.1), channel_id=1, source_target_pairs={{0,2},{1,5},{2,0},{3,7},{4,6},{5,1},{6,4},{7,3},{8,10},{9,13},{10,... | collective-permute-start | bytes 1572872 | tf_op jit(solution)/shard_map/ppermute | solution.py:357
  44.5 5.4 %collective-permute-done.5 = f32[256,256]{1,0:T(8,128)S(1)} collective-permute-done((f32[256,256]{1,0:T(8,128)S(1)}, f32[256,256]{1,0:T(8,128)S(1)}, u32[]{:S(2)}, u32[]{:S(2)}) %collective-permute-start.5) | collective-permute-done | bytes 262176 | tf_op jit(solution)/shard_map/ppermute | solution.py:357
  50.0 2.5 %collective-permute-start.6 = (f32[192,256]{1,0:T(8,128)S(1)}, f32[192,256]{1,0:T(8,128)S(1)}, u32[]{:S(2)}, u32[]{:S(2)}) collective-permute-start(f32[192,256]{1,0:T(8,128)S(1)} %pad_maximum_fusion.8), channel_id=1, source_target_pairs={{0,16},{1,9},{2,18},{3,11},{4,20},{5,13},{6,22},{7,15},{8,24},{9,1... | collective-permute-start | bytes 589832 | tf_op jit(solution)/shard_map/ppermute | solution.py:357
  52.5 4.7 %collective-permute-done.6 = f32[192,256]{1,0:T(8,128)S(1)} collective-permute-done((f32[192,256]{1,0:T(8,128)S(1)}, f32[192,256]{1,0:T(8,128)S(1)}, u32[]{:S(2)}, u32[]{:S(2)}) %collective-permute-start.6) | collective-permute-done | bytes 196640 | tf_op jit(solution)/shard_map/ppermute | solution.py:357
  57.2 0.1 fusion
  57.4 1.6 %collective-permute-start.8 = (f32[256,256]{1,0:T(8,128)S(1)}, f32[256,256]{1,0:T(8,128)S(1)}, u32[]{:S(2)}, u32[]{:S(2)}) collective-permute-start(f32[256,256]{1,0:T(8,128)S(1)} %slice.113), channel_id=1, source_target_pairs={{0,4},{1,3},{2,6},{3,1},{4,0},{5,7},{6,2},{7,5},{8,12},{9,11},{10,... | collective-permute-start | bytes 786440 | tf_op jit(solution)/shard_map/ppermute | solution.py:357
  59.0 2.0 %collective-permute-start.9 = (f32[64,256]{1,0:T(8,128)S(1)}, f32[64,256]{1,0:T(8,128)S(1)}, u32[]{:S(2)}, u32[]{:S(2)}) collective-permute-start(f32[64,256]{1,0:T(8,128)S(1)} %slice_add_fusion.14), channel_id=1, source_target_pairs={{0,16},{1,9},{2,18},{3,11},{4,20},{5,13},{6,22},{7,15},{8,24},{9,1... | collective-permute-start | bytes 196616 | tf_op jit(solution)/shard_map/ppermute | solution.py:357
  60.9 3.2 %collective-permute-done.9 = f32[64,256]{1,0:T(8,128)S(1)} collective-permute-done((f32[64,256]{1,0:T(8,128)S(1)}, f32[64,256]{1,0:T(8,128)S(1)}, u32[]{:S(2)}, u32[]{:S(2)}) %collective-permute-start.9) | collective-permute-done | bytes 65568 | tf_op jit(solution)/shard_map/ppermute | solution.py:357
  64.1 4.4 %collective-permute-start.11 = (f32[128,256]{1,0:T(8,128)S(1)}, f32[128,256]{1,0:T(8,128)S(1)}, u32[]{:S(2)}, u32[]{:S(2)}) collective-permute-start(f32[128,256]{1,0:T(8,128)S(1)} %pad_maximum_fusion.9), channel_id=1, source_target_pairs={{0,8},{1,17},{2,10},{3,19},{4,12},{5,21},{6,14},{7,23},{8,0},{9,25... | collective-permute-start | bytes 393224 | tf_op jit(solution)/shard_map/ppermute | solution.py:357
  68.6 0.1 collective-permute-start.10
  68.7 3.2 %collective-permute-done.11 = f32[128,256]{1,0:T(8,128)S(1)} collective-permute-done((f32[128,256]{1,0:T(8,128)S(1)}, f32[128,256]{1,0:T(8,128)S(1)}, u32[]{:S(2)}, u32[]{:S(2)}) %collective-permute-start.11) | collective-permute-done | bytes 131104 | tf_op jit(solution)/shard_map/ppermute | solution.py:357
  71.9 2.4 %collective-permute-done.10 = f32[128,256]{1,0:T(8,128)S(1)} collective-permute-done((f32[128,256]{1,0:T(8,128)S(1)}, f32[128,256]{1,0:T(8,128)S(1)}, u32[]{:S(2)}, u32[]{:S(2)}) %collective-permute-start.10) | collective-permute-done | bytes 131104 | tf_op jit(solution)/shard_map/ppermute | solution.py:357
  74.3 2.8 %collective-permute-start.12 = (f32[64,256]{1,0:T(8,128)S(1)}, f32[64,256]{1,0:T(8,128)S(1)}, u32[]{:S(2)}, u32[]{:S(2)}) collective-permute-start(f32[64,256]{1,0:T(8,128)S(1)} %slice.119), channel_id=1, source_target_pairs={{0,16},{1,9},{2,18},{3,11},{4,20},{5,13},{6,22},{7,15},{8,24},{9,1... | collective-permute-start | bytes 196616 | tf_op jit(solution)/shard_map/ppermute | solution.py:357
  77.1 0.7 collective-permute-start.13
  77.8 1.9 %collective-permute-done.12 = f32[64,256]{1,0:T(8,128)S(1)} collective-permute-done((f32[64,256]{1,0:T(8,128)S(1)}, f32[64,256]{1,0:T(8,128)S(1)}, u32[]{:S(2)}, u32[]{:S(2)}) %collective-permute-start.12) | collective-permute-done | bytes 65568 | tf_op jit(solution)/shard_map/ppermute | solution.py:357
  79.7 3.8 %collective-permute-done.13 = f32[256,256]{1,0:T(8,128)S(1)} collective-permute-done((f32[256,256]{1,0:T(8,128)S(1)}, f32[256,256]{1,0:T(8,128)S(1)}, u32[]{:S(2)}, u32[]{:S(2)}) %collective-permute-start.13) | collective-permute-done | bytes 262176 | tf_op jit(solution)/shard_map/ppermute | solution.py:357
  83.5 0.3 collective-permute-start.15
  83.8 4.9 %collective-permute-done.15 = f32[64,256]{1,0:T(8,128)S(1)} collective-permute-done((f32[64,256]{1,0:T(8,128)S(1)}, f32[64,256]{1,0:T(8,128)S(1)}, u32[]{:S(2)}, u32[]{:S(2)}) %collective-permute-start.15) | collective-permute-done | bytes 65568 | tf_op jit(solution)/shard_map/ppermute | solution.py:357
  88.8 2.0 %collective-permute-start.16 = (f32[128,256]{1,0:T(8,128)S(1)}, f32[128,256]{1,0:T(8,128)S(1)}, u32[]{:S(2)}, u32[]{:S(2)}) collective-permute-start(f32[128,256]{1,0:T(8,128)S(1)} %pad_maximum_fusion.10), channel_id=1, source_target_pairs={{0,8},{1,17},{2,10},{3,19},{4,12},{5,21},{6,14},{7,23},{8,0},{9,25... | collective-permute-start | bytes 393224 | tf_op jit(solution)/shard_map/ppermute | solution.py:357
  90.8 0.5 collective-permute-start.20
  91.3 0.8 collective-permute-start.18
  92.2 1.6 %collective-permute-done.16 = f32[128,256]{1,0:T(8,128)S(1)} collective-permute-done((f32[128,256]{1,0:T(8,128)S(1)}, f32[128,256]{1,0:T(8,128)S(1)}, u32[]{:S(2)}, u32[]{:S(2)}) %collective-permute-start.16) | collective-permute-done | bytes 131104 | tf_op jit(solution)/shard_map/ppermute | solution.py:357
  93.8 0.7 collective-permute-start.17
  94.6 6.2 %factor.2 = (f32[128,256]{1,0:T(8,128)S(1)}, bf16[128,256]{1,0:T(8,128)(2,1)S(1)}, bf16[128,256]{1,0:T(8,128)(2,1)S(1)}, f32[256,512]{1,0:T(8,128)S(1)}) custom-call(s32[11]{0:T(128)S(1)} %copy-done.2, f32[128,256]{1,0:T(8,128)S(1)} %slice_add_fusion.8.refs_0_, f32[128,256]{1,0:T(8,128)S(1)} %collective-permute-done.14.refs_1_), custom_call_target="tpu_custom_call" | custom-call | flops 5000000000 | bytes 524288 | tf_op jit(solution)/shard_map/factor/pallas_call | solution.py:265
  100.8 1.6 %collective-permute-done.17 = f32[256,256]{1,0:T(8,128)S(1)} collective-permute-done((f32[256,256]{1,0:T(8,128)S(1)}, f32[256,256]{1,0:T(8,128)S(1)}, u32[]{:S(2)}, u32[]{:S(2)}) %collective-permute-start.17) | collective-permute-done | bytes 262176 | tf_op jit(solution)/shard_map/ppermute | solution.py:357
  102.4 0.4 collective-permute-done.18.refs_3_
  102.8 1.3 %collective-permute-start.19 = (f32[512,256]{1,0:T(8,128)S(1)}, f32[512,256]{1,0:T(8,128)S(1)}, u32[]{:S(2)}, u32[]{:S(2)}) collective-permute-start(f32[512,256]{1,0:T(8,128)S(1)} %pad_maximum_fusion.2.refs_3_), channel_id=1, source_target_pairs={{0,2},{1,5},{2,0},{3,7},{4,6},{5,1},{6,4},{7,3},{8,10},{9,13},{10,... | collective-permute-start | bytes 1572872 | tf_op jit(solution)/shard_map/ppermute | solution.py:357
  104.2 6.0 %factor.3 = (f32[128,256]{1,0:T(8,128)S(1)}, bf16[128,256]{1,0:T(8,128)(2,1)S(1)}, bf16[128,256]{1,0:T(8,128)(2,1)S(1)}, f32[256,512]{1,0:T(8,128)}) custom-call(s32[11]{0:T(128)S(1)} %copy-done.2, f32[256,512]{1,0:T(8,128)S(1)} %get-tuple-element.77.refs_0_), custom_call_target="tpu_custom_call" | custom-call | flops 5000000000 | bytes 524288 | tf_op jit(solution)/shard_map/factor/pallas_call | solution.py:265
  110.3 2.7 %basis.1 = bf16[2048,256]{1,0:T(8,128)(2,1)} custom-call(f32[2048,256]{1,0:T(8,128)S(1)} %copy-done, bf16[256,256]{1,0:T(8,128)(2,1)S(1)} %pad_maximum_fusion.11.high, bf16[256,256]{1,0:T(8,128)(2,1)S(1)} %constant_dynamic-update-slice_fusion.low), custom_call_target="tpu_custom_call" | custom-call | flops 805306368 | bytes 3145728 | tf_op jit(solution)/shard_map/basis/pallas_call | solution.py:292
  113.0 2.4 %project.2.refs_0_ = f32[256,4096]{1,0:T(8,128)} custom-call(s32[11]{0:T(128)S(1)} %copy-done.2, bf16[256,256]{1,0:T(8,128)(2,1)S(1)} %pad_maximum_fusion.11.high, bf16[256,256]{1,0:T(8,128)(2,1)S(1)} %constant_dynamic-update-slice_fusion.low, f32[512,256]{1,0:T(8,128)S(1)} %collective-permute-done.20.refs_0_, ...), custom_call_target="tpu_custom_call" | custom-call | flops 805306368 | bytes 2097152 | tf_op jit(solution)/shard_map/project/pallas_call | solution.py:332
  115.4 0.5 collective-permute-start.23
  115.9 0.7 pad_maximum_fusion.7
  116.6 0.8 collective-permute-done.23.refs_2_
  117.4 2.4 %project.3 = f32[256,4096]{1,0:T(8,128)} custom-call(s32[11]{0:T(128)S(1)} %stack.86.info, bf16[256,256]{1,0:T(8,128)(2,1)S(1)} %pad_maximum_fusion.11.high, bf16[256,256]{1,0:T(8,128)(2,1)S(1)} %constant_dynamic-update-slice_fusion.low, f32[256,4096]{1,0:T(8,128)} %project.2.refs_0_, ...), custom_call_target="tpu_custom_call", output_to_operand_aliasing={{}: (3, {})} | custom-call | flops 805306368 | bytes 2097152 | tf_op jit(solution)/shard_map/project/pallas_call | solution.py:332
  (51 shorter events, 0.8 us)
Async XLA Ops:
  15.3 4.1 %collective-permute-start.1 = (f32[1024,256]{1,0:T(8,128)}, f32[1024,256]{1,0:T(8,128)S(1)}, u32[]{:S(2)}, u32[]{:S(2)}) collective-permute-start(f32[1024,256]{1,0:T(8,128)} %get-tuple-element.49), channel_id=1, source_target_pairs={{0,1},{1,0},{2,3},{3,2},{4,5},{5,4},{6,7},{7,6},{8,9},{9,8},{10,11... | collective-permute-start | bytes 3145736 | tf_op jit(solution)/shard_map/ppermute | solution.py:354
  15.9 2.7 %collective-permute-start = (f32[128,256]{1,0:T(8,128)}, f32[128,256]{1,0:T(8,128)S(1)}, u32[]{:S(2)}, u32[]{:S(2)}) collective-permute-start(f32[128,256]{1,0:T(8,128)} %get-tuple-element.47), channel_id=1, source_target_pairs={{0,1},{1,0},{2,3},{3,2},{4,5},{5,4},{6,7},{7,6},{8,9},{9,8},{10,11... | collective-permute-start | bytes 393224 | tf_op jit(solution)/shard_map/ppermute | solution.py:354
  20.6 12.6 %collective-permute-start.2 = (f32[640,256]{1,0:T(8,128)S(1)}, f32[640,256]{1,0:T(8,128)S(1)}, u32[]{:S(2)}, u32[]{:S(2)}) collective-permute-start(f32[640,256]{1,0:T(8,128)S(1)} %pad_maximum_fusion), channel_id=1, source_target_pairs={{0,2},{1,5},{2,0},{3,7},{4,6},{5,1},{6,4},{7,3},{8,10},{9,13},{10,... | collective-permute-start | bytes 1966088 | tf_op jit(solution)/shard_map/ppermute | solution.py:357
  23.6 1.2 %copy-start.1 = (bf16[256,2048]{1,0:T(8,128)(2,1)S(1)}, bf16[256,2048]{1,0:T(8,128)(2,1)}, u32[]{:S(2)}) copy-start(bf16[256,2048]{1,0:T(8,128)(2,1)} %get-tuple-element.53.rounded_t) | copy-start | bytes 3145732
  24.9 8.4 %copy-start.3 = (f32[512,256]{1,0:T(8,128)S(1)}, f32[512,256]{1,0:T(8,128)}, u32[]{:S(2)}) copy-start(f32[512,256]{1,0:T(8,128)} %get-tuple-element.51) | copy-start | bytes 1572868
  33.2 8.2 %collective-permute-start.4 = (f32[1024,256]{1,0:T(8,128)S(1)}, f32[1024,256]{1,0:T(8,128)S(1)}, u32[]{:S(2)}, u32[]{:S(2)}) collective-permute-start(f32[1024,256]{1,0:T(8,128)S(1)} %get-tuple-element.55), channel_id=1, source_target_pairs={{0,1},{1,0},{2,3},{3,2},{4,5},{5,4},{6,7},{7,6},{8,9},{9,8},{10,11... | collective-permute-start | bytes 3145736 | tf_op jit(solution)/shard_map/ppermute | solution.py:354
  33.5 7.8 %collective-permute-start.3 = (f32[384,256]{1,0:T(8,128)S(1)}, f32[384,256]{1,0:T(8,128)S(1)}, u32[]{:S(2)}, u32[]{:S(2)}) collective-permute-start(f32[384,256]{1,0:T(8,128)S(1)} %pad_maximum_fusion.3), channel_id=1, source_target_pairs={{0,4},{1,3},{2,6},{3,1},{4,0},{5,7},{6,2},{7,5},{8,12},{9,11},{10,... | collective-permute-start | bytes 1179656 | tf_op jit(solution)/shard_map/ppermute | solution.py:357
  41.5 8.4 %collective-permute-start.5 = (f32[256,256]{1,0:T(8,128)S(1)}, f32[256,256]{1,0:T(8,128)S(1)}, u32[]{:S(2)}, u32[]{:S(2)}) collective-permute-start(f32[256,256]{1,0:T(8,128)S(1)} %pad_maximum_fusion.4), channel_id=1, source_target_pairs={{0,8},{1,17},{2,10},{3,19},{4,12},{5,21},{6,14},{7,23},{8,0},{9,25... | collective-permute-start | bytes 786440 | tf_op jit(solution)/shard_map/ppermute | solution.py:357
  43.1 14.1 %collective-permute-start.7 = (f32[512,256]{1,0:T(8,128)S(1)}, f32[512,256]{1,0:T(8,128)S(1)}, u32[]{:S(2)}, u32[]{:S(2)}) collective-permute-start(f32[512,256]{1,0:T(8,128)S(1)} %slice_add_fusion.1), channel_id=1, source_target_pairs={{0,2},{1,5},{2,0},{3,7},{4,6},{5,1},{6,4},{7,3},{8,10},{9,13},{10,... | collective-permute-start | bytes 1572872 | tf_op jit(solution)/shard_map/ppermute | solution.py:357
  49.9 44.7 %copy-start.2 = (s32[11]{0:T(128)S(1)}, s32[11]{0:T(128)}, u32[]{:S(2)}) copy-start(s32[11]{0:T(128)} %stack.77.info) | copy-start | bytes 136
  50.0 7.2 %collective-permute-start.6 = (f32[192,256]{1,0:T(8,128)S(1)}, f32[192,256]{1,0:T(8,128)S(1)}, u32[]{:S(2)}, u32[]{:S(2)}) collective-permute-start(f32[192,256]{1,0:T(8,128)S(1)} %pad_maximum_fusion.8), channel_id=1, source_target_pairs={{0,16},{1,9},{2,18},{3,11},{4,20},{5,13},{6,22},{7,15},{8,24},{9,1... | collective-permute-start | bytes 589832 | tf_op jit(solution)/shard_map/ppermute | solution.py:357
  57.4 11.2 %collective-permute-start.8 = (f32[256,256]{1,0:T(8,128)S(1)}, f32[256,256]{1,0:T(8,128)S(1)}, u32[]{:S(2)}, u32[]{:S(2)}) collective-permute-start(f32[256,256]{1,0:T(8,128)S(1)} %slice.113), channel_id=1, source_target_pairs={{0,4},{1,3},{2,6},{3,1},{4,0},{5,7},{6,2},{7,5},{8,12},{9,11},{10,... | collective-permute-start | bytes 786440 | tf_op jit(solution)/shard_map/ppermute | solution.py:357
  59.0 5.2 %collective-permute-start.9 = (f32[64,256]{1,0:T(8,128)S(1)}, f32[64,256]{1,0:T(8,128)S(1)}, u32[]{:S(2)}, u32[]{:S(2)}) collective-permute-start(f32[64,256]{1,0:T(8,128)S(1)} %slice_add_fusion.14), channel_id=1, source_target_pairs={{0,16},{1,9},{2,18},{3,11},{4,20},{5,13},{6,22},{7,15},{8,24},{9,1... | collective-permute-start | bytes 196616 | tf_op jit(solution)/shard_map/ppermute | solution.py:357
  64.1 7.7 %collective-permute-start.11 = (f32[128,256]{1,0:T(8,128)S(1)}, f32[128,256]{1,0:T(8,128)S(1)}, u32[]{:S(2)}, u32[]{:S(2)}) collective-permute-start(f32[128,256]{1,0:T(8,128)S(1)} %pad_maximum_fusion.9), channel_id=1, source_target_pairs={{0,8},{1,17},{2,10},{3,19},{4,12},{5,21},{6,14},{7,23},{8,0},{9,25... | collective-permute-start | bytes 393224 | tf_op jit(solution)/shard_map/ppermute | solution.py:357
  68.6 5.7 %collective-permute-start.10 = (f32[128,256]{1,0:T(8,128)S(1)}, f32[128,256]{1,0:T(8,128)S(1)}, u32[]{:S(2)}, u32[]{:S(2)}) collective-permute-start(f32[128,256]{1,0:T(8,128)S(1)} %slice.117), channel_id=1, source_target_pairs={{0,8},{1,17},{2,10},{3,19},{4,12},{5,21},{6,14},{7,23},{8,0},{9,25... | collective-permute-start | bytes 393224 | tf_op jit(solution)/shard_map/ppermute | solution.py:357
  74.3 5.3 %collective-permute-start.12 = (f32[64,256]{1,0:T(8,128)S(1)}, f32[64,256]{1,0:T(8,128)S(1)}, u32[]{:S(2)}, u32[]{:S(2)}) collective-permute-start(f32[64,256]{1,0:T(8,128)S(1)} %slice.119), channel_id=1, source_target_pairs={{0,16},{1,9},{2,18},{3,11},{4,20},{5,13},{6,22},{7,15},{8,24},{9,1... | collective-permute-start | bytes 196616 | tf_op jit(solution)/shard_map/ppermute | solution.py:357
  77.1 6.4 %collective-permute-start.13 = (f32[256,256]{1,0:T(8,128)S(1)}, f32[256,256]{1,0:T(8,128)S(1)}, u32[]{:S(2)}, u32[]{:S(2)}) collective-permute-start(f32[256,256]{1,0:T(8,128)S(1)} %pad_maximum_fusion.5), channel_id=1, source_target_pairs={{0,4},{1,3},{2,6},{3,1},{4,0},{5,7},{6,2},{7,5},{8,12},{9,11},{10,... | collective-permute-start | bytes 786440 | tf_op jit(solution)/shard_map/ppermute | solution.py:357
  83.5 5.2 %collective-permute-start.15 = (f32[64,256]{1,0:T(8,128)S(1)}, f32[64,256]{1,0:T(8,128)S(1)}, u32[]{:S(2)}, u32[]{:S(2)}) collective-permute-start(f32[64,256]{1,0:T(8,128)S(1)} %slice_add_fusion.13), channel_id=1, source_target_pairs={{0,16},{1,9},{2,18},{3,11},{4,20},{5,13},{6,22},{7,15},{8,24},{9,1... | collective-permute-start | bytes 196616 | tf_op jit(solution)/shard_map/ppermute | solution.py:357
  88.8 5.0 %collective-permute-start.16 = (f32[128,256]{1,0:T(8,128)S(1)}, f32[128,256]{1,0:T(8,128)S(1)}, u32[]{:S(2)}, u32[]{:S(2)}) collective-permute-start(f32[128,256]{1,0:T(8,128)S(1)} %pad_maximum_fusion.10), channel_id=1, source_target_pairs={{0,8},{1,17},{2,10},{3,19},{4,12},{5,21},{6,14},{7,23},{8,0},{9,25... | collective-permute-start | bytes 393224 | tf_op jit(solution)/shard_map/ppermute | solution.py:357
  90.8 3.7 %collective-permute-start.14 = (f32[128,256]{1,0:T(8,128)S(1)}, f32[128,256]{1,0:T(8,128)S(1)}, u32[]{:S(2)}, u32[]{:S(2)}) collective-permute-start(f32[128,256]{1,0:T(8,128)S(1)} %slice_add_fusion.8.refs_0_), channel_id=1, source_target_pairs={{0,1},{1,0},{2,3},{3,2},{4,5},{5,4},{6,7},{7,6},{8,9},{9,8},{10,11... | collective-permute-start | bytes 393224 | tf_op jit(solution)/shard_map/ppermute | solution.py:354
  90.8 22.1 %collective-permute-start.20 = (f32[512,256]{1,0:T(8,128)S(1)}, f32[512,256]{1,0:T(8,128)S(1)}, u32[]{:S(2)}, u32[]{:S(2)}) collective-permute-start(f32[512,256]{1,0:T(8,128)S(1)} %pad_maximum_fusion.1.refs_2_), channel_id=1, source_target_pairs={{0,1},{1,0},{2,3},{3,2},{4,5},{5,4},{6,7},{7,6},{8,9},{9,8},{10,11... | collective-permute-start | bytes 1572872 | tf_op jit(solution)/shard_map/ppermute | solution.py:354
  91.3 11.5 %collective-permute-start.18 = (f32[512,256]{1,0:T(8,128)S(1)}, f32[512,256]{1,0:T(8,128)S(1)}, u32[]{:S(2)}, u32[]{:S(2)}) collective-permute-start(f32[512,256]{1,0:T(8,128)S(1)} %pad_maximum_fusion.1.refs_2_), channel_id=1, source_target_pairs={{0,2},{1,5},{2,0},{3,7},{4,6},{5,1},{6,4},{7,3},{8,10},{9,13},{10,... | collective-permute-start | bytes 1572872 | tf_op jit(solution)/shard_map/ppermute | solution.py:357
  93.8 8.5 %collective-permute-start.17 = (f32[256,256]{1,0:T(8,128)S(1)}, f32[256,256]{1,0:T(8,128)S(1)}, u32[]{:S(2)}, u32[]{:S(2)}) collective-permute-start(f32[256,256]{1,0:T(8,128)S(1)} %pad_maximum_fusion.6), channel_id=1, source_target_pairs={{0,4},{1,3},{2,6},{3,1},{4,0},{5,7},{6,2},{7,5},{8,12},{9,11},{10,... | collective-permute-start | bytes 786440 | tf_op jit(solution)/shard_map/ppermute | solution.py:357
  102.8 13.8 %collective-permute-start.22 = (f32[512,256]{1,0:T(8,128)S(1)}, f32[512,256]{1,0:T(8,128)S(1)}, u32[]{:S(2)}, u32[]{:S(2)}) collective-permute-start(f32[512,256]{1,0:T(8,128)S(1)} %pad_maximum_fusion.2.refs_3_), channel_id=1, source_target_pairs={{0,1},{1,0},{2,3},{3,2},{4,5},{5,4},{6,7},{7,6},{8,9},{9,8},{10,11... | collective-permute-start | bytes 1572872 | tf_op jit(solution)/shard_map/ppermute | solution.py:354
  102.8 12.5 %collective-permute-start.19 = (f32[512,256]{1,0:T(8,128)S(1)}, f32[512,256]{1,0:T(8,128)S(1)}, u32[]{:S(2)}, u32[]{:S(2)}) collective-permute-start(f32[512,256]{1,0:T(8,128)S(1)} %pad_maximum_fusion.2.refs_3_), channel_id=1, source_target_pairs={{0,2},{1,5},{2,0},{3,7},{4,6},{5,1},{6,4},{7,3},{8,10},{9,13},{10,... | collective-permute-start | bytes 1572872 | tf_op jit(solution)/shard_map/ppermute | solution.py:357
  104.2 8.8 %collective-permute-start.21 = (f32[512,256]{1,0:T(8,128)S(1)}, f32[512,256]{1,0:T(8,128)S(1)}, u32[]{:S(2)}, u32[]{:S(2)}) collective-permute-start(f32[512,256]{1,0:T(8,128)S(1)} %collective-permute-done.18.refs_3_), channel_id=1, source_target_pairs={{0,1},{1,0},{2,3},{3,2},{4,5},{5,4},{6,7},{7,6},{8,9},{9,8},{10,11... | collective-permute-start | bytes 1572872 | tf_op jit(solution)/shard_map/ppermute | solution.py:354
  104.2 6.0 %copy-start = (f32[2048,256]{1,0:T(8,128)S(1)}, f32[2048,256]{1,0:T(8,128)}, u32[]{:S(2)}) copy-start(f32[2048,256]{1,0:T(8,128)} %get-tuple-element.79.sketch) | copy-start | bytes 6291460
  115.4 2.1 %collective-permute-start.23 = (f32[512,256]{1,0:T(8,128)S(1)}, f32[512,256]{1,0:T(8,128)S(1)}, u32[]{:S(2)}, u32[]{:S(2)}) collective-permute-start(f32[512,256]{1,0:T(8,128)S(1)} %collective-permute-done.19.refs_4_), channel_id=1, source_target_pairs={{0,1},{1,0},{2,3},{3,2},{4,5},{5,4},{6,7},{7,6},{8,9},{9,8},{10,11... | collective-permute-start | bytes 1572872 | tf_op jit(solution)/shard_map/ppermute | solution.py:354

commit v4 on v3

v4 whole, which is shorter than its diff:
```python
import functools
import math

import jax
import jax.numpy as jnp
from jax import lax
from jax.experimental import pallas as pl
from jax.experimental.pallas import tpu as pltpu
from jax.sharding import PartitionSpec as P

AXES = ("gx", "gy")
CHUNKS = 2
MIB = 1 << 20


def dot(a, b, dims=((1,), (0,))):
    return lax.dot_general(a, b, (dims, ((), ())), preferred_element_type=jnp.float32)


def split(a):
    high = a.astype(jnp.bfloat16)
    return high, (a - high.astype(jnp.float32)).astype(jnp.bfloat16)


def orders_of(n_devices):
    bits = list(range(1, n_devices.bit_length() - 1))
    swapped = bits[:]
    for i in range(0, len(bits) - 1, 2):
        swapped[i], swapped[i + 1] = bits[i + 1], bits[i]
    return bits, swapped


def bits_of(me, order):
    value = jnp.int32(0)
    for b in order:
        value = value * 2 + ((me >> b) & 1)
    return value

VMEM_SPEC = pl.BlockSpec(memory_space=pltpu.VMEM)
SMEM_SPEC = pl.BlockSpec(memory_space=pltpu.SMEM)
ANY_SPEC = pl.BlockSpec(memory_space=pl.ANY)


def pinned(*arrays):
    return [pltpu.with_memory_space_constraint(a, pltpu.VMEM) for a in arrays]


def front_kernel(in_scale, gram_scale, scale, groups, width, info, e, signs, sketch_out, gram_sent, gram_kept, *refs):
    e_kept, sketch, rounded_t, s32, s16, acc, pieces, sem, out_sem = refs[-9:]
    chunk_outs = refs[:-9]
    rows = e.shape[0]
    k = rounded_t.shape[0]
    n = sem.shape[0] - 1
    block = rows // n
    signs_copy = pltpu.make_async_copy(signs, s32, sem.at[n])
    signs_copy.start()

    def rows_copy(i):
        at = pl.ds(pl.multiple_of(i * block, block), block)
        return pltpu.make_async_copy(e.at[at], e_kept.at[at], sem.at[i])

    for i in range(n):
        rows_copy(i).start()
    signs_copy.wait()
    s16[...] = s32[...].astype(jnp.bfloat16)

    def step(i, carry):
        rows_copy(i).wait()
        at = pl.ds(pl.multiple_of(i * block, block), block)
        sk = dot(e_kept[at, :], s16[...]) * in_scale
        sketch[at, :] = sk
        rounded_t[:, at] = sk.astype(jnp.bfloat16).T
        return carry

    lax.fori_loop(0, n, step, 0)
    outs = [pltpu.make_async_copy(sketch, sketch_out, out_sem.at[0])]
    outs[0].start()
    high, low = split(sketch[...])
    acc[...] = dot(rounded_t[...], low)
    acc[...] = (dot(rounded_t[...], high) + (acc[...] + acc[...].T)) * gram_scale
    half = k // 2
    own = info[10] & 1
    size = half // groups
    for g in range(groups):
        for to, region, order in ((gram_kept, own, info[9]), (gram_sent, 1 - own, info[8])):
            at = pl.multiple_of(region * half + g * size, size)
            to[pl.ds(pl.multiple_of((order ^ g) * size, size), size), :] = acc[pl.ds(at, size), :]
    size = k // groups
    for chunk in range(len(chunk_outs) // 3):
        sent, kept, first = chunk_outs[3 * chunk : 3 * chunk + 3]
        for piece in range(8):
            at = pl.ds(pl.multiple_of((info[piece] + 8 * chunk) * width, width), width)
            value = dot(rounded_t[...], e_kept[:, at]) * scale
            slot = 8 * chunk + piece
            for g in range(groups):
                to = pl.multiple_of((info[8 + piece // 4] ^ g) * size, size)
                pieces[slot, pl.ds(to, size), :] = value[g * size : (g + 1) * size]
            if piece < 4:
                to = sent.at[pl.ds(piece * k, k)]
            else:
                to = (kept if piece < 6 else first).at[pl.ds(piece % 2 * k, k)]
            outs.append(pltpu.make_async_copy(pieces.at[slot], to, out_sem.at[1 + slot]))
            outs[-1].start()
    for copy in outs:
        copy.wait()


def front_call(info, e, signs, rows_all, groups, width, chunks):
    rows, d = e.shape
    k = signs.shape[1]
    copies = 4
    return pl.pallas_call(
        functools.partial(
            front_kernel, 1.0 / math.sqrt(d), 1.0 / rows_all, 1.0 / math.sqrt(rows_all), groups, width
        ),
        in_specs=[SMEM_SPEC, ANY_SPEC, ANY_SPEC],
        out_specs=[ANY_SPEC] + [VMEM_SPEC] * 2 + [ANY_SPEC] * (3 * chunks),
        out_shape=[
            jax.ShapeDtypeStruct((rows, k), jnp.float32),
            jax.ShapeDtypeStruct((k // 2, k), jnp.float32),
            jax.ShapeDtypeStruct((k // 2, k), jnp.float32),
        ]
        + [jax.ShapeDtypeStruct((n * k, width), jnp.float32) for n in (4, 2, 2)] * chunks,
        scratch_shapes=[
            pltpu.VMEM((rows, d), e.dtype),
            pltpu.VMEM((rows, k), jnp.float32),
            pltpu.VMEM((k, rows), jnp.bfloat16),
            pltpu.VMEM((d, k), jnp.int32),
            pltpu.VMEM((d, k), jnp.bfloat16),
            pltpu.VMEM((k, k), jnp.float32),
            pltpu.VMEM((8 * chunks, k, width), jnp.float32),
            pltpu.SemaphoreType.DMA((copies + 1,)),
            pltpu.SemaphoreType.DMA((1 + 8 * chunks,)),
        ],
        compiler_params=pltpu.CompilerParams(vmem_limit_bytes=56 * MIB),
        cost_estimate=pl.CostEstimate(flops=4 * rows * d * k, bytes_accessed=rows * d * 2 + d * k * 4, transcendentals=0),
        name="front",
    )(info, e, pltpu.with_memory_space_constraint(signs, pltpu.HBM))


def factor_kernel(part, groups, info, *refs):
    triangle, high, low, work = refs[-4:]
    half, k = triangle.shape
    b = 64
    if part == 0:
        kept, got = refs[:2]
        own = info[10] & 1
        size = half // groups
        for g in range(groups):
            for rows, region, order in ((kept, own, info[9]), (got, 1 - own, info[8])):
                at = pl.ds(pl.multiple_of((order ^ g) * size, size), size)
                work[pl.ds(pl.multiple_of(region * half + g * size, size), size), :k] = rows[at, :]
        rows_k = lax.broadcasted_iota(jnp.int32, (k, k), 0)
        cols_k = lax.broadcasted_iota(jnp.int32, (k, k), 1)
        work[:, k:] = jnp.where(rows_k == cols_k, 1.0, 0.0)
    else:
        work[...] = refs[0][...]
    lane = lax.broadcasted_iota(jnp.int32, (8, 2 * b), 1)
    sub = lax.broadcasted_iota(jnp.int32, (8, 2 * b), 0)

    def over_lanes(a, at):
        return jnp.broadcast_to(a[:, at : at + 1], (8, 2 * b))

    for n in range(part * (half // b), (part + 1) * (half // b)):
        put = slice(n * b - part * half, (n + 1) * b - part * half)
        first = (n % 2) * b
        pair = (n // 2) * 2 * b
        own_lanes = (lane >= first) & (lane < first + b)
        w = []
        for v in range(b // 8):
            a = work[n * b + 8 * v : n * b + 8 * v + 8, pair : pair + 2 * b]
            ident = jnp.where(lane == (b - first) + 8 * v + sub, 1.0, 0.0)
            w.append(jnp.where(own_lanes, a, ident))
        inv = []
        for q in range(b // 8):
            at = first + 8 * q
            row = [jnp.broadcast_to(w[q][i : i + 1, :], (8, 2 * b)) for i in range(8)]
            s = {(i, j): over_lanes(row[i], at + j) for i in range(8) for j in range(i, 8)}
            factor = {}
            scaled = []
            for j in range(8):
                r = 1.0 / s[j, j]
                for i in range(j + 1, 8):
                    factor[i, j] = s[j, i] * r
                    for m in range(i, 8):
                        s[i, m] = s[i, m] - factor[i, j] * s[j, m]
                    row[i] = row[i] - factor[i, j] * row[j]
                scaled.append(row[j] * r)
            new, pivots = row[0], s[0, 0]
            for i in range(1, 8):
                new = jnp.where(sub == i, row[i], new)
                pivots = jnp.where(sub == i, s[i, i], pivots)
            for v in range(q + 1, b // 8):
                col = [over_lanes(w[v], at + j) for j in range(8)]
                for j in range(8):
                    for m in range(j + 1, 8):
                        col[m] = col[m] - col[j] * factor[m, j]
                t = [col[j] * scaled[j] for j in range(8)]
                w[v] = w[v] - (((t[0] + t[1]) + (t[2] + t[3])) + ((t[4] + t[5]) + (t[6] + t[7])))
            moved = pltpu.roll(new * (1.0 / jnp.sqrt(pivots)), b, 1)
            inv.append(jnp.where(own_lanes, moved, 0.0))
        inv = jnp.concatenate(inv, axis=0)
        y = lax.dot_general(
            inv, work[pair : pair + 2 * b, :], (((1,), (0,)), ((), ())),
            precision=lax.Precision.HIGHEST, preferred_element_type=jnp.float32,
        )
        r_rows, i_rows = y[:, :k], y[:, k:]
        at = lax.broadcasted_iota(jnp.int32, (b, k), 0) + n * b
        to = lax.broadcasted_iota(jnp.int32, (b, k), 1)
        triangle[put, :] = jnp.where(to >= at, r_rows, 0.0)
        i_rows = jnp.where(to <= at, i_rows, 0.0)
        i_high, i_low = split(i_rows)
        high[put, :] = i_high
        low[put, :] = i_low
        if (n + 1) * b < k:
            later = jnp.where(to >= (n + 1) * b, r_rows, 0.0)
            work[...] -= lax.dot_general(
                later, y, (((0,), (0,)), ((), ())),
                precision=lax.Precision.HIGHEST, preferred_element_type=jnp.float32,
            )


def factor_call(part, groups, info, *inputs):
    k = inputs[0].shape[0] * (2 - part)
    return pl.pallas_call(
        functools.partial(factor_kernel, part, groups),
        in_specs=[SMEM_SPEC] + [VMEM_SPEC] * len(inputs),
        out_specs=[VMEM_SPEC] * 4,
        out_shape=[
            jax.ShapeDtypeStruct((k // 2, k), jnp.float32),
            jax.ShapeDtypeStruct((k // 2, k), jnp.bfloat16),
            jax.ShapeDtypeStruct((k // 2, k), jnp.bfloat16),
            jax.ShapeDtypeStruct((k, 2 * k), jnp.float32),
        ],
        compiler_params=pltpu.CompilerParams(vmem_limit_bytes=16 * MIB),
        cost_estimate=pl.CostEstimate(flops=5 * 10**9, bytes_accessed=k * k * 8, transcendentals=0),
        name="factor",
    )(info, *inputs)


def basis_kernel(sketch, high, low, out):
    s_high, s_low = split(sketch[...])
    right = ((1,), (1,))
    out[...] = (
        dot(s_high, high[...], right) + (dot(s_high, low[...], right) + dot(s_low, high[...], right))
    ).astype(out.dtype)


def basis_call(sketch, high, low):
    rows, k = sketch.shape
    block = rows // 4
    return pl.pallas_call(
        basis_kernel,
        grid=(rows // block,),
        in_specs=[pl.BlockSpec((block, k), lambda i: (i, 0))] + [pl.BlockSpec((k, k), lambda i: (0, 0))] * 2,
        out_specs=pl.BlockSpec((block, k), lambda i: (i, 0)),
        out_shape=jax.ShapeDtypeStruct((rows, k), jnp.bfloat16),
        compiler_params=pltpu.CompilerParams(vmem_limit_bytes=16 * MIB),
        cost_estimate=pl.CostEstimate(flops=6 * rows * k * k, bytes_accessed=rows * k * 6, transcendentals=0),
        name="basis",
    )(sketch, high, low)


def project_kernel(groups, width, chunk, info, high, low, *refs):
    *blocks, out, value, sem = refs
    blocks = blocks[-4:]
    k = high.shape[0]
    size = k // groups
    copies = []
    for n in range(8):
        block, order = blocks[n // 2], info[8 + n // 4]
        c_high, c_low = split(
            jnp.concatenate(
                [
                    block[pl.ds(pl.multiple_of((n % 2) * k + (order ^ g) * size, size), size), :]
                    for g in range(groups)
                ],
                axis=0,
            )
        )
        value[n] = dot(high[...], c_high) + (dot(high[...], c_low) + dot(low[...], c_high))
        at = pl.ds(pl.multiple_of((info[n] + 8 * chunk) * width, width), width)
        copies.append(pltpu.make_async_copy(value.at[n], out.at[:, at], sem.at[n]))
        copies[-1].start()
    for copy in copies:
        copy.wait()


def project_call(chunk, info, high, low, blocks, groups, d, before):
    k, width = high.shape[0], blocks[0].shape[1]
    extra = [] if before is None else [before]
    return pl.pallas_call(
        functools.partial(project_kernel, groups, width, chunk),
        in_specs=[SMEM_SPEC, VMEM_SPEC, VMEM_SPEC] + [ANY_SPEC] * len(extra) + [VMEM_SPEC] * 4,
        out_specs=ANY_SPEC,
        out_shape=jax.ShapeDtypeStruct((k, d), jnp.float32),
        input_output_aliases={3: 0} if extra else {},
        scratch_shapes=[pltpu.VMEM((8, k, width), jnp.float32), pltpu.SemaphoreType.DMA((8,))],
        compiler_params=pltpu.CompilerParams(vmem_limit_bytes=16 * MIB),
        cost_estimate=pl.CostEstimate(flops=6 * k * k * width * 8, bytes_accessed=k * width * 32, transcendentals=0),
        name="project",
    )(info, *pinned(high, low), *extra, *pinned(*blocks))


def solution(mesh):
    n_devices = math.prod(mesh.shape.values())
    orders = orders_of(n_devices)
    rest_bits = len(orders[0]) - 2
    groups = 1 << rest_bits

    def permutation(mask_of):
        return [(i, i ^ mask_of(i)) for i in range(n_devices)]

    def rest_mask(i, g):
        return sum(1 << b for t, b in enumerate(orders[i & 1][2:]) if g >> (rest_bits - 1 - t) & 1)

    pairs = permutation(lambda i: 1)
    swaps = [permutation(lambda i, s=s: 1 << orders[i & 1][s]) for s in range(2)]
    across = [permutation(lambda i, g=g: rest_mask(i, g)) for g in range(groups)]

    def with_pair(a):
        return lax.ppermute(a, AXES, pairs)

    def swap(a, s):
        return lax.ppermute(a, AXES, swaps[s])

    def join(*arrays):
        return arrays[0] if len(arrays) == 1 else jnp.concatenate(arrays, axis=0)

    def shards(e, signs):
        rows_all = e.shape[0] * n_devices
        d = e.shape[1]
        k = signs.shape[1]
        width = d // (8 * CHUNKS)
        me = lax.axis_index(AXES).astype(jnp.int32)
        own = me & 1
        place = [bits_of(me, o[:2]) for o in orders]
        rest = [bits_of(me, o[2:]) for o in orders]
        mine = lambda pair: jnp.where(own == 0, pair[0], pair[1])
        other = lambda pair: jnp.where(own == 0, pair[1], pair[0])
        info = jnp.stack(
            [(1 - own) * 4 + (other(place) ^ n) for n in range(4)]
            + [own * 4 + (mine(place) ^ n) for n in range(4)]
            + [other(rest), mine(rest), me]
        )
        last = [me]

        def in_turn(*arrays):
            *arrays, _ = lax.optimization_barrier((*arrays, last[0]))
            last[0] = arrays[-1]
            return arrays if len(arrays) > 1 else arrays[0]

        held, coming = [None] * CHUNKS, [None] * CHUNKS
        grams = None

        def first_sum(chunk, kept, first, got, *more):
            send, got = in_turn(join(first + got[2 * k :], *more), got)
            coming[chunk] = swap(send, 0)
            held[chunk] = (kept, got[: 2 * k])

        def second_sum(chunk):
            nonlocal grams
            kept, got = held[chunk]
            r = coming[chunk]
            more = []
            if chunk == 0:
                grams = grams + r[2 * k :]
                more = [grams]
            send, r = in_turn(join((kept[k:] + got[k:]) + r[k : 2 * k], *more), r)
            coming[chunk] = swap(send, 1)
            held[chunk] = (kept[:k], got[:k], r[:k])

        def scatter(chunk):
            nonlocal grams
            kept, got, before = held[chunk]
            r = coming[chunk]
            a = ((kept + got) + before) + r[:k]
            size = k // groups
            parts = [a[g * size : (g + 1) * size] for g in range(groups)]
            if chunk == 0:
                grams = grams + r[k:]
                half = size // 2
                parts = [join(p, grams[g * half : (g + 1) * half]) for g, p in enumerate(parts)]
            parts = in_turn(*parts)
            held[chunk] = parts[0]
            coming[chunk] = [lax.ppermute(parts[g], AXES, across[g]) for g in range(1, groups)]

        def gather(chunk):
            a = held[chunk]
            for r in coming[chunk]:
                a = a + r
            a = in_turn(a)
            held[chunk] = a
            coming[chunk] = [lax.ppermute(a, AXES, across[g]) for g in range(1, groups)]

        def second_gather(chunk):
            nonlocal grams
            size = k // groups
            parts = [held[chunk], *coming[chunk]]
            if chunk == 0:
                grams = join(*[p[size:] for p in parts])
            a = in_turn(join(*[p[:size] for p in parts]))
            held[chunk] = a
            coming[chunk] = swap(a, 1)

        def first_gather(chunk):
            a = in_turn(join(held[chunk], coming[chunk]))
            held[chunk] = a
            coming[chunk] = swap(a, 0)

        sketch, gram_sent, gram, *products = front_call(info, e, signs, rows_all, groups, width, CHUNKS)
        got = [with_pair(products[0]), None]
        grams = gram + with_pair(gram_sent)
        got[1] = with_pair(products[3])
        first_sum(0, *products[1:3], got[0], grams)
        second_sum(0)
        first_sum(1, *products[4:6], got[1])
        scatter(0)
        second_sum(1)
        gather(0)
        scatter(1)
        second_gather(0)
        gram_got = with_pair(grams)
        gather(1)
        first_gather(0)
        triangle_a, high_a, low_a, work = factor_call(0, groups, info, in_turn(grams), gram_got)
        second_gather(1)
        far = in_turn(coming[0])
        pair_blocks = [with_pair(held[0]), with_pair(far)]
        first_gather(1)
        pair_held = with_pair(held[1])
        triangle_b, high_b, low_b, _ = factor_call(1, groups, info, in_turn(work))
        triangle = join(triangle_a, triangle_b)
        high, low = in_turn(join(high_a, high_b)), join(low_a, low_b)
        basis = in_turn(basis_call(sketch, high, low))
        far1 = in_turn(coming[1])
        pair_far = with_pair(far1)
        projected = project_call(0, info, high, low, [*pair_blocks, held[0], far], groups, d, None)
        projected = project_call(1, info, high, low, [pair_held, pair_far, held[1], far1], groups, d, projected)
        return triangle, basis, projected

    return jax.shard_map(
        shards,
        mesh=mesh,
        in_specs=(P(AXES, None), P()),
        out_specs=(P(), P(AXES, None), P()),
        check_vma=False,
    )
```

time: 120 us -> 118 us (0.983)
  Pallas kernels: 42 us -> 36.2 us
  starting transfers between devices: 28.5 us -> 32.7 us
  local copies, waits for them, and re-layouts: 2.02 us -> 0.76 us
    ppermute x0 -> x12, waiting for transfers between devices: none -> 19.8 us  [the longest x6 10.3 us: gather(): coming[chunk] = [lax.ppermute(a, AXES, across[g]) for g in range(1, groups)]]
    ppermute x16 -> x8, waiting for transfers between devices: 39.4 us -> 20.2 us  [swap(): return lax.ppermute(a, AXES, swaps[s])]
    ppermute x0 -> x12, starting transfers between devices: none -> 18.2 us  [the longest x6 9.34 us: scatter(): lax.ppermute(parts[g], AXES, across[g])]
    ppermute x16 -> x8, starting transfers between devices: 26.8 us -> 13.2 us  [swap(): return lax.ppermute(a, AXES, swaps[s])]
    pallas_call x5 -> x4, Pallas kernels: 25.3 us -> 17.2 us  [the longest x2 12.3 us: factor_call(): pl.pallas_call(functools.partial(factor_kernel, part, groups), in_specs=[...]
    pallas_call x1, Pallas kernels: 14 us -> 16.3 us  [front_call(): pl.pallas_call(functools.partial(front_kernel, 1.0 / math.sqrt(d), 1.0 /...]
    unnamed x9 -> x11, local copies, waits for them, and re-layouts: 1.24 us -> 0.03 us
    add x14 -> x11, other arithmetic: 2.51 us -> 3.39 us  [the longest x2 1.18 us: first_sum(): send, got = in_turn(join(first + got[2 * k:], *more), got)]
  transfers between devices with their start and end apart: 24 -> 28, of which waited for: 14 -> 14; matrix products, arithmetic and copies ran while one was open for 2% -> 3% of each run, Pallas kernels for 21% -> 15%
where the time goes in v4:
time: 118 us
  waiting for transfers between devices  42.6 us (36%)
  Pallas kernels  36.2 us (31%)
  starting transfers between devices  32.7 us (28%)
  other arithmetic  4.34 us (4%)
    ppermute x8, waiting for transfers between devices, swap(): return lax.ppermute(a, AXES, swaps[s])  20.2 us
    pallas_call x1, Pallas kernels, front_call(): pl.pallas_call(functools.partial(front_kernel, 1.0 / math.sqrt(d), 1.0 /...  16.3 us
    ppermute x8, starting transfers between devices, swap(): return lax.ppermute(a, AXES, swaps[s])  13.2 us
    pallas_call x2, Pallas kernels, factor_call(): pl.pallas_call(functools.partial(factor_kernel, part, groups), in_specs=[...  12.3 us
    ppermute x6, waiting for transfers between devices, gather(): coming[chunk] = [lax.ppermute(a, AXES, across[g]) for g in range(1, groups)]  10.3 us
    ppermute x6, waiting for transfers between devices, scatter(): lax.ppermute(parts[g], AXES, across[g])  9.57 us
    ppermute x6, starting transfers between devices, scatter(): lax.ppermute(parts[g], AXES, across[g])  9.34 us
    ppermute x6, starting transfers between devices, gather(): coming[chunk] = [lax.ppermute(a, AXES, across[g]) for g in range(1, groups)]  8.91 us
  transfers between devices with their start and end apart: 28, of which 14 were waited for; matrix products, arithmetic and copies ran while one was open for 3% of the time, Pallas kernels for 15%

profile of v4, /device:TPU:0, one launch (start us, length us, event | category | flops | bytes accessed | tf_op | source)
XLA Modules:
  0.0 117.8 jit_solution(3612638467769811649)
XLA Ops:
  0.7 0.6 stack.47.info
  1.3 16.3 %front.1 = (f32[2048,256]{1,0:T(8,128)}, f32[128,256]{1,0:T(8,128)}, f32[128,256]{1,0:T(8,128)}, f32[1024,256]{1,0:T(8,128)}, f32[512,256]{1,0:T(8,128)}, /*inde...) custom-call(s32[11]{0:T(128)} %stack.47.info, bf16[2048,4096]{1,0:T(8,128)(2,1)} %e.1, ...), custom_call_target="tpu_custom_call" | custom-call | flops 8589934592 | bytes 20971520 | tf_op jit(solution)/shard_map/front/pallas_call | solution.py:112
  17.7 0.5 collective-permute-start
  18.2 0.1 collective-permute-start.1
  18.3 2.6 %collective-permute-done.1 = f32[128,256]{1,0:T(8,128)S(1)} collective-permute-done((f32[128,256]{1,0:T(8,128)}, f32[128,256]{1,0:T(8,128)S(1)}, u32[]{:S(2)}, u32[]{:S(2)}) %collective-permute-start.1) | collective-permute-done | bytes 131104 | tf_op jit(solution)/shard_map/ppermute | solution.py:322
  20.9 0.9 add.116
  21.8 1.1 slice_add_fusion.1
  23.0 2.9 %collective-permute-start.2 = (f32[640,256]{1,0:T(8,128)S(1)}, f32[640,256]{1,0:T(8,128)S(1)}, u32[]{:S(2)}, u32[]{:S(2)}) collective-permute-start(f32[640,256]{1,0:T(8,128)S(1)} %pad_maximum_fusion), channel_id=1, source_target_pairs={{0,2},{1,5},{2,0},{3,7},{4,6},{5,1},{6,4},{7,3},{8,10},{9,13},{10,... | collective-permute-start | bytes 1966088 | tf_op jit(solution)/shard_map/ppermute | solution.py:325
  25.9 8.6 %collective-permute-done.2 = f32[640,256]{1,0:T(8,128)S(1)} collective-permute-done((f32[640,256]{1,0:T(8,128)S(1)}, f32[640,256]{1,0:T(8,128)S(1)}, u32[]{:S(2)}, u32[]{:S(2)}) %collective-permute-start.2) | collective-permute-done | bytes 655392 | tf_op jit(solution)/shard_map/ppermute | solution.py:325
  34.5 1.0 slice_add_fusion.4
  35.5 2.1 %collective-permute-start.3 = (f32[384,256]{1,0:T(8,128)S(1)}, f32[384,256]{1,0:T(8,128)S(1)}, u32[]{:S(2)}, u32[]{:S(2)}) collective-permute-start(f32[384,256]{1,0:T(8,128)S(1)} %pad_maximum_fusion.3), channel_id=1, source_target_pairs={{0,4},{1,3},{2,6},{3,1},{4,0},{5,7},{6,2},{7,5},{8,12},{9,11},{10,... | collective-permute-start | bytes 1179656 | tf_op jit(solution)/shard_map/ppermute | solution.py:325
  37.7 1.6 %collective-permute-start.8 = (f32[512,256]{1,0:T(8,128)S(1)}, f32[512,256]{1,0:T(8,128)S(1)}, u32[]{:S(2)}, u32[]{:S(2)}) collective-permute-start(f32[512,256]{1,0:T(8,128)S(1)} %slice_add_fusion), channel_id=1, source_target_pairs={{0,2},{1,5},{2,0},{3,7},{4,6},{5,1},{6,4},{7,3},{8,10},{9,13},{10,... | collective-permute-start | bytes 1572872 | tf_op jit(solution)/shard_map/ppermute | solution.py:325
  39.3 8.2 %collective-permute-done.3 = f32[384,256]{1,0:T(8,128)S(1)} collective-permute-done((f32[384,256]{1,0:T(8,128)S(1)}, f32[384,256]{1,0:T(8,128)S(1)}, u32[]{:S(2)}, u32[]{:S(2)}) %collective-permute-start.3) | collective-permute-done | bytes 393248 | tf_op jit(solution)/shard_map/ppermute | solution.py:325
  47.7 3.3 %collective-permute-start.5 = (f32[96,256]{1,0:T(8,128)S(1)}, f32[96,256]{1,0:T(8,128)S(1)}, u32[]{:S(2)}, u32[]{:S(2)}) collective-permute-start(f32[96,256]{1,0:T(8,128)S(1)} %get-tuple-element.60), channel_id=1, source_target_pairs={{0,16},{1,9},{2,18},{3,11},{4,20},{5,13},{6,22},{7,15},{8,24},{9,1... | collective-permute-start | bytes 294920 | tf_op jit(solution)/shard_map/ppermute | solution.py:386
  51.0 1.6 %collective-permute-start.6 = (f32[96,256]{1,0:T(8,128)S(1)}, f32[96,256]{1,0:T(8,128)S(1)}, u32[]{:S(2)}, u32[]{:S(2)}) collective-permute-start(f32[96,256]{1,0:T(8,128)S(1)} %get-tuple-element.61), channel_id=1, source_target_pairs={{0,8},{1,17},{2,10},{3,19},{4,12},{5,21},{6,14},{7,23},{8,0},{9,25... | collective-permute-start | bytes 294920 | tf_op jit(solution)/shard_map/ppermute | solution.py:386
  52.6 1.8 %collective-permute-start.12 = (f32[256,256]{1,0:T(8,128)S(1)}, f32[256,256]{1,0:T(8,128)S(1)}, u32[]{:S(2)}, u32[]{:S(2)}) collective-permute-start(f32[256,256]{1,0:T(8,128)S(1)} %slice_add_fusion.2), channel_id=1, source_target_pairs={{0,4},{1,3},{2,6},{3,1},{4,0},{5,7},{6,2},{7,5},{8,12},{9,11},{10,... | collective-permute-start | bytes 786440 | tf_op jit(solution)/shard_map/ppermute | solution.py:325
  54.4 1.2 collective-permute-done.6
  55.6 4.4 %collective-permute-done.7 = f32[96,256]{1,0:T(8,128)S(1)} collective-permute-done((f32[96,256]{1,0:T(8,128)S(1)}, f32[96,256]{1,0:T(8,128)S(1)}, u32[]{:S(2)}, u32[]{:S(2)}) %collective-permute-start.7) | collective-permute-done | bytes 98336 | tf_op jit(solution)/shard_map/ppermute | solution.py:386
  60.1 2.6 %collective-permute-start.11 = (f32[96,256]{1,0:T(8,128)S(1)}, f32[96,256]{1,0:T(8,128)S(1)}, u32[]{:S(2)}, u32[]{:S(2)}) collective-permute-start(f32[96,256]{1,0:T(8,128)S(1)} %add_add_fusion.1), channel_id=1, source_target_pairs={{0,24},{1,25},{2,26},{3,27},{4,28},{5,29},{6,30},{7,31},{8,16},{9,... | collective-permute-start | bytes 294920 | tf_op jit(solution)/shard_map/ppermute | solution.py:394
  62.7 1.8 %collective-permute-start.10 = (f32[96,256]{1,0:T(8,128)S(1)}, f32[96,256]{1,0:T(8,128)S(1)}, u32[]{:S(2)}, u32[]{:S(2)}) collective-permute-start(f32[96,256]{1,0:T(8,128)S(1)} %add_add_fusion.1), channel_id=1, source_target_pairs={{0,8},{1,17},{2,10},{3,19},{4,12},{5,21},{6,14},{7,23},{8,0},{9,25... | collective-permute-start | bytes 294920 | tf_op jit(solution)/shard_map/ppermute | solution.py:394
  64.4 0.1 collective-permute-start.9
  64.5 2.9 %collective-permute-done.11 = f32[96,256]{1,0:T(8,128)S(1)} collective-permute-done((f32[96,256]{1,0:T(8,128)S(1)}, f32[96,256]{1,0:T(8,128)S(1)}, u32[]{:S(2)}, u32[]{:S(2)}) %collective-permute-start.11) | collective-permute-done | bytes 98336 | tf_op jit(solution)/shard_map/ppermute | solution.py:394
  67.4 0.9 collective-permute-done.10
  68.3 4.1 %collective-permute-done.9 = f32[96,256]{1,0:T(8,128)S(1)} collective-permute-done((f32[96,256]{1,0:T(8,128)S(1)}, f32[96,256]{1,0:T(8,128)S(1)}, u32[]{:S(2)}, u32[]{:S(2)}) %collective-permute-start.9) | collective-permute-done | bytes 98336 | tf_op jit(solution)/shard_map/ppermute | solution.py:394
  72.5 0.1 add_add_fusion
  72.6 0.5 collective-permute-start.14
  73.0 2.8 %collective-permute-start.15 = (f32[64,256]{1,0:T(8,128)S(1)}, f32[64,256]{1,0:T(8,128)S(1)}, u32[]{:S(2)}, u32[]{:S(2)}) collective-permute-start(f32[64,256]{1,0:T(8,128)S(1)} %get-tuple-element.72), channel_id=1, source_target_pairs={{0,8},{1,17},{2,10},{3,19},{4,12},{5,21},{6,14},{7,23},{8,0},{9,25... | collective-permute-start | bytes 196616 | tf_op jit(solution)/shard_map/ppermute | solution.py:386
  75.8 1.2 %collective-permute-start.16 = (f32[64,256]{1,0:T(8,128)S(1)}, f32[64,256]{1,0:T(8,128)S(1)}, u32[]{:S(2)}, u32[]{:S(2)}) collective-permute-start(f32[64,256]{1,0:T(8,128)S(1)} %get-tuple-element.68), channel_id=1, source_target_pairs={{0,24},{1,25},{2,26},{3,27},{4,28},{5,29},{6,30},{7,31},{8,16},{9,... | collective-permute-start | bytes 196616 | tf_op jit(solution)/shard_map/ppermute | solution.py:386
  77.0 0.9 collective-permute-start.13
  77.9 0.8 collective-permute-done.14
  78.7 3.1 %collective-permute-done.16 = f32[64,256]{1,0:T(8,128)S(1)} collective-permute-done((f32[64,256]{1,0:T(8,128)S(1)}, f32[64,256]{1,0:T(8,128)S(1)}, u32[]{:S(2)}, u32[]{:S(2)}) %collective-permute-start.16) | collective-permute-done | bytes 65568 | tf_op jit(solution)/shard_map/ppermute | solution.py:386
  81.9 1.3 %collective-permute-start.20 = (f32[64,256]{1,0:T(8,128)S(1)}, f32[64,256]{1,0:T(8,128)S(1)}, u32[]{:S(2)}, u32[]{:S(2)}) collective-permute-start(f32[64,256]{1,0:T(8,128)S(1)} %add_add_fusion.2), channel_id=1, source_target_pairs={{0,24},{1,25},{2,26},{3,27},{4,28},{5,29},{6,30},{7,31},{8,16},{9,... | collective-permute-start | bytes 196616 | tf_op jit(solution)/shard_map/ppermute | solution.py:394
  83.2 3.2 %collective-permute-start.18 = (f32[64,256]{1,0:T(8,128)S(1)}, f32[64,256]{1,0:T(8,128)S(1)}, u32[]{:S(2)}, u32[]{:S(2)}) collective-permute-start(f32[64,256]{1,0:T(8,128)S(1)} %add_add_fusion.2), channel_id=1, source_target_pairs={{0,16},{1,9},{2,18},{3,11},{4,20},{5,13},{6,22},{7,15},{8,24},{9,1... | collective-permute-start | bytes 196616 | tf_op jit(solution)/shard_map/ppermute | solution.py:394
  86.4 1.7 %collective-permute-done.20 = f32[64,256]{1,0:T(8,128)S(1)} collective-permute-done((f32[64,256]{1,0:T(8,128)S(1)}, f32[64,256]{1,0:T(8,128)S(1)}, u32[]{:S(2)}, u32[]{:S(2)}) %collective-permute-start.20) | collective-permute-done | bytes 65568 | tf_op jit(solution)/shard_map/ppermute | solution.py:394
  88.1 0.7 collective-permute-done.18
  88.9 0.1 collective-permute-start.23
  89.0 1.6 %collective-permute-start.22 = (f32[512,256]{1,0:T(8,128)S(1)}, f32[512,256]{1,0:T(8,128)S(1)}, u32[]{:S(2)}, u32[]{:S(2)}) collective-permute-start(f32[512,256]{1,0:T(8,128)S(1)} %pad_maximum_fusion.1.refs_2_), channel_id=1, source_target_pairs={{0,2},{1,5},{2,0},{3,7},{4,6},{5,1},{6,4},{7,3},{8,10},{9,13},{10,... | collective-permute-start | bytes 1572872 | tf_op jit(solution)/shard_map/ppermute | solution.py:325
  90.6 0.8 collective-permute-start.21
  91.4 6.1 %factor.2 = (f32[128,256]{1,0:T(8,128)S(1)}, bf16[128,256]{1,0:T(8,128)(2,1)S(1)}, bf16[128,256]{1,0:T(8,128)(2,1)S(1)}, f32[256,512]{1,0:T(8,128)S(1)}) custom-call(s32[11]{0:T(128)S(1)} %copy-done.1, f32[128,256]{1,0:T(8,128)S(1)} %pad_maximum_fusion.7.refs_0_, f32[128,256]{1,0:T(8,128)S(1)} %collective-permute-done.17.refs_1_), custom_call_target="tpu_custom_call" | custom-call | flops 5000000000 | bytes 524288 | tf_op jit(solution)/shard_map/factor/pallas_call | solution.py:225
  97.6 2.3 %collective-permute-done.21 = f32[256,256]{1,0:T(8,128)S(1)} collective-permute-done((f32[256,256]{1,0:T(8,128)S(1)}, f32[256,256]{1,0:T(8,128)S(1)}, u32[]{:S(2)}, u32[]{:S(2)}) %collective-permute-start.21) | collective-permute-done | bytes 262176 | tf_op jit(solution)/shard_map/ppermute | solution.py:325
  99.9 1.2 collective-permute-done.22.refs_3_
  101.0 1.5 %collective-permute-start.26 = (f32[512,256]{1,0:T(8,128)S(1)}, f32[512,256]{1,0:T(8,128)S(1)}, u32[]{:S(2)}, u32[]{:S(2)}) collective-permute-start(f32[512,256]{1,0:T(8,128)S(1)} %pad_maximum_fusion.2.refs_3_), channel_id=1, source_target_pairs={{0,2},{1,5},{2,0},{3,7},{4,6},{5,1},{6,4},{7,3},{8,10},{9,13},{10,... | collective-permute-start | bytes 1572872 | tf_op jit(solution)/shard_map/ppermute | solution.py:325
  102.6 0.5 collective-permute-start.24
  103.1 6.2 %factor.3 = (f32[128,256]{1,0:T(8,128)S(1)}, bf16[128,256]{1,0:T(8,128)(2,1)S(1)}, bf16[128,256]{1,0:T(8,128)(2,1)S(1)}, f32[256,512]{1,0:T(8,128)}) custom-call(s32[11]{0:T(128)S(1)} %copy-done.1, f32[256,512]{1,0:T(8,128)S(1)} %get-tuple-element.81.refs_0_), custom_call_target="tpu_custom_call" | custom-call | flops 5000000000 | bytes 524288 | tf_op jit(solution)/shard_map/factor/pallas_call | solution.py:225
  109.3 2.7 %basis.1 = bf16[2048,256]{1,0:T(8,128)(2,1)} custom-call(f32[2048,256]{1,0:T(8,128)S(1)} %copy-done, bf16[256,256]{1,0:T(8,128)(2,1)S(1)} %pad_maximum_fusion.8.high, bf16[256,256]{1,0:T(8,128)(2,1)S(1)} %constant_dynamic-update-slice_fusion.low), custom_call_target="tpu_custom_call" | custom-call | flops 805306368 | bytes 3145728 | tf_op jit(solution)/shard_map/basis/pallas_call | solution.py:252
  112.0 0.7 pad_maximum_fusion.6
  112.7 2.4 %project.2.refs_0_ = f32[256,4096]{1,0:T(8,128)} custom-call(s32[11]{0:T(128)S(1)} %copy-done.1, bf16[256,256]{1,0:T(8,128)(2,1)S(1)} %pad_maximum_fusion.8.high, bf16[256,256]{1,0:T(8,128)(2,1)S(1)} %constant_dynamic-update-slice_fusion.low, f32[512,256]{1,0:T(8,128)S(1)} %collective-permute-done.23.refs_0_, ...), custom_call_target="tpu_custom_call" | custom-call | flops 805306368 | bytes 2097152 | tf_op jit(solution)/shard_map/project/pallas_call | solution.py:292
  115.2 2.4 %project.3 = f32[256,4096]{1,0:T(8,128)} custom-call(s32[11]{0:T(128)S(1)} %copy-done.1, bf16[256,256]{1,0:T(8,128)(2,1)S(1)} %pad_maximum_fusion.8.high, bf16[256,256]{1,0:T(8,128)(2,1)S(1)} %constant_dynamic-update-slice_fusion.low, f32[256,4096]{1,0:T(8,128)} %project.2.refs_0_, ...), custom_call_target="tpu_custom_call", output_to_operand_aliasing={{}: (3, {})} | custom-call | flops 805306368 | bytes 2097152 | tf_op jit(solution)/shard_map/project/pallas_call | solution.py:292
  (60 shorter events, 0.8 us)
Async XLA Ops:
  17.6 20.0 %copy-start.2 = (f32[512,256]{1,0:T(8,128)S(1)}, f32[512,256]{1,0:T(8,128)}, u32[]{:S(2)}) copy-start(f32[512,256]{1,0:T(8,128)} %get-tuple-element.56) | copy-start | bytes 1572868
  17.7 29.8 %copy-start.4 = (f32[512,256]{1,0:T(8,128)S(1)}, f32[512,256]{1,0:T(8,128)}, u32[]{:S(2)}) copy-start(f32[512,256]{1,0:T(8,128)} %get-tuple-element.47) | copy-start | bytes 1572868
  17.7 4.1 %collective-permute-start = (f32[1024,256]{1,0:T(8,128)}, f32[1024,256]{1,0:T(8,128)S(1)}, u32[]{:S(2)}, u32[]{:S(2)}) collective-permute-start(f32[1024,256]{1,0:T(8,128)} %get-tuple-element.49), channel_id=1, source_target_pairs={{0,1},{1,0},{2,3},{3,2},{4,5},{5,4},{6,7},{7,6},{8,9},{9,8},{10,11... | collective-permute-start | bytes 3145736 | tf_op jit(solution)/shard_map/ppermute | solution.py:322
  18.2 2.7 %collective-permute-start.1 = (f32[128,256]{1,0:T(8,128)}, f32[128,256]{1,0:T(8,128)S(1)}, u32[]{:S(2)}, u32[]{:S(2)}) collective-permute-start(f32[128,256]{1,0:T(8,128)} %get-tuple-element.51), channel_id=1, source_target_pairs={{0,1},{1,0},{2,3},{3,2},{4,5},{5,4},{6,7},{7,6},{8,9},{9,8},{10,11... | collective-permute-start | bytes 393224 | tf_op jit(solution)/shard_map/ppermute | solution.py:322
  22.9 29.6 %copy-start.3 = (f32[512,256]{1,0:T(8,128)S(1)}, f32[512,256]{1,0:T(8,128)}, u32[]{:S(2)}) copy-start(f32[512,256]{1,0:T(8,128)} %get-tuple-element.63) | copy-start | bytes 1572868
  23.0 11.5 %collective-permute-start.2 = (f32[640,256]{1,0:T(8,128)S(1)}, f32[640,256]{1,0:T(8,128)S(1)}, u32[]{:S(2)}, u32[]{:S(2)}) collective-permute-start(f32[640,256]{1,0:T(8,128)S(1)} %pad_maximum_fusion), channel_id=1, source_target_pairs={{0,2},{1,5},{2,0},{3,7},{4,6},{5,1},{6,4},{7,3},{8,10},{9,13},{10,... | collective-permute-start | bytes 1966088 | tf_op jit(solution)/shard_map/ppermute | solution.py:325
  25.9 11.8 %collective-permute-start.4 = (f32[1024,256]{1,0:T(8,128)}, f32[1024,256]{1,0:T(8,128)S(1)}, u32[]{:S(2)}, u32[]{:S(2)}) collective-permute-start(f32[1024,256]{1,0:T(8,128)} %get-tuple-element.57), channel_id=1, source_target_pairs={{0,1},{1,0},{2,3},{3,2},{4,5},{5,4},{6,7},{7,6},{8,9},{9,8},{10,11... | collective-permute-start | bytes 3145736 | tf_op jit(solution)/shard_map/ppermute | solution.py:322
  35.5 11.9 %collective-permute-start.3 = (f32[384,256]{1,0:T(8,128)S(1)}, f32[384,256]{1,0:T(8,128)S(1)}, u32[]{:S(2)}, u32[]{:S(2)}) collective-permute-start(f32[384,256]{1,0:T(8,128)S(1)} %pad_maximum_fusion.3), channel_id=1, source_target_pairs={{0,4},{1,3},{2,6},{3,1},{4,0},{5,7},{6,2},{7,5},{8,12},{9,11},{10,... | collective-permute-start | bytes 1179656 | tf_op jit(solution)/shard_map/ppermute | solution.py:325
  37.7 14.8 %collective-permute-start.8 = (f32[512,256]{1,0:T(8,128)S(1)}, f32[512,256]{1,0:T(8,128)S(1)}, u32[]{:S(2)}, u32[]{:S(2)}) collective-permute-start(f32[512,256]{1,0:T(8,128)S(1)} %slice_add_fusion), channel_id=1, source_target_pairs={{0,2},{1,5},{2,0},{3,7},{4,6},{5,1},{6,4},{7,3},{8,10},{9,13},{10,... | collective-permute-start | bytes 1572872 | tf_op jit(solution)/shard_map/ppermute | solution.py:325
  47.6 43.9 %copy-start.1 = (s32[11]{0:T(128)S(1)}, s32[11]{0:T(128)}, u32[]{:S(2)}) copy-start(s32[11]{0:T(128)} %stack.47.info) | copy-start | bytes 136
  47.7 6.8 %collective-permute-start.5 = (f32[96,256]{1,0:T(8,128)S(1)}, f32[96,256]{1,0:T(8,128)S(1)}, u32[]{:S(2)}, u32[]{:S(2)}) collective-permute-start(f32[96,256]{1,0:T(8,128)S(1)} %get-tuple-element.60), channel_id=1, source_target_pairs={{0,16},{1,9},{2,18},{3,11},{4,20},{5,13},{6,22},{7,15},{8,24},{9,1... | collective-permute-start | bytes 294920 | tf_op jit(solution)/shard_map/ppermute | solution.py:386
  51.0 4.6 %collective-permute-start.6 = (f32[96,256]{1,0:T(8,128)S(1)}, f32[96,256]{1,0:T(8,128)S(1)}, u32[]{:S(2)}, u32[]{:S(2)}) collective-permute-start(f32[96,256]{1,0:T(8,128)S(1)} %get-tuple-element.61), channel_id=1, source_target_pairs={{0,8},{1,17},{2,10},{3,19},{4,12},{5,21},{6,14},{7,23},{8,0},{9,25... | collective-permute-start | bytes 294920 | tf_op jit(solution)/shard_map/ppermute | solution.py:386
  52.5 7.5 %collective-permute-start.7 = (f32[96,256]{1,0:T(8,128)S(1)}, f32[96,256]{1,0:T(8,128)S(1)}, u32[]{:S(2)}, u32[]{:S(2)}) collective-permute-start(f32[96,256]{1,0:T(8,128)S(1)} %get-tuple-element.62), channel_id=1, source_target_pairs={{0,24},{1,25},{2,26},{3,27},{4,28},{5,29},{6,30},{7,31},{8,16},{9,... | collective-permute-start | bytes 294920 | tf_op jit(solution)/shard_map/ppermute | solution.py:386
  52.6 19.8 %collective-permute-start.12 = (f32[256,256]{1,0:T(8,128)S(1)}, f32[256,256]{1,0:T(8,128)S(1)}, u32[]{:S(2)}, u32[]{:S(2)}) collective-permute-start(f32[256,256]{1,0:T(8,128)S(1)} %slice_add_fusion.2), channel_id=1, source_target_pairs={{0,4},{1,3},{2,6},{3,1},{4,0},{5,7},{6,2},{7,5},{8,12},{9,11},{10,... | collective-permute-start | bytes 786440 | tf_op jit(solution)/shard_map/ppermute | solution.py:325
  60.1 7.4 %collective-permute-start.11 = (f32[96,256]{1,0:T(8,128)S(1)}, f32[96,256]{1,0:T(8,128)S(1)}, u32[]{:S(2)}, u32[]{:S(2)}) collective-permute-start(f32[96,256]{1,0:T(8,128)S(1)} %add_add_fusion.1), channel_id=1, source_target_pairs={{0,24},{1,25},{2,26},{3,27},{4,28},{5,29},{6,30},{7,31},{8,16},{9,... | collective-permute-start | bytes 294920 | tf_op jit(solution)/shard_map/ppermute | solution.py:394
  62.7 5.6 %collective-permute-start.10 = (f32[96,256]{1,0:T(8,128)S(1)}, f32[96,256]{1,0:T(8,128)S(1)}, u32[]{:S(2)}, u32[]{:S(2)}) collective-permute-start(f32[96,256]{1,0:T(8,128)S(1)} %add_add_fusion.1), channel_id=1, source_target_pairs={{0,8},{1,17},{2,10},{3,19},{4,12},{5,21},{6,14},{7,23},{8,0},{9,25... | collective-permute-start | bytes 294920 | tf_op jit(solution)/shard_map/ppermute | solution.py:394
  64.4 8.0 %collective-permute-start.9 = (f32[96,256]{1,0:T(8,128)S(1)}, f32[96,256]{1,0:T(8,128)S(1)}, u32[]{:S(2)}, u32[]{:S(2)}) collective-permute-start(f32[96,256]{1,0:T(8,128)S(1)} %add_add_fusion.1), channel_id=1, source_target_pairs={{0,16},{1,9},{2,18},{3,11},{4,20},{5,13},{6,22},{7,15},{8,24},{9,1... | collective-permute-start | bytes 294920 | tf_op jit(solution)/shard_map/ppermute | solution.py:394
  72.6 6.2 %collective-permute-start.14 = (f32[64,256]{1,0:T(8,128)S(1)}, f32[64,256]{1,0:T(8,128)S(1)}, u32[]{:S(2)}, u32[]{:S(2)}) collective-permute-start(f32[64,256]{1,0:T(8,128)S(1)} %get-tuple-element.71), channel_id=1, source_target_pairs={{0,16},{1,9},{2,18},{3,11},{4,20},{5,13},{6,22},{7,15},{8,24},{9,1... | collective-permute-start | bytes 196616 | tf_op jit(solution)/shard_map/ppermute | solution.py:386
  73.0 5.7 %collective-permute-start.15 = (f32[64,256]{1,0:T(8,128)S(1)}, f32[64,256]{1,0:T(8,128)S(1)}, u32[]{:S(2)}, u32[]{:S(2)}) collective-permute-start(f32[64,256]{1,0:T(8,128)S(1)} %get-tuple-element.72), channel_id=1, source_target_pairs={{0,8},{1,17},{2,10},{3,19},{4,12},{5,21},{6,14},{7,23},{8,0},{9,25... | collective-permute-start | bytes 196616 | tf_op jit(solution)/shard_map/ppermute | solution.py:386
  75.8 6.1 %collective-permute-start.16 = (f32[64,256]{1,0:T(8,128)S(1)}, f32[64,256]{1,0:T(8,128)S(1)}, u32[]{:S(2)}, u32[]{:S(2)}) collective-permute-start(f32[64,256]{1,0:T(8,128)S(1)} %get-tuple-element.68), channel_id=1, source_target_pairs={{0,24},{1,25},{2,26},{3,27},{4,28},{5,29},{6,30},{7,31},{8,16},{9,... | collective-permute-start | bytes 196616 | tf_op jit(solution)/shard_map/ppermute | solution.py:386
  77.0 11.8 %collective-permute-start.13 = (f32[256,256]{1,0:T(8,128)S(1)}, f32[256,256]{1,0:T(8,128)S(1)}, u32[]{:S(2)}, u32[]{:S(2)}) collective-permute-start(f32[256,256]{1,0:T(8,128)S(1)} %pad_maximum_fusion.4), channel_id=1, source_target_pairs={{0,4},{1,3},{2,6},{3,1},{4,0},{5,7},{6,2},{7,5},{8,12},{9,11},{10,... | collective-permute-start | bytes 786440 | tf_op jit(solution)/shard_map/ppermute | solution.py:325
  81.9 6.2 %collective-permute-start.20 = (f32[64,256]{1,0:T(8,128)S(1)}, f32[64,256]{1,0:T(8,128)S(1)}, u32[]{:S(2)}, u32[]{:S(2)}) collective-permute-start(f32[64,256]{1,0:T(8,128)S(1)} %add_add_fusion.2), channel_id=1, source_target_pairs={{0,24},{1,25},{2,26},{3,27},{4,28},{5,29},{6,30},{7,31},{8,16},{9,... | collective-permute-start | bytes 196616 | tf_op jit(solution)/shard_map/ppermute | solution.py:394
  83.2 5.0 %collective-permute-start.19 = (f32[64,256]{1,0:T(8,128)S(1)}, f32[64,256]{1,0:T(8,128)S(1)}, u32[]{:S(2)}, u32[]{:S(2)}) collective-permute-start(f32[64,256]{1,0:T(8,128)S(1)} %add_add_fusion.2), channel_id=1, source_target_pairs={{0,8},{1,17},{2,10},{3,19},{4,12},{5,21},{6,14},{7,23},{8,0},{9,25... | collective-permute-start | bytes 196616 | tf_op jit(solution)/shard_map/ppermute | solution.py:394
  83.2 5.7 %collective-permute-start.18 = (f32[64,256]{1,0:T(8,128)S(1)}, f32[64,256]{1,0:T(8,128)S(1)}, u32[]{:S(2)}, u32[]{:S(2)}) collective-permute-start(f32[64,256]{1,0:T(8,128)S(1)} %add_add_fusion.2), channel_id=1, source_target_pairs={{0,16},{1,9},{2,18},{3,11},{4,20},{5,13},{6,22},{7,15},{8,24},{9,1... | collective-permute-start | bytes 196616 | tf_op jit(solution)/shard_map/ppermute | solution.py:394
  86.4 5.0 %collective-permute-start.17 = (f32[128,256]{1,0:T(8,128)S(1)}, f32[128,256]{1,0:T(8,128)S(1)}, u32[]{:S(2)}, u32[]{:S(2)}) collective-permute-start(f32[128,256]{1,0:T(8,128)S(1)} %pad_maximum_fusion.7.refs_0_), channel_id=1, source_target_pairs={{0,1},{1,0},{2,3},{3,2},{4,5},{5,4},{6,7},{7,6},{8,9},{9,8},{10,11... | collective-permute-start | bytes 393224 | tf_op jit(solution)/shard_map/ppermute | solution.py:322
  88.9 23.8 %collective-permute-start.23 = (f32[512,256]{1,0:T(8,128)S(1)}, f32[512,256]{1,0:T(8,128)S(1)}, u32[]{:S(2)}, u32[]{:S(2)}) collective-permute-start(f32[512,256]{1,0:T(8,128)S(1)} %pad_maximum_fusion.1.refs_2_), channel_id=1, source_target_pairs={{0,1},{1,0},{2,3},{3,2},{4,5},{5,4},{6,7},{7,6},{8,9},{9,8},{10,11... | collective-permute-start | bytes 1572872 | tf_op jit(solution)/shard_map/ppermute | solution.py:322
  89.0 12.1 %collective-permute-start.22 = (f32[512,256]{1,0:T(8,128)S(1)}, f32[512,256]{1,0:T(8,128)S(1)}, u32[]{:S(2)}, u32[]{:S(2)}) collective-permute-start(f32[512,256]{1,0:T(8,128)S(1)} %pad_maximum_fusion.1.refs_2_), channel_id=1, source_target_pairs={{0,2},{1,5},{2,0},{3,7},{4,6},{5,1},{6,4},{7,3},{8,10},{9,13},{10,... | collective-permute-start | bytes 1572872 | tf_op jit(solution)/shard_map/ppermute | solution.py:325
  90.6 9.2 %collective-permute-start.21 = (f32[256,256]{1,0:T(8,128)S(1)}, f32[256,256]{1,0:T(8,128)S(1)}, u32[]{:S(2)}, u32[]{:S(2)}) collective-permute-start(f32[256,256]{1,0:T(8,128)S(1)} %pad_maximum_fusion.5), channel_id=1, source_target_pairs={{0,4},{1,3},{2,6},{3,1},{4,0},{5,7},{6,2},{7,5},{8,12},{9,11},{10,... | collective-permute-start | bytes 786440 | tf_op jit(solution)/shard_map/ppermute | solution.py:325
  101.0 10.9 %collective-permute-start.26 = (f32[512,256]{1,0:T(8,128)S(1)}, f32[512,256]{1,0:T(8,128)S(1)}, u32[]{:S(2)}, u32[]{:S(2)}) collective-permute-start(f32[512,256]{1,0:T(8,128)S(1)} %pad_maximum_fusion.2.refs_3_), channel_id=1, source_target_pairs={{0,2},{1,5},{2,0},{3,7},{4,6},{5,1},{6,4},{7,3},{8,10},{9,13},{10,... | collective-permute-start | bytes 1572872 | tf_op jit(solution)/shard_map/ppermute | solution.py:325
  102.6 12.6 %collective-permute-start.25 = (f32[512,256]{1,0:T(8,128)S(1)}, f32[512,256]{1,0:T(8,128)S(1)}, u32[]{:S(2)}, u32[]{:S(2)}) collective-permute-start(f32[512,256]{1,0:T(8,128)S(1)} %pad_maximum_fusion.2.refs_3_), channel_id=1, source_target_pairs={{0,1},{1,0},{2,3},{3,2},{4,5},{5,4},{6,7},{7,6},{8,9},{9,8},{10,11... | collective-permute-start | bytes 1572872 | tf_op jit(solution)/shard_map/ppermute | solution.py:322
  102.6 10.1 %collective-permute-start.24 = (f32[512,256]{1,0:T(8,128)S(1)}, f32[512,256]{1,0:T(8,128)S(1)}, u32[]{:S(2)}, u32[]{:S(2)}) collective-permute-start(f32[512,256]{1,0:T(8,128)S(1)} %collective-permute-done.22.refs_3_), channel_id=1, source_target_pairs={{0,1},{1,0},{2,3},{3,2},{4,5},{5,4},{6,7},{7,6},{8,9},{9,8},{10,11... | collective-permute-start | bytes 1572872 | tf_op jit(solution)/shard_map/ppermute | solution.py:322
  103.1 6.2 %copy-start = (f32[2048,256]{1,0:T(8,128)S(1)}, f32[2048,256]{1,0:T(8,128)}, u32[]{:S(2)}) copy-start(f32[2048,256]{1,0:T(8,128)} %get-tuple-element.83.sketch) | copy-start | bytes 6291460
  112.0 3.2 %collective-permute-start.27 = (f32[512,256]{1,0:T(8,128)S(1)}, f32[512,256]{1,0:T(8,128)S(1)}, u32[]{:S(2)}, u32[]{:S(2)}) collective-permute-start(f32[512,256]{1,0:T(8,128)S(1)} %collective-permute-done.26.refs_4_), channel_id=1, source_target_pairs={{0,1},{1,0},{2,3},{3,2},{4,5},{5,4},{6,7},{7,6},{8,9},{9,8},{10,11... | collective-permute-start | bytes 1572872 | tf_op jit(solution)/shard_map/ppermute | solution.py:322

commit v5 on v2

v5 whole, which is shorter than its diff:
```python
import functools
import math

import jax
import jax.numpy as jnp
from jax import lax
from jax.experimental import pallas as pl
from jax.experimental.pallas import tpu as pltpu
from jax.sharding import PartitionSpec as P

AXES = ("gx", "gy")
MIB = 1 << 20
LINE_FIRST = 0.375


def dot(a, b, dims=((1,), (0,))):
    return lax.dot_general(a, b, (dims, ((), ())), preferred_element_type=jnp.float32)


def split(a):
    high = a.astype(jnp.bfloat16)
    return high, (a - high.astype(jnp.float32)).astype(jnp.bfloat16)


VMEM_SPEC = pl.BlockSpec(memory_space=pltpu.VMEM)
SMEM_SPEC = pl.BlockSpec(memory_space=pltpu.SMEM)
ANY_SPEC = pl.BlockSpec(memory_space=pl.ANY)


def pinned(*arrays):
    return [pltpu.with_memory_space_constraint(a, pltpu.VMEM) for a in arrays]


PLANE = 4


def row_classes(k, line):
    unit = 8 * line
    second = max(1, round(k * LINE_FIRST / unit)) * unit
    return k - second, second


def front_kernel(
    in_scale, gram_scale, scale, line,
    info, e, signs, sketch_out, gram_sent, gram_kept, sent1, sent2, kept1, kept2,
    e_kept, sketch, rounded_t, s32, s16, acc, class1, class2, sem, out_sem,
):
    rows, d = e.shape
    k = rounded_t.shape[0]
    n = sem.shape[0] - 1
    block = rows // n
    signs_copy = pltpu.make_async_copy(signs, s32, sem.at[n])
    signs_copy.start()

    def rows_copy(i):
        at = pl.ds(pl.multiple_of(i * block, block), block)
        return pltpu.make_async_copy(e.at[at], e_kept.at[at], sem.at[i])

    for i in range(n):
        rows_copy(i).start()
    signs_copy.wait()
    s16[...] = s32[...].astype(jnp.bfloat16)

    def step(i, carry):
        rows_copy(i).wait()
        at = pl.ds(pl.multiple_of(i * block, block), block)
        sk = dot(e_kept[at, :], s16[...]) * in_scale
        sketch[at, :] = sk
        rounded_t[:, at] = sk.astype(jnp.bfloat16).T
        return carry

    lax.fori_loop(0, n, step, 0)
    outs = [pltpu.make_async_copy(sketch, sketch_out, out_sem.at[0])]
    outs[0].start()
    high, low = split(sketch[...])
    acc[...] = dot(rounded_t[...], low)
    acc[...] = (dot(rounded_t[...], high) + (acc[...] + acc[...].T)) * gram_scale
    own, in_plane, in_line = info[0], info[1], info[2]
    half = k // 2
    size = half // line
    for g in range(line):
        to = pl.ds(pl.multiple_of((in_line ^ g) * size, size), size)
        for out, region in ((gram_kept, own), (gram_sent, 1 - own)):
            out[to, :] = acc[pl.ds(pl.multiple_of(region * half + g * size, size), size), :]
    rows1, rows2 = row_classes(k, line)
    size1, size2 = rows1 // line, rows2 // line
    width = d // (2 * PLANE)
    for r, region in enumerate((1 - own, own)):
        for p in range(PLANE):
            at = pl.ds(pl.multiple_of((region * PLANE + (in_plane ^ p)) * width, width), width)
            value = dot(rounded_t[...], e_kept[:, at]) * scale
            for g in range(line):
                to = in_line ^ g
                for h in range(2):
                    part = value[:, h * width // 2 : (h + 1) * width // 2]
                    to1 = pl.multiple_of(p * 2 * rows1 + (2 * to + h) * size1, 8)
                    class1[r, pl.ds(to1, size1), :] = part[g * size1 : (g + 1) * size1]
                    to2 = pl.multiple_of(((to * PLANE + (in_plane ^ p)) * 2 + h) * size2, 8)
                    class2[r, pl.ds(to2, size2), :] = part[rows1 + g * size2 : rows1 + (g + 1) * size2]
            at = pl.ds(p * 2 * rows1, 2 * rows1)
            outs.append(pltpu.make_async_copy(class1.at[r, at], (sent1, kept1)[r].at[at], out_sem.at[1 + r * PLANE + p]))
            outs[-1].start()
        outs.append(pltpu.make_async_copy(class2.at[r], (sent2, kept2)[r], out_sem.at[1 + 2 * PLANE + r]))
        outs[-1].start()
    for copy in outs:
        copy.wait()


def front_call(info, e, signs, rows_all, line):
    rows, d = e.shape
    k = signs.shape[1]
    copies = 4
    rows1, rows2 = row_classes(k, line)
    width = d // (4 * PLANE)
    classes = [(2 * PLANE * rows1, width), (2 * PLANE * rows2, width)]
    f32 = lambda *shape: jax.ShapeDtypeStruct(shape, jnp.float32)
    return pl.pallas_call(
        functools.partial(front_kernel, 1.0 / math.sqrt(d), 1.0 / rows_all, 1.0 / math.sqrt(rows_all), line),
        in_specs=[SMEM_SPEC, ANY_SPEC, ANY_SPEC],
        out_specs=[ANY_SPEC] + [VMEM_SPEC] * 2 + [ANY_SPEC] * 4,
        out_shape=[f32(rows, k), f32(k // 2, k), f32(k // 2, k)] + [f32(*c) for c in classes] * 2,
        scratch_shapes=[
            pltpu.VMEM((rows, d), e.dtype),
            pltpu.VMEM((rows, k), jnp.float32),
            pltpu.VMEM((k, rows), jnp.bfloat16),
            pltpu.VMEM((d, k), jnp.int32),
            pltpu.VMEM((d, k), jnp.bfloat16),
            pltpu.VMEM((k, k), jnp.float32),
            pltpu.VMEM((2, *classes[0]), jnp.float32),
            pltpu.VMEM((2, *classes[1]), jnp.float32),
            pltpu.SemaphoreType.DMA((copies + 1,)),
            pltpu.SemaphoreType.DMA((3 + 2 * PLANE,)),
        ],
        compiler_params=pltpu.CompilerParams(vmem_limit_bytes=56 * MIB),
        cost_estimate=pl.CostEstimate(flops=4 * rows * d * k, bytes_accessed=rows * d * 2 + d * k * 4, transcendentals=0),
        name="front",
    )(info, e, pltpu.with_memory_space_constraint(signs, pltpu.HBM))


def factor_kernel(line, info, kept, got, triangle, high, low, work):
    k = triangle.shape[0]
    half = k // 2
    b = 64
    own, in_line = info[0], info[2]
    size = half // line
    for g in range(line):
        at = pl.ds(pl.multiple_of((in_line ^ g) * size, size), size)
        for rows, region in ((kept, own), (got, 1 - own)):
            work[pl.ds(pl.multiple_of(region * half + g * size, size), size), :k] = rows[at, :]
    rows_k = lax.broadcasted_iota(jnp.int32, (k, k), 0)
    cols_k = lax.broadcasted_iota(jnp.int32, (k, k), 1)
    work[:, k:] = jnp.where(rows_k == cols_k, 1.0, 0.0)
    lane = lax.broadcasted_iota(jnp.int32, (8, 2 * b), 1)
    sub = lax.broadcasted_iota(jnp.int32, (8, 2 * b), 0)

    def over_lanes(a, at):
        return jnp.broadcast_to(a[:, at : at + 1], (8, 2 * b))

    for n in range(k // b):
        put = slice(n * b, (n + 1) * b)
        first = (n % 2) * b
        pair = (n // 2) * 2 * b
        own_lanes = (lane >= first) & (lane < first + b)
        w = []
        for v in range(b // 8):
            a = work[n * b + 8 * v : n * b + 8 * v + 8, pair : pair + 2 * b]
            ident = jnp.where(lane == (b - first) + 8 * v + sub, 1.0, 0.0)
            w.append(jnp.where(own_lanes, a, ident))
        inv = []
        for q in range(b // 8):
            at = first + 8 * q
            row = [jnp.broadcast_to(w[q][i : i + 1, :], (8, 2 * b)) for i in range(8)]
            s = {(i, j): over_lanes(row[i], at + j) for i in range(8) for j in range(i, 8)}
            factor = {}
            scaled = []
            for j in range(8):
                r = 1.0 / s[j, j]
                for i in range(j + 1, 8):
                    factor[i, j] = s[j, i] * r
                    for m in range(i, 8):
                        s[i, m] = s[i, m] - factor[i, j] * s[j, m]
                    row[i] = row[i] - factor[i, j] * row[j]
                scaled.append(row[j] * r)
            new, pivots = row[0], s[0, 0]
            for i in range(1, 8):
                new = jnp.where(sub == i, row[i], new)
                pivots = jnp.where(sub == i, s[i, i], pivots)
            for v in range(q + 1, b // 8):
                col = [over_lanes(w[v], at + j) for j in range(8)]
                for j in range(8):
                    for m in range(j + 1, 8):
                        col[m] = col[m] - col[j] * factor[m, j]
                t = [col[j] * scaled[j] for j in range(8)]
                w[v] = w[v] - (((t[0] + t[1]) + (t[2] + t[3])) + ((t[4] + t[5]) + (t[6] + t[7])))
            moved = pltpu.roll(new * (1.0 / jnp.sqrt(pivots)), b, 1)
            inv.append(jnp.where(own_lanes, moved, 0.0))
        inv = jnp.concatenate(inv, axis=0)
        y = lax.dot_general(
            inv, work[pair : pair + 2 * b, :], (((1,), (0,)), ((), ())),
            precision=lax.Precision.HIGHEST, preferred_element_type=jnp.float32,
        )
        r_rows, i_rows = y[:, :k], y[:, k:]
        at = lax.broadcasted_iota(jnp.int32, (b, k), 0) + n * b
        to = lax.broadcasted_iota(jnp.int32, (b, k), 1)
        triangle[put, :] = jnp.where(to >= at, r_rows, 0.0)
        i_rows = jnp.where(to <= at, i_rows, 0.0)
        i_high, i_low = split(i_rows)
        high[put, :] = i_high
        low[put, :] = i_low
        if (n + 1) * b < k:
            later = jnp.where(to >= (n + 1) * b, r_rows, 0.0)
            work[...] -= lax.dot_general(
                later, y, (((0,), (0,)), ((), ())),
                precision=lax.Precision.HIGHEST, preferred_element_type=jnp.float32,
            )


def factor_call(line, info, kept, got):
    k = kept.shape[1]
    return pl.pallas_call(
        functools.partial(factor_kernel, line),
        in_specs=[SMEM_SPEC, VMEM_SPEC, VMEM_SPEC],
        out_specs=[VMEM_SPEC] * 3,
        out_shape=[
            jax.ShapeDtypeStruct((k, k), jnp.float32),
            jax.ShapeDtypeStruct((k, k), jnp.bfloat16),
            jax.ShapeDtypeStruct((k, k), jnp.bfloat16),
        ],
        scratch_shapes=[pltpu.VMEM((k, 2 * k), jnp.float32)],
        compiler_params=pltpu.CompilerParams(vmem_limit_bytes=16 * MIB),
        cost_estimate=pl.CostEstimate(flops=10**10, bytes_accessed=k * k * 8, transcendentals=0),
        name="factor",
    )(info, kept, got)


def basis_kernel(sketch, high, low, out):
    s_high, s_low = split(sketch[...])
    right = ((1,), (1,))
    out[...] = (
        dot(s_high, high[...], right) + (dot(s_high, low[...], right) + dot(s_low, high[...], right))
    ).astype(out.dtype)


def basis_call(sketch, high, low):
    rows, k = sketch.shape
    block = rows // 4
    return pl.pallas_call(
        basis_kernel,
        grid=(rows // block,),
        in_specs=[pl.BlockSpec((block, k), lambda i: (i, 0))] + [pl.BlockSpec((k, k), lambda i: (0, 0))] * 2,
        out_specs=pl.BlockSpec((block, k), lambda i: (i, 0)),
        out_shape=jax.ShapeDtypeStruct((rows, k), jnp.bfloat16),
        compiler_params=pltpu.CompilerParams(vmem_limit_bytes=16 * MIB),
        cost_estimate=pl.CostEstimate(flops=6 * rows * k * k, bytes_accessed=rows * k * 6, transcendentals=0),
        name="basis",
    )(sketch, high, low)


def project_kernel(line, is_own, info, high, low, *refs):
    *blocks, out, whole, value, sem = refs
    class1, class2 = blocks[-(PLANE + line) : -line], blocks[-line:]
    k = high.shape[0]
    rows1, rows2 = row_classes(k, line)
    size1, size2 = rows1 // line, rows2 // line
    own, in_plane, in_line = info[0], info[1], info[2]
    region = own if is_own else 1 - own
    width = value.shape[2]
    copies = []
    for p in range(PLANE):
        for g in range(line):
            to = in_line ^ g
            for h in range(2):
                cols = slice(h * width // 2, (h + 1) * width // 2)
                to1 = pl.ds(pl.multiple_of(to * size1, 8), size1)
                whole[p, to1, cols] = class1[p][(2 * g + h) * size1 : (2 * g + h + 1) * size1, :]
                to2 = pl.ds(pl.multiple_of(rows1 + to * size2, 8), size2)
                at2 = pl.ds(pl.multiple_of(((in_plane ^ p) * 2 + h) * size2, 8), size2)
                whole[p, to2, cols] = class2[g][at2, :]
        c_high, c_low = split(whole[p])
        value[p] = dot(high[...], c_high) + (dot(high[...], c_low) + dot(low[...], c_high))
        at = pl.ds(pl.multiple_of((region * PLANE + (in_plane ^ p)) * width, width), width)
        copies.append(pltpu.make_async_copy(value.at[p], out.at[:, at], sem.at[p]))
        copies[-1].start()
    for copy in copies:
        copy.wait()


def project_call(line, is_own, info, high, low, blocks, d, before):
    k = high.shape[0]
    width = d // (2 * PLANE)
    extra = [] if before is None else [before]
    return pl.pallas_call(
        functools.partial(project_kernel, line, is_own),
        in_specs=[SMEM_SPEC, VMEM_SPEC, VMEM_SPEC] + [ANY_SPEC] * len(extra) + [VMEM_SPEC] * len(blocks),
        out_specs=ANY_SPEC,
        out_shape=jax.ShapeDtypeStruct((k, d), jnp.float32),
        input_output_aliases={3: 0} if extra else {},
        scratch_shapes=[
            pltpu.VMEM((PLANE, k, width), jnp.float32),
            pltpu.VMEM((PLANE, k, width), jnp.float32),
            pltpu.SemaphoreType.DMA((PLANE,)),
        ],
        compiler_params=pltpu.CompilerParams(vmem_limit_bytes=16 * MIB),
        cost_estimate=pl.CostEstimate(flops=3 * k * k * d, bytes_accessed=k * d * 4, transcendentals=0),
        name="project",
    )(info, *pinned(high, low), *extra, *pinned(*blocks))


def solution(mesh):
    n_devices = math.prod(mesh.shape.values())
    line = n_devices // (2 * PLANE)

    def over(mask):
        pairs = [(i, i ^ mask) for i in range(n_devices)]
        return lambda a: lax.ppermute(a, AXES, pairs)

    with_pair = over(1)
    over_plane = [over(2 * g) for g in range(PLANE)]
    over_line = [over(2 * PLANE * g) for g in range(line)]

    def parts_of(a, n):
        size = a.shape[0] // n
        return [a[i * size : (i + 1) * size] for i in range(n)]

    def join(*arrays):
        return jnp.concatenate(arrays, axis=0)

    def shards(e, signs):
        rows_all = e.shape[0] * n_devices
        d = e.shape[1]
        k = signs.shape[1]
        rows1, rows2 = row_classes(k, line)
        me = lax.axis_index(AXES).astype(jnp.int32)
        info = jnp.stack([me & 1, (me >> 1) & (PLANE - 1), me // (2 * PLANE)])
        last = [me]

        def in_turn(*arrays):
            *arrays, _ = lax.optimization_barrier((*arrays, last[0]))
            last[0] = arrays[-1]
            return arrays if len(arrays) > 1 else arrays[0]

        sketch, gram_sent, gram, sent1, sent2, kept1, kept2 = front_call(info, e, signs, rows_all, line)
        got2, gram_got, got1 = with_pair(sent2), with_pair(gram_sent), with_pair(sent1)
        grams = parts_of(gram + gram_got, line)
        parts2 = [join(a + b, g) for a, b, g in zip(parts_of(kept2, line), parts_of(got2, line), grams)]
        parts2 = in_turn(*parts2)
        from_line = [over_line[g](parts2[g]) for g in range(1, line)]
        parts1 = in_turn(*[a + b for a, b in zip(parts_of(kept1, PLANE), parts_of(got1, PLANE))])
        from_plane = [over_plane[g](parts1[g]) for g in range(1, PLANE)]
        a2 = in_turn(sum(from_line, parts2[0]))
        whole2 = [over_plane[g](a2) for g in range(1, PLANE)]
        parts1 = in_turn(*parts_of(sum(from_plane, parts1[0]), line))
        from_line = [over_line[g](parts1[g]) for g in range(1, line)]
        a2 = (a2 + whole2[0]) + (whole2[1] + whole2[2])
        n2 = a2.shape[0] - gram.shape[0] // line
        a1 = in_turn(join(sum(from_line, parts1[0]), a2[n2:]))
        n1 = a1.shape[0] - gram.shape[0] // line
        from_line = [over_line[g](a1) for g in range(1, line)]
        a2 = in_turn(a2[:n2])
        class2 = [a2] + [over_line[g](a2) for g in range(1, line)]
        gathered = [a1, *from_line]
        a1 = in_turn(join(*[a[:n1] for a in gathered]))
        class1 = [a1] + [over_plane[g](a1) for g in range(1, PLANE)]
        gram = in_turn(join(*[a[n1:] for a in gathered]))
        triangle, high, low = factor_call(line, info, gram, with_pair(gram))
        high = in_turn(high)
        basis = in_turn(basis_call(sketch, high, low))
        ours = in_turn(*class1, *class2)
        theirs = [with_pair(a) for a in ours]
        projected = project_call(line, True, info, high, low, ours, d, None)
        projected = project_call(line, False, info, high, low, theirs, d, projected)
        return triangle, basis, projected

    return jax.shard_map(
        shards,
        mesh=mesh,
        in_specs=(P(AXES, None), P()),
        out_specs=(P(), P(AXES, None), P()),
        check_vma=False,
    )
```

time: 158 us -> 109 us (0.69)
  local copies, waits for them, and re-layouts: 31 us -> 0.11 us
  waiting for transfers between devices: 47.3 us -> 29.6 us
  starting transfers between devices: 34 us -> 39.1 us
  Pallas kernels: 39.1 us -> 36 us
    unnamed x18 -> x6, local copies, waits for them, and re-layouts: 30.4 us -> 0.01 us
    ppermute x24 -> x33, waiting for transfers between devices: 47.3 us -> 29.6 us  [over(): return lambda a: lax.ppermute(a, AXES, pairs)]
    pallas_call x7 -> x3, Pallas kernels: 26.8 us -> 17 us  [the longest x1 12.1 us: factor_call(): pl.pallas_call(functools.partial(factor_kernel, line), in_specs=[SMEM_SPE...]
    pallas_call x1, Pallas kernels: 9.66 us -> 16.3 us  [front_call(): pl.pallas_call(functools.partial(front_kernel, 1.0 / math.sqrt(d), 1.0 /...]
    ppermute x24 -> x33, starting transfers between devices: 34 us -> 39.1 us  [over(): return lambda a: lax.ppermute(a, AXES, pairs)]
    add x14 -> x7, other arithmetic: 4.77 us -> 2.74 us  [the longest x2 1.59 us: shards(): a + b]
  transfers between devices with their start and end apart: 24 -> 33, of which waited for: 12 -> 8; matrix products, arithmetic and copies ran while one was open for 3% -> 3% of each run, Pallas kernels for 15% -> 16%
where the time goes in v5:
time: 109 us
  starting transfers between devices  39.1 us (36%)
  Pallas kernels  36 us (33%)
  waiting for transfers between devices  29.6 us (27%)
  other arithmetic  3.43 us (3%)
  between operations  1.13 us (1%)
    ppermute x33, starting transfers between devices, over(): return lambda a: lax.ppermute(a, AXES, pairs)  39.1 us
    ppermute x33, waiting for transfers between devices, over(): return lambda a: lax.ppermute(a, AXES, pairs)  29.6 us
    pallas_call x1, Pallas kernels, front_call(): pl.pallas_call(functools.partial(front_kernel, 1.0 / math.sqrt(d), 1.0 /...  16.3 us
    pallas_call x1, Pallas kernels, factor_call(): pl.pallas_call(functools.partial(factor_kernel, line), in_specs=[SMEM_SPE...  12.1 us
    pallas_call x2, Pallas kernels, project_call(): pl.pallas_call(functools.partial(project_kernel, line, is_own), in_specs=...  4.96 us
    pallas_call x1, Pallas kernels, basis_call(): pl.pallas_call(basis_kernel, grid=(rows // block,), in_specs=[pl.BlockSpe...  2.64 us
  transfers between devices with their start and end apart: 33, of which 8 were waited for; matrix products, arithmetic and copies ran while one was open for 3% of the time, Pallas kernels for 16%

profile of v5, /device:TPU:0, one launch (start us, length us, event | category | flops | bytes accessed | tf_op | source)
XLA Modules:
  0.0 109.3 jit_solution(6424556932527424519)
XLA Ops:
  0.6 0.6 pad_add_fusion.info
  1.2 16.3 %front.1 = (f32[2048,256]{1,0:T(8,128)}, f32[128,256]{1,0:T(8,128)}, f32[128,256]{1,0:T(8,128)}, f32[1280,256]{1,0:T(8,128)}, f32[768,256]{1,0:T(8,128)}, /*index=5*/f32[1280,256]{1,0:T(8,128)}, f32[768,256]{1,0:T(8,128)}) custom-call(s32[3]{0:T(128)} %pad_add_fusion.info, bf16[2048,4096]{1,0:T(8,128)(2,1)} %e.1, s32[4096,256]{1,0:T(8,128)} %signs.1), custom_call_target="tpu_custom_call" | custom-call | flops 8589934592 | bytes 20971520 | tf_op jit(solution)/shard_map/front/pallas_call | solution.py:117
  17.5 0.5 collective-permute-start
  18.1 0.1 collective-permute-start.1
  18.1 0.4 collective-permute-start.2
  18.6 3.7 %collective-permute-done.2 = f32[128,256]{1,0:T(8,128)S(1)} collective-permute-done((f32[128,256]{1,0:T(8,128)}, f32[128,256]{1,0:T(8,128)S(1)}, u32[]{:S(2)}, u32[]{:S(2)}) %collective-permute-start.2) | collective-permute-done | bytes 131104 | tf_op jit(solution)/shard_map/ppermute | solution.py:315
  22.2 0.9 add.73
  23.2 1.4 %slice_add_fusion.4 = (f32[192,256]{1,0:T(8,128)S(1)}, f32[192,256]{1,0:T(8,128)S(1)}, f32[192,256]{1,0:T(8,128)S(1)}, f32[192,256]{1,0:T(8,128)S(1)}) fusion(f32[768,256]{1,0:T(8,128)S(1)} %collective-permute-done.1, f32[768,256]{1,0:T(8,128)} %get-tuple-element.42), kind=kLoop, calls=%fused_computation.12 | loop fusion | flops 196608 | bytes 2359296 | tf_op jit(solution)/shard_map/add | solution.py:345
  24.7 3.0 %collective-permute-start.6 = (f32[224,256]{1,0:T(8,128)S(1)}, f32[224,256]{1,0:T(8,128)S(1)}, u32[]{:S(2)}, u32[]{:S(2)}) collective-permute-start(f32[224,256]{1,0:T(8,128)S(1)} %get-tuple-element.52), channel_id=1, source_target_pairs={{0,8},{1,9},{2,10},{3,11},{4,12},{5,13},{6,14},{7,15},{8,0},{9,1},... | collective-permute-start | bytes 688136 | tf_op jit(solution)/shard_map/ppermute | solution.py:315
  27.7 2.6 %collective-permute-start.7 = (f32[224,256]{1,0:T(8,128)S(1)}, f32[224,256]{1,0:T(8,128)S(1)}, u32[]{:S(2)}, u32[]{:S(2)}) collective-permute-start(f32[224,256]{1,0:T(8,128)S(1)} %get-tuple-element.53), channel_id=1, source_target_pairs={{0,16},{1,17},{2,18},{3,19},{4,20},{5,21},{6,22},{7,23},{8,24},{9,... | collective-permute-start | bytes 688136 | tf_op jit(solution)/shard_map/ppermute | solution.py:315
  30.3 0.2 slice_add_fusion
  30.5 1.8 %collective-permute-start.3 = (f32[320,256]{1,0:T(8,128)S(1)}, f32[320,256]{1,0:T(8,128)S(1)}, u32[]{:S(2)}, u32[]{:S(2)}) collective-permute-start(f32[320,256]{1,0:T(8,128)S(1)} %get-tuple-element.48), channel_id=1, source_target_pairs={{0,2},{1,3},{2,0},{3,1},{4,6},{5,7},{6,4},{7,5},{8,10},{9,11},{10,... | collective-permute-start | bytes 983048 | tf_op jit(solution)/shard_map/ppermute | solution.py:315
  32.3 1.5 %collective-permute-start.4 = (f32[320,256]{1,0:T(8,128)S(1)}, f32[320,256]{1,0:T(8,128)S(1)}, u32[]{:S(2)}, u32[]{:S(2)}) collective-permute-start(f32[320,256]{1,0:T(8,128)S(1)} %get-tuple-element.49), channel_id=1, source_target_pairs={{0,4},{1,5},{2,6},{3,7},{4,0},{5,1},{6,2},{7,3},{8,12},{9,13},{10,... | collective-permute-start | bytes 983048 | tf_op jit(solution)/shard_map/ppermute | solution.py:315
  33.8 4.1 %collective-permute-done.6 = f32[224,256]{1,0:T(8,128)S(1)} collective-permute-done((f32[224,256]{1,0:T(8,128)S(1)}, f32[224,256]{1,0:T(8,128)S(1)}, u32[]{:S(2)}, u32[]{:S(2)}) %collective-permute-start.6) | collective-permute-done | bytes 229408 | tf_op jit(solution)/shard_map/ppermute | solution.py:315
  37.9 2.6 %collective-permute-start.5 = (f32[320,256]{1,0:T(8,128)S(1)}, f32[320,256]{1,0:T(8,128)S(1)}, u32[]{:S(2)}, u32[]{:S(2)}) collective-permute-start(f32[320,256]{1,0:T(8,128)S(1)} %get-tuple-element.50), channel_id=1, source_target_pairs={{0,6},{1,7},{2,4},{3,5},{4,2},{5,3},{6,0},{7,1},{8,14},{9,15},{10,... | collective-permute-start | bytes 983048 | tf_op jit(solution)/shard_map/ppermute | solution.py:315
  40.6 6.4 %collective-permute-done.7 = f32[224,256]{1,0:T(8,128)S(1)} collective-permute-done((f32[224,256]{1,0:T(8,128)S(1)}, f32[224,256]{1,0:T(8,128)S(1)}, u32[]{:S(2)}, u32[]{:S(2)}) %collective-permute-start.7) | collective-permute-done | bytes 229408 | tf_op jit(solution)/shard_map/ppermute | solution.py:315
  47.0 2.5 %collective-permute-start.14 = (f32[224,256]{1,0:T(8,128)S(1)}, f32[224,256]{1,0:T(8,128)S(1)}, u32[]{:S(2)}, u32[]{:S(2)}) collective-permute-start(f32[224,256]{1,0:T(8,128)S(1)} %add_add_fusion.2), channel_id=1, source_target_pairs={{0,6},{1,7},{2,4},{3,5},{4,2},{5,3},{6,0},{7,1},{8,14},{9,15},{10,... | collective-permute-start | bytes 688136 | tf_op jit(solution)/shard_map/ppermute | solution.py:315
  49.5 0.5 collective-permute-start.13
  50.0 0.5 collective-permute-start.12
  50.6 0.1 add_add_fusion
  50.7 4.5 %collective-permute-start.9 = (f32[80,256]{1,0:T(8,128)S(1)}, f32[80,256]{1,0:T(8,128)S(1)}, u32[]{:S(2)}, u32[]{:S(2)}) collective-permute-start(f32[80,256]{1,0:T(8,128)S(1)} %get-tuple-element.56), channel_id=1, source_target_pairs={{0,8},{1,9},{2,10},{3,11},{4,12},{5,13},{6,14},{7,15},{8,0},{9,1},... | collective-permute-start | bytes 245768 | tf_op jit(solution)/shard_map/ppermute | solution.py:315
  55.2 1.1 collective-permute-start.10
  56.3 2.5 %collective-permute-start.11 = (f32[80,256]{1,0:T(8,128)S(1)}, f32[80,256]{1,0:T(8,128)S(1)}, u32[]{:S(2)}, u32[]{:S(2)}) collective-permute-start(f32[80,256]{1,0:T(8,128)S(1)} %get-tuple-element.58), channel_id=1, source_target_pairs={{0,24},{1,25},{2,26},{3,27},{4,28},{5,29},{6,30},{7,31},{8,16},{9,... | collective-permute-start | bytes 245768 | tf_op jit(solution)/shard_map/ppermute | solution.py:315
  58.8 4.1 %collective-permute-done.10 = f32[80,256]{1,0:T(8,128)S(1)} collective-permute-done((f32[80,256]{1,0:T(8,128)S(1)}, f32[80,256]{1,0:T(8,128)S(1)}, u32[]{:S(2)}, u32[]{:S(2)}) %collective-permute-start.10) | collective-permute-done | bytes 81952 | tf_op jit(solution)/shard_map/ppermute | solution.py:315
  63.0 2.2 %collective-permute-start.17 = (f32[112,256]{1,0:T(8,128)S(1)}, f32[112,256]{1,0:T(8,128)S(1)}, u32[]{:S(2)}, u32[]{:S(2)}) collective-permute-start(f32[112,256]{1,0:T(8,128)S(1)} %pad_maximum_fusion.6), channel_id=1, source_target_pairs={{0,24},{1,25},{2,26},{3,27},{4,28},{5,29},{6,30},{7,31},{8,16},{9,... | collective-permute-start | bytes 344072 | tf_op jit(solution)/shard_map/ppermute | solution.py:315
  65.2 3.1 %collective-permute-start.16 = (f32[112,256]{1,0:T(8,128)S(1)}, f32[112,256]{1,0:T(8,128)S(1)}, u32[]{:S(2)}, u32[]{:S(2)}) collective-permute-start(f32[112,256]{1,0:T(8,128)S(1)} %pad_maximum_fusion.6), channel_id=1, source_target_pairs={{0,16},{1,17},{2,18},{3,19},{4,20},{5,21},{6,22},{7,23},{8,24},{9,... | collective-permute-start | bytes 344072 | tf_op jit(solution)/shard_map/ppermute | solution.py:315
  68.3 2.0 %collective-permute-start.24 = (f32[192,256]{1,0:T(8,128)S(1)}, f32[192,256]{1,0:T(8,128)S(1)}, u32[]{:S(2)}, u32[]{:S(2)}) collective-permute-start(f32[192,256]{1,0:T(8,128)S(1)} %slice.159.refs_4_), channel_id=1, source_target_pairs={{0,24},{1,25},{2,26},{3,27},{4,28},{5,29},{6,30},{7,31},{8,16},{9,... | collective-permute-start | bytes 589832 | tf_op jit(solution)/shard_map/ppermute | solution.py:315
  70.3 0.7 collective-permute-done.17
  70.9 10.0 %collective-permute-done.16 = f32[112,256]{1,0:T(8,128)S(1)} collective-permute-done((f32[112,256]{1,0:T(8,128)S(1)}, f32[112,256]{1,0:T(8,128)S(1)}, u32[]{:S(2)}, u32[]{:S(2)}) %collective-permute-start.16) | collective-permute-done | bytes 114720 | tf_op jit(solution)/shard_map/ppermute | solution.py:315
  81.2 0.1 collective-permute-start.23
  81.2 2.3 %collective-permute-start.22 = (f32[192,256]{1,0:T(8,128)S(1)}, f32[192,256]{1,0:T(8,128)S(1)}, u32[]{:S(2)}, u32[]{:S(2)}) collective-permute-start(f32[192,256]{1,0:T(8,128)S(1)} %slice.159.refs_4_), channel_id=1, source_target_pairs={{0,8},{1,9},{2,10},{3,11},{4,12},{5,13},{6,14},{7,15},{8,0},{9,1},... | collective-permute-start | bytes 589832 | tf_op jit(solution)/shard_map/ppermute | solution.py:315
  83.6 2.6 %collective-permute-start.21 = (f32[320,256]{1,0:T(8,128)S(1)}, f32[320,256]{1,0:T(8,128)S(1)}, u32[]{:S(2)}, u32[]{:S(2)}) collective-permute-start(f32[320,256]{1,0:T(8,128)S(1)} %pad_maximum_fusion.refs_0_), channel_id=1, source_target_pairs={{0,6},{1,7},{2,4},{3,5},{4,2},{5,3},{6,0},{7,1},{8,14},{9,15},{10,... | collective-permute-start | bytes 983048 | tf_op jit(solution)/shard_map/ppermute | solution.py:315
  86.2 0.4 collective-permute-start.20
  86.6 0.5 collective-permute-start.19
  87.1 12.1 %factor.1 = (f32[256,256]{1,0:T(8,128)}, bf16[256,256]{1,0:T(8,128)(2,1)S(1)}, bf16[256,256]{1,0:T(8,128)(2,1)S(1)}) custom-call(s32[3]{0:T(128)S(1)} %copy-done.1, f32[128,256]{1,0:T(8,128)S(1)} %pad_maximum_fusion.5.kept, f32[128,256]{1,0:T(8,128)S(1)} %collective-permute-done.18.got), custom_call_target="tpu_custom_call" | custom-call | flops 10000000000 | bytes 524288 | tf_op jit(solution)/shard_map/factor/pallas_call | solution.py:220
  99.2 2.6 %basis.1 = bf16[2048,256]{1,0:T(8,128)(2,1)} custom-call(f32[2048,256]{1,0:T(8,128)S(1)} %copy-done, bf16[256,256]{1,0:T(8,128)(2,1)S(1)} %get-tuple-element.66.high, bf16[256,256]{1,0:T(8,128)(2,1)S(1)} %get-tuple-element.67.low), custom_call_target="tpu_custom_call" | custom-call | flops 805306368 | bytes 3145728 | tf_op jit(solution)/shard_map/basis/pallas_call | solution.py:247
  101.8 0.1 collective-permute-start.29
  101.9 0.5 collective-permute-start.30
  102.4 0.1 collective-permute-start.31
  102.5 0.4 collective-permute-start.25
  102.9 0.1 collective-permute-start.26
  103.0 0.3 collective-permute-done.29.refs_5_
  103.4 0.1 collective-permute-start.27
  103.5 0.1 collective-permute-done.30.refs_6_
  103.6 0.2 collective-permute-start.28
  103.9 0.2 collective-permute-start.32
  104.1 2.5 %project.2.refs_0_ = f32[256,4096]{1,0:T(8,128)} custom-call(s32[3]{0:T(128)S(1)} %copy-done.1, bf16[256,256]{1,0:T(8,128)(2,1)S(1)} %get-tuple-element.66.high, bf16[256,256]{1,0:T(8,128)(2,1)S(1)} %get-tuple-element.67.low, f32[320,256]{1,0:T(8,128)S(1)} %pad_maximum_fusion.refs_0_, f32[320,256]{1,0:T(8,128)S(1)} %collective-permute-done.19.refs_1_, ...), custom_call_target="tpu_custom_call" | custom-call | flops 805306368 | bytes 4194304 | tf_op jit(solution)/shard_map/project/pallas_call | solution.py:292
  106.7 2.5 %project.3 = f32[256,4096]{1,0:T(8,128)} custom-call(s32[3]{0:T(128)S(1)} %copy-done.1, bf16[256,256]{1,0:T(8,128)(2,1)S(1)} %get-tuple-element.66.high, bf16[256,256]{1,0:T(8,128)(2,1)S(1)} %get-tuple-element.67.low, f32[256,4096]{1,0:T(8,128)} %project.2.refs_0_, f32[320,256]{1,0:T(8,128)S(1)} %collective-permute-done.25.refs_1_, ...), custom_call_target="tpu_custom_call", output_to_operand_aliasing={{}: (3, {})} | custom-call | flops 805306368 | bytes 4194304 | tf_op jit(solution)/shard_map/project/pallas_call | solution.py:292
  (54 shorter events, 0.6 us)
Async XLA Ops:
  17.5 12.8 %collective-permute-start = (f32[1280,256]{1,0:T(8,128)}, f32[1280,256]{1,0:T(8,128)S(1)}, u32[]{:S(2)}, u32[]{:S(2)}) collective-permute-start(f32[1280,256]{1,0:T(8,128)} %get-tuple-element.41), channel_id=1, source_target_pairs={{0,1},{1,0},{2,3},{3,2},{4,5},{5,4},{6,7},{7,6},{8,9},{9,8},{10,11... | collective-permute-start | bytes 3932168 | tf_op jit(solution)/shard_map/ppermute | solution.py:315
  18.1 5.1 %collective-permute-start.1 = (f32[768,256]{1,0:T(8,128)}, f32[768,256]{1,0:T(8,128)S(1)}, u32[]{:S(2)}, u32[]{:S(2)}) collective-permute-start(f32[768,256]{1,0:T(8,128)} %get-tuple-element.43), channel_id=1, source_target_pairs={{0,1},{1,0},{2,3},{3,2},{4,5},{5,4},{6,7},{7,6},{8,9},{9,8},{10,11... | collective-permute-start | bytes 2359304 | tf_op jit(solution)/shard_map/ppermute | solution.py:315
  18.1 4.1 %collective-permute-start.2 = (f32[128,256]{1,0:T(8,128)}, f32[128,256]{1,0:T(8,128)S(1)}, u32[]{:S(2)}, u32[]{:S(2)}) collective-permute-start(f32[128,256]{1,0:T(8,128)} %get-tuple-element.45), channel_id=1, source_target_pairs={{0,1},{1,0},{2,3},{3,2},{4,5},{5,4},{6,7},{7,6},{8,9},{9,8},{10,11... | collective-permute-start | bytes 393224 | tf_op jit(solution)/shard_map/ppermute | solution.py:315
  23.2 7.1 %copy-start.2 = (f32[1280,256]{1,0:T(8,128)S(1)}, f32[1280,256]{1,0:T(8,128)}, u32[]{:S(2)}) copy-start(f32[1280,256]{1,0:T(8,128)} %get-tuple-element.40) | copy-start | bytes 3932164
  24.7 13.2 %collective-permute-start.6 = (f32[224,256]{1,0:T(8,128)S(1)}, f32[224,256]{1,0:T(8,128)S(1)}, u32[]{:S(2)}, u32[]{:S(2)}) collective-permute-start(f32[224,256]{1,0:T(8,128)S(1)} %get-tuple-element.52), channel_id=1, source_target_pairs={{0,8},{1,9},{2,10},{3,11},{4,12},{5,13},{6,14},{7,15},{8,0},{9,1},... | collective-permute-start | bytes 688136 | tf_op jit(solution)/shard_map/ppermute | solution.py:315
  27.7 19.2 %collective-permute-start.7 = (f32[224,256]{1,0:T(8,128)S(1)}, f32[224,256]{1,0:T(8,128)S(1)}, u32[]{:S(2)}, u32[]{:S(2)}) collective-permute-start(f32[224,256]{1,0:T(8,128)S(1)} %get-tuple-element.53), channel_id=1, source_target_pairs={{0,16},{1,17},{2,18},{3,19},{4,20},{5,21},{6,22},{7,23},{8,24},{9,... | collective-permute-start | bytes 688136 | tf_op jit(solution)/shard_map/ppermute | solution.py:315
  30.3 16.6 %collective-permute-start.8 = (f32[224,256]{1,0:T(8,128)S(1)}, f32[224,256]{1,0:T(8,128)S(1)}, u32[]{:S(2)}, u32[]{:S(2)}) collective-permute-start(f32[224,256]{1,0:T(8,128)S(1)} %get-tuple-element.46), channel_id=1, source_target_pairs={{0,24},{1,25},{2,26},{3,27},{4,28},{5,29},{6,30},{7,31},{8,16},{9,... | collective-permute-start | bytes 688136 | tf_op jit(solution)/shard_map/ppermute | solution.py:315
  30.5 19.5 %collective-permute-start.3 = (f32[320,256]{1,0:T(8,128)S(1)}, f32[320,256]{1,0:T(8,128)S(1)}, u32[]{:S(2)}, u32[]{:S(2)}) collective-permute-start(f32[320,256]{1,0:T(8,128)S(1)} %get-tuple-element.48), channel_id=1, source_target_pairs={{0,2},{1,3},{2,0},{3,1},{4,6},{5,7},{6,4},{7,5},{8,10},{9,11},{10,... | collective-permute-start | bytes 983048 | tf_op jit(solution)/shard_map/ppermute | solution.py:315
  32.3 18.3 %collective-permute-start.4 = (f32[320,256]{1,0:T(8,128)S(1)}, f32[320,256]{1,0:T(8,128)S(1)}, u32[]{:S(2)}, u32[]{:S(2)}) collective-permute-start(f32[320,256]{1,0:T(8,128)S(1)} %get-tuple-element.49), channel_id=1, source_target_pairs={{0,4},{1,5},{2,6},{3,7},{4,0},{5,1},{6,2},{7,3},{8,12},{9,13},{10,... | collective-permute-start | bytes 983048 | tf_op jit(solution)/shard_map/ppermute | solution.py:315
  37.9 12.6 %collective-permute-start.5 = (f32[320,256]{1,0:T(8,128)S(1)}, f32[320,256]{1,0:T(8,128)S(1)}, u32[]{:S(2)}, u32[]{:S(2)}) collective-permute-start(f32[320,256]{1,0:T(8,128)S(1)} %get-tuple-element.50), channel_id=1, source_target_pairs={{0,6},{1,7},{2,4},{3,5},{4,2},{5,3},{6,0},{7,1},{8,14},{9,15},{10,... | collective-permute-start | bytes 983048 | tf_op jit(solution)/shard_map/ppermute | solution.py:315
  47.0 9.3 %collective-permute-start.14 = (f32[224,256]{1,0:T(8,128)S(1)}, f32[224,256]{1,0:T(8,128)S(1)}, u32[]{:S(2)}, u32[]{:S(2)}) collective-permute-start(f32[224,256]{1,0:T(8,128)S(1)} %add_add_fusion.2), channel_id=1, source_target_pairs={{0,6},{1,7},{2,4},{3,5},{4,2},{5,3},{6,0},{7,1},{8,14},{9,15},{10,... | collective-permute-start | bytes 688136 | tf_op jit(solution)/shard_map/ppermute | solution.py:315
  49.5 9.2 %collective-permute-start.13 = (f32[224,256]{1,0:T(8,128)S(1)}, f32[224,256]{1,0:T(8,128)S(1)}, u32[]{:S(2)}, u32[]{:S(2)}) collective-permute-start(f32[224,256]{1,0:T(8,128)S(1)} %add_add_fusion.2), channel_id=1, source_target_pairs={{0,4},{1,5},{2,6},{3,7},{4,0},{5,1},{6,2},{7,3},{8,12},{9,13},{10,... | collective-permute-start | bytes 688136 | tf_op jit(solution)/shard_map/ppermute | solution.py:315
  50.0 8.7 %collective-permute-start.12 = (f32[224,256]{1,0:T(8,128)S(1)}, f32[224,256]{1,0:T(8,128)S(1)}, u32[]{:S(2)}, u32[]{:S(2)}) collective-permute-start(f32[224,256]{1,0:T(8,128)S(1)} %add_add_fusion.2), channel_id=1, source_target_pairs={{0,2},{1,3},{2,0},{3,1},{4,6},{5,7},{6,4},{7,5},{8,10},{9,11},{10,... | collective-permute-start | bytes 688136 | tf_op jit(solution)/shard_map/ppermute | solution.py:315
  50.7 36.4 %copy-start.1 = (s32[3]{0:T(128)S(1)}, s32[3]{0:T(128)}, u32[]{:S(2)}) copy-start(s32[3]{0:T(128)} %pad_add_fusion.info) | copy-start | bytes 40
  50.7 8.1 %collective-permute-start.9 = (f32[80,256]{1,0:T(8,128)S(1)}, f32[80,256]{1,0:T(8,128)S(1)}, u32[]{:S(2)}, u32[]{:S(2)}) collective-permute-start(f32[80,256]{1,0:T(8,128)S(1)} %get-tuple-element.56), channel_id=1, source_target_pairs={{0,8},{1,9},{2,10},{3,11},{4,12},{5,13},{6,14},{7,15},{8,0},{9,1},... | collective-permute-start | bytes 245768 | tf_op jit(solution)/shard_map/ppermute | solution.py:315
  55.2 7.8 %collective-permute-start.10 = (f32[80,256]{1,0:T(8,128)S(1)}, f32[80,256]{1,0:T(8,128)S(1)}, u32[]{:S(2)}, u32[]{:S(2)}) collective-permute-start(f32[80,256]{1,0:T(8,128)S(1)} %get-tuple-element.57), channel_id=1, source_target_pairs={{0,16},{1,17},{2,18},{3,19},{4,20},{5,21},{6,22},{7,23},{8,24},{9,... | collective-permute-start | bytes 245768 | tf_op jit(solution)/shard_map/ppermute | solution.py:315
  56.3 6.7 %collective-permute-start.11 = (f32[80,256]{1,0:T(8,128)S(1)}, f32[80,256]{1,0:T(8,128)S(1)}, u32[]{:S(2)}, u32[]{:S(2)}) collective-permute-start(f32[80,256]{1,0:T(8,128)S(1)} %get-tuple-element.58), channel_id=1, source_target_pairs={{0,24},{1,25},{2,26},{3,27},{4,28},{5,29},{6,30},{7,31},{8,16},{9,... | collective-permute-start | bytes 245768 | tf_op jit(solution)/shard_map/ppermute | solution.py:315
  63.0 7.9 %collective-permute-start.17 = (f32[112,256]{1,0:T(8,128)S(1)}, f32[112,256]{1,0:T(8,128)S(1)}, u32[]{:S(2)}, u32[]{:S(2)}) collective-permute-start(f32[112,256]{1,0:T(8,128)S(1)} %pad_maximum_fusion.6), channel_id=1, source_target_pairs={{0,24},{1,25},{2,26},{3,27},{4,28},{5,29},{6,30},{7,31},{8,16},{9,... | collective-permute-start | bytes 344072 | tf_op jit(solution)/shard_map/ppermute | solution.py:315
  65.2 15.8 %collective-permute-start.16 = (f32[112,256]{1,0:T(8,128)S(1)}, f32[112,256]{1,0:T(8,128)S(1)}, u32[]{:S(2)}, u32[]{:S(2)}) collective-permute-start(f32[112,256]{1,0:T(8,128)S(1)} %pad_maximum_fusion.6), channel_id=1, source_target_pairs={{0,16},{1,17},{2,18},{3,19},{4,20},{5,21},{6,22},{7,23},{8,24},{9,... | collective-permute-start | bytes 344072 | tf_op jit(solution)/shard_map/ppermute | solution.py:315
  68.2 12.7 %collective-permute-start.15 = (f32[112,256]{1,0:T(8,128)S(1)}, f32[112,256]{1,0:T(8,128)S(1)}, u32[]{:S(2)}, u32[]{:S(2)}) collective-permute-start(f32[112,256]{1,0:T(8,128)S(1)} %pad_maximum_fusion.6), channel_id=1, source_target_pairs={{0,8},{1,9},{2,10},{3,11},{4,12},{5,13},{6,14},{7,15},{8,0},{9,1},... | collective-permute-start | bytes 344072 | tf_op jit(solution)/shard_map/ppermute | solution.py:315
  68.3 18.0 %collective-permute-start.24 = (f32[192,256]{1,0:T(8,128)S(1)}, f32[192,256]{1,0:T(8,128)S(1)}, u32[]{:S(2)}, u32[]{:S(2)}) collective-permute-start(f32[192,256]{1,0:T(8,128)S(1)} %slice.159.refs_4_), channel_id=1, source_target_pairs={{0,24},{1,25},{2,26},{3,27},{4,28},{5,29},{6,30},{7,31},{8,16},{9,... | collective-permute-start | bytes 589832 | tf_op jit(solution)/shard_map/ppermute | solution.py:315
  81.1 18.1 %copy-start = (f32[2048,256]{1,0:T(8,128)S(1)}, f32[2048,256]{1,0:T(8,128)}, u32[]{:S(2)}) copy-start(f32[2048,256]{1,0:T(8,128)} %get-tuple-element.64.sketch) | copy-start | bytes 6291460
  81.1 5.5 %collective-permute-start.18 = (f32[128,256]{1,0:T(8,128)S(1)}, f32[128,256]{1,0:T(8,128)S(1)}, u32[]{:S(2)}, u32[]{:S(2)}) collective-permute-start(f32[128,256]{1,0:T(8,128)S(1)} %pad_maximum_fusion.5.kept), channel_id=1, source_target_pairs={{0,1},{1,0},{2,3},{3,2},{4,5},{5,4},{6,7},{7,6},{8,9},{9,8},{10,11... | collective-permute-start | bytes 393224 | tf_op jit(solution)/shard_map/ppermute | solution.py:315
  81.2 20.7 %collective-permute-start.23 = (f32[192,256]{1,0:T(8,128)S(1)}, f32[192,256]{1,0:T(8,128)S(1)}, u32[]{:S(2)}, u32[]{:S(2)}) collective-permute-start(f32[192,256]{1,0:T(8,128)S(1)} %slice.159.refs_4_), channel_id=1, source_target_pairs={{0,16},{1,17},{2,18},{3,19},{4,20},{5,21},{6,22},{7,23},{8,24},{9,... | collective-permute-start | bytes 589832 | tf_op jit(solution)/shard_map/ppermute | solution.py:315
  81.2 20.6 %collective-permute-start.22 = (f32[192,256]{1,0:T(8,128)S(1)}, f32[192,256]{1,0:T(8,128)S(1)}, u32[]{:S(2)}, u32[]{:S(2)}) collective-permute-start(f32[192,256]{1,0:T(8,128)S(1)} %slice.159.refs_4_), channel_id=1, source_target_pairs={{0,8},{1,9},{2,10},{3,11},{4,12},{5,13},{6,14},{7,15},{8,0},{9,1},... | collective-permute-start | bytes 589832 | tf_op jit(solution)/shard_map/ppermute | solution.py:315
  83.6 18.2 %collective-permute-start.21 = (f32[320,256]{1,0:T(8,128)S(1)}, f32[320,256]{1,0:T(8,128)S(1)}, u32[]{:S(2)}, u32[]{:S(2)}) collective-permute-start(f32[320,256]{1,0:T(8,128)S(1)} %pad_maximum_fusion.refs_0_), channel_id=1, source_target_pairs={{0,6},{1,7},{2,4},{3,5},{4,2},{5,3},{6,0},{7,1},{8,14},{9,15},{10,... | collective-permute-start | bytes 983048 | tf_op jit(solution)/shard_map/ppermute | solution.py:315
  86.2 15.6 %collective-permute-start.20 = (f32[320,256]{1,0:T(8,128)S(1)}, f32[320,256]{1,0:T(8,128)S(1)}, u32[]{:S(2)}, u32[]{:S(2)}) collective-permute-start(f32[320,256]{1,0:T(8,128)S(1)} %pad_maximum_fusion.refs_0_), channel_id=1, source_target_pairs={{0,4},{1,5},{2,6},{3,7},{4,0},{5,1},{6,2},{7,3},{8,12},{9,13},{10,... | collective-permute-start | bytes 983048 | tf_op jit(solution)/shard_map/ppermute | solution.py:315
  86.6 15.2 %collective-permute-start.19 = (f32[320,256]{1,0:T(8,128)S(1)}, f32[320,256]{1,0:T(8,128)S(1)}, u32[]{:S(2)}, u32[]{:S(2)}) collective-permute-start(f32[320,256]{1,0:T(8,128)S(1)} %pad_maximum_fusion.refs_0_), channel_id=1, source_target_pairs={{0,2},{1,3},{2,0},{3,1},{4,6},{5,7},{6,4},{7,5},{8,10},{9,11},{10,... | collective-permute-start | bytes 983048 | tf_op jit(solution)/shard_map/ppermute | solution.py:315
  101.8 1.5 %collective-permute-start.29 = (f32[192,256]{1,0:T(8,128)S(1)}, f32[192,256]{1,0:T(8,128)S(1)}, u32[]{:S(2)}, u32[]{:S(2)}) collective-permute-start(f32[192,256]{1,0:T(8,128)S(1)} %slice.159.refs_4_), channel_id=1, source_target_pairs={{0,1},{1,0},{2,3},{3,2},{4,5},{5,4},{6,7},{7,6},{8,9},{9,8},{10,11... | collective-permute-start | bytes 589832 | tf_op jit(solution)/shard_map/ppermute | solution.py:315
  101.9 1.7 %collective-permute-start.30 = (f32[192,256]{1,0:T(8,128)S(1)}, f32[192,256]{1,0:T(8,128)S(1)}, u32[]{:S(2)}, u32[]{:S(2)}) collective-permute-start(f32[192,256]{1,0:T(8,128)S(1)} %collective-permute-done.22.refs_5_), channel_id=1, source_target_pairs={{0,1},{1,0},{2,3},{3,2},{4,5},{5,4},{6,7},{7,6},{8,9},{9,8},{10,11... | collective-permute-start | bytes 589832 | tf_op jit(solution)/shard_map/ppermute | solution.py:315
  102.4 1.5 %collective-permute-start.31 = (f32[192,256]{1,0:T(8,128)S(1)}, f32[192,256]{1,0:T(8,128)S(1)}, u32[]{:S(2)}, u32[]{:S(2)}) collective-permute-start(f32[192,256]{1,0:T(8,128)S(1)} %collective-permute-done.23.refs_6_), channel_id=1, source_target_pairs={{0,1},{1,0},{2,3},{3,2},{4,5},{5,4},{6,7},{7,6},{8,9},{9,8},{10,11... | collective-permute-start | bytes 589832 | tf_op jit(solution)/shard_map/ppermute | solution.py:315
  102.5 4.1 %collective-permute-start.25 = (f32[320,256]{1,0:T(8,128)S(1)}, f32[320,256]{1,0:T(8,128)S(1)}, u32[]{:S(2)}, u32[]{:S(2)}) collective-permute-start(f32[320,256]{1,0:T(8,128)S(1)} %pad_maximum_fusion.refs_0_), channel_id=1, source_target_pairs={{0,1},{1,0},{2,3},{3,2},{4,5},{5,4},{6,7},{7,6},{8,9},{9,8},{10,11... | collective-permute-start | bytes 983048 | tf_op jit(solution)/shard_map/ppermute | solution.py:315
  102.9 3.7 %collective-permute-start.26 = (f32[320,256]{1,0:T(8,128)S(1)}, f32[320,256]{1,0:T(8,128)S(1)}, u32[]{:S(2)}, u32[]{:S(2)}) collective-permute-start(f32[320,256]{1,0:T(8,128)S(1)} %collective-permute-done.19.refs_1_), channel_id=1, source_target_pairs={{0,1},{1,0},{2,3},{3,2},{4,5},{5,4},{6,7},{7,6},{8,9},{9,8},{10,11... | collective-permute-start | bytes 983048 | tf_op jit(solution)/shard_map/ppermute | solution.py:315
  103.4 3.3 %collective-permute-start.27 = (f32[320,256]{1,0:T(8,128)S(1)}, f32[320,256]{1,0:T(8,128)S(1)}, u32[]{:S(2)}, u32[]{:S(2)}) collective-permute-start(f32[320,256]{1,0:T(8,128)S(1)} %collective-permute-done.20.refs_2_), channel_id=1, source_target_pairs={{0,1},{1,0},{2,3},{3,2},{4,5},{5,4},{6,7},{7,6},{8,9},{9,8},{10,11... | collective-permute-start | bytes 983048 | tf_op jit(solution)/shard_map/ppermute | solution.py:315
  103.6 3.0 %collective-permute-start.28 = (f32[320,256]{1,0:T(8,128)S(1)}, f32[320,256]{1,0:T(8,128)S(1)}, u32[]{:S(2)}, u32[]{:S(2)}) collective-permute-start(f32[320,256]{1,0:T(8,128)S(1)} %collective-permute-done.21.refs_3_), channel_id=1, source_target_pairs={{0,1},{1,0},{2,3},{3,2},{4,5},{5,4},{6,7},{7,6},{8,9},{9,8},{10,11... | collective-permute-start | bytes 983048 | tf_op jit(solution)/shard_map/ppermute | solution.py:315
  103.9 2.7 %collective-permute-start.32 = (f32[192,256]{1,0:T(8,128)S(1)}, f32[192,256]{1,0:T(8,128)S(1)}, u32[]{:S(2)}, u32[]{:S(2)}) collective-permute-start(f32[192,256]{1,0:T(8,128)S(1)} %collective-permute-done.24.refs_7_), channel_id=1, source_target_pairs={{0,1},{1,0},{2,3},{3,2},{4,5},{5,4},{6,7},{7,6},{8,9},{9,8},{10,11... | collective-permute-start | bytes 589832 | tf_op jit(solution)/shard_map/ppermute | solution.py:315

commit v6 on v5

--- a/solution.py
+++ b/solution.py
@@ -10,7 +10,7 @@
 
 AXES = ("gx", "gy")
 MIB = 1 << 20
-LINE_FIRST = 0.375
+LINE_FIRST = 0.25
 
 
 def dot(a, b, dims=((1,), (0,))):
@@ -94,14 +94,16 @@
                 for h in range(2):
                     part = value[:, h * width // 2 : (h + 1) * width // 2]
                     to1 = pl.multiple_of(p * 2 * rows1 + (2 * to + h) * size1, 8)
-                    class1[r, pl.ds(to1, size1), :] = part[g * size1 : (g + 1) * size1]
+                    (class1, kept1)[r][pl.ds(to1, size1), :] = part[g * size1 : (g + 1) * size1]
                     to2 = pl.multiple_of(((to * PLANE + (in_plane ^ p)) * 2 + h) * size2, 8)
-                    class2[r, pl.ds(to2, size2), :] = part[rows1 + g * size2 : rows1 + (g + 1) * size2]
-            at = pl.ds(p * 2 * rows1, 2 * rows1)
-            outs.append(pltpu.make_async_copy(class1.at[r, at], (sent1, kept1)[r].at[at], out_sem.at[1 + r * PLANE + p]))
+                    (class2, kept2)[r][pl.ds(to2, size2), :] = part[rows1 + g * size2 : rows1 + (g + 1) * size2]
+            if r == 0:
+                at = pl.ds(p * 2 * rows1, 2 * rows1)
+                outs.append(pltpu.make_async_copy(class1.at[at], sent1.at[at], out_sem.at[1 + p]))
+                outs[-1].start()
+        if r == 0:
+            outs.append(pltpu.make_async_copy(class2, sent2, out_sem.at[1 + PLANE]))
             outs[-1].start()
-        outs.append(pltpu.make_async_copy(class2.at[r], (sent2, kept2)[r], out_sem.at[1 + 2 * PLANE + r]))
-        outs[-1].start()
     for copy in outs:
         copy.wait()
 
@@ -117,8 +119,11 @@
     return pl.pallas_call(
         functools.partial(front_kernel, 1.0 / math.sqrt(d), 1.0 / rows_all, 1.0 / math.sqrt(rows_all), line),
         in_specs=[SMEM_SPEC, ANY_SPEC, ANY_SPEC],
-        out_specs=[ANY_SPEC] + [VMEM_SPEC] * 2 + [ANY_SPEC] * 4,
-        out_shape=[f32(rows, k), f32(k // 2, k), f32(k // 2, k)] + [f32(*c) for c in classes] * 2,
+        out_specs=[ANY_SPEC] + [VMEM_SPEC] * 2 + [ANY_SPEC] * 2 + [VMEM_SPEC] * 2,
+        out_shape=[f32(rows, k)]
+        + [pltpu.VMEM((k // 2, k), jnp.float32)] * 2
+        + [f32(*c) for c in classes]
+        + [pltpu.VMEM(c, jnp.float32) for c in classes],
         scratch_shapes=[
             pltpu.VMEM((rows, d), e.dtype),
             pltpu.VMEM((rows, k), jnp.float32),
@@ -126,12 +131,12 @@
             pltpu.VMEM((d, k), jnp.int32),
             pltpu.VMEM((d, k), jnp.bfloat16),
             pltpu.VMEM((k, k), jnp.float32),
-            pltpu.VMEM((2, *classes[0]), jnp.float32),
-            pltpu.VMEM((2, *classes[1]), jnp.float32),
+            pltpu.VMEM(classes[0], jnp.float32),
+            pltpu.VMEM(classes[1], jnp.float32),
             pltpu.SemaphoreType.DMA((copies + 1,)),
-            pltpu.SemaphoreType.DMA((3 + 2 * PLANE,)),
+            pltpu.SemaphoreType.DMA((2 + PLANE,)),
         ],
-        compiler_params=pltpu.CompilerParams(vmem_limit_bytes=56 * MIB),
+        compiler_params=pltpu.CompilerParams(vmem_limit_bytes=48 * MIB),
         cost_estimate=pl.CostEstimate(flops=4 * rows * d * k, bytes_accessed=rows * d * 2 + d * k * 4, transcendentals=0),
         name="front",
     )(info, e, pltpu.with_memory_space_constraint(signs, pltpu.HBM))
@@ -258,7 +263,7 @@
 
 def project_kernel(line, is_own, info, high, low, *refs):
     *blocks, out, whole, value, sem = refs
-    class1, class2 = blocks[-(PLANE + line) : -line], blocks[-line:]
+    class1, class2 = blocks[-PLANE - 1 : -1], blocks[-1]
     k = high.shape[0]
     rows1, rows2 = row_classes(k, line)
     size1, size2 = rows1 // line, rows2 // line
@@ -274,8 +279,8 @@
                 to1 = pl.ds(pl.multiple_of(to * size1, 8), size1)
                 whole[p, to1, cols] = class1[p][(2 * g + h) * size1 : (2 * g + h + 1) * size1, :]
                 to2 = pl.ds(pl.multiple_of(rows1 + to * size2, 8), size2)
-                at2 = pl.ds(pl.multiple_of(((in_plane ^ p) * 2 + h) * size2, 8), size2)
-                whole[p, to2, cols] = class2[g][at2, :]
+                at2 = pl.ds(pl.multiple_of(((g * PLANE + (in_plane ^ p)) * 2 + h) * size2, 8), size2)
+                whole[p, to2, cols] = class2[at2, :]
         c_high, c_low = split(whole[p])
         value[p] = dot(high[...], c_high) + (dot(high[...], c_low) + dot(low[...], c_high))
         at = pl.ds(pl.multiple_of((region * PLANE + (in_plane ^ p)) * width, width), width)
@@ -340,34 +345,37 @@
             return arrays if len(arrays) > 1 else arrays[0]
 
         sketch, gram_sent, gram, sent1, sent2, kept1, kept2 = front_call(info, e, signs, rows_all, line)
-        got2, gram_got, got1 = with_pair(sent2), with_pair(gram_sent), with_pair(sent1)
+        got1, got2, gram_got = with_pair(sent1), with_pair(sent2), with_pair(gram_sent)
+        parts1 = in_turn(*[a + b for a, b in zip(parts_of(kept1, PLANE), parts_of(got1, PLANE))])
+        from_plane = [over_plane[g](parts1[g]) for g in range(1, PLANE)]
         grams = parts_of(gram + gram_got, line)
         parts2 = [join(a + b, g) for a, b, g in zip(parts_of(kept2, line), parts_of(got2, line), grams)]
         parts2 = in_turn(*parts2)
         from_line = [over_line[g](parts2[g]) for g in range(1, line)]
-        parts1 = in_turn(*[a + b for a, b in zip(parts_of(kept1, PLANE), parts_of(got1, PLANE))])
-        from_plane = [over_plane[g](parts1[g]) for g in range(1, PLANE)]
-        a2 = in_turn(sum(from_line, parts2[0]))
-        whole2 = [over_plane[g](a2) for g in range(1, PLANE)]
+        a2 = sum(from_line, parts2[0])
         parts1 = in_turn(*parts_of(sum(from_plane, parts1[0]), line))
         from_line = [over_line[g](parts1[g]) for g in range(1, line)]
+        a2 = in_turn(a2)
+        whole2 = [over_plane[g](a2) for g in range(1, PLANE)]
         a2 = (a2 + whole2[0]) + (whole2[1] + whole2[2])
         n2 = a2.shape[0] - gram.shape[0] // line
         a1 = in_turn(join(sum(from_line, parts1[0]), a2[n2:]))
         n1 = a1.shape[0] - gram.shape[0] // line
-        from_line = [over_line[g](a1) for g in range(1, line)]
+        gathered = [a1] + [over_line[g](a1) for g in range(1, line)]
         a2 = in_turn(a2[:n2])
-        class2 = [a2] + [over_line[g](a2) for g in range(1, line)]
-        gathered = [a1, *from_line]
+        near = over_line[1](a2)
         a1 = in_turn(join(*[a[:n1] for a in gathered]))
         class1 = [a1] + [over_plane[g](a1) for g in range(1, PLANE)]
         gram = in_turn(join(*[a[n1:] for a in gathered]))
-        triangle, high, low = factor_call(line, info, gram, with_pair(gram))
+        gram_got = with_pair(gram)
+        gram_got, a2_later = in_turn(gram_got, a2)
+        class2 = [a2, near] + [over_line[g](a2_later) for g in range(2, line)]
+        triangle, high, low = factor_call(line, info, in_turn(gram), gram_got)
         high = in_turn(high)
-        basis = in_turn(basis_call(sketch, high, low))
-        ours = in_turn(*class1, *class2)
-        theirs = [with_pair(a) for a in ours]
-        projected = project_call(line, True, info, high, low, ours, d, None)
+        *class1, class2 = in_turn(*class1, join(*class2))
+        theirs = [with_pair(a) for a in (*class1, class2)]
+        basis = in_turn(basis_call(in_turn(sketch), high, low))
+        projected = project_call(line, True, info, high, low, [*class1, class2], d, None)
         projected = project_call(line, False, info, high, low, theirs, d, projected)
         return triangle, basis, projected
 

time: 109 us -> 100 us (0.917)
  starting transfers between devices: 39.1 us -> 35.2 us
  waiting for transfers between devices: 29.6 us -> 27 us
  other arithmetic: 3.43 us -> 0.84 us
    ppermute x33 -> x30, starting transfers between devices: 39.1 us -> 35.2 us  [over(): return lambda a: lax.ppermute(a, AXES, pairs)]
    ppermute x33 -> x30, waiting for transfers between devices: 29.6 us -> 27 us  [over(): return lambda a: lax.ppermute(a, AXES, pairs)]
    add x2, other arithmetic: 1.59 us -> 0.4 us  [shards(): a + b]
  transfers between devices with their start and end apart: 33 -> 30, of which waited for: 8 -> 10; matrix products, arithmetic and copies ran while one was open for 3% -> 1% of each run, Pallas kernels for 16% -> 17%
where the time goes in v6:
time: 100 us; the launch traced here: 99.8 us
  Pallas kernels  35.6 us (36%)
  starting transfers between devices  35.2 us (35%)
  waiting for transfers between devices  27 us (27%)
  between operations  1.08 us (1%)
    ppermute x30, starting transfers between devices, over(): return lambda a: lax.ppermute(a, AXES, pairs)  35.2 us
    ppermute x30, waiting for transfers between devices, over(): return lambda a: lax.ppermute(a, AXES, pairs)  27 us
    pallas_call x1, Pallas kernels, front_call(): pl.pallas_call(functools.partial(front_kernel, 1.0 / math.sqrt(d), 1.0 /...  16.1 us
    pallas_call x1, Pallas kernels, factor_call(): pl.pallas_call(functools.partial(factor_kernel, line), in_specs=[SMEM_SPE...  11.9 us
    pallas_call x2, Pallas kernels, project_call(): pl.pallas_call(functools.partial(project_kernel, line, is_own), in_specs=...  4.93 us
    pallas_call x1, Pallas kernels, basis_call(): pl.pallas_call(basis_kernel, grid=(rows // block,), in_specs=[pl.BlockSpe...  2.64 us
  transfers between devices with their start and end apart: 30, of which 10 were waited for; matrix products, arithmetic and copies ran while one was open for 1% of the time, Pallas kernels for 17%

profile of v6, /device:TPU:0, one launch (start us, length us, event | category | flops | bytes accessed | tf_op | source)
XLA Modules:
  0.0 99.8 jit_solution(10879412975381086835)
XLA Ops:
  0.6 0.1 pad_add_fusion.info
  0.7 16.1 %front.1 = (f32[2048,256]{1,0:T(8,128)}, f32[128,256]{1,0:T(8,128)S(1)}, f32[128,256]{1,0:T(8,128)S(1)}, f32[1536,256]{1,0:T(8,128)S(1)}, f32[512,256]{1,0:T(8,1...) custom-call(s32[3]{0:T(128)S(1)} %pad_add_fusion.info, bf16[2048,4096]{1,0:T(8,128)(2,1)} %e.1, s32[4096,256]{1,0:T(8,128)} %signs.1), custom_call_target="tpu_custom_call" | custom-call | flops 8589934592 | bytes 20971520 | tf_op jit(solution)/shard_map/front/pallas_call | solution.py:119
  16.8 0.5 collective-permute-start
  17.3 0.1 collective-permute-start.5
  17.4 0.4 collective-permute-start.4
  17.8 2.7 %collective-permute-done.5 = f32[128,256]{1,0:T(8,128)S(1)} collective-permute-done((f32[128,256]{1,0:T(8,128)S(1)}, f32[128,256]{1,0:T(8,128)S(1)}, u32[]{:S(2)}, u32[]{:S(2)}) %collective-permute-start.5) | collective-permute-done | bytes 131104 | tf_op jit(solution)/shard_map/ppermute | solution.py:320
  20.6 0.3 slice_add_fusion
  20.9 2.9 %collective-permute-start.1 = (f32[384,256]{1,0:T(8,128)S(1)}, f32[384,256]{1,0:T(8,128)S(1)}, u32[]{:S(2)}, u32[]{:S(2)}) collective-permute-start(f32[384,256]{1,0:T(8,128)S(1)} %get-tuple-element.44), channel_id=1, source_target_pairs={{0,2},{1,3},{2,0},{3,1},{4,6},{5,7},{6,4},{7,5},{8,10},{9,11},{10,... | collective-permute-start | bytes 1179656 | tf_op jit(solution)/shard_map/ppermute | solution.py:320
  23.8 1.5 %collective-permute-start.2 = (f32[384,256]{1,0:T(8,128)S(1)}, f32[384,256]{1,0:T(8,128)S(1)}, u32[]{:S(2)}, u32[]{:S(2)}) collective-permute-start(f32[384,256]{1,0:T(8,128)S(1)} %get-tuple-element.45), channel_id=1, source_target_pairs={{0,4},{1,5},{2,6},{3,7},{4,0},{5,1},{6,2},{7,3},{8,12},{9,13},{10,... | collective-permute-start | bytes 1179656 | tf_op jit(solution)/shard_map/ppermute | solution.py:320
  25.4 0.0 collective-permute-start.3
  25.4 0.1 slice_add_fusion.4
  25.6 2.1 %collective-permute-start.9 = (f32[160,256]{1,0:T(8,128)S(1)}, f32[160,256]{1,0:T(8,128)S(1)}, u32[]{:S(2)}, u32[]{:S(2)}) collective-permute-start(f32[160,256]{1,0:T(8,128)S(1)} %get-tuple-element.57), channel_id=1, source_target_pairs={{0,8},{1,9},{2,10},{3,11},{4,12},{5,13},{6,14},{7,15},{8,0},{9,1},... | collective-permute-start | bytes 491528 | tf_op jit(solution)/shard_map/ppermute | solution.py:320
  27.6 2.6 %collective-permute-start.10 = (f32[160,256]{1,0:T(8,128)S(1)}, f32[160,256]{1,0:T(8,128)S(1)}, u32[]{:S(2)}, u32[]{:S(2)}) collective-permute-start(f32[160,256]{1,0:T(8,128)S(1)} %get-tuple-element.58), channel_id=1, source_target_pairs={{0,16},{1,17},{2,18},{3,19},{4,20},{5,21},{6,22},{7,23},{8,24},{9,... | collective-permute-start | bytes 491528 | tf_op jit(solution)/shard_map/ppermute | solution.py:320
  30.2 3.5 %collective-permute-done.1 = f32[384,256]{1,0:T(8,128)S(1)} collective-permute-done((f32[384,256]{1,0:T(8,128)S(1)}, f32[384,256]{1,0:T(8,128)S(1)}, u32[]{:S(2)}, u32[]{:S(2)}) %collective-permute-start.1) | collective-permute-done | bytes 393248 | tf_op jit(solution)/shard_map/ppermute | solution.py:320
  33.7 4.2 %collective-permute-start.11 = (f32[160,256]{1,0:T(8,128)S(1)}, f32[160,256]{1,0:T(8,128)S(1)}, u32[]{:S(2)}, u32[]{:S(2)}) collective-permute-start(f32[160,256]{1,0:T(8,128)S(1)} %get-tuple-element.51), channel_id=1, source_target_pairs={{0,24},{1,25},{2,26},{3,27},{4,28},{5,29},{6,30},{7,31},{8,16},{9,... | collective-permute-start | bytes 491528 | tf_op jit(solution)/shard_map/ppermute | solution.py:320
  37.9 5.2 %collective-permute-done.2 = f32[384,256]{1,0:T(8,128)S(1)} collective-permute-done((f32[384,256]{1,0:T(8,128)S(1)}, f32[384,256]{1,0:T(8,128)S(1)}, u32[]{:S(2)}, u32[]{:S(2)}) %collective-permute-start.2) | collective-permute-done | bytes 393248 | tf_op jit(solution)/shard_map/ppermute | solution.py:320
  43.2 0.1 add_add_fusion
  43.3 1.6 %collective-permute-start.6 = (f32[96,256]{1,0:T(8,128)S(1)}, f32[96,256]{1,0:T(8,128)S(1)}, u32[]{:S(2)}, u32[]{:S(2)}) collective-permute-start(f32[96,256]{1,0:T(8,128)S(1)} %get-tuple-element.53), channel_id=1, source_target_pairs={{0,8},{1,9},{2,10},{3,11},{4,12},{5,13},{6,14},{7,15},{8,0},{9,1},... | collective-permute-start | bytes 294920 | tf_op jit(solution)/shard_map/ppermute | solution.py:320
  44.9 2.6 %collective-permute-start.7 = (f32[96,256]{1,0:T(8,128)S(1)}, f32[96,256]{1,0:T(8,128)S(1)}, u32[]{:S(2)}, u32[]{:S(2)}) collective-permute-start(f32[96,256]{1,0:T(8,128)S(1)} %get-tuple-element.54), channel_id=1, source_target_pairs={{0,16},{1,17},{2,18},{3,19},{4,20},{5,21},{6,22},{7,23},{8,24},{9,... | collective-permute-start | bytes 294920 | tf_op jit(solution)/shard_map/ppermute | solution.py:320
  47.5 0.2 collective-permute-start.8
  47.8 1.5 %collective-permute-start.14 = (f32[160,256]{1,0:T(8,128)S(1)}, f32[160,256]{1,0:T(8,128)S(1)}, u32[]{:S(2)}, u32[]{:S(2)}) collective-permute-start(f32[160,256]{1,0:T(8,128)S(1)} %add_add_fusion.2), channel_id=1, source_target_pairs={{0,6},{1,7},{2,4},{3,5},{4,2},{5,3},{6,0},{7,1},{8,14},{9,15},{10,... | collective-permute-start | bytes 491528 | tf_op jit(solution)/shard_map/ppermute | solution.py:320
  49.3 1.2 %collective-permute-start.13 = (f32[160,256]{1,0:T(8,128)S(1)}, f32[160,256]{1,0:T(8,128)S(1)}, u32[]{:S(2)}, u32[]{:S(2)}) collective-permute-start(f32[160,256]{1,0:T(8,128)S(1)} %add_add_fusion.2), channel_id=1, source_target_pairs={{0,4},{1,5},{2,6},{3,7},{4,0},{5,1},{6,2},{7,3},{8,12},{9,13},{10,... | collective-permute-start | bytes 491528 | tf_op jit(solution)/shard_map/ppermute | solution.py:320
  50.6 0.8 collective-permute-start.12
  51.4 3.2 %collective-permute-done.7 = f32[96,256]{1,0:T(8,128)S(1)} collective-permute-done((f32[96,256]{1,0:T(8,128)S(1)}, f32[96,256]{1,0:T(8,128)S(1)}, u32[]{:S(2)}, u32[]{:S(2)}) %collective-permute-start.7) | collective-permute-done | bytes 98336 | tf_op jit(solution)/shard_map/ppermute | solution.py:320
  54.6 0.4 collective-permute-done.14
  55.1 1.7 %collective-permute-done.13 = f32[160,256]{1,0:T(8,128)S(1)} collective-permute-done((f32[160,256]{1,0:T(8,128)S(1)}, f32[160,256]{1,0:T(8,128)S(1)}, u32[]{:S(2)}, u32[]{:S(2)}) %collective-permute-start.13) | collective-permute-done | bytes 163872 | tf_op jit(solution)/shard_map/ppermute | solution.py:320
  56.8 3.6 %collective-permute-start.17 = (f32[128,256]{1,0:T(8,128)S(1)}, f32[128,256]{1,0:T(8,128)S(1)}, u32[]{:S(2)}, u32[]{:S(2)}) collective-permute-start(f32[128,256]{1,0:T(8,128)S(1)} %pad_maximum_fusion.6), channel_id=1, source_target_pairs={{0,24},{1,25},{2,26},{3,27},{4,28},{5,29},{6,30},{7,31},{8,16},{9,... | collective-permute-start | bytes 393224 | tf_op jit(solution)/shard_map/ppermute | solution.py:320
  60.4 0.9 collective-permute-start.15
  61.3 3.8 %collective-permute-done.17 = f32[128,256]{1,0:T(8,128)S(1)} collective-permute-done((f32[128,256]{1,0:T(8,128)S(1)}, f32[128,256]{1,0:T(8,128)S(1)}, u32[]{:S(2)}, u32[]{:S(2)}) %collective-permute-start.17) | collective-permute-done | bytes 131104 | tf_op jit(solution)/shard_map/ppermute | solution.py:320
  65.1 4.8 %collective-permute-done.16 = f32[128,256]{1,0:T(8,128)S(1)} collective-permute-done((f32[128,256]{1,0:T(8,128)S(1)}, f32[128,256]{1,0:T(8,128)S(1)}, u32[]{:S(2)}, u32[]{:S(2)}) %collective-permute-start.16) | collective-permute-done | bytes 131104 | tf_op jit(solution)/shard_map/ppermute | solution.py:320
  70.0 0.0 copy-start
  70.0 0.1 collective-permute-start.18
  70.1 0.3 collective-permute-start.22
  70.5 1.4 %collective-permute-start.21 = (f32[384,256]{1,0:T(8,128)S(1)}, f32[384,256]{1,0:T(8,128)S(1)}, u32[]{:S(2)}, u32[]{:S(2)}) collective-permute-start(f32[384,256]{1,0:T(8,128)S(1)} %pad_maximum_fusion.1.refs_0_), channel_id=1, source_target_pairs={{0,6},{1,7},{2,4},{3,5},{4,2},{5,3},{6,0},{7,1},{8,14},{9,15},{10,... | collective-permute-start | bytes 1179656 | tf_op jit(solution)/shard_map/ppermute | solution.py:320
  71.9 1.6 %collective-permute-start.20 = (f32[384,256]{1,0:T(8,128)S(1)}, f32[384,256]{1,0:T(8,128)S(1)}, u32[]{:S(2)}, u32[]{:S(2)}) collective-permute-start(f32[384,256]{1,0:T(8,128)S(1)} %pad_maximum_fusion.1.refs_0_), channel_id=1, source_target_pairs={{0,4},{1,5},{2,6},{3,7},{4,0},{5,1},{6,2},{7,3},{8,12},{9,13},{10,... | collective-permute-start | bytes 1179656 | tf_op jit(solution)/shard_map/ppermute | solution.py:320
  73.5 0.5 collective-permute-start.19
  74.0 2.5 %collective-permute-start.24 = (f32[128,256]{1,0:T(8,128)S(1)}, f32[128,256]{1,0:T(8,128)S(1)}, u32[]{:S(2)}, u32[]{:S(2)}) collective-permute-start(f32[128,256]{1,0:T(8,128)S(1)} %slice.159), channel_id=1, source_target_pairs={{0,24},{1,25},{2,26},{3,27},{4,28},{5,29},{6,30},{7,31},{8,16},{9,... | collective-permute-start | bytes 393224 | tf_op jit(solution)/shard_map/ppermute | solution.py:320
  76.4 1.1 %collective-permute-start.23 = (f32[128,256]{1,0:T(8,128)S(1)}, f32[128,256]{1,0:T(8,128)S(1)}, u32[]{:S(2)}, u32[]{:S(2)}) collective-permute-start(f32[128,256]{1,0:T(8,128)S(1)} %slice.159), channel_id=1, source_target_pairs={{0,16},{1,17},{2,18},{3,19},{4,20},{5,21},{6,22},{7,23},{8,24},{9,... | collective-permute-start | bytes 393224 | tf_op jit(solution)/shard_map/ppermute | solution.py:320
  77.5 11.9 %factor.1 = (f32[256,256]{1,0:T(8,128)}, bf16[256,256]{1,0:T(8,128)(2,1)S(1)}, bf16[256,256]{1,0:T(8,128)(2,1)S(1)}) custom-call(s32[3]{0:T(128)S(1)} %pad_add_fusion.info, f32[128,256]{1,0:T(8,128)S(1)} %pad_maximum_fusion.7.kept, f32[128,256]{1,0:T(8,128)S(1)} %collective-permute-done.18.got), custom_call_target="tpu_custom_call" | custom-call | flops 10000000000 | bytes 524288 | tf_op jit(solution)/shard_map/factor/pallas_call | solution.py:225
  89.5 1.5 %collective-permute-done.20.refs_2_ = f32[384,256]{1,0:T(8,128)S(1)} collective-permute-done((f32[384,256]{1,0:T(8,128)S(1)}, f32[384,256]{1,0:T(8,128)S(1)}, u32[]{:S(2)}, u32[]{:S(2)}) %collective-permute-start.20) | collective-permute-done | bytes 393248 | tf_op jit(solution)/shard_map/ppermute | solution.py:320
  91.0 0.1 collective-permute-done.19.refs_1_
  91.0 0.5 collective-permute-start.25
  91.5 0.0 collective-permute-start.26
  91.5 0.5 collective-permute-start.27
  92.0 0.0 collective-permute-start.28
  92.1 2.6 %basis.1 = bf16[2048,256]{1,0:T(8,128)(2,1)} custom-call(f32[2048,256]{1,0:T(8,128)S(1)} %copy-done, bf16[256,256]{1,0:T(8,128)(2,1)S(1)} %get-tuple-element.70.high, bf16[256,256]{1,0:T(8,128)(2,1)S(1)} %get-tuple-element.73.low), custom_call_target="tpu_custom_call" | custom-call | flops 805306368 | bytes 3145728 | tf_op jit(solution)/shard_map/basis/pallas_call | solution.py:252
  94.7 2.5 %project.2.refs_0_ = f32[256,4096]{1,0:T(8,128)} custom-call(s32[3]{0:T(128)S(1)} %pad_add_fusion.info, bf16[256,256]{1,0:T(8,128)(2,1)S(1)} %get-tuple-element.70.high, bf16[256,256]{1,0:T(8,128)(2,1)S(1)} %get-tuple-element.73.low, f32[384,256]{1,0:T(8,128)S(1)} %pad_maximum_fusion.1.refs_0_, f32[384,256]{1,0:T(8,128)S(1)} %collective-permute-done.19.refs_1_, ...), custom_call_target="tpu_custom_call" | custom-call | flops 805306368 | bytes 4194304 | tf_op jit(solution)/shard_map/project/pallas_call | solution.py:297
  97.2 2.5 %project.3 = f32[256,4096]{1,0:T(8,128)} custom-call(s32[3]{0:T(128)S(1)} %pad_add_fusion.info, bf16[256,256]{1,0:T(8,128)(2,1)S(1)} %get-tuple-element.70.high, bf16[256,256]{1,0:T(8,128)(2,1)S(1)} %get-tuple-element.73.low, f32[256,4096]{1,0:T(8,128)} %project.2.refs_0_, ...), custom_call_target="tpu_custom_call", output_to_operand_aliasing={{}: (3, {})} | custom-call | flops 805306368 | bytes 4194304 | tf_op jit(solution)/shard_map/project/pallas_call | solution.py:297
  (45 shorter events, 0.4 us)
Async XLA Ops:
  16.8 3.8 %collective-permute-start = (f32[1536,256]{1,0:T(8,128)S(1)}, f32[1536,256]{1,0:T(8,128)S(1)}, u32[]{:S(2)}, u32[]{:S(2)}) collective-permute-start(f32[1536,256]{1,0:T(8,128)S(1)} %get-tuple-element.42), channel_id=1, source_target_pairs={{0,1},{1,0},{2,3},{3,2},{4,5},{5,4},{6,7},{7,6},{8,9},{9,8},{10,11... | collective-permute-start | bytes 4718600 | tf_op jit(solution)/shard_map/ppermute | solution.py:320
  17.3 3.2 %collective-permute-start.5 = (f32[128,256]{1,0:T(8,128)S(1)}, f32[128,256]{1,0:T(8,128)S(1)}, u32[]{:S(2)}, u32[]{:S(2)}) collective-permute-start(f32[128,256]{1,0:T(8,128)S(1)} %get-tuple-element.50), channel_id=1, source_target_pairs={{0,1},{1,0},{2,3},{3,2},{4,5},{5,4},{6,7},{7,6},{8,9},{9,8},{10,11... | collective-permute-start | bytes 393224 | tf_op jit(solution)/shard_map/ppermute | solution.py:320
  17.4 8.0 %collective-permute-start.4 = (f32[512,256]{1,0:T(8,128)S(1)}, f32[512,256]{1,0:T(8,128)S(1)}, u32[]{:S(2)}, u32[]{:S(2)}) collective-permute-start(f32[512,256]{1,0:T(8,128)S(1)} %get-tuple-element.48), channel_id=1, source_target_pairs={{0,1},{1,0},{2,3},{3,2},{4,5},{5,4},{6,7},{7,6},{8,9},{9,8},{10,11... | collective-permute-start | bytes 1572872 | tf_op jit(solution)/shard_map/ppermute | solution.py:320
  20.9 12.8 %collective-permute-start.1 = (f32[384,256]{1,0:T(8,128)S(1)}, f32[384,256]{1,0:T(8,128)S(1)}, u32[]{:S(2)}, u32[]{:S(2)}) collective-permute-start(f32[384,256]{1,0:T(8,128)S(1)} %get-tuple-element.44), channel_id=1, source_target_pairs={{0,2},{1,3},{2,0},{3,1},{4,6},{5,7},{6,4},{7,5},{8,10},{9,11},{10,... | collective-permute-start | bytes 1179656 | tf_op jit(solution)/shard_map/ppermute | solution.py:320
  23.8 19.3 %collective-permute-start.2 = (f32[384,256]{1,0:T(8,128)S(1)}, f32[384,256]{1,0:T(8,128)S(1)}, u32[]{:S(2)}, u32[]{:S(2)}) collective-permute-start(f32[384,256]{1,0:T(8,128)S(1)} %get-tuple-element.45), channel_id=1, source_target_pairs={{0,4},{1,5},{2,6},{3,7},{4,0},{5,1},{6,2},{7,3},{8,12},{9,13},{10,... | collective-permute-start | bytes 1179656 | tf_op jit(solution)/shard_map/ppermute | solution.py:320
  25.4 17.8 %collective-permute-start.3 = (f32[384,256]{1,0:T(8,128)S(1)}, f32[384,256]{1,0:T(8,128)S(1)}, u32[]{:S(2)}, u32[]{:S(2)}) collective-permute-start(f32[384,256]{1,0:T(8,128)S(1)} %get-tuple-element.46), channel_id=1, source_target_pairs={{0,6},{1,7},{2,4},{3,5},{4,2},{5,3},{6,0},{7,1},{8,14},{9,15},{10,... | collective-permute-start | bytes 1179656 | tf_op jit(solution)/shard_map/ppermute | solution.py:320
  25.6 22.0 %collective-permute-start.9 = (f32[160,256]{1,0:T(8,128)S(1)}, f32[160,256]{1,0:T(8,128)S(1)}, u32[]{:S(2)}, u32[]{:S(2)}) collective-permute-start(f32[160,256]{1,0:T(8,128)S(1)} %get-tuple-element.57), channel_id=1, source_target_pairs={{0,8},{1,9},{2,10},{3,11},{4,12},{5,13},{6,14},{7,15},{8,0},{9,1},... | collective-permute-start | bytes 491528 | tf_op jit(solution)/shard_map/ppermute | solution.py:320
  27.6 20.1 %collective-permute-start.10 = (f32[160,256]{1,0:T(8,128)S(1)}, f32[160,256]{1,0:T(8,128)S(1)}, u32[]{:S(2)}, u32[]{:S(2)}) collective-permute-start(f32[160,256]{1,0:T(8,128)S(1)} %get-tuple-element.58), channel_id=1, source_target_pairs={{0,16},{1,17},{2,18},{3,19},{4,20},{5,21},{6,22},{7,23},{8,24},{9,... | collective-permute-start | bytes 491528 | tf_op jit(solution)/shard_map/ppermute | solution.py:320
  33.7 14.0 %collective-permute-start.11 = (f32[160,256]{1,0:T(8,128)S(1)}, f32[160,256]{1,0:T(8,128)S(1)}, u32[]{:S(2)}, u32[]{:S(2)}) collective-permute-start(f32[160,256]{1,0:T(8,128)S(1)} %get-tuple-element.51), channel_id=1, source_target_pairs={{0,24},{1,25},{2,26},{3,27},{4,28},{5,29},{6,30},{7,31},{8,16},{9,... | collective-permute-start | bytes 491528 | tf_op jit(solution)/shard_map/ppermute | solution.py:320
  43.3 7.3 %collective-permute-start.6 = (f32[96,256]{1,0:T(8,128)S(1)}, f32[96,256]{1,0:T(8,128)S(1)}, u32[]{:S(2)}, u32[]{:S(2)}) collective-permute-start(f32[96,256]{1,0:T(8,128)S(1)} %get-tuple-element.53), channel_id=1, source_target_pairs={{0,8},{1,9},{2,10},{3,11},{4,12},{5,13},{6,14},{7,15},{8,0},{9,1},... | collective-permute-start | bytes 294920 | tf_op jit(solution)/shard_map/ppermute | solution.py:320
  44.9 9.7 %collective-permute-start.7 = (f32[96,256]{1,0:T(8,128)S(1)}, f32[96,256]{1,0:T(8,128)S(1)}, u32[]{:S(2)}, u32[]{:S(2)}) collective-permute-start(f32[96,256]{1,0:T(8,128)S(1)} %get-tuple-element.54), channel_id=1, source_target_pairs={{0,16},{1,17},{2,18},{3,19},{4,20},{5,21},{6,22},{7,23},{8,24},{9,... | collective-permute-start | bytes 294920 | tf_op jit(solution)/shard_map/ppermute | solution.py:320
  47.5 7.1 %collective-permute-start.8 = (f32[96,256]{1,0:T(8,128)S(1)}, f32[96,256]{1,0:T(8,128)S(1)}, u32[]{:S(2)}, u32[]{:S(2)}) collective-permute-start(f32[96,256]{1,0:T(8,128)S(1)} %get-tuple-element.55), channel_id=1, source_target_pairs={{0,24},{1,25},{2,26},{3,27},{4,28},{5,29},{6,30},{7,31},{8,16},{9,... | collective-permute-start | bytes 294920 | tf_op jit(solution)/shard_map/ppermute | solution.py:320
  47.8 7.2 %collective-permute-start.14 = (f32[160,256]{1,0:T(8,128)S(1)}, f32[160,256]{1,0:T(8,128)S(1)}, u32[]{:S(2)}, u32[]{:S(2)}) collective-permute-start(f32[160,256]{1,0:T(8,128)S(1)} %add_add_fusion.2), channel_id=1, source_target_pairs={{0,6},{1,7},{2,4},{3,5},{4,2},{5,3},{6,0},{7,1},{8,14},{9,15},{10,... | collective-permute-start | bytes 491528 | tf_op jit(solution)/shard_map/ppermute | solution.py:320
  49.3 7.4 %collective-permute-start.13 = (f32[160,256]{1,0:T(8,128)S(1)}, f32[160,256]{1,0:T(8,128)S(1)}, u32[]{:S(2)}, u32[]{:S(2)}) collective-permute-start(f32[160,256]{1,0:T(8,128)S(1)} %add_add_fusion.2), channel_id=1, source_target_pairs={{0,4},{1,5},{2,6},{3,7},{4,0},{5,1},{6,2},{7,3},{8,12},{9,13},{10,... | collective-permute-start | bytes 491528 | tf_op jit(solution)/shard_map/ppermute | solution.py:320
  50.6 6.1 %collective-permute-start.12 = (f32[160,256]{1,0:T(8,128)S(1)}, f32[160,256]{1,0:T(8,128)S(1)}, u32[]{:S(2)}, u32[]{:S(2)}) collective-permute-start(f32[160,256]{1,0:T(8,128)S(1)} %add_add_fusion.2), channel_id=1, source_target_pairs={{0,2},{1,3},{2,0},{3,1},{4,6},{5,7},{6,4},{7,5},{8,10},{9,11},{10,... | collective-permute-start | bytes 491528 | tf_op jit(solution)/shard_map/ppermute | solution.py:320
  56.8 8.3 %collective-permute-start.17 = (f32[128,256]{1,0:T(8,128)S(1)}, f32[128,256]{1,0:T(8,128)S(1)}, u32[]{:S(2)}, u32[]{:S(2)}) collective-permute-start(f32[128,256]{1,0:T(8,128)S(1)} %pad_maximum_fusion.6), channel_id=1, source_target_pairs={{0,24},{1,25},{2,26},{3,27},{4,28},{5,29},{6,30},{7,31},{8,16},{9,... | collective-permute-start | bytes 393224 | tf_op jit(solution)/shard_map/ppermute | solution.py:320
  60.4 9.5 %collective-permute-start.16 = (f32[128,256]{1,0:T(8,128)S(1)}, f32[128,256]{1,0:T(8,128)S(1)}, u32[]{:S(2)}, u32[]{:S(2)}) collective-permute-start(f32[128,256]{1,0:T(8,128)S(1)} %pad_maximum_fusion.6), channel_id=1, source_target_pairs={{0,16},{1,17},{2,18},{3,19},{4,20},{5,21},{6,22},{7,23},{8,24},{9,... | collective-permute-start | bytes 393224 | tf_op jit(solution)/shard_map/ppermute | solution.py:320
  60.4 9.5 %collective-permute-start.15 = (f32[128,256]{1,0:T(8,128)S(1)}, f32[128,256]{1,0:T(8,128)S(1)}, u32[]{:S(2)}, u32[]{:S(2)}) collective-permute-start(f32[128,256]{1,0:T(8,128)S(1)} %pad_maximum_fusion.6), channel_id=1, source_target_pairs={{0,8},{1,9},{2,10},{3,11},{4,12},{5,13},{6,14},{7,15},{8,0},{9,1},... | collective-permute-start | bytes 393224 | tf_op jit(solution)/shard_map/ppermute | solution.py:320
  70.0 22.0 %copy-start = (f32[2048,256]{1,0:T(8,128)S(1)}, f32[2048,256]{1,0:T(8,128)}, u32[]{:S(2)}) copy-start(f32[2048,256]{1,0:T(8,128)} %get-tuple-element.72.sketch) | copy-start | bytes 6291460
  70.0 3.9 %collective-permute-start.18 = (f32[128,256]{1,0:T(8,128)S(1)}, f32[128,256]{1,0:T(8,128)S(1)}, u32[]{:S(2)}, u32[]{:S(2)}) collective-permute-start(f32[128,256]{1,0:T(8,128)S(1)} %pad_maximum_fusion.7.kept), channel_id=1, source_target_pairs={{0,1},{1,0},{2,3},{3,2},{4,5},{5,4},{6,7},{7,6},{8,9},{9,8},{10,11... | collective-permute-start | bytes 393224 | tf_op jit(solution)/shard_map/ppermute | solution.py:320
  70.1 6.3 %collective-permute-start.22 = (f32[128,256]{1,0:T(8,128)S(1)}, f32[128,256]{1,0:T(8,128)S(1)}, u32[]{:S(2)}, u32[]{:S(2)}) collective-permute-start(f32[128,256]{1,0:T(8,128)S(1)} %slice.159), channel_id=1, source_target_pairs={{0,8},{1,9},{2,10},{3,11},{4,12},{5,13},{6,14},{7,15},{8,0},{9,1},... | collective-permute-start | bytes 393224 | tf_op jit(solution)/shard_map/ppermute | solution.py:320
  70.5 19.0 %collective-permute-start.21 = (f32[384,256]{1,0:T(8,128)S(1)}, f32[384,256]{1,0:T(8,128)S(1)}, u32[]{:S(2)}, u32[]{:S(2)}) collective-permute-start(f32[384,256]{1,0:T(8,128)S(1)} %pad_maximum_fusion.1.refs_0_), channel_id=1, source_target_pairs={{0,6},{1,7},{2,4},{3,5},{4,2},{5,3},{6,0},{7,1},{8,14},{9,15},{10,... | collective-permute-start | bytes 1179656 | tf_op jit(solution)/shard_map/ppermute | solution.py:320
  71.9 19.1 %collective-permute-start.20 = (f32[384,256]{1,0:T(8,128)S(1)}, f32[384,256]{1,0:T(8,128)S(1)}, u32[]{:S(2)}, u32[]{:S(2)}) collective-permute-start(f32[384,256]{1,0:T(8,128)S(1)} %pad_maximum_fusion.1.refs_0_), channel_id=1, source_target_pairs={{0,4},{1,5},{2,6},{3,7},{4,0},{5,1},{6,2},{7,3},{8,12},{9,13},{10,... | collective-permute-start | bytes 1179656 | tf_op jit(solution)/shard_map/ppermute | solution.py:320
  73.5 17.6 %collective-permute-start.19 = (f32[384,256]{1,0:T(8,128)S(1)}, f32[384,256]{1,0:T(8,128)S(1)}, u32[]{:S(2)}, u32[]{:S(2)}) collective-permute-start(f32[384,256]{1,0:T(8,128)S(1)} %pad_maximum_fusion.1.refs_0_), channel_id=1, source_target_pairs={{0,2},{1,3},{2,0},{3,1},{4,6},{5,7},{6,4},{7,5},{8,10},{9,11},{10,... | collective-permute-start | bytes 1179656 | tf_op jit(solution)/shard_map/ppermute | solution.py:320
  74.0 15.5 %collective-permute-start.24 = (f32[128,256]{1,0:T(8,128)S(1)}, f32[128,256]{1,0:T(8,128)S(1)}, u32[]{:S(2)}, u32[]{:S(2)}) collective-permute-start(f32[128,256]{1,0:T(8,128)S(1)} %slice.159), channel_id=1, source_target_pairs={{0,24},{1,25},{2,26},{3,27},{4,28},{5,29},{6,30},{7,31},{8,16},{9,... | collective-permute-start | bytes 393224 | tf_op jit(solution)/shard_map/ppermute | solution.py:320
  76.4 13.0 %collective-permute-start.23 = (f32[128,256]{1,0:T(8,128)S(1)}, f32[128,256]{1,0:T(8,128)S(1)}, u32[]{:S(2)}, u32[]{:S(2)}) collective-permute-start(f32[128,256]{1,0:T(8,128)S(1)} %slice.159), channel_id=1, source_target_pairs={{0,16},{1,17},{2,18},{3,19},{4,20},{5,21},{6,22},{7,23},{8,24},{9,... | collective-permute-start | bytes 393224 | tf_op jit(solution)/shard_map/ppermute | solution.py:320
  91.0 6.2 %collective-permute-start.29 = (f32[512,256]{1,0:T(8,128)S(1)}, f32[512,256]{1,0:T(8,128)S(1)}, u32[]{:S(2)}, u32[]{:S(2)}) collective-permute-start(f32[512,256]{1,0:T(8,128)S(1)} %pad_maximum_fusion.refs_4_), channel_id=1, source_target_pairs={{0,1},{1,0},{2,3},{3,2},{4,5},{5,4},{6,7},{7,6},{8,9},{9,8},{10,11... | collective-permute-start | bytes 1572872 | tf_op jit(solution)/shard_map/ppermute | solution.py:320
  91.0 6.1 %collective-permute-start.25 = (f32[384,256]{1,0:T(8,128)S(1)}, f32[384,256]{1,0:T(8,128)S(1)}, u32[]{:S(2)}, u32[]{:S(2)}) collective-permute-start(f32[384,256]{1,0:T(8,128)S(1)} %pad_maximum_fusion.1.refs_0_), channel_id=1, source_target_pairs={{0,1},{1,0},{2,3},{3,2},{4,5},{5,4},{6,7},{7,6},{8,9},{9,8},{10,11... | collective-permute-start | bytes 1179656 | tf_op jit(solution)/shard_map/ppermute | solution.py:320
  91.5 5.6 %collective-permute-start.26 = (f32[384,256]{1,0:T(8,128)S(1)}, f32[384,256]{1,0:T(8,128)S(1)}, u32[]{:S(2)}, u32[]{:S(2)}) collective-permute-start(f32[384,256]{1,0:T(8,128)S(1)} %collective-permute-done.19.refs_1_), channel_id=1, source_target_pairs={{0,1},{1,0},{2,3},{3,2},{4,5},{5,4},{6,7},{7,6},{8,9},{9,8},{10,11... | collective-permute-start | bytes 1179656 | tf_op jit(solution)/shard_map/ppermute | solution.py:320
  91.5 5.6 %collective-permute-start.27 = (f32[384,256]{1,0:T(8,128)S(1)}, f32[384,256]{1,0:T(8,128)S(1)}, u32[]{:S(2)}, u32[]{:S(2)}) collective-permute-start(f32[384,256]{1,0:T(8,128)S(1)} %collective-permute-done.20.refs_2_), channel_id=1, source_target_pairs={{0,1},{1,0},{2,3},{3,2},{4,5},{5,4},{6,7},{7,6},{8,9},{9,8},{10,11... | collective-permute-start | bytes 1179656 | tf_op jit(solution)/shard_map/ppermute | solution.py:320
  92.0 5.2 %collective-permute-start.28 = (f32[384,256]{1,0:T(8,128)S(1)}, f32[384,256]{1,0:T(8,128)S(1)}, u32[]{:S(2)}, u32[]{:S(2)}) collective-permute-start(f32[384,256]{1,0:T(8,128)S(1)} %collective-permute-done.21.refs_3_), channel_id=1, source_target_pairs={{0,1},{1,0},{2,3},{3,2},{4,5},{5,4},{6,7},{7,6},{8,9},{9,8},{10,11... | collective-permute-start | bytes 1179656 | tf_op jit(solution)/shard_map/ppermute | solution.py:320

commit v7 on v6

--- a/solution.py
+++ b/solution.py
@@ -40,10 +40,28 @@
     return k - second, second
 
 
+def put_products(scale, line, info, region, rounded_t, columns, width, class1, class2, done=None):
+    in_plane, in_line = info[1], info[2]
+    rows1, rows2 = row_classes(rounded_t.shape[0], line)
+    size1, size2 = rows1 // line, rows2 // line
+    for p in range(PLANE):
+        value = dot(rounded_t[...], columns(p)) * scale
+        for g in range(line):
+            to = in_line ^ g
+            for h in range(2):
+                part = value[:, h * width // 2 : (h + 1) * width // 2]
+                to1 = pl.multiple_of(p * 2 * rows1 + (2 * to + h) * size1, 8)
+                class1[pl.ds(to1, size1), :] = part[g * size1 : (g + 1) * size1]
+                to2 = pl.multiple_of(((to * PLANE + (in_plane ^ p)) * 2 + h) * size2, 8)
+                class2[pl.ds(to2, size2), :] = part[rows1 + g * size2 : rows1 + (g + 1) * size2]
+        if done is not None:
+            done(p, 2 * rows1)
+
+
 def front_kernel(
     in_scale, gram_scale, scale, line,
-    info, e, signs, sketch_out, gram_sent, gram_kept, sent1, sent2, kept1, kept2,
-    e_kept, sketch, rounded_t, s32, s16, acc, class1, class2, sem, out_sem,
+    info, e, signs, sketch_out, rounded_t, gram_sent, gram_kept, sent1, sent2,
+    e_kept, sketch, s32, s16, acc, class1, class2, sem, out_sem,
 ):
     rows, d = e.shape
     k = rounded_t.shape[0]
@@ -82,52 +100,43 @@
         to = pl.ds(pl.multiple_of((in_line ^ g) * size, size), size)
         for out, region in ((gram_kept, own), (gram_sent, 1 - own)):
             out[to, :] = acc[pl.ds(pl.multiple_of(region * half + g * size, size), size), :]
-    rows1, rows2 = row_classes(k, line)
-    size1, size2 = rows1 // line, rows2 // line
     width = d // (2 * PLANE)
-    for r, region in enumerate((1 - own, own)):
-        for p in range(PLANE):
-            at = pl.ds(pl.multiple_of((region * PLANE + (in_plane ^ p)) * width, width), width)
-            value = dot(rounded_t[...], e_kept[:, at]) * scale
-            for g in range(line):
-                to = in_line ^ g
-                for h in range(2):
-                    part = value[:, h * width // 2 : (h + 1) * width // 2]
-                    to1 = pl.multiple_of(p * 2 * rows1 + (2 * to + h) * size1, 8)
-                    (class1, kept1)[r][pl.ds(to1, size1), :] = part[g * size1 : (g + 1) * size1]
-                    to2 = pl.multiple_of(((to * PLANE + (in_plane ^ p)) * 2 + h) * size2, 8)
-                    (class2, kept2)[r][pl.ds(to2, size2), :] = part[rows1 + g * size2 : rows1 + (g + 1) * size2]
-            if r == 0:
-                at = pl.ds(p * 2 * rows1, 2 * rows1)
-                outs.append(pltpu.make_async_copy(class1.at[at], sent1.at[at], out_sem.at[1 + p]))
-                outs[-1].start()
-        if r == 0:
-            outs.append(pltpu.make_async_copy(class2, sent2, out_sem.at[1 + PLANE]))
-            outs[-1].start()
+
+    def columns(p):
+        return e_kept[:, pl.ds(pl.multiple_of(((1 - own) * PLANE + (in_plane ^ p)) * width, width), width)]
+
+    def done(p, size):
+        at = pl.ds(p * size, size)
+        outs.append(pltpu.make_async_copy(class1.at[at], sent1.at[at], out_sem.at[1 + p]))
+        outs[-1].start()
+
+    put_products(scale, line, info, 1 - own, rounded_t, columns, width, class1, class2, done)
+    outs.append(pltpu.make_async_copy(class2, sent2, out_sem.at[1 + PLANE]))
+    outs[-1].start()
     for copy in outs:
         copy.wait()
+
+
+def classes_of(k, d, line):
+    return [(2 * PLANE * rows, d // (4 * PLANE)) for rows in row_classes(k, line)]
 
 
 def front_call(info, e, signs, rows_all, line):
     rows, d = e.shape
     k = signs.shape[1]
     copies = 4
-    rows1, rows2 = row_classes(k, line)
-    width = d // (4 * PLANE)
-    classes = [(2 * PLANE * rows1, width), (2 * PLANE * rows2, width)]
+    classes = classes_of(k, d, line)
     f32 = lambda *shape: jax.ShapeDtypeStruct(shape, jnp.float32)
     return pl.pallas_call(
         functools.partial(front_kernel, 1.0 / math.sqrt(d), 1.0 / rows_all, 1.0 / math.sqrt(rows_all), line),
         in_specs=[SMEM_SPEC, ANY_SPEC, ANY_SPEC],
-        out_specs=[ANY_SPEC] + [VMEM_SPEC] * 2 + [ANY_SPEC] * 2 + [VMEM_SPEC] * 2,
-        out_shape=[f32(rows, k)]
+        out_specs=[ANY_SPEC] + [VMEM_SPEC] * 3 + [ANY_SPEC] * 2,
+        out_shape=[f32(rows, k), pltpu.VMEM((k, rows), jnp.bfloat16)]
         + [pltpu.VMEM((k // 2, k), jnp.float32)] * 2
-        + [f32(*c) for c in classes]
-        + [pltpu.VMEM(c, jnp.float32) for c in classes],
+        + [f32(*c) for c in classes],
         scratch_shapes=[
             pltpu.VMEM((rows, d), e.dtype),
             pltpu.VMEM((rows, k), jnp.float32),
-            pltpu.VMEM((k, rows), jnp.bfloat16),
             pltpu.VMEM((d, k), jnp.int32),
             pltpu.VMEM((d, k), jnp.bfloat16),
             pltpu.VMEM((k, k), jnp.float32),
@@ -137,12 +146,46 @@
             pltpu.SemaphoreType.DMA((2 + PLANE,)),
         ],
         compiler_params=pltpu.CompilerParams(vmem_limit_bytes=48 * MIB),
-        cost_estimate=pl.CostEstimate(flops=4 * rows * d * k, bytes_accessed=rows * d * 2 + d * k * 4, transcendentals=0),
+        cost_estimate=pl.CostEstimate(flops=3 * rows * d * k, bytes_accessed=rows * d * 2 + d * k * 4, transcendentals=0),
         name="front",
     )(info, e, pltpu.with_memory_space_constraint(signs, pltpu.HBM))
 
 
-def factor_kernel(line, info, kept, got, triangle, high, low, work):
+def cross_kernel(scale, line, info, e, rounded_t, kept1, kept2, blocks, sem):
+    own, in_plane = info[0], info[1]
+    width = blocks.shape[2]
+
+    def copy(p):
+        at = pl.ds(pl.multiple_of((own * PLANE + (in_plane ^ p)) * width, width), width)
+        return pltpu.make_async_copy(e.at[:, at], blocks.at[p], sem.at[p])
+
+    for p in range(PLANE):
+        copy(p).start()
+
+    def columns(p):
+        copy(p).wait()
+        return blocks[p]
+
+    put_products(scale, line, info, own, rounded_t, columns, width, kept1, kept2)
+
+
+def cross_call(info, e, rounded_t, rows_all, line):
+    rows, d = e.shape
+    k = rounded_t.shape[0]
+    width = d // (2 * PLANE)
+    return pl.pallas_call(
+        functools.partial(cross_kernel, 1.0 / math.sqrt(rows_all), line),
+        in_specs=[SMEM_SPEC, ANY_SPEC, VMEM_SPEC],
+        out_specs=[VMEM_SPEC] * 2,
+        out_shape=[pltpu.VMEM(c, jnp.float32) for c in classes_of(k, d, line)],
+        scratch_shapes=[pltpu.VMEM((PLANE, rows, width), e.dtype), pltpu.SemaphoreType.DMA((PLANE,))],
+        compiler_params=pltpu.CompilerParams(vmem_limit_bytes=24 * MIB),
+        cost_estimate=pl.CostEstimate(flops=rows * d * k, bytes_accessed=rows * d, transcendentals=0),
+        name="cross",
+    )(info, pltpu.with_memory_space_constraint(e, pltpu.HBM), *pinned(rounded_t))
+
+
+def factor_kernel(line, info, kept, got, triangle, inverse, work):
     k = triangle.shape[0]
     half = k // 2
     b = 64
@@ -162,7 +205,6 @@
         return jnp.broadcast_to(a[:, at : at + 1], (8, 2 * b))
 
     for n in range(k // b):
-        put = slice(n * b, (n + 1) * b)
         first = (n % 2) * b
         pair = (n // 2) * 2 * b
         own_lanes = (lane >= first) & (lane < first + b)
@@ -200,22 +242,29 @@
             moved = pltpu.roll(new * (1.0 / jnp.sqrt(pivots)), b, 1)
             inv.append(jnp.where(own_lanes, moved, 0.0))
         inv = jnp.concatenate(inv, axis=0)
+        end = k + pair + 2 * b
         y = lax.dot_general(
-            inv, work[pair : pair + 2 * b, :], (((1,), (0,)), ((), ())),
+            inv, work[pair : pair + 2 * b, pair:end], (((1,), (0,)), ((), ())),
             precision=lax.Precision.HIGHEST, preferred_element_type=jnp.float32,
         )
-        r_rows, i_rows = y[:, :k], y[:, k:]
-        at = lax.broadcasted_iota(jnp.int32, (b, k), 0) + n * b
-        to = lax.broadcasted_iota(jnp.int32, (b, k), 1)
-        triangle[put, :] = jnp.where(to >= at, r_rows, 0.0)
-        i_rows = jnp.where(to <= at, i_rows, 0.0)
-        i_high, i_low = split(i_rows)
-        high[put, :] = i_high
-        low[put, :] = i_low
+        r_rows, i_rows = y[:, : k - pair], y[:, k - pair :]
+        at = lax.broadcasted_iota(jnp.int32, r_rows.shape, 0) + n * b
+        to = lax.broadcasted_iota(jnp.int32, r_rows.shape, 1) + pair
+        put = slice(n * b, (n + 1) * b)
+        if pair:
+            triangle[put, :pair] = jnp.zeros((b, pair), jnp.float32)
+        triangle[put, pair:] = jnp.where(to >= at, r_rows, 0.0)
+        i_at = lax.broadcasted_iota(jnp.int32, i_rows.shape, 0) + n * b
+        i_to = lax.broadcasted_iota(jnp.int32, i_rows.shape, 1)
+        for row, part in zip((n * b, k + n * b), split(jnp.where(i_to <= i_at, i_rows, 0.0))):
+            inverse[row : row + b, : pair + 2 * b] = part
+            if pair + 2 * b < k:
+                inverse[row : row + b, pair + 2 * b :] = jnp.zeros((b, k - pair - 2 * b), part.dtype)
         if (n + 1) * b < k:
-            later = jnp.where(to >= (n + 1) * b, r_rows, 0.0)
-            work[...] -= lax.dot_general(
-                later, y, (((0,), (0,)), ((), ())),
+            rest = (n + 1) // 2 * 2 * b
+            later = jnp.where(to >= (n + 1) * b, r_rows, 0.0)[:, rest - pair :]
+            work[rest:, rest:end] -= lax.dot_general(
+                later, y[:, rest - pair :], (((0,), (0,)), ((), ())),
                 precision=lax.Precision.HIGHEST, preferred_element_type=jnp.float32,
             )
 
@@ -225,11 +274,10 @@
     return pl.pallas_call(
         functools.partial(factor_kernel, line),
         in_specs=[SMEM_SPEC, VMEM_SPEC, VMEM_SPEC],
-        out_specs=[VMEM_SPEC] * 3,
+        out_specs=[VMEM_SPEC] * 2,
         out_shape=[
             jax.ShapeDtypeStruct((k, k), jnp.float32),
-            jax.ShapeDtypeStruct((k, k), jnp.bfloat16),
-            jax.ShapeDtypeStruct((k, k), jnp.bfloat16),
+            jax.ShapeDtypeStruct((2 * k, k), jnp.bfloat16),
         ],
         scratch_shapes=[pltpu.VMEM((k, 2 * k), jnp.float32)],
         compiler_params=pltpu.CompilerParams(vmem_limit_bytes=16 * MIB),
@@ -238,33 +286,33 @@
     )(info, kept, got)
 
 
-def basis_kernel(sketch, high, low, out):
+def basis_kernel(sketch, inverse, out):
+    k = sketch.shape[1]
     s_high, s_low = split(sketch[...])
     right = ((1,), (1,))
-    out[...] = (
-        dot(s_high, high[...], right) + (dot(s_high, low[...], right) + dot(s_low, high[...], right))
-    ).astype(out.dtype)
-
-
-def basis_call(sketch, high, low):
+    both = dot(s_high, inverse[...], right)
+    out[...] = (both[:, :k] + (both[:, k:] + dot(s_low, inverse[:k, :], right))).astype(out.dtype)
+
+
+def basis_call(sketch, inverse):
     rows, k = sketch.shape
     block = rows // 4
     return pl.pallas_call(
         basis_kernel,
         grid=(rows // block,),
-        in_specs=[pl.BlockSpec((block, k), lambda i: (i, 0))] + [pl.BlockSpec((k, k), lambda i: (0, 0))] * 2,
+        in_specs=[pl.BlockSpec((block, k), lambda i: (i, 0)), pl.BlockSpec((2 * k, k), lambda i: (0, 0))],
         out_specs=pl.BlockSpec((block, k), lambda i: (i, 0)),
         out_shape=jax.ShapeDtypeStruct((rows, k), jnp.bfloat16),
         compiler_params=pltpu.CompilerParams(vmem_limit_bytes=16 * MIB),
         cost_estimate=pl.CostEstimate(flops=6 * rows * k * k, bytes_accessed=rows * k * 6, transcendentals=0),
         name="basis",
-    )(sketch, high, low)
-
-
-def project_kernel(line, is_own, info, high, low, *refs):
+    )(sketch, inverse)
+
+
+def project_kernel(line, is_own, info, inverse, *refs):
     *blocks, out, whole, value, sem = refs
     class1, class2 = blocks[-PLANE - 1 : -1], blocks[-1]
-    k = high.shape[0]
+    k = inverse.shape[1]
     rows1, rows2 = row_classes(k, line)
     size1, size2 = rows1 // line, rows2 // line
     own, in_plane, in_line = info[0], info[1], info[2]
@@ -282,7 +330,8 @@
                 at2 = pl.ds(pl.multiple_of(((g * PLANE + (in_plane ^ p)) * 2 + h) * size2, 8), size2)
                 whole[p, to2, cols] = class2[at2, :]
         c_high, c_low = split(whole[p])
-        value[p] = dot(high[...], c_high) + (dot(high[...], c_low) + dot(low[...], c_high))
+        both = dot(inverse[...], c_high)
+        value[p] = both[:k] + (both[k:] + dot(inverse[:k, :], c_low))
         at = pl.ds(pl.multiple_of((region * PLANE + (in_plane ^ p)) * width, width), width)
         copies.append(pltpu.make_async_copy(value.at[p], out.at[:, at], sem.at[p]))
         copies[-1].start()
@@ -290,16 +339,16 @@
         copy.wait()
 
 
-def project_call(line, is_own, info, high, low, blocks, d, before):
-    k = high.shape[0]
+def project_call(line, is_own, info, inverse, blocks, d, before):
+    k = inverse.shape[1]
     width = d // (2 * PLANE)
     extra = [] if before is None else [before]
     return pl.pallas_call(
         functools.partial(project_kernel, line, is_own),
-        in_specs=[SMEM_SPEC, VMEM_SPEC, VMEM_SPEC] + [ANY_SPEC] * len(extra) + [VMEM_SPEC] * len(blocks),
+        in_specs=[SMEM_SPEC, VMEM_SPEC] + [ANY_SPEC] * len(extra) + [VMEM_SPEC] * len(blocks),
         out_specs=ANY_SPEC,
         out_shape=jax.ShapeDtypeStruct((k, d), jnp.float32),
-        input_output_aliases={3: 0} if extra else {},
+        input_output_aliases={2: 0} if extra else {},
         scratch_shapes=[
             pltpu.VMEM((PLANE, k, width), jnp.float32),
             pltpu.VMEM((PLANE, k, width), jnp.float32),
@@ -308,7 +357,7 @@
         compiler_params=pltpu.CompilerParams(vmem_limit_bytes=16 * MIB),
         cost_estimate=pl.CostEstimate(flops=3 * k * k * d, bytes_accessed=k * d * 4, transcendentals=0),
         name="project",
-    )(info, *pinned(high, low), *extra, *pinned(*blocks))
+    )(info, *pinned(inverse), *extra, *pinned(*blocks))
 
 
 def solution(mesh):
@@ -344,8 +393,9 @@
             last[0] = arrays[-1]
             return arrays if len(arrays) > 1 else arrays[0]
 
-        sketch, gram_sent, gram, sent1, sent2, kept1, kept2 = front_call(info, e, signs, rows_all, line)
+        sketch, rounded_t, gram_sent, gram, sent1, sent2 = front_call(info, e, signs, rows_all, line)
         got1, got2, gram_got = with_pair(sent1), with_pair(sent2), with_pair(gram_sent)
+        kept1, kept2 = cross_call(info, e, rounded_t, rows_all, line)
         parts1 = in_turn(*[a + b for a, b in zip(parts_of(kept1, PLANE), parts_of(got1, PLANE))])
         from_plane = [over_plane[g](parts1[g]) for g in range(1, PLANE)]
         grams = parts_of(gram + gram_got, line)
@@ -362,21 +412,23 @@
         a1 = in_turn(join(sum(from_line, parts1[0]), a2[n2:]))
         n1 = a1.shape[0] - gram.shape[0] // line
         gathered = [a1] + [over_line[g](a1) for g in range(1, line)]
-        a2 = in_turn(a2[:n2])
-        near = over_line[1](a2)
+        class2 = in_turn(a2[:n2])
+        class2 = join(class2, over_line[1](class2))
+        *gathered, class2 = in_turn(*gathered, class2)
         a1 = in_turn(join(*[a[:n1] for a in gathered]))
-        class1 = [a1] + [over_plane[g](a1) for g in range(1, PLANE)]
+        class1 = [over_plane[g](a1) for g in range(1, PLANE)]
         gram = in_turn(join(*[a[n1:] for a in gathered]))
-        gram_got = with_pair(gram)
-        gram_got, a2_later = in_turn(gram_got, a2)
-        class2 = [a2, near] + [over_line[g](a2_later) for g in range(2, line)]
-        triangle, high, low = factor_call(line, info, in_turn(gram), gram_got)
-        high = in_turn(high)
-        *class1, class2 = in_turn(*class1, join(*class2))
-        theirs = [with_pair(a) for a in (*class1, class2)]
-        basis = in_turn(basis_call(in_turn(sketch), high, low))
-        projected = project_call(line, True, info, high, low, [*class1, class2], d, None)
-        projected = project_call(line, False, info, high, low, theirs, d, projected)
+        gram_got, class2 = in_turn(with_pair(gram), class2)
+        for bit in range(1, line.bit_length() - 1):
+            class2 = join(class2, over_line[1 << bit](class2))
+        triangle, inverse = factor_call(line, info, in_turn(gram), gram_got)
+        inverse, class2 = in_turn(inverse, class2)
+        theirs = [with_pair(a1), with_pair(class2)]
+        basis = in_turn(basis_call(in_turn(sketch), inverse))
+        class1 = in_turn(*class1)
+        theirs = [theirs[0], *[with_pair(a) for a in class1], theirs[1]]
+        projected = project_call(line, True, info, inverse, [a1, *class1, class2], d, None)
+        projected = project_call(line, False, info, inverse, theirs, d, projected)
         return triangle, basis, projected
 
     return jax.shard_map(

time: 100 us -> 99.8 us (level)
  starting transfers between devices: 35.2 us -> 32.1 us
  Pallas kernels: 35.6 us -> 38.1 us
    pallas_call x0 -> x1, Pallas kernels: none -> 5.26 us  [cross_call(): pl.pallas_call(functools.partial(cross_kernel, 1.0 / math.sqrt(rows_all),...]
    ppermute x30 -> x29, starting transfers between devices: 35.2 us -> 32.1 us  [over(): return lambda a: lax.ppermute(a, AXES, pairs)]
    pallas_call x1, Pallas kernels: 16.1 us -> 13.9 us  [front_call(): pl.pallas_call(functools.partial(front_kernel, 1.0 / math.sqrt(d), 1.0 /...]
    ppermute x30 -> x29, waiting for transfers between devices: 27 us -> 27.5 us  [over(): return lambda a: lax.ppermute(a, AXES, pairs)]
  transfers between devices with their start and end apart: 30 -> 29, of which waited for: 10 -> 8; matrix products, arithmetic and copies ran while one was open for 1% -> 1% of each run, Pallas kernels for 17% -> 22%
where the time goes in v7:
time: 99.8 us; the launch traced here: 99.7 us
  Pallas kernels  38.1 us (38%)
  starting transfers between devices  32.1 us (32%)
  waiting for transfers between devices  27.5 us (28%)
  between operations  1.09 us (1%)
    ppermute x29, starting transfers between devices, over(): return lambda a: lax.ppermute(a, AXES, pairs)  32.1 us
    ppermute x29, waiting for transfers between devices, over(): return lambda a: lax.ppermute(a, AXES, pairs)  27.5 us
    pallas_call x1, Pallas kernels, front_call(): pl.pallas_call(functools.partial(front_kernel, 1.0 / math.sqrt(d), 1.0 /...  13.9 us
    pallas_call x1, Pallas kernels, factor_call(): pl.pallas_call(functools.partial(factor_kernel, line), in_specs=[SMEM_SPE...  11.4 us
    pallas_call x1, Pallas kernels, cross_call(): pl.pallas_call(functools.partial(cross_kernel, 1.0 / math.sqrt(rows_all),...  5.26 us
    pallas_call x2, Pallas kernels, project_call(): pl.pallas_call(functools.partial(project_kernel, line, is_own), in_specs=...  4.86 us
    pallas_call x1, Pallas kernels, basis_call(): pl.pallas_call(basis_kernel, grid=(rows // block,), in_specs=[pl.BlockSpe...  2.64 us
  transfers between devices with their start and end apart: 29, of which 8 were waited for; matrix products, arithmetic and copies ran while one was open for 1% of the time, Pallas kernels for 22%

profile of v7, /device:TPU:0, one launch (start us, length us, event | category | flops | bytes accessed | tf_op | source)
XLA Modules:
  0.0 99.7 jit_solution(17049786023412455821)
XLA Ops:
  0.6 0.1 pad_add_fusion.info
  0.7 13.9 %front.1 = (f32[2048,256]{1,0:T(8,128)S(1)}, bf16[256,2048]{1,0:T(8,128)(2,1)S(1)}, f32[128,256]{1,0:T(8,128)S(1)}, f32[128,256]{1,0:T(8,128)S(1)}, f32[1536,256]{1,0:T(8,128)S(1)}, /*index=5*/f32[512,256]{1,0:T(8,128)S(1)}) custom-call(s32[3]{0:T(128)S(1)} %pad_add_fusion.info, bf16[2048,4096]{1,0:T(8,128)(2,1)} %e.3, s32[4096,256]{1,0:T(8,128)} %signs.1), custom_call_target="tpu_custom_call" | custom-call | flops 6442450944 | bytes 20971520 | tf_op jit(solution)/shard_map/front/pallas_call | solution.py:130
  14.6 0.5 collective-permute-start
  15.2 0.1 collective-permute-start.5
  15.2 0.4 collective-permute-start.4
  15.7 5.3 %cross.1 = (f32[1536,256]{1,0:T(8,128)S(1)}, f32[512,256]{1,0:T(8,128)S(1)}) custom-call(s32[3]{0:T(128)S(1)} %pad_add_fusion.info, bf16[2048,4096]{1,0:T(8,128)(2,1)} %e.3, bf16[256,2048]{1,0:T(8,128)(2,1)S(1)} %get-tuple-element.45.rounded_t), custom_call_target="tpu_custom_call" | custom-call | flops 2147483648 | bytes 8388608 | tf_op jit(solution)/shard_map/cross/pallas_call | solution.py:176
  20.9 0.0 collective-permute-done.5
  21.0 0.2 slice_add_fusion
  21.2 2.6 %collective-permute-start.1 = (f32[384,256]{1,0:T(8,128)S(1)}, f32[384,256]{1,0:T(8,128)S(1)}, u32[]{:S(2)}, u32[]{:S(2)}) collective-permute-start(f32[384,256]{1,0:T(8,128)S(1)} %get-tuple-element.49), channel_id=1, source_target_pairs={{0,2},{1,3},{2,0},{3,1},{4,6},{5,7},{6,4},{7,5},{8,10},{9,11},{10,... | collective-permute-start | bytes 1179656 | tf_op jit(solution)/shard_map/ppermute | solution.py:369
  23.8 1.5 %collective-permute-start.2 = (f32[384,256]{1,0:T(8,128)S(1)}, f32[384,256]{1,0:T(8,128)S(1)}, u32[]{:S(2)}, u32[]{:S(2)}) collective-permute-start(f32[384,256]{1,0:T(8,128)S(1)} %get-tuple-element.50), channel_id=1, source_target_pairs={{0,4},{1,5},{2,6},{3,7},{4,0},{5,1},{6,2},{7,3},{8,12},{9,13},{10,... | collective-permute-start | bytes 1179656 | tf_op jit(solution)/shard_map/ppermute | solution.py:369
  25.4 0.0 collective-permute-start.3
  25.4 0.1 slice_add_fusion.4
  25.5 2.1 %collective-permute-start.9 = (f32[160,256]{1,0:T(8,128)S(1)}, f32[160,256]{1,0:T(8,128)S(1)}, u32[]{:S(2)}, u32[]{:S(2)}) collective-permute-start(f32[160,256]{1,0:T(8,128)S(1)} %get-tuple-element.62), channel_id=1, source_target_pairs={{0,8},{1,9},{2,10},{3,11},{4,12},{5,13},{6,14},{7,15},{8,0},{9,1},... | collective-permute-start | bytes 491528 | tf_op jit(solution)/shard_map/ppermute | solution.py:369
  27.6 2.6 %collective-permute-start.10 = (f32[160,256]{1,0:T(8,128)S(1)}, f32[160,256]{1,0:T(8,128)S(1)}, u32[]{:S(2)}, u32[]{:S(2)}) collective-permute-start(f32[160,256]{1,0:T(8,128)S(1)} %get-tuple-element.63), channel_id=1, source_target_pairs={{0,16},{1,17},{2,18},{3,19},{4,20},{5,21},{6,22},{7,23},{8,24},{9,... | collective-permute-start | bytes 491528 | tf_op jit(solution)/shard_map/ppermute | solution.py:369
  30.2 3.6 %collective-permute-done.1 = f32[384,256]{1,0:T(8,128)S(1)} collective-permute-done((f32[384,256]{1,0:T(8,128)S(1)}, f32[384,256]{1,0:T(8,128)S(1)}, u32[]{:S(2)}, u32[]{:S(2)}) %collective-permute-start.1) | collective-permute-done | bytes 393248 | tf_op jit(solution)/shard_map/ppermute | solution.py:369
  33.8 4.1 %collective-permute-start.11 = (f32[160,256]{1,0:T(8,128)S(1)}, f32[160,256]{1,0:T(8,128)S(1)}, u32[]{:S(2)}, u32[]{:S(2)}) collective-permute-start(f32[160,256]{1,0:T(8,128)S(1)} %get-tuple-element.56), channel_id=1, source_target_pairs={{0,24},{1,25},{2,26},{3,27},{4,28},{5,29},{6,30},{7,31},{8,16},{9,... | collective-permute-start | bytes 491528 | tf_op jit(solution)/shard_map/ppermute | solution.py:369
  37.9 5.6 %collective-permute-done.2 = f32[384,256]{1,0:T(8,128)S(1)} collective-permute-done((f32[384,256]{1,0:T(8,128)S(1)}, f32[384,256]{1,0:T(8,128)S(1)}, u32[]{:S(2)}, u32[]{:S(2)}) %collective-permute-start.2) | collective-permute-done | bytes 393248 | tf_op jit(solution)/shard_map/ppermute | solution.py:369
  43.5 0.1 add_add_fusion
  43.6 1.6 %collective-permute-start.6 = (f32[96,256]{1,0:T(8,128)S(1)}, f32[96,256]{1,0:T(8,128)S(1)}, u32[]{:S(2)}, u32[]{:S(2)}) collective-permute-start(f32[96,256]{1,0:T(8,128)S(1)} %get-tuple-element.58), channel_id=1, source_target_pairs={{0,8},{1,9},{2,10},{3,11},{4,12},{5,13},{6,14},{7,15},{8,0},{9,1},... | collective-permute-start | bytes 294920 | tf_op jit(solution)/shard_map/ppermute | solution.py:369
  45.2 2.6 %collective-permute-start.7 = (f32[96,256]{1,0:T(8,128)S(1)}, f32[96,256]{1,0:T(8,128)S(1)}, u32[]{:S(2)}, u32[]{:S(2)}) collective-permute-start(f32[96,256]{1,0:T(8,128)S(1)} %get-tuple-element.59), channel_id=1, source_target_pairs={{0,16},{1,17},{2,18},{3,19},{4,20},{5,21},{6,22},{7,23},{8,24},{9,... | collective-permute-start | bytes 294920 | tf_op jit(solution)/shard_map/ppermute | solution.py:369
  47.8 0.2 collective-permute-start.8
  48.1 1.6 %collective-permute-start.14 = (f32[160,256]{1,0:T(8,128)S(1)}, f32[160,256]{1,0:T(8,128)S(1)}, u32[]{:S(2)}, u32[]{:S(2)}) collective-permute-start(f32[160,256]{1,0:T(8,128)S(1)} %add_add_fusion.2), channel_id=1, source_target_pairs={{0,6},{1,7},{2,4},{3,5},{4,2},{5,3},{6,0},{7,1},{8,14},{9,15},{10,... | collective-permute-start | bytes 491528 | tf_op jit(solution)/shard_map/ppermute | solution.py:369
  49.7 1.2 %collective-permute-start.13 = (f32[160,256]{1,0:T(8,128)S(1)}, f32[160,256]{1,0:T(8,128)S(1)}, u32[]{:S(2)}, u32[]{:S(2)}) collective-permute-start(f32[160,256]{1,0:T(8,128)S(1)} %add_add_fusion.2), channel_id=1, source_target_pairs={{0,4},{1,5},{2,6},{3,7},{4,0},{5,1},{6,2},{7,3},{8,12},{9,13},{10,... | collective-permute-start | bytes 491528 | tf_op jit(solution)/shard_map/ppermute | solution.py:369
  50.9 0.8 collective-permute-start.12
  51.7 3.6 %collective-permute-done.7 = f32[96,256]{1,0:T(8,128)S(1)} collective-permute-done((f32[96,256]{1,0:T(8,128)S(1)}, f32[96,256]{1,0:T(8,128)S(1)}, u32[]{:S(2)}, u32[]{:S(2)}) %collective-permute-start.7) | collective-permute-done | bytes 98336 | tf_op jit(solution)/shard_map/ppermute | solution.py:369
  55.3 0.4 collective-permute-done.14
  55.7 1.6 %collective-permute-done.13 = f32[160,256]{1,0:T(8,128)S(1)} collective-permute-done((f32[160,256]{1,0:T(8,128)S(1)}, f32[160,256]{1,0:T(8,128)S(1)}, u32[]{:S(2)}, u32[]{:S(2)}) %collective-permute-start.13) | collective-permute-done | bytes 163872 | tf_op jit(solution)/shard_map/ppermute | solution.py:369
  57.5 0.7 collective-permute-start.18
  58.1 3.0 %collective-permute-start.17 = (f32[128,256]{1,0:T(8,128)S(1)}, f32[128,256]{1,0:T(8,128)S(1)}, u32[]{:S(2)}, u32[]{:S(2)}) collective-permute-start(f32[128,256]{1,0:T(8,128)S(1)} %pad_maximum_fusion.7), channel_id=1, source_target_pairs={{0,24},{1,25},{2,26},{3,27},{4,28},{5,29},{6,30},{7,31},{8,16},{9,... | collective-permute-start | bytes 393224 | tf_op jit(solution)/shard_map/ppermute | solution.py:369
  61.2 0.5 collective-permute-start.16
  61.6 0.9 collective-permute-start.15
  62.6 5.7 %collective-permute-done.17 = f32[128,256]{1,0:T(8,128)S(1)} collective-permute-done((f32[128,256]{1,0:T(8,128)S(1)}, f32[128,256]{1,0:T(8,128)S(1)}, u32[]{:S(2)}, u32[]{:S(2)}) %collective-permute-start.17) | collective-permute-done | bytes 131104 | tf_op jit(solution)/shard_map/ppermute | solution.py:369
  68.3 4.3 %collective-permute-done.16 = f32[128,256]{1,0:T(8,128)S(1)} collective-permute-done((f32[128,256]{1,0:T(8,128)S(1)}, f32[128,256]{1,0:T(8,128)S(1)}, u32[]{:S(2)}, u32[]{:S(2)}) %collective-permute-start.16) | collective-permute-done | bytes 131104 | tf_op jit(solution)/shard_map/ppermute | solution.py:369
  72.7 0.1 collective-permute-start.19
  72.8 1.5 %collective-permute-start.23 = (f32[384,256]{1,0:T(8,128)S(1)}, f32[384,256]{1,0:T(8,128)S(1)}, u32[]{:S(2)}, u32[]{:S(2)}) collective-permute-start(f32[384,256]{1,0:T(8,128)S(1)} %pad_maximum_fusion.1.refs_0_), channel_id=1, source_target_pairs={{0,6},{1,7},{2,4},{3,5},{4,2},{5,3},{6,0},{7,1},{8,14},{9,15},{10,... | collective-permute-start | bytes 1179656 | tf_op jit(solution)/shard_map/ppermute | solution.py:369
  74.2 1.6 %collective-permute-start.22 = (f32[384,256]{1,0:T(8,128)S(1)}, f32[384,256]{1,0:T(8,128)S(1)}, u32[]{:S(2)}, u32[]{:S(2)}) collective-permute-start(f32[384,256]{1,0:T(8,128)S(1)} %pad_maximum_fusion.1.refs_0_), channel_id=1, source_target_pairs={{0,4},{1,5},{2,6},{3,7},{4,0},{5,1},{6,2},{7,3},{8,12},{9,13},{10,... | collective-permute-start | bytes 1179656 | tf_op jit(solution)/shard_map/ppermute | solution.py:369
  75.8 0.5 collective-permute-start.21
  76.4 0.3 collective-permute-start.20
  76.6 11.4 %factor.1 = (f32[256,256]{1,0:T(8,128)}, bf16[512,256]{1,0:T(8,128)(2,1)S(1)}) custom-call(s32[3]{0:T(128)S(1)} %pad_add_fusion.info, f32[128,256]{1,0:T(8,128)S(1)} %pad_maximum_fusion.8.kept, f32[128,256]{1,0:T(8,128)S(1)} %collective-permute-done.19.got), custom_call_target="tpu_custom_call" | custom-call | flops 10000000000 | bytes 524288 | tf_op jit(solution)/shard_map/factor/pallas_call | solution.py:274
  88.1 2.6 %collective-permute-done.20 = f32[256,256]{1,0:T(8,128)S(1)} collective-permute-done((f32[256,256]{1,0:T(8,128)S(1)}, f32[256,256]{1,0:T(8,128)S(1)}, u32[]{:S(2)}, u32[]{:S(2)}) %collective-permute-start.20) | collective-permute-done | bytes 262176 | tf_op jit(solution)/shard_map/ppermute | solution.py:369
  90.7 0.1 collective-permute-start.28
  90.8 0.5 collective-permute-start.24
  91.3 2.6 %basis.1 = bf16[2048,256]{1,0:T(8,128)(2,1)} custom-call(f32[2048,256]{1,0:T(8,128)S(1)} %get-tuple-element.81.sketch, bf16[512,256]{1,0:T(8,128)(2,1)S(1)} %get-tuple-element.82.inverse), custom_call_target="tpu_custom_call" | custom-call | flops 805306368 | bytes 3145728 | tf_op jit(solution)/shard_map/basis/pallas_call | solution.py:300
  94.0 0.1 collective-permute-start.25
  94.1 0.4 collective-permute-start.26
  94.5 0.1 collective-permute-start.27
  94.6 2.4 %project.2.refs_0_ = f32[256,4096]{1,0:T(8,128)} custom-call(s32[3]{0:T(128)S(1)} %pad_add_fusion.info, bf16[512,256]{1,0:T(8,128)(2,1)S(1)} %get-tuple-element.82.inverse, f32[384,256]{1,0:T(8,128)S(1)} %pad_maximum_fusion.1.refs_0_, f32[384,256]{1,0:T(8,128)S(1)} %collective-permute-done.21.refs_1_, f32[384,256]{1,0:T(8,128)S(1)} %collective-permute-done.22.refs_2_, ...), custom_call_target="tpu_custom_call" | custom-call | flops 805306368 | bytes 4194304 | tf_op jit(solution)/shard_map/project/pallas_call | solution.py:346
  97.1 2.4 %project.3 = f32[256,4096]{1,0:T(8,128)} custom-call(s32[3]{0:T(128)S(1)} %pad_add_fusion.info, bf16[512,256]{1,0:T(8,128)(2,1)S(1)} %get-tuple-element.82.inverse, f32[256,4096]{1,0:T(8,128)} %project.2.refs_0_, f32[384,256]{1,0:T(8,128)S(1)} %collective-permute-done.24.refs_1_, ...), custom_call_target="tpu_custom_call", output_to_operand_aliasing={{}: (2, {})} | custom-call | flops 805306368 | bytes 4194304 | tf_op jit(solution)/shard_map/project/pallas_call | solution.py:346
  (43 shorter events, 0.4 us)
Async XLA Ops:
  14.6 6.4 %collective-permute-start = (f32[1536,256]{1,0:T(8,128)S(1)}, f32[1536,256]{1,0:T(8,128)S(1)}, u32[]{:S(2)}, u32[]{:S(2)}) collective-permute-start(f32[1536,256]{1,0:T(8,128)S(1)} %get-tuple-element.47), channel_id=1, source_target_pairs={{0,1},{1,0},{2,3},{3,2},{4,5},{5,4},{6,7},{7,6},{8,9},{9,8},{10,11... | collective-permute-start | bytes 4718600 | tf_op jit(solution)/shard_map/ppermute | solution.py:369
  15.2 5.8 %collective-permute-start.5 = (f32[128,256]{1,0:T(8,128)S(1)}, f32[128,256]{1,0:T(8,128)S(1)}, u32[]{:S(2)}, u32[]{:S(2)}) collective-permute-start(f32[128,256]{1,0:T(8,128)S(1)} %get-tuple-element.55), channel_id=1, source_target_pairs={{0,1},{1,0},{2,3},{3,2},{4,5},{5,4},{6,7},{7,6},{8,9},{9,8},{10,11... | collective-permute-start | bytes 393224 | tf_op jit(solution)/shard_map/ppermute | solution.py:369
  15.2 10.2 %collective-permute-start.4 = (f32[512,256]{1,0:T(8,128)S(1)}, f32[512,256]{1,0:T(8,128)S(1)}, u32[]{:S(2)}, u32[]{:S(2)}) collective-permute-start(f32[512,256]{1,0:T(8,128)S(1)} %get-tuple-element.53), channel_id=1, source_target_pairs={{0,1},{1,0},{2,3},{3,2},{4,5},{5,4},{6,7},{7,6},{8,9},{9,8},{10,11... | collective-permute-start | bytes 1572872 | tf_op jit(solution)/shard_map/ppermute | solution.py:369
  21.2 12.6 %collective-permute-start.1 = (f32[384,256]{1,0:T(8,128)S(1)}, f32[384,256]{1,0:T(8,128)S(1)}, u32[]{:S(2)}, u32[]{:S(2)}) collective-permute-start(f32[384,256]{1,0:T(8,128)S(1)} %get-tuple-element.49), channel_id=1, source_target_pairs={{0,2},{1,3},{2,0},{3,1},{4,6},{5,7},{6,4},{7,5},{8,10},{9,11},{10,... | collective-permute-start | bytes 1179656 | tf_op jit(solution)/shard_map/ppermute | solution.py:369
  23.8 19.6 %collective-permute-start.2 = (f32[384,256]{1,0:T(8,128)S(1)}, f32[384,256]{1,0:T(8,128)S(1)}, u32[]{:S(2)}, u32[]{:S(2)}) collective-permute-start(f32[384,256]{1,0:T(8,128)S(1)} %get-tuple-element.50), channel_id=1, source_target_pairs={{0,4},{1,5},{2,6},{3,7},{4,0},{5,1},{6,2},{7,3},{8,12},{9,13},{10,... | collective-permute-start | bytes 1179656 | tf_op jit(solution)/shard_map/ppermute | solution.py:369
  25.4 18.1 %collective-permute-start.3 = (f32[384,256]{1,0:T(8,128)S(1)}, f32[384,256]{1,0:T(8,128)S(1)}, u32[]{:S(2)}, u32[]{:S(2)}) collective-permute-start(f32[384,256]{1,0:T(8,128)S(1)} %get-tuple-element.51), channel_id=1, source_target_pairs={{0,6},{1,7},{2,4},{3,5},{4,2},{5,3},{6,0},{7,1},{8,14},{9,15},{10,... | collective-permute-start | bytes 1179656 | tf_op jit(solution)/shard_map/ppermute | solution.py:369
  25.5 22.3 %collective-permute-start.9 = (f32[160,256]{1,0:T(8,128)S(1)}, f32[160,256]{1,0:T(8,128)S(1)}, u32[]{:S(2)}, u32[]{:S(2)}) collective-permute-start(f32[160,256]{1,0:T(8,128)S(1)} %get-tuple-element.62), channel_id=1, source_target_pairs={{0,8},{1,9},{2,10},{3,11},{4,12},{5,13},{6,14},{7,15},{8,0},{9,1},... | collective-permute-start | bytes 491528 | tf_op jit(solution)/shard_map/ppermute | solution.py:369
  27.6 20.4 %collective-permute-start.10 = (f32[160,256]{1,0:T(8,128)S(1)}, f32[160,256]{1,0:T(8,128)S(1)}, u32[]{:S(2)}, u32[]{:S(2)}) collective-permute-start(f32[160,256]{1,0:T(8,128)S(1)} %get-tuple-element.63), channel_id=1, source_target_pairs={{0,16},{1,17},{2,18},{3,19},{4,20},{5,21},{6,22},{7,23},{8,24},{9,... | collective-permute-start | bytes 491528 | tf_op jit(solution)/shard_map/ppermute | solution.py:369
  33.8 14.2 %collective-permute-start.11 = (f32[160,256]{1,0:T(8,128)S(1)}, f32[160,256]{1,0:T(8,128)S(1)}, u32[]{:S(2)}, u32[]{:S(2)}) collective-permute-start(f32[160,256]{1,0:T(8,128)S(1)} %get-tuple-element.56), channel_id=1, source_target_pairs={{0,24},{1,25},{2,26},{3,27},{4,28},{5,29},{6,30},{7,31},{8,16},{9,... | collective-permute-start | bytes 491528 | tf_op jit(solution)/shard_map/ppermute | solution.py:369
  43.6 7.3 %collective-permute-start.6 = (f32[96,256]{1,0:T(8,128)S(1)}, f32[96,256]{1,0:T(8,128)S(1)}, u32[]{:S(2)}, u32[]{:S(2)}) collective-permute-start(f32[96,256]{1,0:T(8,128)S(1)} %get-tuple-element.58), channel_id=1, source_target_pairs={{0,8},{1,9},{2,10},{3,11},{4,12},{5,13},{6,14},{7,15},{8,0},{9,1},... | collective-permute-start | bytes 294920 | tf_op jit(solution)/shard_map/ppermute | solution.py:369
  45.2 10.0 %collective-permute-start.7 = (f32[96,256]{1,0:T(8,128)S(1)}, f32[96,256]{1,0:T(8,128)S(1)}, u32[]{:S(2)}, u32[]{:S(2)}) collective-permute-start(f32[96,256]{1,0:T(8,128)S(1)} %get-tuple-element.59), channel_id=1, source_target_pairs={{0,16},{1,17},{2,18},{3,19},{4,20},{5,21},{6,22},{7,23},{8,24},{9,... | collective-permute-start | bytes 294920 | tf_op jit(solution)/shard_map/ppermute | solution.py:369
  47.8 7.5 %collective-permute-start.8 = (f32[96,256]{1,0:T(8,128)S(1)}, f32[96,256]{1,0:T(8,128)S(1)}, u32[]{:S(2)}, u32[]{:S(2)}) collective-permute-start(f32[96,256]{1,0:T(8,128)S(1)} %get-tuple-element.60), channel_id=1, source_target_pairs={{0,24},{1,25},{2,26},{3,27},{4,28},{5,29},{6,30},{7,31},{8,16},{9,... | collective-permute-start | bytes 294920 | tf_op jit(solution)/shard_map/ppermute | solution.py:369
  48.1 7.6 %collective-permute-start.14 = (f32[160,256]{1,0:T(8,128)S(1)}, f32[160,256]{1,0:T(8,128)S(1)}, u32[]{:S(2)}, u32[]{:S(2)}) collective-permute-start(f32[160,256]{1,0:T(8,128)S(1)} %add_add_fusion.2), channel_id=1, source_target_pairs={{0,6},{1,7},{2,4},{3,5},{4,2},{5,3},{6,0},{7,1},{8,14},{9,15},{10,... | collective-permute-start | bytes 491528 | tf_op jit(solution)/shard_map/ppermute | solution.py:369
  49.7 7.7 %collective-permute-start.13 = (f32[160,256]{1,0:T(8,128)S(1)}, f32[160,256]{1,0:T(8,128)S(1)}, u32[]{:S(2)}, u32[]{:S(2)}) collective-permute-start(f32[160,256]{1,0:T(8,128)S(1)} %add_add_fusion.2), channel_id=1, source_target_pairs={{0,4},{1,5},{2,6},{3,7},{4,0},{5,1},{6,2},{7,3},{8,12},{9,13},{10,... | collective-permute-start | bytes 491528 | tf_op jit(solution)/shard_map/ppermute | solution.py:369
  50.9 6.5 %collective-permute-start.12 = (f32[160,256]{1,0:T(8,128)S(1)}, f32[160,256]{1,0:T(8,128)S(1)}, u32[]{:S(2)}, u32[]{:S(2)}) collective-permute-start(f32[160,256]{1,0:T(8,128)S(1)} %add_add_fusion.2), channel_id=1, source_target_pairs={{0,2},{1,3},{2,0},{3,1},{4,6},{5,7},{6,4},{7,5},{8,10},{9,11},{10,... | collective-permute-start | bytes 491528 | tf_op jit(solution)/shard_map/ppermute | solution.py:369
  57.5 5.1 %collective-permute-start.18 = (f32[128,256]{1,0:T(8,128)S(1)}, f32[128,256]{1,0:T(8,128)S(1)}, u32[]{:S(2)}, u32[]{:S(2)}) collective-permute-start(f32[128,256]{1,0:T(8,128)S(1)} %slice.153), channel_id=1, source_target_pairs={{0,8},{1,9},{2,10},{3,11},{4,12},{5,13},{6,14},{7,15},{8,0},{9,1},... | collective-permute-start | bytes 393224 | tf_op jit(solution)/shard_map/ppermute | solution.py:369
  58.1 10.1 %collective-permute-start.17 = (f32[128,256]{1,0:T(8,128)S(1)}, f32[128,256]{1,0:T(8,128)S(1)}, u32[]{:S(2)}, u32[]{:S(2)}) collective-permute-start(f32[128,256]{1,0:T(8,128)S(1)} %pad_maximum_fusion.7), channel_id=1, source_target_pairs={{0,24},{1,25},{2,26},{3,27},{4,28},{5,29},{6,30},{7,31},{8,16},{9,... | collective-permute-start | bytes 393224 | tf_op jit(solution)/shard_map/ppermute | solution.py:369
  61.2 11.4 %collective-permute-start.16 = (f32[128,256]{1,0:T(8,128)S(1)}, f32[128,256]{1,0:T(8,128)S(1)}, u32[]{:S(2)}, u32[]{:S(2)}) collective-permute-start(f32[128,256]{1,0:T(8,128)S(1)} %pad_maximum_fusion.7), channel_id=1, source_target_pairs={{0,16},{1,17},{2,18},{3,19},{4,20},{5,21},{6,22},{7,23},{8,24},{9,... | collective-permute-start | bytes 393224 | tf_op jit(solution)/shard_map/ppermute | solution.py:369
  61.6 10.9 %collective-permute-start.15 = (f32[128,256]{1,0:T(8,128)S(1)}, f32[128,256]{1,0:T(8,128)S(1)}, u32[]{:S(2)}, u32[]{:S(2)}) collective-permute-start(f32[128,256]{1,0:T(8,128)S(1)} %pad_maximum_fusion.7), channel_id=1, source_target_pairs={{0,8},{1,9},{2,10},{3,11},{4,12},{5,13},{6,14},{7,15},{8,0},{9,1},... | collective-permute-start | bytes 393224 | tf_op jit(solution)/shard_map/ppermute | solution.py:369
  72.7 3.6 %collective-permute-start.19 = (f32[128,256]{1,0:T(8,128)S(1)}, f32[128,256]{1,0:T(8,128)S(1)}, u32[]{:S(2)}, u32[]{:S(2)}) collective-permute-start(f32[128,256]{1,0:T(8,128)S(1)} %pad_maximum_fusion.8.kept), channel_id=1, source_target_pairs={{0,1},{1,0},{2,3},{3,2},{4,5},{5,4},{6,7},{7,6},{8,9},{9,8},{10,11... | collective-permute-start | bytes 393224 | tf_op jit(solution)/shard_map/ppermute | solution.py:369
  72.8 21.2 %collective-permute-start.23 = (f32[384,256]{1,0:T(8,128)S(1)}, f32[384,256]{1,0:T(8,128)S(1)}, u32[]{:S(2)}, u32[]{:S(2)}) collective-permute-start(f32[384,256]{1,0:T(8,128)S(1)} %pad_maximum_fusion.1.refs_0_), channel_id=1, source_target_pairs={{0,6},{1,7},{2,4},{3,5},{4,2},{5,3},{6,0},{7,1},{8,14},{9,15},{10,... | collective-permute-start | bytes 1179656 | tf_op jit(solution)/shard_map/ppermute | solution.py:369
  74.2 19.7 %collective-permute-start.22 = (f32[384,256]{1,0:T(8,128)S(1)}, f32[384,256]{1,0:T(8,128)S(1)}, u32[]{:S(2)}, u32[]{:S(2)}) collective-permute-start(f32[384,256]{1,0:T(8,128)S(1)} %pad_maximum_fusion.1.refs_0_), channel_id=1, source_target_pairs={{0,4},{1,5},{2,6},{3,7},{4,0},{5,1},{6,2},{7,3},{8,12},{9,13},{10,... | collective-permute-start | bytes 1179656 | tf_op jit(solution)/shard_map/ppermute | solution.py:369
  75.8 18.1 %collective-permute-start.21 = (f32[384,256]{1,0:T(8,128)S(1)}, f32[384,256]{1,0:T(8,128)S(1)}, u32[]{:S(2)}, u32[]{:S(2)}) collective-permute-start(f32[384,256]{1,0:T(8,128)S(1)} %pad_maximum_fusion.1.refs_0_), channel_id=1, source_target_pairs={{0,2},{1,3},{2,0},{3,1},{4,6},{5,7},{6,4},{7,5},{8,10},{9,11},{10,... | collective-permute-start | bytes 1179656 | tf_op jit(solution)/shard_map/ppermute | solution.py:369
  76.4 14.3 %collective-permute-start.20 = (f32[256,256]{1,0:T(8,128)S(1)}, f32[256,256]{1,0:T(8,128)S(1)}, u32[]{:S(2)}, u32[]{:S(2)}) collective-permute-start(f32[256,256]{1,0:T(8,128)S(1)} %pad_maximum_fusion.2), channel_id=1, source_target_pairs={{0,16},{1,17},{2,18},{3,19},{4,20},{5,21},{6,22},{7,23},{8,24},{9,... | collective-permute-start | bytes 786440 | tf_op jit(solution)/shard_map/ppermute | solution.py:369
  90.7 6.4 %collective-permute-start.28 = (f32[512,256]{1,0:T(8,128)S(1)}, f32[512,256]{1,0:T(8,128)S(1)}, u32[]{:S(2)}, u32[]{:S(2)}) collective-permute-start(f32[512,256]{1,0:T(8,128)S(1)} %pad_maximum_fusion.refs_4_), channel_id=1, source_target_pairs={{0,1},{1,0},{2,3},{3,2},{4,5},{5,4},{6,7},{7,6},{8,9},{9,8},{10,11... | collective-permute-start | bytes 1572872 | tf_op jit(solution)/shard_map/ppermute | solution.py:369
  90.8 6.2 %collective-permute-start.24 = (f32[384,256]{1,0:T(8,128)S(1)}, f32[384,256]{1,0:T(8,128)S(1)}, u32[]{:S(2)}, u32[]{:S(2)}) collective-permute-start(f32[384,256]{1,0:T(8,128)S(1)} %pad_maximum_fusion.1.refs_0_), channel_id=1, source_target_pairs={{0,1},{1,0},{2,3},{3,2},{4,5},{5,4},{6,7},{7,6},{8,9},{9,8},{10,11... | collective-permute-start | bytes 1179656 | tf_op jit(solution)/shard_map/ppermute | solution.py:369
  94.0 3.1 %collective-permute-start.25 = (f32[384,256]{1,0:T(8,128)S(1)}, f32[384,256]{1,0:T(8,128)S(1)}, u32[]{:S(2)}, u32[]{:S(2)}) collective-permute-start(f32[384,256]{1,0:T(8,128)S(1)} %collective-permute-done.21.refs_1_), channel_id=1, source_target_pairs={{0,1},{1,0},{2,3},{3,2},{4,5},{5,4},{6,7},{7,6},{8,9},{9,8},{10,11... | collective-permute-start | bytes 1179656 | tf_op jit(solution)/shard_map/ppermute | solution.py:369
  94.1 3.0 %collective-permute-start.26 = (f32[384,256]{1,0:T(8,128)S(1)}, f32[384,256]{1,0:T(8,128)S(1)}, u32[]{:S(2)}, u32[]{:S(2)}) collective-permute-start(f32[384,256]{1,0:T(8,128)S(1)} %collective-permute-done.22.refs_2_), channel_id=1, source_target_pairs={{0,1},{1,0},{2,3},{3,2},{4,5},{5,4},{6,7},{7,6},{8,9},{9,8},{10,11... | collective-permute-start | bytes 1179656 | tf_op jit(solution)/shard_map/ppermute | solution.py:369
  94.5 2.5 %collective-permute-start.27 = (f32[384,256]{1,0:T(8,128)S(1)}, f32[384,256]{1,0:T(8,128)S(1)}, u32[]{:S(2)}, u32[]{:S(2)}) collective-permute-start(f32[384,256]{1,0:T(8,128)S(1)} %collective-permute-done.23.refs_3_), channel_id=1, source_target_pairs={{0,1},{1,0},{2,3},{3,2},{4,5},{5,4},{6,7},{7,6},{8,9},{9,8},{10,11... | collective-permute-start | bytes 1179656 | tf_op jit(solution)/shard_map/ppermute | solution.py:369

commit v8 on v6

--- a/solution.py
+++ b/solution.py
@@ -142,7 +142,7 @@
     )(info, e, pltpu.with_memory_space_constraint(signs, pltpu.HBM))
 
 
-def factor_kernel(line, info, kept, got, triangle, high, low, work):
+def factor_kernel(line, info, kept, got, triangle, inverse, work):
     k = triangle.shape[0]
     half = k // 2
     b = 64
@@ -162,7 +162,6 @@
         return jnp.broadcast_to(a[:, at : at + 1], (8, 2 * b))
 
     for n in range(k // b):
-        put = slice(n * b, (n + 1) * b)
         first = (n % 2) * b
         pair = (n // 2) * 2 * b
         own_lanes = (lane >= first) & (lane < first + b)
@@ -200,22 +199,29 @@
             moved = pltpu.roll(new * (1.0 / jnp.sqrt(pivots)), b, 1)
             inv.append(jnp.where(own_lanes, moved, 0.0))
         inv = jnp.concatenate(inv, axis=0)
+        end = k + pair + 2 * b
         y = lax.dot_general(
-            inv, work[pair : pair + 2 * b, :], (((1,), (0,)), ((), ())),
+            inv, work[pair : pair + 2 * b, pair:end], (((1,), (0,)), ((), ())),
             precision=lax.Precision.HIGHEST, preferred_element_type=jnp.float32,
         )
-        r_rows, i_rows = y[:, :k], y[:, k:]
-        at = lax.broadcasted_iota(jnp.int32, (b, k), 0) + n * b
-        to = lax.broadcasted_iota(jnp.int32, (b, k), 1)
-        triangle[put, :] = jnp.where(to >= at, r_rows, 0.0)
-        i_rows = jnp.where(to <= at, i_rows, 0.0)
-        i_high, i_low = split(i_rows)
-        high[put, :] = i_high
-        low[put, :] = i_low
+        r_rows, i_rows = y[:, : k - pair], y[:, k - pair :]
+        at = lax.broadcasted_iota(jnp.int32, r_rows.shape, 0) + n * b
+        to = lax.broadcasted_iota(jnp.int32, r_rows.shape, 1) + pair
+        put = slice(n * b, (n + 1) * b)
+        if pair:
+            triangle[put, :pair] = jnp.zeros((b, pair), jnp.float32)
+        triangle[put, pair:] = jnp.where(to >= at, r_rows, 0.0)
+        i_at = lax.broadcasted_iota(jnp.int32, i_rows.shape, 0) + n * b
+        i_to = lax.broadcasted_iota(jnp.int32, i_rows.shape, 1)
+        for row, part in zip((n * b, k + n * b), split(jnp.where(i_to <= i_at, i_rows, 0.0))):
+            inverse[row : row + b, : pair + 2 * b] = part
+            if pair + 2 * b < k:
+                inverse[row : row + b, pair + 2 * b :] = jnp.zeros((b, k - pair - 2 * b), part.dtype)
         if (n + 1) * b < k:
-            later = jnp.where(to >= (n + 1) * b, r_rows, 0.0)
-            work[...] -= lax.dot_general(
-                later, y, (((0,), (0,)), ((), ())),
+            rest = (n + 1) // 2 * 2 * b
+            later = jnp.where(to >= (n + 1) * b, r_rows, 0.0)[:, rest - pair :]
+            work[rest:, rest:end] -= lax.dot_general(
+                later, y[:, rest - pair :], (((0,), (0,)), ((), ())),
                 precision=lax.Precision.HIGHEST, preferred_element_type=jnp.float32,
             )
 
@@ -225,11 +231,10 @@
     return pl.pallas_call(
         functools.partial(factor_kernel, line),
         in_specs=[SMEM_SPEC, VMEM_SPEC, VMEM_SPEC],
-        out_specs=[VMEM_SPEC] * 3,
+        out_specs=[VMEM_SPEC] * 2,
         out_shape=[
             jax.ShapeDtypeStruct((k, k), jnp.float32),
-            jax.ShapeDtypeStruct((k, k), jnp.bfloat16),
-            jax.ShapeDtypeStruct((k, k), jnp.bfloat16),
+            jax.ShapeDtypeStruct((2 * k, k), jnp.bfloat16),
         ],
         scratch_shapes=[pltpu.VMEM((k, 2 * k), jnp.float32)],
         compiler_params=pltpu.CompilerParams(vmem_limit_bytes=16 * MIB),
@@ -238,33 +243,33 @@
     )(info, kept, got)
 
 
-def basis_kernel(sketch, high, low, out):
+def basis_kernel(sketch, inverse, out):
+    k = sketch.shape[1]
     s_high, s_low = split(sketch[...])
     right = ((1,), (1,))
-    out[...] = (
-        dot(s_high, high[...], right) + (dot(s_high, low[...], right) + dot(s_low, high[...], right))
-    ).astype(out.dtype)
-
-
-def basis_call(sketch, high, low):
+    both = dot(s_high, inverse[...], right)
+    out[...] = (both[:, :k] + (both[:, k:] + dot(s_low, inverse[:k, :], right))).astype(out.dtype)
+
+
+def basis_call(sketch, inverse):
     rows, k = sketch.shape
     block = rows // 4
     return pl.pallas_call(
         basis_kernel,
         grid=(rows // block,),
-        in_specs=[pl.BlockSpec((block, k), lambda i: (i, 0))] + [pl.BlockSpec((k, k), lambda i: (0, 0))] * 2,
+        in_specs=[pl.BlockSpec((block, k), lambda i: (i, 0)), pl.BlockSpec((2 * k, k), lambda i: (0, 0))],
         out_specs=pl.BlockSpec((block, k), lambda i: (i, 0)),
         out_shape=jax.ShapeDtypeStruct((rows, k), jnp.bfloat16),
         compiler_params=pltpu.CompilerParams(vmem_limit_bytes=16 * MIB),
         cost_estimate=pl.CostEstimate(flops=6 * rows * k * k, bytes_accessed=rows * k * 6, transcendentals=0),
         name="basis",
-    )(sketch, high, low)
-
-
-def project_kernel(line, is_own, info, high, low, *refs):
+    )(sketch, inverse)
+
+
+def project_kernel(line, is_own, info, inverse, *refs):
     *blocks, out, whole, value, sem = refs
     class1, class2 = blocks[-PLANE - 1 : -1], blocks[-1]
-    k = high.shape[0]
+    k = inverse.shape[1]
     rows1, rows2 = row_classes(k, line)
     size1, size2 = rows1 // line, rows2 // line
     own, in_plane, in_line = info[0], info[1], info[2]
@@ -282,7 +287,8 @@
                 at2 = pl.ds(pl.multiple_of(((g * PLANE + (in_plane ^ p)) * 2 + h) * size2, 8), size2)
                 whole[p, to2, cols] = class2[at2, :]
         c_high, c_low = split(whole[p])
-        value[p] = dot(high[...], c_high) + (dot(high[...], c_low) + dot(low[...], c_high))
+        both = dot(inverse[...], c_high)
+        value[p] = both[:k] + (both[k:] + dot(inverse[:k, :], c_low))
         at = pl.ds(pl.multiple_of((region * PLANE + (in_plane ^ p)) * width, width), width)
         copies.append(pltpu.make_async_copy(value.at[p], out.at[:, at], sem.at[p]))
         copies[-1].start()
@@ -290,16 +296,16 @@
         copy.wait()
 
 
-def project_call(line, is_own, info, high, low, blocks, d, before):
-    k = high.shape[0]
+def project_call(line, is_own, info, inverse, blocks, d, before):
+    k = inverse.shape[1]
     width = d // (2 * PLANE)
     extra = [] if before is None else [before]
     return pl.pallas_call(
         functools.partial(project_kernel, line, is_own),
-        in_specs=[SMEM_SPEC, VMEM_SPEC, VMEM_SPEC] + [ANY_SPEC] * len(extra) + [VMEM_SPEC] * len(blocks),
+        in_specs=[SMEM_SPEC, VMEM_SPEC] + [ANY_SPEC] * len(extra) + [VMEM_SPEC] * len(blocks),
         out_specs=ANY_SPEC,
         out_shape=jax.ShapeDtypeStruct((k, d), jnp.float32),
-        input_output_aliases={3: 0} if extra else {},
+        input_output_aliases={2: 0} if extra else {},
         scratch_shapes=[
             pltpu.VMEM((PLANE, k, width), jnp.float32),
             pltpu.VMEM((PLANE, k, width), jnp.float32),
@@ -308,7 +314,7 @@
         compiler_params=pltpu.CompilerParams(vmem_limit_bytes=16 * MIB),
         cost_estimate=pl.CostEstimate(flops=3 * k * k * d, bytes_accessed=k * d * 4, transcendentals=0),
         name="project",
-    )(info, *pinned(high, low), *extra, *pinned(*blocks))
+    )(info, *pinned(inverse), *extra, *pinned(*blocks))
 
 
 def solution(mesh):
@@ -352,31 +358,32 @@
         parts2 = [join(a + b, g) for a, b, g in zip(parts_of(kept2, line), parts_of(got2, line), grams)]
         parts2 = in_turn(*parts2)
         from_line = [over_line[g](parts2[g]) for g in range(1, line)]
+        parts1 = in_turn(*parts_of(sum(from_plane, parts1[0]), line))
         a2 = sum(from_line, parts2[0])
-        parts1 = in_turn(*parts_of(sum(from_plane, parts1[0]), line))
         from_line = [over_line[g](parts1[g]) for g in range(1, line)]
         a2 = in_turn(a2)
         whole2 = [over_plane[g](a2) for g in range(1, PLANE)]
         a2 = (a2 + whole2[0]) + (whole2[1] + whole2[2])
         n2 = a2.shape[0] - gram.shape[0] // line
-        a1 = in_turn(join(sum(from_line, parts1[0]), a2[n2:]))
+        a1 = join(sum(from_line, parts1[0]), a2[n2:])
+        near, a1, a2 = in_turn(join(a1, a2[:n2]), a1, a2[:n2])
+        near = over_line[1](near)
+        gathered = [a1, near[: a1.shape[0]]] + [over_line[g](a1) for g in range(2, line)]
+        class2 = join(a2, near[a1.shape[0] :])
         n1 = a1.shape[0] - gram.shape[0] // line
-        gathered = [a1] + [over_line[g](a1) for g in range(1, line)]
-        a2 = in_turn(a2[:n2])
-        near = over_line[1](a2)
         a1 = in_turn(join(*[a[:n1] for a in gathered]))
-        class1 = [a1] + [over_plane[g](a1) for g in range(1, PLANE)]
+        class1 = [over_plane[g](a1) for g in range(1, PLANE)]
         gram = in_turn(join(*[a[n1:] for a in gathered]))
-        gram_got = with_pair(gram)
-        gram_got, a2_later = in_turn(gram_got, a2)
-        class2 = [a2, near] + [over_line[g](a2_later) for g in range(2, line)]
-        triangle, high, low = factor_call(line, info, in_turn(gram), gram_got)
-        high = in_turn(high)
-        *class1, class2 = in_turn(*class1, join(*class2))
-        theirs = [with_pair(a) for a in (*class1, class2)]
-        basis = in_turn(basis_call(in_turn(sketch), high, low))
-        projected = project_call(line, True, info, high, low, [*class1, class2], d, None)
-        projected = project_call(line, False, info, high, low, theirs, d, projected)
+        gram_got, class2 = in_turn(with_pair(gram), class2)
+        for bit in range(1, line.bit_length() - 1):
+            class2 = join(class2, over_line[1 << bit](class2))
+        triangle, inverse = factor_call(line, info, in_turn(gram), gram_got)
+        inverse = in_turn(inverse)
+        basis = in_turn(basis_call(in_turn(sketch), inverse))
+        *class1, class2 = in_turn(*class1, class2)
+        theirs = [with_pair(a) for a in (a1, *class1, class2)]
+        projected = project_call(line, True, info, inverse, [a1, *class1, class2], d, None)
+        projected = project_call(line, False, info, inverse, theirs, d, projected)
         return triangle, basis, projected
 
     return jax.shard_map(

time: 100 us -> 100 us (level)
  waiting for transfers between devices: 27 us -> 31.9 us
  starting transfers between devices: 35.2 us -> 31.2 us
    ppermute x30 -> x28, waiting for transfers between devices: 27 us -> 31.9 us  [over(): return lambda a: lax.ppermute(a, AXES, pairs)]
    ppermute x30 -> x28, starting transfers between devices: 35.2 us -> 31.2 us  [over(): return lambda a: lax.ppermute(a, AXES, pairs)]
  transfers between devices with their start and end apart: 30 -> 28, of which waited for: 10 -> 12; matrix products, arithmetic and copies ran while one was open for 1% -> 1% of each run, Pallas kernels for 17% -> 16%
where the time goes in v8:
time: 100 us
  Pallas kernels  35 us (35%)
  waiting for transfers between devices  31.9 us (32%)
  starting transfers between devices  31.2 us (31%)
  between operations  1.06 us (1%)
    ppermute x28, waiting for transfers between devices, over(): return lambda a: lax.ppermute(a, AXES, pairs)  31.9 us
    ppermute x28, starting transfers between devices, over(): return lambda a: lax.ppermute(a, AXES, pairs)  31.2 us
    pallas_call x1, Pallas kernels, front_call(): pl.pallas_call(functools.partial(front_kernel, 1.0 / math.sqrt(d), 1.0 /...  16.1 us
    pallas_call x1, Pallas kernels, factor_call(): pl.pallas_call(functools.partial(factor_kernel, line), in_specs=[SMEM_SPE...  11.4 us
    pallas_call x2, Pallas kernels, project_call(): pl.pallas_call(functools.partial(project_kernel, line, is_own), in_specs=...  4.86 us
    pallas_call x1, Pallas kernels, basis_call(): pl.pallas_call(basis_kernel, grid=(rows // block,), in_specs=[pl.BlockSpe...  2.65 us
  transfers between devices with their start and end apart: 28, of which 12 were waited for; matrix products, arithmetic and copies ran while one was open for 1% of the time, Pallas kernels for 16%

profile of v8, /device:TPU:0, one launch (start us, length us, event | category | flops | bytes accessed | tf_op | source)
XLA Modules:
  0.0 100.2 jit_solution(15786801868810771795)
XLA Ops:
  0.6 0.1 pad_add_fusion.info
  0.7 16.1 %front.1 = (f32[2048,256]{1,0:T(8,128)}, f32[128,256]{1,0:T(8,128)S(1)}, f32[128,256]{1,0:T(8,128)S(1)}, f32[1536,256]{1,0:T(8,128)S(1)}, f32[512,256]{1,0:T(8,1...) custom-call(s32[3]{0:T(128)S(1)} %pad_add_fusion.info, bf16[2048,4096]{1,0:T(8,128)(2,1)} %e.1, s32[4096,256]{1,0:T(8,128)} %signs.1), custom_call_target="tpu_custom_call" | custom-call | flops 8589934592 | bytes 20971520 | tf_op jit(solution)/shard_map/front/pallas_call | solution.py:119
  16.8 0.5 collective-permute-start
  17.3 0.1 collective-permute-start.5
  17.4 0.4 collective-permute-start.4
  17.8 2.7 %collective-permute-done.5 = f32[128,256]{1,0:T(8,128)S(1)} collective-permute-done((f32[128,256]{1,0:T(8,128)S(1)}, f32[128,256]{1,0:T(8,128)S(1)}, u32[]{:S(2)}, u32[]{:S(2)}) %collective-permute-start.5) | collective-permute-done | bytes 131104 | tf_op jit(solution)/shard_map/ppermute | solution.py:326
  20.6 0.3 slice_add_fusion
  20.9 2.9 %collective-permute-start.1 = (f32[384,256]{1,0:T(8,128)S(1)}, f32[384,256]{1,0:T(8,128)S(1)}, u32[]{:S(2)}, u32[]{:S(2)}) collective-permute-start(f32[384,256]{1,0:T(8,128)S(1)} %get-tuple-element.43), channel_id=1, source_target_pairs={{0,2},{1,3},{2,0},{3,1},{4,6},{5,7},{6,4},{7,5},{8,10},{9,11},{10,... | collective-permute-start | bytes 1179656 | tf_op jit(solution)/shard_map/ppermute | solution.py:326
  23.8 1.5 %collective-permute-start.2 = (f32[384,256]{1,0:T(8,128)S(1)}, f32[384,256]{1,0:T(8,128)S(1)}, u32[]{:S(2)}, u32[]{:S(2)}) collective-permute-start(f32[384,256]{1,0:T(8,128)S(1)} %get-tuple-element.44), channel_id=1, source_target_pairs={{0,4},{1,5},{2,6},{3,7},{4,0},{5,1},{6,2},{7,3},{8,12},{9,13},{10,... | collective-permute-start | bytes 1179656 | tf_op jit(solution)/shard_map/ppermute | solution.py:326
  25.4 0.0 collective-permute-start.3
  25.4 0.1 slice_add_fusion.4
  25.6 2.1 %collective-permute-start.9 = (f32[160,256]{1,0:T(8,128)S(1)}, f32[160,256]{1,0:T(8,128)S(1)}, u32[]{:S(2)}, u32[]{:S(2)}) collective-permute-start(f32[160,256]{1,0:T(8,128)S(1)} %get-tuple-element.56), channel_id=1, source_target_pairs={{0,8},{1,9},{2,10},{3,11},{4,12},{5,13},{6,14},{7,15},{8,0},{9,1},... | collective-permute-start | bytes 491528 | tf_op jit(solution)/shard_map/ppermute | solution.py:326
  27.6 2.6 %collective-permute-start.10 = (f32[160,256]{1,0:T(8,128)S(1)}, f32[160,256]{1,0:T(8,128)S(1)}, u32[]{:S(2)}, u32[]{:S(2)}) collective-permute-start(f32[160,256]{1,0:T(8,128)S(1)} %get-tuple-element.57), channel_id=1, source_target_pairs={{0,16},{1,17},{2,18},{3,19},{4,20},{5,21},{6,22},{7,23},{8,24},{9,... | collective-permute-start | bytes 491528 | tf_op jit(solution)/shard_map/ppermute | solution.py:326
  30.2 3.5 %collective-permute-done.1 = f32[384,256]{1,0:T(8,128)S(1)} collective-permute-done((f32[384,256]{1,0:T(8,128)S(1)}, f32[384,256]{1,0:T(8,128)S(1)}, u32[]{:S(2)}, u32[]{:S(2)}) %collective-permute-start.1) | collective-permute-done | bytes 393248 | tf_op jit(solution)/shard_map/ppermute | solution.py:326
  33.7 4.2 %collective-permute-start.11 = (f32[160,256]{1,0:T(8,128)S(1)}, f32[160,256]{1,0:T(8,128)S(1)}, u32[]{:S(2)}, u32[]{:S(2)}) collective-permute-start(f32[160,256]{1,0:T(8,128)S(1)} %get-tuple-element.50), channel_id=1, source_target_pairs={{0,24},{1,25},{2,26},{3,27},{4,28},{5,29},{6,30},{7,31},{8,16},{9,... | collective-permute-start | bytes 491528 | tf_op jit(solution)/shard_map/ppermute | solution.py:326
  37.9 5.2 %collective-permute-done.2 = f32[384,256]{1,0:T(8,128)S(1)} collective-permute-done((f32[384,256]{1,0:T(8,128)S(1)}, f32[384,256]{1,0:T(8,128)S(1)}, u32[]{:S(2)}, u32[]{:S(2)}) %collective-permute-start.2) | collective-permute-done | bytes 393248 | tf_op jit(solution)/shard_map/ppermute | solution.py:326
  43.2 0.1 add_add_fusion
  43.3 1.6 %collective-permute-start.6 = (f32[96,256]{1,0:T(8,128)S(1)}, f32[96,256]{1,0:T(8,128)S(1)}, u32[]{:S(2)}, u32[]{:S(2)}) collective-permute-start(f32[96,256]{1,0:T(8,128)S(1)} %get-tuple-element.52), channel_id=1, source_target_pairs={{0,8},{1,9},{2,10},{3,11},{4,12},{5,13},{6,14},{7,15},{8,0},{9,1},... | collective-permute-start | bytes 294920 | tf_op jit(solution)/shard_map/ppermute | solution.py:326
  44.9 2.6 %collective-permute-start.7 = (f32[96,256]{1,0:T(8,128)S(1)}, f32[96,256]{1,0:T(8,128)S(1)}, u32[]{:S(2)}, u32[]{:S(2)}) collective-permute-start(f32[96,256]{1,0:T(8,128)S(1)} %get-tuple-element.53), channel_id=1, source_target_pairs={{0,16},{1,17},{2,18},{3,19},{4,20},{5,21},{6,22},{7,23},{8,24},{9,... | collective-permute-start | bytes 294920 | tf_op jit(solution)/shard_map/ppermute | solution.py:326
  47.5 0.2 collective-permute-start.8
  47.8 1.5 %collective-permute-start.14 = (f32[160,256]{1,0:T(8,128)S(1)}, f32[160,256]{1,0:T(8,128)S(1)}, u32[]{:S(2)}, u32[]{:S(2)}) collective-permute-start(f32[160,256]{1,0:T(8,128)S(1)} %add_add_fusion.2), channel_id=1, source_target_pairs={{0,6},{1,7},{2,4},{3,5},{4,2},{5,3},{6,0},{7,1},{8,14},{9,15},{10,... | collective-permute-start | bytes 491528 | tf_op jit(solution)/shard_map/ppermute | solution.py:326
  49.3 1.2 %collective-permute-start.13 = (f32[160,256]{1,0:T(8,128)S(1)}, f32[160,256]{1,0:T(8,128)S(1)}, u32[]{:S(2)}, u32[]{:S(2)}) collective-permute-start(f32[160,256]{1,0:T(8,128)S(1)} %add_add_fusion.2), channel_id=1, source_target_pairs={{0,4},{1,5},{2,6},{3,7},{4,0},{5,1},{6,2},{7,3},{8,12},{9,13},{10,... | collective-permute-start | bytes 491528 | tf_op jit(solution)/shard_map/ppermute | solution.py:326
  50.6 0.8 collective-permute-start.12
  51.4 3.2 %collective-permute-done.7 = f32[96,256]{1,0:T(8,128)S(1)} collective-permute-done((f32[96,256]{1,0:T(8,128)S(1)}, f32[96,256]{1,0:T(8,128)S(1)}, u32[]{:S(2)}, u32[]{:S(2)}) %collective-permute-start.7) | collective-permute-done | bytes 98336 | tf_op jit(solution)/shard_map/ppermute | solution.py:326
  54.6 0.4 collective-permute-done.14
  55.1 1.7 %collective-permute-done.13 = f32[160,256]{1,0:T(8,128)S(1)} collective-permute-done((f32[160,256]{1,0:T(8,128)S(1)}, f32[160,256]{1,0:T(8,128)S(1)}, u32[]{:S(2)}, u32[]{:S(2)}) %collective-permute-start.13) | collective-permute-done | bytes 163872 | tf_op jit(solution)/shard_map/ppermute | solution.py:326
  56.8 0.7 collective-permute-start.15
  57.5 3.0 %collective-permute-start.17 = (f32[128,256]{1,0:T(8,128)S(1)}, f32[128,256]{1,0:T(8,128)S(1)}, u32[]{:S(2)}, u32[]{:S(2)}) collective-permute-start(f32[128,256]{1,0:T(8,128)S(1)} %pad_maximum_fusion.8), channel_id=1, source_target_pairs={{0,24},{1,25},{2,26},{3,27},{4,28},{5,29},{6,30},{7,31},{8,16},{9,... | collective-permute-start | bytes 393224 | tf_op jit(solution)/shard_map/ppermute | solution.py:326
  60.5 0.5 collective-permute-start.16
  61.0 9.0 %collective-permute-done.17 = f32[128,256]{1,0:T(8,128)S(1)} collective-permute-done((f32[128,256]{1,0:T(8,128)S(1)}, f32[128,256]{1,0:T(8,128)S(1)}, u32[]{:S(2)}, u32[]{:S(2)}) %collective-permute-start.17) | collective-permute-done | bytes 131104 | tf_op jit(solution)/shard_map/ppermute | solution.py:326
  70.0 2.3 %collective-permute-done.16 = f32[128,256]{1,0:T(8,128)S(1)} collective-permute-done((f32[128,256]{1,0:T(8,128)S(1)}, f32[128,256]{1,0:T(8,128)S(1)}, u32[]{:S(2)}, u32[]{:S(2)}) %collective-permute-start.16) | collective-permute-done | bytes 131104 | tf_op jit(solution)/shard_map/ppermute | solution.py:326
  72.4 0.1 collective-permute-start.18
  72.5 1.5 %collective-permute-start.21 = (f32[384,256]{1,0:T(8,128)S(1)}, f32[384,256]{1,0:T(8,128)S(1)}, u32[]{:S(2)}, u32[]{:S(2)}) collective-permute-start(f32[384,256]{1,0:T(8,128)S(1)} %pad_maximum_fusion.1.refs_0_), channel_id=1, source_target_pairs={{0,6},{1,7},{2,4},{3,5},{4,2},{5,3},{6,0},{7,1},{8,14},{9,15},{10,... | collective-permute-start | bytes 1179656 | tf_op jit(solution)/shard_map/ppermute | solution.py:326
  74.0 1.5 %collective-permute-start.20 = (f32[384,256]{1,0:T(8,128)S(1)}, f32[384,256]{1,0:T(8,128)S(1)}, u32[]{:S(2)}, u32[]{:S(2)}) collective-permute-start(f32[384,256]{1,0:T(8,128)S(1)} %pad_maximum_fusion.1.refs_0_), channel_id=1, source_target_pairs={{0,4},{1,5},{2,6},{3,7},{4,0},{5,1},{6,2},{7,3},{8,12},{9,13},{10,... | collective-permute-start | bytes 1179656 | tf_op jit(solution)/shard_map/ppermute | solution.py:326
  75.5 0.5 collective-permute-start.19
  76.1 0.0 copy-start
  76.1 0.1 collective-permute-start.22
  76.2 11.4 %factor.1 = (f32[256,256]{1,0:T(8,128)}, bf16[512,256]{1,0:T(8,128)(2,1)S(1)}) custom-call(s32[3]{0:T(128)S(1)} %pad_add_fusion.info, f32[128,256]{1,0:T(8,128)S(1)} %pad_maximum_fusion.9.kept, f32[128,256]{1,0:T(8,128)S(1)} %collective-permute-done.18.got), custom_call_target="tpu_custom_call" | custom-call | flops 10000000000 | bytes 524288 | tf_op jit(solution)/shard_map/factor/pallas_call | solution.py:231
  87.6 2.6 %basis.1 = bf16[2048,256]{1,0:T(8,128)(2,1)} custom-call(f32[2048,256]{1,0:T(8,128)S(1)} %copy-done, bf16[512,256]{1,0:T(8,128)(2,1)S(1)} %get-tuple-element.70.inverse), custom_call_target="tpu_custom_call" | custom-call | flops 805306368 | bytes 3145728 | tf_op jit(solution)/shard_map/basis/pallas_call | solution.py:257
  90.3 3.0 %collective-permute-done.20.refs_2_ = f32[384,256]{1,0:T(8,128)S(1)} collective-permute-done((f32[384,256]{1,0:T(8,128)S(1)}, f32[384,256]{1,0:T(8,128)S(1)}, u32[]{:S(2)}, u32[]{:S(2)}) %collective-permute-start.20) | collective-permute-done | bytes 393248 | tf_op jit(solution)/shard_map/ppermute | solution.py:326
  93.3 0.1 collective-permute-done.19.refs_1_
  93.4 0.5 collective-permute-start.23
  93.9 0.0 collective-permute-start.24
  93.9 0.5 collective-permute-start.25
  94.4 2.4 %project.2.refs_0_ = f32[256,4096]{1,0:T(8,128)} custom-call(s32[3]{0:T(128)S(1)} %pad_add_fusion.info, bf16[512,256]{1,0:T(8,128)(2,1)S(1)} %get-tuple-element.70.inverse, f32[384,256]{1,0:T(8,128)S(1)} %pad_maximum_fusion.1.refs_0_, f32[384,256]{1,0:T(8,128)S(1)} %collective-permute-done.19.refs_1_, f32[384,256]{1,0:T(8,128)S(1)} %collective-permute-done.20.refs_2_, ...), custom_call_target="tpu_custom_call" | custom-call | flops 805306368 | bytes 4194304 | tf_op jit(solution)/shard_map/project/pallas_call | solution.py:303
  96.9 0.1 collective-permute-done.25.refs_3_
  97.0 0.6 collective-permute-done.26.refs_4_
  97.6 2.4 %project.3 = f32[256,4096]{1,0:T(8,128)} custom-call(s32[3]{0:T(128)S(1)} %pad_add_fusion.info, bf16[512,256]{1,0:T(8,128)(2,1)S(1)} %get-tuple-element.70.inverse, f32[256,4096]{1,0:T(8,128)} %project.2.refs_0_, f32[384,256]{1,0:T(8,128)S(1)} %collective-permute-done.23.refs_1_, ...), custom_call_target="tpu_custom_call", output_to_operand_aliasing={{}: (2, {})} | custom-call | flops 805306368 | bytes 4194304 | tf_op jit(solution)/shard_map/project/pallas_call | solution.py:303
  (44 shorter events, 0.5 us)
Async XLA Ops:
  16.8 3.8 %collective-permute-start = (f32[1536,256]{1,0:T(8,128)S(1)}, f32[1536,256]{1,0:T(8,128)S(1)}, u32[]{:S(2)}, u32[]{:S(2)}) collective-permute-start(f32[1536,256]{1,0:T(8,128)S(1)} %get-tuple-element.41), channel_id=1, source_target_pairs={{0,1},{1,0},{2,3},{3,2},{4,5},{5,4},{6,7},{7,6},{8,9},{9,8},{10,11... | collective-permute-start | bytes 4718600 | tf_op jit(solution)/shard_map/ppermute | solution.py:326
  17.3 3.2 %collective-permute-start.5 = (f32[128,256]{1,0:T(8,128)S(1)}, f32[128,256]{1,0:T(8,128)S(1)}, u32[]{:S(2)}, u32[]{:S(2)}) collective-permute-start(f32[128,256]{1,0:T(8,128)S(1)} %get-tuple-element.49), channel_id=1, source_target_pairs={{0,1},{1,0},{2,3},{3,2},{4,5},{5,4},{6,7},{7,6},{8,9},{9,8},{10,11... | collective-permute-start | bytes 393224 | tf_op jit(solution)/shard_map/ppermute | solution.py:326
  17.4 8.0 %collective-permute-start.4 = (f32[512,256]{1,0:T(8,128)S(1)}, f32[512,256]{1,0:T(8,128)S(1)}, u32[]{:S(2)}, u32[]{:S(2)}) collective-permute-start(f32[512,256]{1,0:T(8,128)S(1)} %get-tuple-element.47), channel_id=1, source_target_pairs={{0,1},{1,0},{2,3},{3,2},{4,5},{5,4},{6,7},{7,6},{8,9},{9,8},{10,11... | collective-permute-start | bytes 1572872 | tf_op jit(solution)/shard_map/ppermute | solution.py:326
  20.9 12.8 %collective-permute-start.1 = (f32[384,256]{1,0:T(8,128)S(1)}, f32[384,256]{1,0:T(8,128)S(1)}, u32[]{:S(2)}, u32[]{:S(2)}) collective-permute-start(f32[384,256]{1,0:T(8,128)S(1)} %get-tuple-element.43), channel_id=1, source_target_pairs={{0,2},{1,3},{2,0},{3,1},{4,6},{5,7},{6,4},{7,5},{8,10},{9,11},{10,... | collective-permute-start | bytes 1179656 | tf_op jit(solution)/shard_map/ppermute | solution.py:326
  23.8 19.3 %collective-permute-start.2 = (f32[384,256]{1,0:T(8,128)S(1)}, f32[384,256]{1,0:T(8,128)S(1)}, u32[]{:S(2)}, u32[]{:S(2)}) collective-permute-start(f32[384,256]{1,0:T(8,128)S(1)} %get-tuple-element.44), channel_id=1, source_target_pairs={{0,4},{1,5},{2,6},{3,7},{4,0},{5,1},{6,2},{7,3},{8,12},{9,13},{10,... | collective-permute-start | bytes 1179656 | tf_op jit(solution)/shard_map/ppermute | solution.py:326
  25.4 17.8 %collective-permute-start.3 = (f32[384,256]{1,0:T(8,128)S(1)}, f32[384,256]{1,0:T(8,128)S(1)}, u32[]{:S(2)}, u32[]{:S(2)}) collective-permute-start(f32[384,256]{1,0:T(8,128)S(1)} %get-tuple-element.45), channel_id=1, source_target_pairs={{0,6},{1,7},{2,4},{3,5},{4,2},{5,3},{6,0},{7,1},{8,14},{9,15},{10,... | collective-permute-start | bytes 1179656 | tf_op jit(solution)/shard_map/ppermute | solution.py:326
  25.6 22.0 %collective-permute-start.9 = (f32[160,256]{1,0:T(8,128)S(1)}, f32[160,256]{1,0:T(8,128)S(1)}, u32[]{:S(2)}, u32[]{:S(2)}) collective-permute-start(f32[160,256]{1,0:T(8,128)S(1)} %get-tuple-element.56), channel_id=1, source_target_pairs={{0,8},{1,9},{2,10},{3,11},{4,12},{5,13},{6,14},{7,15},{8,0},{9,1},... | collective-permute-start | bytes 491528 | tf_op jit(solution)/shard_map/ppermute | solution.py:326
  27.6 20.1 %collective-permute-start.10 = (f32[160,256]{1,0:T(8,128)S(1)}, f32[160,256]{1,0:T(8,128)S(1)}, u32[]{:S(2)}, u32[]{:S(2)}) collective-permute-start(f32[160,256]{1,0:T(8,128)S(1)} %get-tuple-element.57), channel_id=1, source_target_pairs={{0,16},{1,17},{2,18},{3,19},{4,20},{5,21},{6,22},{7,23},{8,24},{9,... | collective-permute-start | bytes 491528 | tf_op jit(solution)/shard_map/ppermute | solution.py:326
  33.7 14.0 %collective-permute-start.11 = (f32[160,256]{1,0:T(8,128)S(1)}, f32[160,256]{1,0:T(8,128)S(1)}, u32[]{:S(2)}, u32[]{:S(2)}) collective-permute-start(f32[160,256]{1,0:T(8,128)S(1)} %get-tuple-element.50), channel_id=1, source_target_pairs={{0,24},{1,25},{2,26},{3,27},{4,28},{5,29},{6,30},{7,31},{8,16},{9,... | collective-permute-start | bytes 491528 | tf_op jit(solution)/shard_map/ppermute | solution.py:326
  43.3 7.3 %collective-permute-start.6 = (f32[96,256]{1,0:T(8,128)S(1)}, f32[96,256]{1,0:T(8,128)S(1)}, u32[]{:S(2)}, u32[]{:S(2)}) collective-permute-start(f32[96,256]{1,0:T(8,128)S(1)} %get-tuple-element.52), channel_id=1, source_target_pairs={{0,8},{1,9},{2,10},{3,11},{4,12},{5,13},{6,14},{7,15},{8,0},{9,1},... | collective-permute-start | bytes 294920 | tf_op jit(solution)/shard_map/ppermute | solution.py:326
  44.9 9.7 %collective-permute-start.7 = (f32[96,256]{1,0:T(8,128)S(1)}, f32[96,256]{1,0:T(8,128)S(1)}, u32[]{:S(2)}, u32[]{:S(2)}) collective-permute-start(f32[96,256]{1,0:T(8,128)S(1)} %get-tuple-element.53), channel_id=1, source_target_pairs={{0,16},{1,17},{2,18},{3,19},{4,20},{5,21},{6,22},{7,23},{8,24},{9,... | collective-permute-start | bytes 294920 | tf_op jit(solution)/shard_map/ppermute | solution.py:326
  47.5 7.1 %collective-permute-start.8 = (f32[96,256]{1,0:T(8,128)S(1)}, f32[96,256]{1,0:T(8,128)S(1)}, u32[]{:S(2)}, u32[]{:S(2)}) collective-permute-start(f32[96,256]{1,0:T(8,128)S(1)} %get-tuple-element.54), channel_id=1, source_target_pairs={{0,24},{1,25},{2,26},{3,27},{4,28},{5,29},{6,30},{7,31},{8,16},{9,... | collective-permute-start | bytes 294920 | tf_op jit(solution)/shard_map/ppermute | solution.py:326
  47.8 7.2 %collective-permute-start.14 = (f32[160,256]{1,0:T(8,128)S(1)}, f32[160,256]{1,0:T(8,128)S(1)}, u32[]{:S(2)}, u32[]{:S(2)}) collective-permute-start(f32[160,256]{1,0:T(8,128)S(1)} %add_add_fusion.2), channel_id=1, source_target_pairs={{0,6},{1,7},{2,4},{3,5},{4,2},{5,3},{6,0},{7,1},{8,14},{9,15},{10,... | collective-permute-start | bytes 491528 | tf_op jit(solution)/shard_map/ppermute | solution.py:326
  49.3 7.4 %collective-permute-start.13 = (f32[160,256]{1,0:T(8,128)S(1)}, f32[160,256]{1,0:T(8,128)S(1)}, u32[]{:S(2)}, u32[]{:S(2)}) collective-permute-start(f32[160,256]{1,0:T(8,128)S(1)} %add_add_fusion.2), channel_id=1, source_target_pairs={{0,4},{1,5},{2,6},{3,7},{4,0},{5,1},{6,2},{7,3},{8,12},{9,13},{10,... | collective-permute-start | bytes 491528 | tf_op jit(solution)/shard_map/ppermute | solution.py:326
  50.6 6.1 %collective-permute-start.12 = (f32[160,256]{1,0:T(8,128)S(1)}, f32[160,256]{1,0:T(8,128)S(1)}, u32[]{:S(2)}, u32[]{:S(2)}) collective-permute-start(f32[160,256]{1,0:T(8,128)S(1)} %add_add_fusion.2), channel_id=1, source_target_pairs={{0,2},{1,3},{2,0},{3,1},{4,6},{5,7},{6,4},{7,5},{8,10},{9,11},{10,... | collective-permute-start | bytes 491528 | tf_op jit(solution)/shard_map/ppermute | solution.py:326
  56.8 15.5 %collective-permute-start.15 = (f32[256,256]{1,0:T(8,128)S(1)}, f32[256,256]{1,0:T(8,128)S(1)}, u32[]{:S(2)}, u32[]{:S(2)}) collective-permute-start(f32[256,256]{1,0:T(8,128)S(1)} %pad_maximum_fusion.2), channel_id=1, source_target_pairs={{0,8},{1,9},{2,10},{3,11},{4,12},{5,13},{6,14},{7,15},{8,0},{9,1},... | collective-permute-start | bytes 786440 | tf_op jit(solution)/shard_map/ppermute | solution.py:326
  57.5 12.5 %collective-permute-start.17 = (f32[128,256]{1,0:T(8,128)S(1)}, f32[128,256]{1,0:T(8,128)S(1)}, u32[]{:S(2)}, u32[]{:S(2)}) collective-permute-start(f32[128,256]{1,0:T(8,128)S(1)} %pad_maximum_fusion.8), channel_id=1, source_target_pairs={{0,24},{1,25},{2,26},{3,27},{4,28},{5,29},{6,30},{7,31},{8,16},{9,... | collective-permute-start | bytes 393224 | tf_op jit(solution)/shard_map/ppermute | solution.py:326
  60.5 11.8 %collective-permute-start.16 = (f32[128,256]{1,0:T(8,128)S(1)}, f32[128,256]{1,0:T(8,128)S(1)}, u32[]{:S(2)}, u32[]{:S(2)}) collective-permute-start(f32[128,256]{1,0:T(8,128)S(1)} %pad_maximum_fusion.8), channel_id=1, source_target_pairs={{0,16},{1,17},{2,18},{3,19},{4,20},{5,21},{6,22},{7,23},{8,24},{9,... | collective-permute-start | bytes 393224 | tf_op jit(solution)/shard_map/ppermute | solution.py:326
  72.4 3.7 %collective-permute-start.18 = (f32[128,256]{1,0:T(8,128)S(1)}, f32[128,256]{1,0:T(8,128)S(1)}, u32[]{:S(2)}, u32[]{:S(2)}) collective-permute-start(f32[128,256]{1,0:T(8,128)S(1)} %pad_maximum_fusion.9.kept), channel_id=1, source_target_pairs={{0,1},{1,0},{2,3},{3,2},{4,5},{5,4},{6,7},{7,6},{8,9},{9,8},{10,11... | collective-permute-start | bytes 393224 | tf_op jit(solution)/shard_map/ppermute | solution.py:326
  72.5 17.8 %collective-permute-start.21 = (f32[384,256]{1,0:T(8,128)S(1)}, f32[384,256]{1,0:T(8,128)S(1)}, u32[]{:S(2)}, u32[]{:S(2)}) collective-permute-start(f32[384,256]{1,0:T(8,128)S(1)} %pad_maximum_fusion.1.refs_0_), channel_id=1, source_target_pairs={{0,6},{1,7},{2,4},{3,5},{4,2},{5,3},{6,0},{7,1},{8,14},{9,15},{10,... | collective-permute-start | bytes 1179656 | tf_op jit(solution)/shard_map/ppermute | solution.py:326
  74.0 19.4 %collective-permute-start.20 = (f32[384,256]{1,0:T(8,128)S(1)}, f32[384,256]{1,0:T(8,128)S(1)}, u32[]{:S(2)}, u32[]{:S(2)}) collective-permute-start(f32[384,256]{1,0:T(8,128)S(1)} %pad_maximum_fusion.1.refs_0_), channel_id=1, source_target_pairs={{0,4},{1,5},{2,6},{3,7},{4,0},{5,1},{6,2},{7,3},{8,12},{9,13},{10,... | collective-permute-start | bytes 1179656 | tf_op jit(solution)/shard_map/ppermute | solution.py:326
  75.5 17.9 %collective-permute-start.19 = (f32[384,256]{1,0:T(8,128)S(1)}, f32[384,256]{1,0:T(8,128)S(1)}, u32[]{:S(2)}, u32[]{:S(2)}) collective-permute-start(f32[384,256]{1,0:T(8,128)S(1)} %pad_maximum_fusion.1.refs_0_), channel_id=1, source_target_pairs={{0,2},{1,3},{2,0},{3,1},{4,6},{5,7},{6,4},{7,5},{8,10},{9,11},{10,... | collective-permute-start | bytes 1179656 | tf_op jit(solution)/shard_map/ppermute | solution.py:326
  76.1 11.5 %copy-start = (f32[2048,256]{1,0:T(8,128)S(1)}, f32[2048,256]{1,0:T(8,128)}, u32[]{:S(2)}) copy-start(f32[2048,256]{1,0:T(8,128)} %get-tuple-element.71.sketch) | copy-start | bytes 6291460
  76.1 14.2 %collective-permute-start.22 = (f32[256,256]{1,0:T(8,128)S(1)}, f32[256,256]{1,0:T(8,128)S(1)}, u32[]{:S(2)}, u32[]{:S(2)}) collective-permute-start(f32[256,256]{1,0:T(8,128)S(1)} %pad_maximum_fusion.3), channel_id=1, source_target_pairs={{0,16},{1,17},{2,18},{3,19},{4,20},{5,21},{6,22},{7,23},{8,24},{9,... | collective-permute-start | bytes 786440 | tf_op jit(solution)/shard_map/ppermute | solution.py:326
  93.4 4.2 %collective-permute-start.27 = (f32[512,256]{1,0:T(8,128)S(1)}, f32[512,256]{1,0:T(8,128)S(1)}, u32[]{:S(2)}, u32[]{:S(2)}) collective-permute-start(f32[512,256]{1,0:T(8,128)S(1)} %pad_maximum_fusion.refs_4_), channel_id=1, source_target_pairs={{0,1},{1,0},{2,3},{3,2},{4,5},{5,4},{6,7},{7,6},{8,9},{9,8},{10,11... | collective-permute-start | bytes 1572872 | tf_op jit(solution)/shard_map/ppermute | solution.py:326
  93.4 3.5 %collective-permute-start.23 = (f32[384,256]{1,0:T(8,128)S(1)}, f32[384,256]{1,0:T(8,128)S(1)}, u32[]{:S(2)}, u32[]{:S(2)}) collective-permute-start(f32[384,256]{1,0:T(8,128)S(1)} %pad_maximum_fusion.1.refs_0_), channel_id=1, source_target_pairs={{0,1},{1,0},{2,3},{3,2},{4,5},{5,4},{6,7},{7,6},{8,9},{9,8},{10,11... | collective-permute-start | bytes 1179656 | tf_op jit(solution)/shard_map/ppermute | solution.py:326
  93.9 3.0 %collective-permute-start.24 = (f32[384,256]{1,0:T(8,128)S(1)}, f32[384,256]{1,0:T(8,128)S(1)}, u32[]{:S(2)}, u32[]{:S(2)}) collective-permute-start(f32[384,256]{1,0:T(8,128)S(1)} %collective-permute-done.19.refs_1_), channel_id=1, source_target_pairs={{0,1},{1,0},{2,3},{3,2},{4,5},{5,4},{6,7},{7,6},{8,9},{9,8},{10,11... | collective-permute-start | bytes 1179656 | tf_op jit(solution)/shard_map/ppermute | solution.py:326
  93.9 3.1 %collective-permute-start.25 = (f32[384,256]{1,0:T(8,128)S(1)}, f32[384,256]{1,0:T(8,128)S(1)}, u32[]{:S(2)}, u32[]{:S(2)}) collective-permute-start(f32[384,256]{1,0:T(8,128)S(1)} %collective-permute-done.20.refs_2_), channel_id=1, source_target_pairs={{0,1},{1,0},{2,3},{3,2},{4,5},{5,4},{6,7},{7,6},{8,9},{9,8},{10,11... | collective-permute-start | bytes 1179656 | tf_op jit(solution)/shard_map/ppermute | solution.py:326
  94.4 3.1 %collective-permute-start.26 = (f32[384,256]{1,0:T(8,128)S(1)}, f32[384,256]{1,0:T(8,128)S(1)}, u32[]{:S(2)}, u32[]{:S(2)}) collective-permute-start(f32[384,256]{1,0:T(8,128)S(1)} %collective-permute-done.21.refs_3_), channel_id=1, source_target_pairs={{0,1},{1,0},{2,3},{3,2},{4,5},{5,4},{6,7},{7,6},{8,9},{9,8},{10,11... | collective-permute-start | bytes 1179656 | tf_op jit(solution)/shard_map/ppermute | solution.py:326

commit v9 on v8

--- a/solution.py
+++ b/solution.py
@@ -365,23 +365,27 @@
         whole2 = [over_plane[g](a2) for g in range(1, PLANE)]
         a2 = (a2 + whole2[0]) + (whole2[1] + whole2[2])
         n2 = a2.shape[0] - gram.shape[0] // line
-        a1 = join(sum(from_line, parts1[0]), a2[n2:])
-        near, a1, a2 = in_turn(join(a1, a2[:n2]), a1, a2[:n2])
-        near = over_line[1](near)
-        gathered = [a1, near[: a1.shape[0]]] + [over_line[g](a1) for g in range(2, line)]
-        class2 = join(a2, near[a1.shape[0] :])
+        a1 = in_turn(join(sum(from_line, parts1[0]), a2[n2:]))
+        gathered = [a1] + [over_line[g](a1) for g in range(1, line)]
         n1 = a1.shape[0] - gram.shape[0] // line
         a1 = in_turn(join(*[a[:n1] for a in gathered]))
         class1 = [over_plane[g](a1) for g in range(1, PLANE)]
         gram = in_turn(join(*[a[n1:] for a in gathered]))
-        gram_got, class2 = in_turn(with_pair(gram), class2)
+        gram_got = with_pair(gram)
+        class2 = in_turn(a2[:n2])
+        class2 = join(class2, over_line[1](class2))
+        gram_got, class2 = in_turn(gram_got, class2)
         for bit in range(1, line.bit_length() - 1):
             class2 = join(class2, over_line[1 << bit](class2))
+        a1 = in_turn(a1)
+        their1 = with_pair(a1)
         triangle, inverse = factor_call(line, info, in_turn(gram), gram_got)
-        inverse = in_turn(inverse)
+        their1, inverse = in_turn(their1, inverse)
         basis = in_turn(basis_call(in_turn(sketch), inverse))
-        *class1, class2 = in_turn(*class1, class2)
-        theirs = [with_pair(a) for a in (a1, *class1, class2)]
+        class2 = in_turn(class2)
+        their2 = with_pair(class2)
+        class1 = in_turn(*class1)
+        theirs = [their1, *[with_pair(a) for a in class1], their2]
         projected = project_call(line, True, info, inverse, [a1, *class1, class2], d, None)
         projected = project_call(line, False, info, inverse, theirs, d, projected)
         return triangle, basis, projected

time: 100 us -> 97.7 us (0.977)
  waiting for transfers between devices: 31.9 us -> 27 us
  starting transfers between devices: 31.2 us -> 33.5 us
    ppermute x28 -> x29, waiting for transfers between devices: 31.9 us -> 27 us  [over(): return lambda a: lax.ppermute(a, AXES, pairs)]
    ppermute x28 -> x29, starting transfers between devices: 31.2 us -> 33.5 us  [over(): return lambda a: lax.ppermute(a, AXES, pairs)]
  transfers between devices with their start and end apart: 28 -> 29, of which waited for: 12 -> 10; matrix products, arithmetic and copies ran while one was open for 1% -> 1% of each run, Pallas kernels for 16% -> 17%
where the time goes in v9:
time: 97.7 us; the launch traced here: 97.6 us
  Pallas kernels  35 us (36%)
  starting transfers between devices  33.5 us (34%)
  waiting for transfers between devices  27 us (28%)
  between operations  1.06 us (1%)
    ppermute x29, starting transfers between devices, over(): return lambda a: lax.ppermute(a, AXES, pairs)  33.5 us
    ppermute x29, waiting for transfers between devices, over(): return lambda a: lax.ppermute(a, AXES, pairs)  27 us
    pallas_call x1, Pallas kernels, front_call(): pl.pallas_call(functools.partial(front_kernel, 1.0 / math.sqrt(d), 1.0 /...  16.1 us
    pallas_call x1, Pallas kernels, factor_call(): pl.pallas_call(functools.partial(factor_kernel, line), in_specs=[SMEM_SPE...  11.4 us
    pallas_call x2, Pallas kernels, project_call(): pl.pallas_call(functools.partial(project_kernel, line, is_own), in_specs=...  4.86 us
    pallas_call x1, Pallas kernels, basis_call(): pl.pallas_call(basis_kernel, grid=(rows // block,), in_specs=[pl.BlockSpe...  2.66 us
  transfers between devices with their start and end apart: 29, of which 10 were waited for; matrix products, arithmetic and copies ran while one was open for 1% of the time, Pallas kernels for 17%

profile of v9, /device:TPU:0, one launch (start us, length us, event | category | flops | bytes accessed | tf_op | source)
XLA Modules:
  0.0 97.6 jit_solution(9884549787766656905)
XLA Ops:
  0.6 0.1 pad_add_fusion.info
  0.7 16.1 %front.1 = (f32[2048,256]{1,0:T(8,128)}, f32[128,256]{1,0:T(8,128)S(1)}, f32[128,256]{1,0:T(8,128)S(1)}, f32[1536,256]{1,0:T(8,128)S(1)}, f32[512,256]{1,0:T(8,1...) custom-call(s32[3]{0:T(128)S(1)} %pad_add_fusion.info, bf16[2048,4096]{1,0:T(8,128)(2,1)} %e.1, s32[4096,256]{1,0:T(8,128)} %signs.1), custom_call_target="tpu_custom_call" | custom-call | flops 8589934592 | bytes 20971520 | tf_op jit(solution)/shard_map/front/pallas_call | solution.py:119
  16.8 0.5 collective-permute-start
  17.3 0.1 collective-permute-start.5
  17.4 0.4 collective-permute-start.4
  17.8 2.7 %collective-permute-done.5 = f32[128,256]{1,0:T(8,128)S(1)} collective-permute-done((f32[128,256]{1,0:T(8,128)S(1)}, f32[128,256]{1,0:T(8,128)S(1)}, u32[]{:S(2)}, u32[]{:S(2)}) %collective-permute-start.5) | collective-permute-done | bytes 131104 | tf_op jit(solution)/shard_map/ppermute | solution.py:326
  20.6 0.0 collective-permute-done
  20.6 0.3 slice_add_fusion
  20.9 2.9 %collective-permute-start.1 = (f32[384,256]{1,0:T(8,128)S(1)}, f32[384,256]{1,0:T(8,128)S(1)}, u32[]{:S(2)}, u32[]{:S(2)}) collective-permute-start(f32[384,256]{1,0:T(8,128)S(1)} %get-tuple-element.44), channel_id=1, source_target_pairs={{0,2},{1,3},{2,0},{3,1},{4,6},{5,7},{6,4},{7,5},{8,10},{9,11},{10,... | collective-permute-start | bytes 1179656 | tf_op jit(solution)/shard_map/ppermute | solution.py:326
  23.8 1.5 %collective-permute-start.2 = (f32[384,256]{1,0:T(8,128)S(1)}, f32[384,256]{1,0:T(8,128)S(1)}, u32[]{:S(2)}, u32[]{:S(2)}) collective-permute-start(f32[384,256]{1,0:T(8,128)S(1)} %get-tuple-element.45), channel_id=1, source_target_pairs={{0,4},{1,5},{2,6},{3,7},{4,0},{5,1},{6,2},{7,3},{8,12},{9,13},{10,... | collective-permute-start | bytes 1179656 | tf_op jit(solution)/shard_map/ppermute | solution.py:326
  25.4 0.0 collective-permute-start.3
  25.4 0.1 slice_add_fusion.4
  25.6 2.1 %collective-permute-start.9 = (f32[160,256]{1,0:T(8,128)S(1)}, f32[160,256]{1,0:T(8,128)S(1)}, u32[]{:S(2)}, u32[]{:S(2)}) collective-permute-start(f32[160,256]{1,0:T(8,128)S(1)} %get-tuple-element.57), channel_id=1, source_target_pairs={{0,8},{1,9},{2,10},{3,11},{4,12},{5,13},{6,14},{7,15},{8,0},{9,1},... | collective-permute-start | bytes 491528 | tf_op jit(solution)/shard_map/ppermute | solution.py:326
  27.6 2.6 %collective-permute-start.10 = (f32[160,256]{1,0:T(8,128)S(1)}, f32[160,256]{1,0:T(8,128)S(1)}, u32[]{:S(2)}, u32[]{:S(2)}) collective-permute-start(f32[160,256]{1,0:T(8,128)S(1)} %get-tuple-element.58), channel_id=1, source_target_pairs={{0,16},{1,17},{2,18},{3,19},{4,20},{5,21},{6,22},{7,23},{8,24},{9,... | collective-permute-start | bytes 491528 | tf_op jit(solution)/shard_map/ppermute | solution.py:326
  30.2 3.5 %collective-permute-done.1 = f32[384,256]{1,0:T(8,128)S(1)} collective-permute-done((f32[384,256]{1,0:T(8,128)S(1)}, f32[384,256]{1,0:T(8,128)S(1)}, u32[]{:S(2)}, u32[]{:S(2)}) %collective-permute-start.1) | collective-permute-done | bytes 393248 | tf_op jit(solution)/shard_map/ppermute | solution.py:326
  33.7 4.2 %collective-permute-start.11 = (f32[160,256]{1,0:T(8,128)S(1)}, f32[160,256]{1,0:T(8,128)S(1)}, u32[]{:S(2)}, u32[]{:S(2)}) collective-permute-start(f32[160,256]{1,0:T(8,128)S(1)} %get-tuple-element.51), channel_id=1, source_target_pairs={{0,24},{1,25},{2,26},{3,27},{4,28},{5,29},{6,30},{7,31},{8,16},{9,... | collective-permute-start | bytes 491528 | tf_op jit(solution)/shard_map/ppermute | solution.py:326
  37.9 5.2 %collective-permute-done.2 = f32[384,256]{1,0:T(8,128)S(1)} collective-permute-done((f32[384,256]{1,0:T(8,128)S(1)}, f32[384,256]{1,0:T(8,128)S(1)}, u32[]{:S(2)}, u32[]{:S(2)}) %collective-permute-start.2) | collective-permute-done | bytes 393248 | tf_op jit(solution)/shard_map/ppermute | solution.py:326
  43.2 0.1 add_add_fusion
  43.3 1.6 %collective-permute-start.6 = (f32[96,256]{1,0:T(8,128)S(1)}, f32[96,256]{1,0:T(8,128)S(1)}, u32[]{:S(2)}, u32[]{:S(2)}) collective-permute-start(f32[96,256]{1,0:T(8,128)S(1)} %get-tuple-element.53), channel_id=1, source_target_pairs={{0,8},{1,9},{2,10},{3,11},{4,12},{5,13},{6,14},{7,15},{8,0},{9,1},... | collective-permute-start | bytes 294920 | tf_op jit(solution)/shard_map/ppermute | solution.py:326
  44.9 2.6 %collective-permute-start.7 = (f32[96,256]{1,0:T(8,128)S(1)}, f32[96,256]{1,0:T(8,128)S(1)}, u32[]{:S(2)}, u32[]{:S(2)}) collective-permute-start(f32[96,256]{1,0:T(8,128)S(1)} %get-tuple-element.54), channel_id=1, source_target_pairs={{0,16},{1,17},{2,18},{3,19},{4,20},{5,21},{6,22},{7,23},{8,24},{9,... | collective-permute-start | bytes 294920 | tf_op jit(solution)/shard_map/ppermute | solution.py:326
  47.5 0.2 collective-permute-start.8
  47.8 1.5 %collective-permute-start.14 = (f32[160,256]{1,0:T(8,128)S(1)}, f32[160,256]{1,0:T(8,128)S(1)}, u32[]{:S(2)}, u32[]{:S(2)}) collective-permute-start(f32[160,256]{1,0:T(8,128)S(1)} %add_add_fusion.2), channel_id=1, source_target_pairs={{0,6},{1,7},{2,4},{3,5},{4,2},{5,3},{6,0},{7,1},{8,14},{9,15},{10,... | collective-permute-start | bytes 491528 | tf_op jit(solution)/shard_map/ppermute | solution.py:326
  49.3 1.2 %collective-permute-start.13 = (f32[160,256]{1,0:T(8,128)S(1)}, f32[160,256]{1,0:T(8,128)S(1)}, u32[]{:S(2)}, u32[]{:S(2)}) collective-permute-start(f32[160,256]{1,0:T(8,128)S(1)} %add_add_fusion.2), channel_id=1, source_target_pairs={{0,4},{1,5},{2,6},{3,7},{4,0},{5,1},{6,2},{7,3},{8,12},{9,13},{10,... | collective-permute-start | bytes 491528 | tf_op jit(solution)/shard_map/ppermute | solution.py:326
  50.6 0.8 collective-permute-start.12
  51.4 3.2 %collective-permute-done.7 = f32[96,256]{1,0:T(8,128)S(1)} collective-permute-done((f32[96,256]{1,0:T(8,128)S(1)}, f32[96,256]{1,0:T(8,128)S(1)}, u32[]{:S(2)}, u32[]{:S(2)}) %collective-permute-start.7) | collective-permute-done | bytes 98336 | tf_op jit(solution)/shard_map/ppermute | solution.py:326
  54.6 0.4 collective-permute-done.14
  55.1 1.7 %collective-permute-done.13 = f32[160,256]{1,0:T(8,128)S(1)} collective-permute-done((f32[160,256]{1,0:T(8,128)S(1)}, f32[160,256]{1,0:T(8,128)S(1)}, u32[]{:S(2)}, u32[]{:S(2)}) %collective-permute-start.13) | collective-permute-done | bytes 163872 | tf_op jit(solution)/shard_map/ppermute | solution.py:326
  56.8 3.6 %collective-permute-start.17 = (f32[128,256]{1,0:T(8,128)S(1)}, f32[128,256]{1,0:T(8,128)S(1)}, u32[]{:S(2)}, u32[]{:S(2)}) collective-permute-start(f32[128,256]{1,0:T(8,128)S(1)} %pad_maximum_fusion.7), channel_id=1, source_target_pairs={{0,24},{1,25},{2,26},{3,27},{4,28},{5,29},{6,30},{7,31},{8,16},{9,... | collective-permute-start | bytes 393224 | tf_op jit(solution)/shard_map/ppermute | solution.py:326
  60.4 0.9 collective-permute-start.15
  61.3 3.8 %collective-permute-done.17 = f32[128,256]{1,0:T(8,128)S(1)} collective-permute-done((f32[128,256]{1,0:T(8,128)S(1)}, f32[128,256]{1,0:T(8,128)S(1)}, u32[]{:S(2)}, u32[]{:S(2)}) %collective-permute-start.17) | collective-permute-done | bytes 131104 | tf_op jit(solution)/shard_map/ppermute | solution.py:326
  65.1 4.8 %collective-permute-done.16 = f32[128,256]{1,0:T(8,128)S(1)} collective-permute-done((f32[128,256]{1,0:T(8,128)S(1)}, f32[128,256]{1,0:T(8,128)S(1)}, u32[]{:S(2)}, u32[]{:S(2)}) %collective-permute-start.16) | collective-permute-done | bytes 131104 | tf_op jit(solution)/shard_map/ppermute | solution.py:326
  70.0 0.3 collective-permute-start.19
  70.4 1.4 %collective-permute-start.23 = (f32[384,256]{1,0:T(8,128)S(1)}, f32[384,256]{1,0:T(8,128)S(1)}, u32[]{:S(2)}, u32[]{:S(2)}) collective-permute-start(f32[384,256]{1,0:T(8,128)S(1)} %pad_maximum_fusion.1.refs_0_), channel_id=1, source_target_pairs={{0,6},{1,7},{2,4},{3,5},{4,2},{5,3},{6,0},{7,1},{8,14},{9,15},{10,... | collective-permute-start | bytes 1179656 | tf_op jit(solution)/shard_map/ppermute | solution.py:326
  71.8 1.6 %collective-permute-start.22 = (f32[384,256]{1,0:T(8,128)S(1)}, f32[384,256]{1,0:T(8,128)S(1)}, u32[]{:S(2)}, u32[]{:S(2)}) collective-permute-start(f32[384,256]{1,0:T(8,128)S(1)} %pad_maximum_fusion.1.refs_0_), channel_id=1, source_target_pairs={{0,4},{1,5},{2,6},{3,7},{4,0},{5,1},{6,2},{7,3},{8,12},{9,13},{10,... | collective-permute-start | bytes 1179656 | tf_op jit(solution)/shard_map/ppermute | solution.py:326
  73.4 0.5 collective-permute-start.21
  73.9 1.2 %collective-permute-done.19 = f32[128,256]{1,0:T(8,128)S(1)} collective-permute-done((f32[128,256]{1,0:T(8,128)S(1)}, f32[128,256]{1,0:T(8,128)S(1)}, u32[]{:S(2)}, u32[]{:S(2)}) %collective-permute-start.19) | collective-permute-done | bytes 131104 | tf_op jit(solution)/shard_map/ppermute | solution.py:326
  75.1 0.0 copy-start
  75.1 1.8 %collective-permute-start.24 = (f32[256,256]{1,0:T(8,128)S(1)}, f32[256,256]{1,0:T(8,128)S(1)}, u32[]{:S(2)}, u32[]{:S(2)}) collective-permute-start(f32[256,256]{1,0:T(8,128)S(1)} %pad_maximum_fusion.2), channel_id=1, source_target_pairs={{0,16},{1,17},{2,18},{3,19},{4,20},{5,21},{6,22},{7,23},{8,24},{9,... | collective-permute-start | bytes 786440 | tf_op jit(solution)/shard_map/ppermute | solution.py:326
  76.9 11.4 %factor.1 = (f32[256,256]{1,0:T(8,128)}, bf16[512,256]{1,0:T(8,128)(2,1)S(1)}) custom-call(s32[3]{0:T(128)S(1)} %pad_add_fusion.info, f32[128,256]{1,0:T(8,128)S(1)} %pad_maximum_fusion.8.kept, f32[128,256]{1,0:T(8,128)S(1)} %collective-permute-done.18.got), custom_call_target="tpu_custom_call" | custom-call | flops 10000000000 | bytes 524288 | tf_op jit(solution)/shard_map/factor/pallas_call | solution.py:231
  88.3 0.3 collective-permute-done.24
  88.7 2.7 %basis.1 = bf16[2048,256]{1,0:T(8,128)(2,1)} custom-call(f32[2048,256]{1,0:T(8,128)S(1)} %copy-done, bf16[512,256]{1,0:T(8,128)(2,1)S(1)} %get-tuple-element.71.inverse), custom_call_target="tpu_custom_call" | custom-call | flops 805306368 | bytes 3145728 | tf_op jit(solution)/shard_map/basis/pallas_call | solution.py:257
  91.4 0.2 collective-permute-start.28
  91.6 0.4 collective-permute-start.25
  92.0 0.2 collective-permute-start.26
  92.2 0.3 collective-permute-start.27
  92.5 2.4 %project.2.refs_0_ = f32[256,4096]{1,0:T(8,128)} custom-call(s32[3]{0:T(128)S(1)} %pad_add_fusion.info, bf16[512,256]{1,0:T(8,128)(2,1)S(1)} %get-tuple-element.71.inverse, f32[384,256]{1,0:T(8,128)S(1)} %pad_maximum_fusion.1.refs_0_, f32[384,256]{1,0:T(8,128)S(1)} %collective-permute-done.21.refs_1_, f32[384,256]{1,0:T(8,128)S(1)} %collective-permute-done.22.refs_2_, ...), custom_call_target="tpu_custom_call" | custom-call | flops 805306368 | bytes 4194304 | tf_op jit(solution)/shard_map/project/pallas_call | solution.py:303
  95.0 0.0 collective-permute-done.27.refs_4_
  95.0 2.4 %project.3 = f32[256,4096]{1,0:T(8,128)} custom-call(s32[3]{0:T(128)S(1)} %pad_add_fusion.info, bf16[512,256]{1,0:T(8,128)(2,1)S(1)} %get-tuple-element.71.inverse, f32[256,4096]{1,0:T(8,128)} %project.2.refs_0_, f32[384,256]{1,0:T(8,128)S(1)} %collective-permute-done.20.refs_1_, ...), custom_call_target="tpu_custom_call", output_to_operand_aliasing={{}: (2, {})} | custom-call | flops 805306368 | bytes 4194304 | tf_op jit(solution)/shard_map/project/pallas_call | solution.py:303
  (44 shorter events, 0.4 us)
Async XLA Ops:
  16.8 3.8 %collective-permute-start = (f32[1536,256]{1,0:T(8,128)S(1)}, f32[1536,256]{1,0:T(8,128)S(1)}, u32[]{:S(2)}, u32[]{:S(2)}) collective-permute-start(f32[1536,256]{1,0:T(8,128)S(1)} %get-tuple-element.42), channel_id=1, source_target_pairs={{0,1},{1,0},{2,3},{3,2},{4,5},{5,4},{6,7},{7,6},{8,9},{9,8},{10,11... | collective-permute-start | bytes 4718600 | tf_op jit(solution)/shard_map/ppermute | solution.py:326
  17.3 3.2 %collective-permute-start.5 = (f32[128,256]{1,0:T(8,128)S(1)}, f32[128,256]{1,0:T(8,128)S(1)}, u32[]{:S(2)}, u32[]{:S(2)}) collective-permute-start(f32[128,256]{1,0:T(8,128)S(1)} %get-tuple-element.50), channel_id=1, source_target_pairs={{0,1},{1,0},{2,3},{3,2},{4,5},{5,4},{6,7},{7,6},{8,9},{9,8},{10,11... | collective-permute-start | bytes 393224 | tf_op jit(solution)/shard_map/ppermute | solution.py:326
  17.4 8.0 %collective-permute-start.4 = (f32[512,256]{1,0:T(8,128)S(1)}, f32[512,256]{1,0:T(8,128)S(1)}, u32[]{:S(2)}, u32[]{:S(2)}) collective-permute-start(f32[512,256]{1,0:T(8,128)S(1)} %get-tuple-element.48), channel_id=1, source_target_pairs={{0,1},{1,0},{2,3},{3,2},{4,5},{5,4},{6,7},{7,6},{8,9},{9,8},{10,11... | collective-permute-start | bytes 1572872 | tf_op jit(solution)/shard_map/ppermute | solution.py:326
  20.9 12.8 %collective-permute-start.1 = (f32[384,256]{1,0:T(8,128)S(1)}, f32[384,256]{1,0:T(8,128)S(1)}, u32[]{:S(2)}, u32[]{:S(2)}) collective-permute-start(f32[384,256]{1,0:T(8,128)S(1)} %get-tuple-element.44), channel_id=1, source_target_pairs={{0,2},{1,3},{2,0},{3,1},{4,6},{5,7},{6,4},{7,5},{8,10},{9,11},{10,... | collective-permute-start | bytes 1179656 | tf_op jit(solution)/shard_map/ppermute | solution.py:326
  23.8 19.3 %collective-permute-start.2 = (f32[384,256]{1,0:T(8,128)S(1)}, f32[384,256]{1,0:T(8,128)S(1)}, u32[]{:S(2)}, u32[]{:S(2)}) collective-permute-start(f32[384,256]{1,0:T(8,128)S(1)} %get-tuple-element.45), channel_id=1, source_target_pairs={{0,4},{1,5},{2,6},{3,7},{4,0},{5,1},{6,2},{7,3},{8,12},{9,13},{10,... | collective-permute-start | bytes 1179656 | tf_op jit(solution)/shard_map/ppermute | solution.py:326
  25.4 17.8 %collective-permute-start.3 = (f32[384,256]{1,0:T(8,128)S(1)}, f32[384,256]{1,0:T(8,128)S(1)}, u32[]{:S(2)}, u32[]{:S(2)}) collective-permute-start(f32[384,256]{1,0:T(8,128)S(1)} %get-tuple-element.46), channel_id=1, source_target_pairs={{0,6},{1,7},{2,4},{3,5},{4,2},{5,3},{6,0},{7,1},{8,14},{9,15},{10,... | collective-permute-start | bytes 1179656 | tf_op jit(solution)/shard_map/ppermute | solution.py:326
  25.6 22.0 %collective-permute-start.9 = (f32[160,256]{1,0:T(8,128)S(1)}, f32[160,256]{1,0:T(8,128)S(1)}, u32[]{:S(2)}, u32[]{:S(2)}) collective-permute-start(f32[160,256]{1,0:T(8,128)S(1)} %get-tuple-element.57), channel_id=1, source_target_pairs={{0,8},{1,9},{2,10},{3,11},{4,12},{5,13},{6,14},{7,15},{8,0},{9,1},... | collective-permute-start | bytes 491528 | tf_op jit(solution)/shard_map/ppermute | solution.py:326
  27.6 20.1 %collective-permute-start.10 = (f32[160,256]{1,0:T(8,128)S(1)}, f32[160,256]{1,0:T(8,128)S(1)}, u32[]{:S(2)}, u32[]{:S(2)}) collective-permute-start(f32[160,256]{1,0:T(8,128)S(1)} %get-tuple-element.58), channel_id=1, source_target_pairs={{0,16},{1,17},{2,18},{3,19},{4,20},{5,21},{6,22},{7,23},{8,24},{9,... | collective-permute-start | bytes 491528 | tf_op jit(solution)/shard_map/ppermute | solution.py:326
  33.7 14.0 %collective-permute-start.11 = (f32[160,256]{1,0:T(8,128)S(1)}, f32[160,256]{1,0:T(8,128)S(1)}, u32[]{:S(2)}, u32[]{:S(2)}) collective-permute-start(f32[160,256]{1,0:T(8,128)S(1)} %get-tuple-element.51), channel_id=1, source_target_pairs={{0,24},{1,25},{2,26},{3,27},{4,28},{5,29},{6,30},{7,31},{8,16},{9,... | collective-permute-start | bytes 491528 | tf_op jit(solution)/shard_map/ppermute | solution.py:326
  43.3 7.3 %collective-permute-start.6 = (f32[96,256]{1,0:T(8,128)S(1)}, f32[96,256]{1,0:T(8,128)S(1)}, u32[]{:S(2)}, u32[]{:S(2)}) collective-permute-start(f32[96,256]{1,0:T(8,128)S(1)} %get-tuple-element.53), channel_id=1, source_target_pairs={{0,8},{1,9},{2,10},{3,11},{4,12},{5,13},{6,14},{7,15},{8,0},{9,1},... | collective-permute-start | bytes 294920 | tf_op jit(solution)/shard_map/ppermute | solution.py:326
  44.9 9.7 %collective-permute-start.7 = (f32[96,256]{1,0:T(8,128)S(1)}, f32[96,256]{1,0:T(8,128)S(1)}, u32[]{:S(2)}, u32[]{:S(2)}) collective-permute-start(f32[96,256]{1,0:T(8,128)S(1)} %get-tuple-element.54), channel_id=1, source_target_pairs={{0,16},{1,17},{2,18},{3,19},{4,20},{5,21},{6,22},{7,23},{8,24},{9,... | collective-permute-start | bytes 294920 | tf_op jit(solution)/shard_map/ppermute | solution.py:326
  47.5 7.1 %collective-permute-start.8 = (f32[96,256]{1,0:T(8,128)S(1)}, f32[96,256]{1,0:T(8,128)S(1)}, u32[]{:S(2)}, u32[]{:S(2)}) collective-permute-start(f32[96,256]{1,0:T(8,128)S(1)} %get-tuple-element.55), channel_id=1, source_target_pairs={{0,24},{1,25},{2,26},{3,27},{4,28},{5,29},{6,30},{7,31},{8,16},{9,... | collective-permute-start | bytes 294920 | tf_op jit(solution)/shard_map/ppermute | solution.py:326
  47.8 7.2 %collective-permute-start.14 = (f32[160,256]{1,0:T(8,128)S(1)}, f32[160,256]{1,0:T(8,128)S(1)}, u32[]{:S(2)}, u32[]{:S(2)}) collective-permute-start(f32[160,256]{1,0:T(8,128)S(1)} %add_add_fusion.2), channel_id=1, source_target_pairs={{0,6},{1,7},{2,4},{3,5},{4,2},{5,3},{6,0},{7,1},{8,14},{9,15},{10,... | collective-permute-start | bytes 491528 | tf_op jit(solution)/shard_map/ppermute | solution.py:326
  49.3 7.4 %collective-permute-start.13 = (f32[160,256]{1,0:T(8,128)S(1)}, f32[160,256]{1,0:T(8,128)S(1)}, u32[]{:S(2)}, u32[]{:S(2)}) collective-permute-start(f32[160,256]{1,0:T(8,128)S(1)} %add_add_fusion.2), channel_id=1, source_target_pairs={{0,4},{1,5},{2,6},{3,7},{4,0},{5,1},{6,2},{7,3},{8,12},{9,13},{10,... | collective-permute-start | bytes 491528 | tf_op jit(solution)/shard_map/ppermute | solution.py:326
  50.6 6.1 %collective-permute-start.12 = (f32[160,256]{1,0:T(8,128)S(1)}, f32[160,256]{1,0:T(8,128)S(1)}, u32[]{:S(2)}, u32[]{:S(2)}) collective-permute-start(f32[160,256]{1,0:T(8,128)S(1)} %add_add_fusion.2), channel_id=1, source_target_pairs={{0,2},{1,3},{2,0},{3,1},{4,6},{5,7},{6,4},{7,5},{8,10},{9,11},{10,... | collective-permute-start | bytes 491528 | tf_op jit(solution)/shard_map/ppermute | solution.py:326
  56.8 8.3 %collective-permute-start.17 = (f32[128,256]{1,0:T(8,128)S(1)}, f32[128,256]{1,0:T(8,128)S(1)}, u32[]{:S(2)}, u32[]{:S(2)}) collective-permute-start(f32[128,256]{1,0:T(8,128)S(1)} %pad_maximum_fusion.7), channel_id=1, source_target_pairs={{0,24},{1,25},{2,26},{3,27},{4,28},{5,29},{6,30},{7,31},{8,16},{9,... | collective-permute-start | bytes 393224 | tf_op jit(solution)/shard_map/ppermute | solution.py:326
  60.4 9.5 %collective-permute-start.16 = (f32[128,256]{1,0:T(8,128)S(1)}, f32[128,256]{1,0:T(8,128)S(1)}, u32[]{:S(2)}, u32[]{:S(2)}) collective-permute-start(f32[128,256]{1,0:T(8,128)S(1)} %pad_maximum_fusion.7), channel_id=1, source_target_pairs={{0,16},{1,17},{2,18},{3,19},{4,20},{5,21},{6,22},{7,23},{8,24},{9,... | collective-permute-start | bytes 393224 | tf_op jit(solution)/shard_map/ppermute | solution.py:326
  60.4 9.5 %collective-permute-start.15 = (f32[128,256]{1,0:T(8,128)S(1)}, f32[128,256]{1,0:T(8,128)S(1)}, u32[]{:S(2)}, u32[]{:S(2)}) collective-permute-start(f32[128,256]{1,0:T(8,128)S(1)} %pad_maximum_fusion.7), channel_id=1, source_target_pairs={{0,8},{1,9},{2,10},{3,11},{4,12},{5,13},{6,14},{7,15},{8,0},{9,1},... | collective-permute-start | bytes 393224 | tf_op jit(solution)/shard_map/ppermute | solution.py:326
  70.0 5.0 %collective-permute-start.19 = (f32[128,256]{1,0:T(8,128)S(1)}, f32[128,256]{1,0:T(8,128)S(1)}, u32[]{:S(2)}, u32[]{:S(2)}) collective-permute-start(f32[128,256]{1,0:T(8,128)S(1)} %slice.159), channel_id=1, source_target_pairs={{0,8},{1,9},{2,10},{3,11},{4,12},{5,13},{6,14},{7,15},{8,0},{9,1},... | collective-permute-start | bytes 393224 | tf_op jit(solution)/shard_map/ppermute | solution.py:326
  70.4 4.7 %collective-permute-start.18 = (f32[128,256]{1,0:T(8,128)S(1)}, f32[128,256]{1,0:T(8,128)S(1)}, u32[]{:S(2)}, u32[]{:S(2)}) collective-permute-start(f32[128,256]{1,0:T(8,128)S(1)} %pad_maximum_fusion.8.kept), channel_id=1, source_target_pairs={{0,1},{1,0},{2,3},{3,2},{4,5},{5,4},{6,7},{7,6},{8,9},{9,8},{10,11... | collective-permute-start | bytes 393224 | tf_op jit(solution)/shard_map/ppermute | solution.py:326
  70.4 21.2 %collective-permute-start.23 = (f32[384,256]{1,0:T(8,128)S(1)}, f32[384,256]{1,0:T(8,128)S(1)}, u32[]{:S(2)}, u32[]{:S(2)}) collective-permute-start(f32[384,256]{1,0:T(8,128)S(1)} %pad_maximum_fusion.1.refs_0_), channel_id=1, source_target_pairs={{0,6},{1,7},{2,4},{3,5},{4,2},{5,3},{6,0},{7,1},{8,14},{9,15},{10,... | collective-permute-start | bytes 1179656 | tf_op jit(solution)/shard_map/ppermute | solution.py:326
  71.8 19.8 %collective-permute-start.22 = (f32[384,256]{1,0:T(8,128)S(1)}, f32[384,256]{1,0:T(8,128)S(1)}, u32[]{:S(2)}, u32[]{:S(2)}) collective-permute-start(f32[384,256]{1,0:T(8,128)S(1)} %pad_maximum_fusion.1.refs_0_), channel_id=1, source_target_pairs={{0,4},{1,5},{2,6},{3,7},{4,0},{5,1},{6,2},{7,3},{8,12},{9,13},{10,... | collective-permute-start | bytes 1179656 | tf_op jit(solution)/shard_map/ppermute | solution.py:326
  73.4 18.2 %collective-permute-start.21 = (f32[384,256]{1,0:T(8,128)S(1)}, f32[384,256]{1,0:T(8,128)S(1)}, u32[]{:S(2)}, u32[]{:S(2)}) collective-permute-start(f32[384,256]{1,0:T(8,128)S(1)} %pad_maximum_fusion.1.refs_0_), channel_id=1, source_target_pairs={{0,2},{1,3},{2,0},{3,1},{4,6},{5,7},{6,4},{7,5},{8,10},{9,11},{10,... | collective-permute-start | bytes 1179656 | tf_op jit(solution)/shard_map/ppermute | solution.py:326
  75.1 13.6 %copy-start = (f32[2048,256]{1,0:T(8,128)S(1)}, f32[2048,256]{1,0:T(8,128)}, u32[]{:S(2)}) copy-start(f32[2048,256]{1,0:T(8,128)} %get-tuple-element.72.sketch) | copy-start | bytes 6291460
  75.1 13.6 %collective-permute-start.24 = (f32[256,256]{1,0:T(8,128)S(1)}, f32[256,256]{1,0:T(8,128)S(1)}, u32[]{:S(2)}, u32[]{:S(2)}) collective-permute-start(f32[256,256]{1,0:T(8,128)S(1)} %pad_maximum_fusion.2), channel_id=1, source_target_pairs={{0,16},{1,17},{2,18},{3,19},{4,20},{5,21},{6,22},{7,23},{8,24},{9,... | collective-permute-start | bytes 786440 | tf_op jit(solution)/shard_map/ppermute | solution.py:326
  76.9 11.8 %collective-permute-start.20 = (f32[384,256]{1,0:T(8,128)S(1)}, f32[384,256]{1,0:T(8,128)S(1)}, u32[]{:S(2)}, u32[]{:S(2)}) collective-permute-start(f32[384,256]{1,0:T(8,128)S(1)} %pad_maximum_fusion.1.refs_0_), channel_id=1, source_target_pairs={{0,1},{1,0},{2,3},{3,2},{4,5},{5,4},{6,7},{7,6},{8,9},{9,8},{10,11... | collective-permute-start | bytes 1179656 | tf_op jit(solution)/shard_map/ppermute | solution.py:326
  91.4 3.6 %collective-permute-start.28 = (f32[512,256]{1,0:T(8,128)S(1)}, f32[512,256]{1,0:T(8,128)S(1)}, u32[]{:S(2)}, u32[]{:S(2)}) collective-permute-start(f32[512,256]{1,0:T(8,128)S(1)} %pad_maximum_fusion.refs_4_), channel_id=1, source_target_pairs={{0,1},{1,0},{2,3},{3,2},{4,5},{5,4},{6,7},{7,6},{8,9},{9,8},{10,11... | collective-permute-start | bytes 1572872 | tf_op jit(solution)/shard_map/ppermute | solution.py:326
  91.6 3.3 %collective-permute-start.25 = (f32[384,256]{1,0:T(8,128)S(1)}, f32[384,256]{1,0:T(8,128)S(1)}, u32[]{:S(2)}, u32[]{:S(2)}) collective-permute-start(f32[384,256]{1,0:T(8,128)S(1)} %collective-permute-done.21.refs_1_), channel_id=1, source_target_pairs={{0,1},{1,0},{2,3},{3,2},{4,5},{5,4},{6,7},{7,6},{8,9},{9,8},{10,11... | collective-permute-start | bytes 1179656 | tf_op jit(solution)/shard_map/ppermute | solution.py:326
  92.0 3.0 %collective-permute-start.26 = (f32[384,256]{1,0:T(8,128)S(1)}, f32[384,256]{1,0:T(8,128)S(1)}, u32[]{:S(2)}, u32[]{:S(2)}) collective-permute-start(f32[384,256]{1,0:T(8,128)S(1)} %collective-permute-done.22.refs_2_), channel_id=1, source_target_pairs={{0,1},{1,0},{2,3},{3,2},{4,5},{5,4},{6,7},{7,6},{8,9},{9,8},{10,11... | collective-permute-start | bytes 1179656 | tf_op jit(solution)/shard_map/ppermute | solution.py:326
  92.2 2.8 %collective-permute-start.27 = (f32[384,256]{1,0:T(8,128)S(1)}, f32[384,256]{1,0:T(8,128)S(1)}, u32[]{:S(2)}, u32[]{:S(2)}) collective-permute-start(f32[384,256]{1,0:T(8,128)S(1)} %collective-permute-done.23.refs_3_), channel_id=1, source_target_pairs={{0,1},{1,0},{2,3},{3,2},{4,5},{5,4},{6,7},{7,6},{8,9},{9,8},{10,11... | collective-permute-start | bytes 1179656 | tf_op jit(solution)/shard_map/ppermute | solution.py:326

commit v10 on v9

--- a/solution.py
+++ b/solution.py
@@ -42,9 +42,10 @@
 
 def front_kernel(
     in_scale, gram_scale, scale, line,
-    info, e, signs, sketch_out, gram_sent, gram_kept, sent1, sent2, kept1, kept2,
-    e_kept, sketch, rounded_t, s32, s16, acc, class1, class2, sem, out_sem,
+    info, e, signs, sketch_out, gram_sent, gram_kept, sent2, kept1, kept2, *refs,
 ):
+    sent1 = refs[:PLANE]
+    e_kept, sketch, rounded_t, s32, s16, acc, class1, class2, sem, out_sem = refs[PLANE:]
     rows, d = e.shape
     k = rounded_t.shape[0]
     n = sem.shape[0] - 1
@@ -99,7 +100,7 @@
                     (class2, kept2)[r][pl.ds(to2, size2), :] = part[rows1 + g * size2 : rows1 + (g + 1) * size2]
             if r == 0:
                 at = pl.ds(p * 2 * rows1, 2 * rows1)
-                outs.append(pltpu.make_async_copy(class1.at[at], sent1.at[at], out_sem.at[1 + p]))
+                outs.append(pltpu.make_async_copy(class1.at[at], sent1[p], out_sem.at[1 + p]))
                 outs[-1].start()
         if r == 0:
             outs.append(pltpu.make_async_copy(class2, sent2, out_sem.at[1 + PLANE]))
@@ -119,11 +120,12 @@
     return pl.pallas_call(
         functools.partial(front_kernel, 1.0 / math.sqrt(d), 1.0 / rows_all, 1.0 / math.sqrt(rows_all), line),
         in_specs=[SMEM_SPEC, ANY_SPEC, ANY_SPEC],
-        out_specs=[ANY_SPEC] + [VMEM_SPEC] * 2 + [ANY_SPEC] * 2 + [VMEM_SPEC] * 2,
+        out_specs=[ANY_SPEC] + [VMEM_SPEC] * 2 + [ANY_SPEC] + [VMEM_SPEC] * 2 + [ANY_SPEC] * PLANE,
         out_shape=[f32(rows, k)]
         + [pltpu.VMEM((k // 2, k), jnp.float32)] * 2
-        + [f32(*c) for c in classes]
-        + [pltpu.VMEM(c, jnp.float32) for c in classes],
+        + [f32(*classes[1])]
+        + [pltpu.VMEM(c, jnp.float32) for c in classes]
+        + [f32(2 * rows1, width)] * PLANE,
         scratch_shapes=[
             pltpu.VMEM((rows, d), e.dtype),
             pltpu.VMEM((rows, k), jnp.float32),
@@ -243,27 +245,34 @@
     )(info, kept, got)
 
 
-def basis_kernel(sketch, inverse, out):
-    k = sketch.shape[1]
-    s_high, s_low = split(sketch[...])
+def basis_kernel(sketch, inverse, out, value, sem):
+    rows, k = sketch.shape
+    n = sem.shape[0]
     right = ((1,), (1,))
-    both = dot(s_high, inverse[...], right)
-    out[...] = (both[:, :k] + (both[:, k:] + dot(s_low, inverse[:k, :], right))).astype(out.dtype)
+    copies = []
+    for i in range(n):
+        at = pl.ds(i * (rows // n), rows // n)
+        s_high, s_low = split(sketch[at, :])
+        both = dot(s_high, inverse[...], right)
+        value[at, :] = (both[:, :k] + (both[:, k:] + dot(s_low, inverse[:k, :], right))).astype(out.dtype)
+        copies.append(pltpu.make_async_copy(value.at[at], out.at[at], sem.at[i]))
+        copies[-1].start()
+    for copy in copies:
+        copy.wait()
 
 
 def basis_call(sketch, inverse):
     rows, k = sketch.shape
-    block = rows // 4
     return pl.pallas_call(
         basis_kernel,
-        grid=(rows // block,),
-        in_specs=[pl.BlockSpec((block, k), lambda i: (i, 0)), pl.BlockSpec((2 * k, k), lambda i: (0, 0))],
-        out_specs=pl.BlockSpec((block, k), lambda i: (i, 0)),
+        in_specs=[VMEM_SPEC] * 2,
+        out_specs=ANY_SPEC,
         out_shape=jax.ShapeDtypeStruct((rows, k), jnp.bfloat16),
+        scratch_shapes=[pltpu.VMEM((rows, k), jnp.bfloat16), pltpu.SemaphoreType.DMA((4,))],
         compiler_params=pltpu.CompilerParams(vmem_limit_bytes=16 * MIB),
         cost_estimate=pl.CostEstimate(flops=6 * rows * k * k, bytes_accessed=rows * k * 6, transcendentals=0),
         name="basis",
-    )(sketch, inverse)
+    )(*pinned(sketch, inverse))
 
 
 def project_kernel(line, is_own, info, inverse, *refs):
@@ -350,15 +359,21 @@
             last[0] = arrays[-1]
             return arrays if len(arrays) > 1 else arrays[0]
 
-        sketch, gram_sent, gram, sent1, sent2, kept1, kept2 = front_call(info, e, signs, rows_all, line)
-        got1, got2, gram_got = with_pair(sent1), with_pair(sent2), with_pair(gram_sent)
-        parts1 = in_turn(*[a + b for a, b in zip(parts_of(kept1, PLANE), parts_of(got1, PLANE))])
-        from_plane = [over_plane[g](parts1[g]) for g in range(1, PLANE)]
+        sketch, gram_sent, gram, sent2, kept1, kept2, *sent1 = front_call(info, e, signs, rows_all, line)
+        got1 = [with_pair(a) for a in sent1[1:]]
+        gram_got, got2 = with_pair(gram_sent), with_pair(sent2)
+        kept1 = parts_of(kept1, PLANE)
+        from_plane = []
+        for g in range(1, PLANE):
+            if g > 1:
+                got1[g - 1] = in_turn(got1[g - 1])
+            from_plane.append(over_plane[g](in_turn(kept1[g] + got1[g - 1])))
+        a1 = kept1[0] + with_pair(sent1[0])
         grams = parts_of(gram + gram_got, line)
         parts2 = [join(a + b, g) for a, b, g in zip(parts_of(kept2, line), parts_of(got2, line), grams)]
         parts2 = in_turn(*parts2)
         from_line = [over_line[g](parts2[g]) for g in range(1, line)]
-        parts1 = in_turn(*parts_of(sum(from_plane, parts1[0]), line))
+        parts1 = in_turn(*parts_of(sum(from_plane, a1), line))
         a2 = sum(from_line, parts2[0])
         from_line = [over_line[g](parts1[g]) for g in range(1, line)]
         a2 = in_turn(a2)

time: 97.7 us -> 96.3 us (0.986)
  waiting for transfers between devices: 27 us -> 25.8 us
    ppermute x29 -> x32, waiting for transfers between devices: 27 us -> 25.8 us  [over(): return lambda a: lax.ppermute(a, AXES, pairs)]
    ppermute x29 -> x32, starting transfers between devices: 33.5 us -> 34.1 us  [over(): return lambda a: lax.ppermute(a, AXES, pairs)]
  transfers between devices with their start and end apart: 29 -> 32, of which waited for: 10 -> 13; matrix products, arithmetic and copies ran while one was open for 1% -> 1% of each run, Pallas kernels for 17% -> 16%
where the time goes in v10:
time: 96.3 us; the launch traced here: 96.1 us
  Pallas kernels  34.3 us (36%)
  starting transfers between devices  34.1 us (35%)
  waiting for transfers between devices  25.8 us (27%)
  between operations  1.11 us (1%)
    ppermute x32, starting transfers between devices, over(): return lambda a: lax.ppermute(a, AXES, pairs)  34.1 us
    ppermute x32, waiting for transfers between devices, over(): return lambda a: lax.ppermute(a, AXES, pairs)  25.8 us
    pallas_call x1, Pallas kernels, front_call(): pl.pallas_call(functools.partial(front_kernel, 1.0 / math.sqrt(d), 1.0 /...  16.1 us
    pallas_call x1, Pallas kernels, factor_call(): pl.pallas_call(functools.partial(factor_kernel, line), in_specs=[SMEM_SPE...  11.4 us
    pallas_call x2, Pallas kernels, project_call(): pl.pallas_call(functools.partial(project_kernel, line, is_own), in_specs=...  4.87 us
  transfers between devices with their start and end apart: 32, of which 13 were waited for; matrix products, arithmetic and copies ran while one was open for 1% of the time, Pallas kernels for 16%

profile of v10, /device:TPU:0, one launch (start us, length us, event | category | flops | bytes accessed | tf_op | source)
XLA Modules:
  0.0 96.1 jit_solution(8383667889802987892)
XLA Ops:
  0.6 0.1 pad_add_fusion.info
  0.7 16.1 %front.1 = (f32[2048,256]{1,0:T(8,128)}, f32[128,256]{1,0:T(8,128)S(1)}, f32[128,256]{1,0:T(8,128)S(1)}, f32[512,256]{1,0:T(8,128)S(1)}, f32[1536,256]{1,0:T(8,1...) custom-call(s32[3]{0:T(128)S(1)} %pad_add_fusion.info, ...), custom_call_target="tpu_custom_call" | custom-call | flops 8589934592 | bytes 20971520 | tf_op jit(solution)/shard_map/front/pallas_call | solution.py:120
  16.8 0.5 collective-permute-start.1
  17.4 0.1 collective-permute-start.8
  17.4 0.4 collective-permute-start
  17.9 0.1 collective-permute-start.3
  18.0 0.4 collective-permute-start.5
  18.4 0.5 collective-permute-done.8
  18.9 0.4 collective-permute-start.7
  19.4 2.7 %collective-permute-start.2 = (f32[384,256]{1,0:T(8,128)S(1)}, f32[384,256]{1,0:T(8,128)S(1)}, u32[]{:S(2)}, u32[]{:S(2)}) collective-permute-start(f32[384,256]{1,0:T(8,128)S(1)} %slice_add_fusion.2), channel_id=1, source_target_pairs={{0,2},{1,3},{2,0},{3,1},{4,6},{5,7},{6,4},{7,5},{8,10},{9,11},{10,... | collective-permute-start | bytes 1179656 | tf_op jit(solution)/shard_map/ppermute | solution.py:335
  22.2 1.6 %collective-permute-start.4 = (f32[384,256]{1,0:T(8,128)S(1)}, f32[384,256]{1,0:T(8,128)S(1)}, u32[]{:S(2)}, u32[]{:S(2)}) collective-permute-start(f32[384,256]{1,0:T(8,128)S(1)} %slice_add_fusion.1), channel_id=1, source_target_pairs={{0,4},{1,5},{2,6},{3,7},{4,0},{5,1},{6,2},{7,3},{8,12},{9,13},{10,... | collective-permute-start | bytes 1179656 | tf_op jit(solution)/shard_map/ppermute | solution.py:335
  23.8 0.8 collective-permute-start.6
  24.6 0.1 slice_add_fusion.3
  24.8 1.6 %collective-permute-start.12 = (f32[160,256]{1,0:T(8,128)S(1)}, f32[160,256]{1,0:T(8,128)S(1)}, u32[]{:S(2)}, u32[]{:S(2)}) collective-permute-start(f32[160,256]{1,0:T(8,128)S(1)} %get-tuple-element.65), channel_id=1, source_target_pairs={{0,8},{1,9},{2,10},{3,11},{4,12},{5,13},{6,14},{7,15},{8,0},{9,1},... | collective-permute-start | bytes 491528 | tf_op jit(solution)/shard_map/ppermute | solution.py:335
  26.4 2.6 %collective-permute-start.13 = (f32[160,256]{1,0:T(8,128)S(1)}, f32[160,256]{1,0:T(8,128)S(1)}, u32[]{:S(2)}, u32[]{:S(2)}) collective-permute-start(f32[160,256]{1,0:T(8,128)S(1)} %get-tuple-element.66), channel_id=1, source_target_pairs={{0,16},{1,17},{2,18},{3,19},{4,20},{5,21},{6,22},{7,23},{8,24},{9,... | collective-permute-start | bytes 491528 | tf_op jit(solution)/shard_map/ppermute | solution.py:335
  29.0 3.1 %collective-permute-done.2 = f32[384,256]{1,0:T(8,128)S(1)} collective-permute-done((f32[384,256]{1,0:T(8,128)S(1)}, f32[384,256]{1,0:T(8,128)S(1)}, u32[]{:S(2)}, u32[]{:S(2)}) %collective-permute-start.2) | collective-permute-done | bytes 393248 | tf_op jit(solution)/shard_map/ppermute | solution.py:335
  32.1 4.1 %collective-permute-start.14 = (f32[160,256]{1,0:T(8,128)S(1)}, f32[160,256]{1,0:T(8,128)S(1)}, u32[]{:S(2)}, u32[]{:S(2)}) collective-permute-start(f32[160,256]{1,0:T(8,128)S(1)} %get-tuple-element.59), channel_id=1, source_target_pairs={{0,24},{1,25},{2,26},{3,27},{4,28},{5,29},{6,30},{7,31},{8,16},{9,... | collective-permute-start | bytes 491528 | tf_op jit(solution)/shard_map/ppermute | solution.py:335
  36.1 5.6 %collective-permute-done.4 = f32[384,256]{1,0:T(8,128)S(1)} collective-permute-done((f32[384,256]{1,0:T(8,128)S(1)}, f32[384,256]{1,0:T(8,128)S(1)}, u32[]{:S(2)}, u32[]{:S(2)}) %collective-permute-start.4) | collective-permute-done | bytes 393248 | tf_op jit(solution)/shard_map/ppermute | solution.py:335
  41.8 0.1 add_add_fusion
  41.9 1.6 %collective-permute-start.9 = (f32[96,256]{1,0:T(8,128)S(1)}, f32[96,256]{1,0:T(8,128)S(1)}, u32[]{:S(2)}, u32[]{:S(2)}) collective-permute-start(f32[96,256]{1,0:T(8,128)S(1)} %get-tuple-element.61), channel_id=1, source_target_pairs={{0,8},{1,9},{2,10},{3,11},{4,12},{5,13},{6,14},{7,15},{8,0},{9,1},... | collective-permute-start | bytes 294920 | tf_op jit(solution)/shard_map/ppermute | solution.py:335
  43.6 2.6 %collective-permute-start.10 = (f32[96,256]{1,0:T(8,128)S(1)}, f32[96,256]{1,0:T(8,128)S(1)}, u32[]{:S(2)}, u32[]{:S(2)}) collective-permute-start(f32[96,256]{1,0:T(8,128)S(1)} %get-tuple-element.62), channel_id=1, source_target_pairs={{0,16},{1,17},{2,18},{3,19},{4,20},{5,21},{6,22},{7,23},{8,24},{9,... | collective-permute-start | bytes 294920 | tf_op jit(solution)/shard_map/ppermute | solution.py:335
  46.2 0.2 collective-permute-start.11
  46.4 1.9 %collective-permute-start.17 = (f32[160,256]{1,0:T(8,128)S(1)}, f32[160,256]{1,0:T(8,128)S(1)}, u32[]{:S(2)}, u32[]{:S(2)}) collective-permute-start(f32[160,256]{1,0:T(8,128)S(1)} %add_add_fusion.2), channel_id=1, source_target_pairs={{0,6},{1,7},{2,4},{3,5},{4,2},{5,3},{6,0},{7,1},{8,14},{9,15},{10,... | collective-permute-start | bytes 491528 | tf_op jit(solution)/shard_map/ppermute | solution.py:335
  48.3 0.8 collective-permute-start.16
  49.1 0.9 collective-permute-start.15
  50.0 3.4 %collective-permute-done.10 = f32[96,256]{1,0:T(8,128)S(1)} collective-permute-done((f32[96,256]{1,0:T(8,128)S(1)}, f32[96,256]{1,0:T(8,128)S(1)}, u32[]{:S(2)}, u32[]{:S(2)}) %collective-permute-start.10) | collective-permute-done | bytes 98336 | tf_op jit(solution)/shard_map/ppermute | solution.py:335
  53.4 0.4 collective-permute-done.17
  53.8 1.7 %collective-permute-done.16 = f32[160,256]{1,0:T(8,128)S(1)} collective-permute-done((f32[160,256]{1,0:T(8,128)S(1)}, f32[160,256]{1,0:T(8,128)S(1)}, u32[]{:S(2)}, u32[]{:S(2)}) %collective-permute-start.16) | collective-permute-done | bytes 163872 | tf_op jit(solution)/shard_map/ppermute | solution.py:335
  55.5 0.1 collective-permute-done.15
  55.6 3.6 %collective-permute-start.20 = (f32[128,256]{1,0:T(8,128)S(1)}, f32[128,256]{1,0:T(8,128)S(1)}, u32[]{:S(2)}, u32[]{:S(2)}) collective-permute-start(f32[128,256]{1,0:T(8,128)S(1)} %pad_maximum_fusion.7), channel_id=1, source_target_pairs={{0,24},{1,25},{2,26},{3,27},{4,28},{5,29},{6,30},{7,31},{8,16},{9,... | collective-permute-start | bytes 393224 | tf_op jit(solution)/shard_map/ppermute | solution.py:335
  59.2 0.9 collective-permute-start.18
  60.1 3.7 %collective-permute-done.20 = f32[128,256]{1,0:T(8,128)S(1)} collective-permute-done((f32[128,256]{1,0:T(8,128)S(1)}, f32[128,256]{1,0:T(8,128)S(1)}, u32[]{:S(2)}, u32[]{:S(2)}) %collective-permute-start.20) | collective-permute-done | bytes 131104 | tf_op jit(solution)/shard_map/ppermute | solution.py:335
  63.8 4.8 %collective-permute-done.19 = f32[128,256]{1,0:T(8,128)S(1)} collective-permute-done((f32[128,256]{1,0:T(8,128)S(1)}, f32[128,256]{1,0:T(8,128)S(1)}, u32[]{:S(2)}, u32[]{:S(2)}) %collective-permute-start.19) | collective-permute-done | bytes 131104 | tf_op jit(solution)/shard_map/ppermute | solution.py:335
  68.7 0.3 collective-permute-start.22
  69.1 1.4 %collective-permute-start.26 = (f32[384,256]{1,0:T(8,128)S(1)}, f32[384,256]{1,0:T(8,128)S(1)}, u32[]{:S(2)}, u32[]{:S(2)}) collective-permute-start(f32[384,256]{1,0:T(8,128)S(1)} %pad_maximum_fusion.1.refs_0_), channel_id=1, source_target_pairs={{0,6},{1,7},{2,4},{3,5},{4,2},{5,3},{6,0},{7,1},{8,14},{9,15},{10,... | collective-permute-start | bytes 1179656 | tf_op jit(solution)/shard_map/ppermute | solution.py:335
  70.5 1.8 %collective-permute-start.25 = (f32[384,256]{1,0:T(8,128)S(1)}, f32[384,256]{1,0:T(8,128)S(1)}, u32[]{:S(2)}, u32[]{:S(2)}) collective-permute-start(f32[384,256]{1,0:T(8,128)S(1)} %pad_maximum_fusion.1.refs_0_), channel_id=1, source_target_pairs={{0,4},{1,5},{2,6},{3,7},{4,0},{5,1},{6,2},{7,3},{8,12},{9,13},{10,... | collective-permute-start | bytes 1179656 | tf_op jit(solution)/shard_map/ppermute | solution.py:335
  72.3 0.3 collective-permute-start.24
  72.6 1.2 %collective-permute-done.22 = f32[128,256]{1,0:T(8,128)S(1)} collective-permute-done((f32[128,256]{1,0:T(8,128)S(1)}, f32[128,256]{1,0:T(8,128)S(1)}, u32[]{:S(2)}, u32[]{:S(2)}) %collective-permute-start.22) | collective-permute-done | bytes 131104 | tf_op jit(solution)/shard_map/ppermute | solution.py:335
  73.8 1.8 %collective-permute-start.27 = (f32[256,256]{1,0:T(8,128)S(1)}, f32[256,256]{1,0:T(8,128)S(1)}, u32[]{:S(2)}, u32[]{:S(2)}) collective-permute-start(f32[256,256]{1,0:T(8,128)S(1)} %pad_maximum_fusion.2), channel_id=1, source_target_pairs={{0,16},{1,17},{2,18},{3,19},{4,20},{5,21},{6,22},{7,23},{8,24},{9,... | collective-permute-start | bytes 786440 | tf_op jit(solution)/shard_map/ppermute | solution.py:335
  75.6 11.4 %factor.1 = (f32[256,256]{1,0:T(8,128)}, bf16[512,256]{1,0:T(8,128)(2,1)S(1)}) custom-call(s32[3]{0:T(128)S(1)} %pad_add_fusion.info, f32[128,256]{1,0:T(8,128)S(1)} %pad_maximum_fusion.8.kept, f32[128,256]{1,0:T(8,128)S(1)} %collective-permute-done.21.got), custom_call_target="tpu_custom_call" | custom-call | flops 10000000000 | bytes 524288 | tf_op jit(solution)/shard_map/factor/pallas_call | solution.py:233
  87.0 0.4 collective-permute-done.27
  87.5 1.9 %basis.1 = bf16[2048,256]{1,0:T(8,128)(2,1)} custom-call(f32[2048,256]{1,0:T(8,128)S(1)} %copy-done, bf16[512,256]{1,0:T(8,128)(2,1)S(1)} %get-tuple-element.79.inverse), custom_call_target="tpu_custom_call" | custom-call | flops 805306368 | bytes 3145728 | tf_op jit(solution)/shard_map/basis/pallas_call | solution.py:266
  89.4 0.2 collective-permute-start.31
  89.6 0.4 collective-permute-done.25.refs_2_
  89.9 0.5 collective-permute-done.24.refs_1_
  90.5 0.5 collective-permute-start.29
  91.0 2.4 %project.2.refs_0_ = f32[256,4096]{1,0:T(8,128)} custom-call(s32[3]{0:T(128)S(1)} %pad_add_fusion.info, bf16[512,256]{1,0:T(8,128)(2,1)S(1)} %get-tuple-element.79.inverse, f32[384,256]{1,0:T(8,128)S(1)} %pad_maximum_fusion.1.refs_0_, f32[384,256]{1,0:T(8,128)S(1)} %collective-permute-done.24.refs_1_, f32[384,256]{1,0:T(8,128)S(1)} %collective-permute-done.25.refs_2_, ...), custom_call_target="tpu_custom_call" | custom-call | flops 805306368 | bytes 4194304 | tf_op jit(solution)/shard_map/project/pallas_call | solution.py:312
  93.5 2.4 %project.3 = f32[256,4096]{1,0:T(8,128)} custom-call(s32[3]{0:T(128)S(1)} %pad_add_fusion.info, bf16[512,256]{1,0:T(8,128)(2,1)S(1)} %get-tuple-element.79.inverse, f32[256,4096]{1,0:T(8,128)} %project.2.refs_0_, f32[384,256]{1,0:T(8,128)S(1)} %collective-permute-done.23.refs_1_, ...), custom_call_target="tpu_custom_call", output_to_operand_aliasing={{}: (2, {})} | custom-call | flops 805306368 | bytes 4194304 | tf_op jit(solution)/shard_map/project/pallas_call | solution.py:312
  (52 shorter events, 0.6 us)
Async XLA Ops:
  16.8 2.5 %collective-permute-start.1 = (f32[384,256]{1,0:T(8,128)S(1)}, f32[384,256]{1,0:T(8,128)S(1)}, u32[]{:S(2)}, u32[]{:S(2)}) collective-permute-start(f32[384,256]{1,0:T(8,128)S(1)} %get-tuple-element.47), channel_id=1, source_target_pairs={{0,1},{1,0},{2,3},{3,2},{4,5},{5,4},{6,7},{7,6},{8,9},{9,8},{10,11... | collective-permute-start | bytes 1179656 | tf_op jit(solution)/shard_map/ppermute | solution.py:335
  17.4 1.5 %collective-permute-start.8 = (f32[128,256]{1,0:T(8,128)S(1)}, f32[128,256]{1,0:T(8,128)S(1)}, u32[]{:S(2)}, u32[]{:S(2)}) collective-permute-start(f32[128,256]{1,0:T(8,128)S(1)} %get-tuple-element.58), channel_id=1, source_target_pairs={{0,1},{1,0},{2,3},{3,2},{4,5},{5,4},{6,7},{7,6},{8,9},{9,8},{10,11... | collective-permute-start | bytes 393224 | tf_op jit(solution)/shard_map/ppermute | solution.py:335
  17.4 8.9 %collective-permute-start = (f32[384,256]{1,0:T(8,128)S(1)}, f32[384,256]{1,0:T(8,128)S(1)}, u32[]{:S(2)}, u32[]{:S(2)}) collective-permute-start(f32[384,256]{1,0:T(8,128)S(1)} %get-tuple-element.46), channel_id=1, source_target_pairs={{0,1},{1,0},{2,3},{3,2},{4,5},{5,4},{6,7},{7,6},{8,9},{9,8},{10,11... | collective-permute-start | bytes 1179656 | tf_op jit(solution)/shard_map/ppermute | solution.py:335
  17.9 4.2 %collective-permute-start.3 = (f32[384,256]{1,0:T(8,128)S(1)}, f32[384,256]{1,0:T(8,128)S(1)}, u32[]{:S(2)}, u32[]{:S(2)}) collective-permute-start(f32[384,256]{1,0:T(8,128)S(1)} %get-tuple-element.49), channel_id=1, source_target_pairs={{0,1},{1,0},{2,3},{3,2},{4,5},{5,4},{6,7},{7,6},{8,9},{9,8},{10,11... | collective-permute-start | bytes 1179656 | tf_op jit(solution)/shard_map/ppermute | solution.py:335
  18.0 5.8 %collective-permute-start.5 = (f32[384,256]{1,0:T(8,128)S(1)}, f32[384,256]{1,0:T(8,128)S(1)}, u32[]{:S(2)}, u32[]{:S(2)}) collective-permute-start(f32[384,256]{1,0:T(8,128)S(1)} %get-tuple-element.52), channel_id=1, source_target_pairs={{0,1},{1,0},{2,3},{3,2},{4,5},{5,4},{6,7},{7,6},{8,9},{9,8},{10,11... | collective-permute-start | bytes 1179656 | tf_op jit(solution)/shard_map/ppermute | solution.py:335
  18.9 5.7 %collective-permute-start.7 = (f32[512,256]{1,0:T(8,128)S(1)}, f32[512,256]{1,0:T(8,128)S(1)}, u32[]{:S(2)}, u32[]{:S(2)}) collective-permute-start(f32[512,256]{1,0:T(8,128)S(1)} %get-tuple-element.56), channel_id=1, source_target_pairs={{0,1},{1,0},{2,3},{3,2},{4,5},{5,4},{6,7},{7,6},{8,9},{9,8},{10,11... | collective-permute-start | bytes 1572872 | tf_op jit(solution)/shard_map/ppermute | solution.py:335
  19.4 12.7 %collective-permute-start.2 = (f32[384,256]{1,0:T(8,128)S(1)}, f32[384,256]{1,0:T(8,128)S(1)}, u32[]{:S(2)}, u32[]{:S(2)}) collective-permute-start(f32[384,256]{1,0:T(8,128)S(1)} %slice_add_fusion.2), channel_id=1, source_target_pairs={{0,2},{1,3},{2,0},{3,1},{4,6},{5,7},{6,4},{7,5},{8,10},{9,11},{10,... | collective-permute-start | bytes 1179656 | tf_op jit(solution)/shard_map/ppermute | solution.py:335
  22.2 19.6 %collective-permute-start.4 = (f32[384,256]{1,0:T(8,128)S(1)}, f32[384,256]{1,0:T(8,128)S(1)}, u32[]{:S(2)}, u32[]{:S(2)}) collective-permute-start(f32[384,256]{1,0:T(8,128)S(1)} %slice_add_fusion.1), channel_id=1, source_target_pairs={{0,4},{1,5},{2,6},{3,7},{4,0},{5,1},{6,2},{7,3},{8,12},{9,13},{10,... | collective-permute-start | bytes 1179656 | tf_op jit(solution)/shard_map/ppermute | solution.py:335
  23.8 17.9 %collective-permute-start.6 = (f32[384,256]{1,0:T(8,128)S(1)}, f32[384,256]{1,0:T(8,128)S(1)}, u32[]{:S(2)}, u32[]{:S(2)}) collective-permute-start(f32[384,256]{1,0:T(8,128)S(1)} %slice_add_fusion), channel_id=1, source_target_pairs={{0,6},{1,7},{2,4},{3,5},{4,2},{5,3},{6,0},{7,1},{8,14},{9,15},{10,... | collective-permute-start | bytes 1179656 | tf_op jit(solution)/shard_map/ppermute | solution.py:335
  24.8 21.4 %collective-permute-start.12 = (f32[160,256]{1,0:T(8,128)S(1)}, f32[160,256]{1,0:T(8,128)S(1)}, u32[]{:S(2)}, u32[]{:S(2)}) collective-permute-start(f32[160,256]{1,0:T(8,128)S(1)} %get-tuple-element.65), channel_id=1, source_target_pairs={{0,8},{1,9},{2,10},{3,11},{4,12},{5,13},{6,14},{7,15},{8,0},{9,1},... | collective-permute-start | bytes 491528 | tf_op jit(solution)/shard_map/ppermute | solution.py:335
  26.4 20.0 %collective-permute-start.13 = (f32[160,256]{1,0:T(8,128)S(1)}, f32[160,256]{1,0:T(8,128)S(1)}, u32[]{:S(2)}, u32[]{:S(2)}) collective-permute-start(f32[160,256]{1,0:T(8,128)S(1)} %get-tuple-element.66), channel_id=1, source_target_pairs={{0,16},{1,17},{2,18},{3,19},{4,20},{5,21},{6,22},{7,23},{8,24},{9,... | collective-permute-start | bytes 491528 | tf_op jit(solution)/shard_map/ppermute | solution.py:335
  32.1 14.3 %collective-permute-start.14 = (f32[160,256]{1,0:T(8,128)S(1)}, f32[160,256]{1,0:T(8,128)S(1)}, u32[]{:S(2)}, u32[]{:S(2)}) collective-permute-start(f32[160,256]{1,0:T(8,128)S(1)} %get-tuple-element.59), channel_id=1, source_target_pairs={{0,24},{1,25},{2,26},{3,27},{4,28},{5,29},{6,30},{7,31},{8,16},{9,... | collective-permute-start | bytes 491528 | tf_op jit(solution)/shard_map/ppermute | solution.py:335
  41.9 7.1 %collective-permute-start.9 = (f32[96,256]{1,0:T(8,128)S(1)}, f32[96,256]{1,0:T(8,128)S(1)}, u32[]{:S(2)}, u32[]{:S(2)}) collective-permute-start(f32[96,256]{1,0:T(8,128)S(1)} %get-tuple-element.61), channel_id=1, source_target_pairs={{0,8},{1,9},{2,10},{3,11},{4,12},{5,13},{6,14},{7,15},{8,0},{9,1},... | collective-permute-start | bytes 294920 | tf_op jit(solution)/shard_map/ppermute | solution.py:335
  43.6 9.8 %collective-permute-start.10 = (f32[96,256]{1,0:T(8,128)S(1)}, f32[96,256]{1,0:T(8,128)S(1)}, u32[]{:S(2)}, u32[]{:S(2)}) collective-permute-start(f32[96,256]{1,0:T(8,128)S(1)} %get-tuple-element.62), channel_id=1, source_target_pairs={{0,16},{1,17},{2,18},{3,19},{4,20},{5,21},{6,22},{7,23},{8,24},{9,... | collective-permute-start | bytes 294920 | tf_op jit(solution)/shard_map/ppermute | solution.py:335
  46.2 7.2 %collective-permute-start.11 = (f32[96,256]{1,0:T(8,128)S(1)}, f32[96,256]{1,0:T(8,128)S(1)}, u32[]{:S(2)}, u32[]{:S(2)}) collective-permute-start(f32[96,256]{1,0:T(8,128)S(1)} %get-tuple-element.63), channel_id=1, source_target_pairs={{0,24},{1,25},{2,26},{3,27},{4,28},{5,29},{6,30},{7,31},{8,16},{9,... | collective-permute-start | bytes 294920 | tf_op jit(solution)/shard_map/ppermute | solution.py:335
  46.4 7.4 %collective-permute-start.17 = (f32[160,256]{1,0:T(8,128)S(1)}, f32[160,256]{1,0:T(8,128)S(1)}, u32[]{:S(2)}, u32[]{:S(2)}) collective-permute-start(f32[160,256]{1,0:T(8,128)S(1)} %add_add_fusion.2), channel_id=1, source_target_pairs={{0,6},{1,7},{2,4},{3,5},{4,2},{5,3},{6,0},{7,1},{8,14},{9,15},{10,... | collective-permute-start | bytes 491528 | tf_op jit(solution)/shard_map/ppermute | solution.py:335
  48.3 7.1 %collective-permute-start.16 = (f32[160,256]{1,0:T(8,128)S(1)}, f32[160,256]{1,0:T(8,128)S(1)}, u32[]{:S(2)}, u32[]{:S(2)}) collective-permute-start(f32[160,256]{1,0:T(8,128)S(1)} %add_add_fusion.2), channel_id=1, source_target_pairs={{0,4},{1,5},{2,6},{3,7},{4,0},{5,1},{6,2},{7,3},{8,12},{9,13},{10,... | collective-permute-start | bytes 491528 | tf_op jit(solution)/shard_map/ppermute | solution.py:335
  49.1 6.5 %collective-permute-start.15 = (f32[160,256]{1,0:T(8,128)S(1)}, f32[160,256]{1,0:T(8,128)S(1)}, u32[]{:S(2)}, u32[]{:S(2)}) collective-permute-start(f32[160,256]{1,0:T(8,128)S(1)} %add_add_fusion.2), channel_id=1, source_target_pairs={{0,2},{1,3},{2,0},{3,1},{4,6},{5,7},{6,4},{7,5},{8,10},{9,11},{10,... | collective-permute-start | bytes 491528 | tf_op jit(solution)/shard_map/ppermute | solution.py:335
  55.6 8.2 %collective-permute-start.20 = (f32[128,256]{1,0:T(8,128)S(1)}, f32[128,256]{1,0:T(8,128)S(1)}, u32[]{:S(2)}, u32[]{:S(2)}) collective-permute-start(f32[128,256]{1,0:T(8,128)S(1)} %pad_maximum_fusion.7), channel_id=1, source_target_pairs={{0,24},{1,25},{2,26},{3,27},{4,28},{5,29},{6,30},{7,31},{8,16},{9,... | collective-permute-start | bytes 393224 | tf_op jit(solution)/shard_map/ppermute | solution.py:335
  59.2 9.4 %collective-permute-start.19 = (f32[128,256]{1,0:T(8,128)S(1)}, f32[128,256]{1,0:T(8,128)S(1)}, u32[]{:S(2)}, u32[]{:S(2)}) collective-permute-start(f32[128,256]{1,0:T(8,128)S(1)} %pad_maximum_fusion.7), channel_id=1, source_target_pairs={{0,16},{1,17},{2,18},{3,19},{4,20},{5,21},{6,22},{7,23},{8,24},{9,... | collective-permute-start | bytes 393224 | tf_op jit(solution)/shard_map/ppermute | solution.py:335
  59.2 9.4 %collective-permute-start.18 = (f32[128,256]{1,0:T(8,128)S(1)}, f32[128,256]{1,0:T(8,128)S(1)}, u32[]{:S(2)}, u32[]{:S(2)}) collective-permute-start(f32[128,256]{1,0:T(8,128)S(1)} %pad_maximum_fusion.7), channel_id=1, source_target_pairs={{0,8},{1,9},{2,10},{3,11},{4,12},{5,13},{6,14},{7,15},{8,0},{9,1},... | collective-permute-start | bytes 393224 | tf_op jit(solution)/shard_map/ppermute | solution.py:335
  68.7 5.0 %collective-permute-start.22 = (f32[128,256]{1,0:T(8,128)S(1)}, f32[128,256]{1,0:T(8,128)S(1)}, u32[]{:S(2)}, u32[]{:S(2)}) collective-permute-start(f32[128,256]{1,0:T(8,128)S(1)} %slice.139), channel_id=1, source_target_pairs={{0,8},{1,9},{2,10},{3,11},{4,12},{5,13},{6,14},{7,15},{8,0},{9,1},... | collective-permute-start | bytes 393224 | tf_op jit(solution)/shard_map/ppermute | solution.py:335
  69.1 4.7 %collective-permute-start.21 = (f32[128,256]{1,0:T(8,128)S(1)}, f32[128,256]{1,0:T(8,128)S(1)}, u32[]{:S(2)}, u32[]{:S(2)}) collective-permute-start(f32[128,256]{1,0:T(8,128)S(1)} %pad_maximum_fusion.8.kept), channel_id=1, source_target_pairs={{0,1},{1,0},{2,3},{3,2},{4,5},{5,4},{6,7},{7,6},{8,9},{9,8},{10,11... | collective-permute-start | bytes 393224 | tf_op jit(solution)/shard_map/ppermute | solution.py:335
  69.1 20.5 %collective-permute-start.26 = (f32[384,256]{1,0:T(8,128)S(1)}, f32[384,256]{1,0:T(8,128)S(1)}, u32[]{:S(2)}, u32[]{:S(2)}) collective-permute-start(f32[384,256]{1,0:T(8,128)S(1)} %pad_maximum_fusion.1.refs_0_), channel_id=1, source_target_pairs={{0,6},{1,7},{2,4},{3,5},{4,2},{5,3},{6,0},{7,1},{8,14},{9,15},{10,... | collective-permute-start | bytes 1179656 | tf_op jit(solution)/shard_map/ppermute | solution.py:335
  70.5 19.4 %collective-permute-start.25 = (f32[384,256]{1,0:T(8,128)S(1)}, f32[384,256]{1,0:T(8,128)S(1)}, u32[]{:S(2)}, u32[]{:S(2)}) collective-permute-start(f32[384,256]{1,0:T(8,128)S(1)} %pad_maximum_fusion.1.refs_0_), channel_id=1, source_target_pairs={{0,4},{1,5},{2,6},{3,7},{4,0},{5,1},{6,2},{7,3},{8,12},{9,13},{10,... | collective-permute-start | bytes 1179656 | tf_op jit(solution)/shard_map/ppermute | solution.py:335
  72.3 18.2 %collective-permute-start.24 = (f32[384,256]{1,0:T(8,128)S(1)}, f32[384,256]{1,0:T(8,128)S(1)}, u32[]{:S(2)}, u32[]{:S(2)}) collective-permute-start(f32[384,256]{1,0:T(8,128)S(1)} %pad_maximum_fusion.1.refs_0_), channel_id=1, source_target_pairs={{0,2},{1,3},{2,0},{3,1},{4,6},{5,7},{6,4},{7,5},{8,10},{9,11},{10,... | collective-permute-start | bytes 1179656 | tf_op jit(solution)/shard_map/ppermute | solution.py:335
  73.8 13.7 %copy-start = (f32[2048,256]{1,0:T(8,128)S(1)}, f32[2048,256]{1,0:T(8,128)}, u32[]{:S(2)}) copy-start(f32[2048,256]{1,0:T(8,128)} %get-tuple-element.80.sketch) | copy-start | bytes 6291460
  73.8 13.6 %collective-permute-start.27 = (f32[256,256]{1,0:T(8,128)S(1)}, f32[256,256]{1,0:T(8,128)S(1)}, u32[]{:S(2)}, u32[]{:S(2)}) collective-permute-start(f32[256,256]{1,0:T(8,128)S(1)} %pad_maximum_fusion.2), channel_id=1, source_target_pairs={{0,16},{1,17},{2,18},{3,19},{4,20},{5,21},{6,22},{7,23},{8,24},{9,... | collective-permute-start | bytes 786440 | tf_op jit(solution)/shard_map/ppermute | solution.py:335
  75.6 11.9 %collective-permute-start.23 = (f32[384,256]{1,0:T(8,128)S(1)}, f32[384,256]{1,0:T(8,128)S(1)}, u32[]{:S(2)}, u32[]{:S(2)}) collective-permute-start(f32[384,256]{1,0:T(8,128)S(1)} %pad_maximum_fusion.1.refs_0_), channel_id=1, source_target_pairs={{0,1},{1,0},{2,3},{3,2},{4,5},{5,4},{6,7},{7,6},{8,9},{9,8},{10,11... | collective-permute-start | bytes 1179656 | tf_op jit(solution)/shard_map/ppermute | solution.py:335
  89.4 4.1 %collective-permute-start.31 = (f32[512,256]{1,0:T(8,128)S(1)}, f32[512,256]{1,0:T(8,128)S(1)}, u32[]{:S(2)}, u32[]{:S(2)}) collective-permute-start(f32[512,256]{1,0:T(8,128)S(1)} %pad_maximum_fusion.refs_4_), channel_id=1, source_target_pairs={{0,1},{1,0},{2,3},{3,2},{4,5},{5,4},{6,7},{7,6},{8,9},{9,8},{10,11... | collective-permute-start | bytes 1572872 | tf_op jit(solution)/shard_map/ppermute | solution.py:335
  90.5 3.0 %collective-permute-start.28 = (f32[384,256]{1,0:T(8,128)S(1)}, f32[384,256]{1,0:T(8,128)S(1)}, u32[]{:S(2)}, u32[]{:S(2)}) collective-permute-start(f32[384,256]{1,0:T(8,128)S(1)} %collective-permute-done.24.refs_1_), channel_id=1, source_target_pairs={{0,1},{1,0},{2,3},{3,2},{4,5},{5,4},{6,7},{7,6},{8,9},{9,8},{10,11... | collective-permute-start | bytes 1179656 | tf_op jit(solution)/shard_map/ppermute | solution.py:335
  90.5 3.0 %collective-permute-start.29 = (f32[384,256]{1,0:T(8,128)S(1)}, f32[384,256]{1,0:T(8,128)S(1)}, u32[]{:S(2)}, u32[]{:S(2)}) collective-permute-start(f32[384,256]{1,0:T(8,128)S(1)} %collective-permute-done.25.refs_2_), channel_id=1, source_target_pairs={{0,1},{1,0},{2,3},{3,2},{4,5},{5,4},{6,7},{7,6},{8,9},{9,8},{10,11... | collective-permute-start | bytes 1179656 | tf_op jit(solution)/shard_map/ppermute | solution.py:335
  91.0 2.5 %collective-permute-start.30 = (f32[384,256]{1,0:T(8,128)S(1)}, f32[384,256]{1,0:T(8,128)S(1)}, u32[]{:S(2)}, u32[]{:S(2)}) collective-permute-start(f32[384,256]{1,0:T(8,128)S(1)} %collective-permute-done.26.refs_3_), channel_id=1, source_target_pairs={{0,1},{1,0},{2,3},{3,2},{4,5},{5,4},{6,7},{7,6},{8,9},{9,8},{10,11... | collective-permute-start | bytes 1179656 | tf_op jit(solution)/shard_map/ppermute | solution.py:335

commit v11 on v10

--- a/solution.py
+++ b/solution.py
@@ -23,7 +23,6 @@
 
 
 VMEM_SPEC = pl.BlockSpec(memory_space=pltpu.VMEM)
-SMEM_SPEC = pl.BlockSpec(memory_space=pltpu.SMEM)
 ANY_SPEC = pl.BlockSpec(memory_space=pl.ANY)
 
 
@@ -32,6 +31,12 @@
 
 
 PLANE = 4
+FRONT_BLOCKS = (0, 1, 2, 4, 6, 8)
+
+
+def place():
+    index = lax.axis_index(AXES[0]) * lax.axis_size(AXES[1]) + lax.axis_index(AXES[1])
+    return index & 1, (index >> 1) & (PLANE - 1), index // (2 * PLANE)
 
 
 def row_classes(k, line):
@@ -40,51 +45,43 @@
     return k - second, second
 
 
-def front_kernel(
-    in_scale, gram_scale, scale, line,
-    info, e, signs, sketch_out, gram_sent, gram_kept, sent2, kept1, kept2, *refs,
-):
+def front_kernel(in_scale, gram_scale, scale, line, e, signs, sketch_out, sent2, kept1, kept2, *refs):
     sent1 = refs[:PLANE]
     e_kept, sketch, rounded_t, s32, s16, acc, class1, class2, sem, out_sem = refs[PLANE:]
     rows, d = e.shape
     k = rounded_t.shape[0]
     n = sem.shape[0] - 1
-    block = rows // n
     signs_copy = pltpu.make_async_copy(signs, s32, sem.at[n])
     signs_copy.start()
 
-    def rows_copy(i):
-        at = pl.ds(pl.multiple_of(i * block, block), block)
-        return pltpu.make_async_copy(e.at[at], e_kept.at[at], sem.at[i])
-
-    for i in range(n):
-        rows_copy(i).start()
+    starts = [rows * i // 8 for i in FRONT_BLOCKS]
+    blocks = [pl.ds(a, b - a) for a, b in zip(starts, starts[1:])]
+    copies = [pltpu.make_async_copy(e.at[at], e_kept.at[at], sem.at[i]) for i, at in enumerate(blocks)]
+    for copy in copies:
+        copy.start()
     signs_copy.wait()
     s16[...] = s32[...].astype(jnp.bfloat16)
 
-    def step(i, carry):
-        rows_copy(i).wait()
-        at = pl.ds(pl.multiple_of(i * block, block), block)
+    for copy, at in zip(copies, blocks):
+        copy.wait()
         sk = dot(e_kept[at, :], s16[...]) * in_scale
         sketch[at, :] = sk
         rounded_t[:, at] = sk.astype(jnp.bfloat16).T
-        return carry
-
-    lax.fori_loop(0, n, step, 0)
     outs = [pltpu.make_async_copy(sketch, sketch_out, out_sem.at[0])]
     outs[0].start()
     high, low = split(sketch[...])
     acc[...] = dot(rounded_t[...], low)
     acc[...] = (dot(rounded_t[...], high) + (acc[...] + acc[...].T)) * gram_scale
-    own, in_plane, in_line = info[0], info[1], info[2]
+    own, in_plane, in_line = place()
+    rows1, rows2 = row_classes(k, line)
+    size1, size2 = rows1 // line, rows2 // line
     half = k // 2
     size = half // line
+    group = 2 * PLANE * size2 + size
     for g in range(line):
-        to = pl.ds(pl.multiple_of((in_line ^ g) * size, size), size)
-        for out, region in ((gram_kept, own), (gram_sent, 1 - own)):
+        to = pl.ds(pl.multiple_of((in_line ^ g) * group + 2 * PLANE * size2, 8), size)
+        for out, region in ((kept2, own), (class2, 1 - own)):
             out[to, :] = acc[pl.ds(pl.multiple_of(region * half + g * size, size), size), :]
-    rows1, rows2 = row_classes(k, line)
-    size1, size2 = rows1 // line, rows2 // line
     width = d // (2 * PLANE)
     for r, region in enumerate((1 - own, own)):
         for p in range(PLANE):
@@ -96,7 +93,7 @@
                     part = value[:, h * width // 2 : (h + 1) * width // 2]
                     to1 = pl.multiple_of(p * 2 * rows1 + (2 * to + h) * size1, 8)
                     (class1, kept1)[r][pl.ds(to1, size1), :] = part[g * size1 : (g + 1) * size1]
-                    to2 = pl.multiple_of(((to * PLANE + (in_plane ^ p)) * 2 + h) * size2, 8)
+                    to2 = pl.multiple_of(to * group + ((in_plane ^ p) * 2 + h) * size2, 8)
                     (class2, kept2)[r][pl.ds(to2, size2), :] = part[rows1 + g * size2 : rows1 + (g + 1) * size2]
             if r == 0:
                 at = pl.ds(p * 2 * rows1, 2 * rows1)
@@ -109,21 +106,19 @@
         copy.wait()
 
 
-def front_call(info, e, signs, rows_all, line):
+def front_call(e, signs, rows_all, line):
     rows, d = e.shape
     k = signs.shape[1]
-    copies = 4
+    copies = len(FRONT_BLOCKS) - 1
     rows1, rows2 = row_classes(k, line)
     width = d // (4 * PLANE)
-    classes = [(2 * PLANE * rows1, width), (2 * PLANE * rows2, width)]
+    classes = [(2 * PLANE * rows1, width), (2 * PLANE * rows2 + k // 2, width)]
     f32 = lambda *shape: jax.ShapeDtypeStruct(shape, jnp.float32)
     return pl.pallas_call(
         functools.partial(front_kernel, 1.0 / math.sqrt(d), 1.0 / rows_all, 1.0 / math.sqrt(rows_all), line),
-        in_specs=[SMEM_SPEC, ANY_SPEC, ANY_SPEC],
-        out_specs=[ANY_SPEC] + [VMEM_SPEC] * 2 + [ANY_SPEC] + [VMEM_SPEC] * 2 + [ANY_SPEC] * PLANE,
-        out_shape=[f32(rows, k)]
-        + [pltpu.VMEM((k // 2, k), jnp.float32)] * 2
-        + [f32(*classes[1])]
+        in_specs=[ANY_SPEC, ANY_SPEC],
+        out_specs=[ANY_SPEC] * 2 + [VMEM_SPEC] * 2 + [ANY_SPEC] * PLANE,
+        out_shape=[f32(rows, k), f32(*classes[1])]
         + [pltpu.VMEM(c, jnp.float32) for c in classes]
         + [f32(2 * rows1, width)] * PLANE,
         scratch_shapes=[
@@ -141,14 +136,14 @@
         compiler_params=pltpu.CompilerParams(vmem_limit_bytes=48 * MIB),
         cost_estimate=pl.CostEstimate(flops=4 * rows * d * k, bytes_accessed=rows * d * 2 + d * k * 4, transcendentals=0),
         name="front",
-    )(info, e, pltpu.with_memory_space_constraint(signs, pltpu.HBM))
-
-
-def factor_kernel(line, info, kept, got, triangle, inverse, work):
+    )(e, pltpu.with_memory_space_constraint(signs, pltpu.HBM))
+
+
+def factor_kernel(line, kept, got, triangle, inverse, work):
     k = triangle.shape[0]
     half = k // 2
     b = 64
-    own, in_line = info[0], info[2]
+    own, _, in_line = place()
     size = half // line
     for g in range(line):
         at = pl.ds(pl.multiple_of((in_line ^ g) * size, size), size)
@@ -228,11 +223,11 @@
             )
 
 
-def factor_call(line, info, kept, got):
+def factor_call(line, kept, got):
     k = kept.shape[1]
     return pl.pallas_call(
         functools.partial(factor_kernel, line),
-        in_specs=[SMEM_SPEC, VMEM_SPEC, VMEM_SPEC],
+        in_specs=[VMEM_SPEC] * 2,
         out_specs=[VMEM_SPEC] * 2,
         out_shape=[
             jax.ShapeDtypeStruct((k, k), jnp.float32),
@@ -242,7 +237,7 @@
         compiler_params=pltpu.CompilerParams(vmem_limit_bytes=16 * MIB),
         cost_estimate=pl.CostEstimate(flops=10**10, bytes_accessed=k * k * 8, transcendentals=0),
         name="factor",
-    )(info, kept, got)
+    )(kept, got)
 
 
 def basis_kernel(sketch, inverse, out, value, sem):
@@ -275,13 +270,13 @@
     )(*pinned(sketch, inverse))
 
 
-def project_kernel(line, is_own, info, inverse, *refs):
+def project_kernel(line, is_own, inverse, *refs):
     *blocks, out, whole, value, sem = refs
     class1, class2 = blocks[-PLANE - 1 : -1], blocks[-1]
     k = inverse.shape[1]
     rows1, rows2 = row_classes(k, line)
     size1, size2 = rows1 // line, rows2 // line
-    own, in_plane, in_line = info[0], info[1], info[2]
+    own, in_plane, in_line = place()
     region = own if is_own else 1 - own
     width = value.shape[2]
     copies = []
@@ -305,16 +300,16 @@
         copy.wait()
 
 
-def project_call(line, is_own, info, inverse, blocks, d, before):
+def project_call(line, is_own, inverse, blocks, d, before):
     k = inverse.shape[1]
     width = d // (2 * PLANE)
     extra = [] if before is None else [before]
     return pl.pallas_call(
         functools.partial(project_kernel, line, is_own),
-        in_specs=[SMEM_SPEC, VMEM_SPEC] + [ANY_SPEC] * len(extra) + [VMEM_SPEC] * len(blocks),
+        in_specs=[VMEM_SPEC] + [ANY_SPEC] * len(extra) + [VMEM_SPEC] * len(blocks),
         out_specs=ANY_SPEC,
         out_shape=jax.ShapeDtypeStruct((k, d), jnp.float32),
-        input_output_aliases={2: 0} if extra else {},
+        input_output_aliases={1: 0} if extra else {},
         scratch_shapes=[
             pltpu.VMEM((PLANE, k, width), jnp.float32),
             pltpu.VMEM((PLANE, k, width), jnp.float32),
@@ -323,7 +318,7 @@
         compiler_params=pltpu.CompilerParams(vmem_limit_bytes=16 * MIB),
         cost_estimate=pl.CostEstimate(flops=3 * k * k * d, bytes_accessed=k * d * 4, transcendentals=0),
         name="project",
-    )(info, *pinned(inverse), *extra, *pinned(*blocks))
+    )(*pinned(inverse), *extra, *pinned(*blocks))
 
 
 def solution(mesh):
@@ -350,18 +345,16 @@
         d = e.shape[1]
         k = signs.shape[1]
         rows1, rows2 = row_classes(k, line)
-        me = lax.axis_index(AXES).astype(jnp.int32)
-        info = jnp.stack([me & 1, (me >> 1) & (PLANE - 1), me // (2 * PLANE)])
-        last = [me]
+        last = []
 
         def in_turn(*arrays):
-            *arrays, _ = lax.optimization_barrier((*arrays, last[0]))
-            last[0] = arrays[-1]
+            arrays = lax.optimization_barrier((*arrays, *last[-1:]))[: len(arrays)]
+            last.append(arrays[-1])
             return arrays if len(arrays) > 1 else arrays[0]
 
-        sketch, gram_sent, gram, sent2, kept1, kept2, *sent1 = front_call(info, e, signs, rows_all, line)
+        sketch, sent2, kept1, kept2, *sent1 = front_call(e, signs, rows_all, line)
         got1 = [with_pair(a) for a in sent1[1:]]
-        gram_got, got2 = with_pair(gram_sent), with_pair(sent2)
+        got2 = with_pair(sent2)
         kept1 = parts_of(kept1, PLANE)
         from_plane = []
         for g in range(1, PLANE):
@@ -369,20 +362,20 @@
                 got1[g - 1] = in_turn(got1[g - 1])
             from_plane.append(over_plane[g](in_turn(kept1[g] + got1[g - 1])))
         a1 = kept1[0] + with_pair(sent1[0])
-        grams = parts_of(gram + gram_got, line)
-        parts2 = [join(a + b, g) for a, b, g in zip(parts_of(kept2, line), parts_of(got2, line), grams)]
-        parts2 = in_turn(*parts2)
+        parts2 = in_turn(*[a + b for a, b in zip(parts_of(kept2, line), parts_of(got2, line))])
         from_line = [over_line[g](parts2[g]) for g in range(1, line)]
-        parts1 = in_turn(*parts_of(sum(from_plane, a1), line))
+        mine, near, *far = parts_of(sum(from_plane, a1), line)
         a2 = sum(from_line, parts2[0])
-        from_line = [over_line[g](parts1[g]) for g in range(1, line)]
+        mine, *far = in_turn(mine, *far)
+        from_line = [over_line[g](a) for g, a in enumerate(far, 2)]
         a2 = in_turn(a2)
         whole2 = [over_plane[g](a2) for g in range(1, PLANE)]
+        from_line = [over_line[1](in_turn(near)), *from_line]
         a2 = (a2 + whole2[0]) + (whole2[1] + whole2[2])
-        n2 = a2.shape[0] - gram.shape[0] // line
-        a1 = in_turn(join(sum(from_line, parts1[0]), a2[n2:]))
+        n2 = a2.shape[0] - k // 2 // line
+        a1 = in_turn(join(sum(from_line, mine), a2[n2:]))
         gathered = [a1] + [over_line[g](a1) for g in range(1, line)]
-        n1 = a1.shape[0] - gram.shape[0] // line
+        n1 = a1.shape[0] - k // 2 // line
         a1 = in_turn(join(*[a[:n1] for a in gathered]))
         class1 = [over_plane[g](a1) for g in range(1, PLANE)]
         gram = in_turn(join(*[a[n1:] for a in gathered]))
@@ -394,15 +387,15 @@
             class2 = join(class2, over_line[1 << bit](class2))
         a1 = in_turn(a1)
         their1 = with_pair(a1)
-        triangle, inverse = factor_call(line, info, in_turn(gram), gram_got)
+        triangle, inverse = factor_call(line, in_turn(gram), gram_got)
         their1, inverse = in_turn(their1, inverse)
         basis = in_turn(basis_call(in_turn(sketch), inverse))
         class2 = in_turn(class2)
         their2 = with_pair(class2)
         class1 = in_turn(*class1)
         theirs = [their1, *[with_pair(a) for a in class1], their2]
-        projected = project_call(line, True, info, inverse, [a1, *class1, class2], d, None)
-        projected = project_call(line, False, info, inverse, theirs, d, projected)
+        projected = project_call(line, True, inverse, [a1, *class1, class2], d, None)
+        projected = project_call(line, False, inverse, theirs, d, projected)
         return triangle, basis, projected
 
     return jax.shard_map(

time: 96.3 us -> 100 us (1.038)
  Pallas kernels: 34.3 us -> 36.7 us
  waiting for transfers between devices: 25.8 us -> 27.4 us
    pallas_call x1, Pallas kernels: 16.1 us -> 20.2 us  [front_call(): pl.pallas_call(functools.partial(front_kernel, 1.0 / math.sqrt(d), 1.0 /...]
    ppermute x32 -> x31, waiting for transfers between devices: 25.8 us -> 27.4 us  [over(): return lambda a: lax.ppermute(a, AXES, pairs)]
    pallas_call x2, Pallas kernels: 4.87 us -> 3.76 us  [project_call(): pl.pallas_call(functools.partial(project_kernel, line, is_own), in_specs=...]
    ppermute x32 -> x31, starting transfers between devices: 34.1 us -> 34.2 us  [over(): return lambda a: lax.ppermute(a, AXES, pairs)]
  transfers between devices with their start and end apart: 32 -> 31, of which waited for: 13 -> 14; matrix products, arithmetic and copies ran while one was open for 1% -> 1% of each run, Pallas kernels for 16% -> 15%
where the time goes in v11:
time: 100 us
  Pallas kernels  36.7 us (37%)
  starting transfers between devices  34.2 us (34%)
  waiting for transfers between devices  27.4 us (27%)
  between operations  1.07 us (1%)
    ppermute x31, starting transfers between devices, over(): return lambda a: lax.ppermute(a, AXES, pairs)  34.2 us
    ppermute x31, waiting for transfers between devices, over(): return lambda a: lax.ppermute(a, AXES, pairs)  27.4 us
    pallas_call x1, Pallas kernels, front_call(): pl.pallas_call(functools.partial(front_kernel, 1.0 / math.sqrt(d), 1.0 /...  20.2 us
    pallas_call x1, Pallas kernels, factor_call(): pl.pallas_call(functools.partial(factor_kernel, line), in_specs=[VMEM_SPE...  10.9 us
    pallas_call x2, Pallas kernels, project_call(): pl.pallas_call(functools.partial(project_kernel, line, is_own), in_specs=...  3.76 us
  transfers between devices with their start and end apart: 31, of which 14 were waited for; matrix products, arithmetic and copies ran while one was open for 1% of the time, Pallas kernels for 15%

profile of v11, /device:TPU:0, one launch (start us, length us, event | category | flops | bytes accessed | tf_op | source)
XLA Modules:
  0.0 100.0 jit_solution(54683077315075156)
XLA Ops:
  0.6 20.2 %front.1 = (f32[2048,256]{1,0:T(8,128)}, f32[640,256]{1,0:T(8,128)S(1)}, f32[1536,256]{1,0:T(8,128)S(1)}, f32[640,256]{1,0:T(8,128)S(1)}, f32[384,256]{1,0:T(8,1...) custom-call(bf16[2048,4096]{1,0:T(8,128)(2,1)} %e.1, s32[4096,256]{1,0:T(8,128)} %signs.1), custom_call_target="tpu_custom_call" | custom-call | flops 8589934592 | bytes 20971520 | tf_op jit(solution)/shard_map/front/pallas_call | solution.py:117
  20.8 0.5 collective-permute-start.1
  21.4 0.1 collective-permute-start.3
  21.4 0.4 collective-permute-start
  21.9 0.1 collective-permute-start.5
  21.9 0.4 collective-permute-start.7
  22.4 0.3 collective-permute-done.1
  22.8 2.9 %collective-permute-start.2 = (f32[384,256]{1,0:T(8,128)S(1)}, f32[384,256]{1,0:T(8,128)S(1)}, u32[]{:S(2)}, u32[]{:S(2)}) collective-permute-start(f32[384,256]{1,0:T(8,128)S(1)} %slice_add_fusion.2), channel_id=1, source_target_pairs={{0,2},{1,3},{2,0},{3,1},{4,6},{5,7},{6,4},{7,5},{8,10},{9,11},{10,... | collective-permute-start | bytes 1179656 | tf_op jit(solution)/shard_map/ppermute | solution.py:330
  25.7 1.6 %collective-permute-start.4 = (f32[384,256]{1,0:T(8,128)S(1)}, f32[384,256]{1,0:T(8,128)S(1)}, u32[]{:S(2)}, u32[]{:S(2)}) collective-permute-start(f32[384,256]{1,0:T(8,128)S(1)} %slice_add_fusion.1), channel_id=1, source_target_pairs={{0,4},{1,5},{2,6},{3,7},{4,0},{5,1},{6,2},{7,3},{8,12},{9,13},{10,... | collective-permute-start | bytes 1179656 | tf_op jit(solution)/shard_map/ppermute | solution.py:330
  27.4 0.9 collective-permute-start.6
  28.3 0.1 slice_add_fusion.3
  28.4 1.6 %collective-permute-start.8 = (f32[160,256]{1,0:T(8,128)S(1)}, f32[160,256]{1,0:T(8,128)S(1)}, u32[]{:S(2)}, u32[]{:S(2)}) collective-permute-start(f32[160,256]{1,0:T(8,128)S(1)} %get-tuple-element.56), channel_id=1, source_target_pairs={{0,8},{1,9},{2,10},{3,11},{4,12},{5,13},{6,14},{7,15},{8,0},{9,1},... | collective-permute-start | bytes 491528 | tf_op jit(solution)/shard_map/ppermute | solution.py:330
  30.1 2.6 %collective-permute-start.9 = (f32[160,256]{1,0:T(8,128)S(1)}, f32[160,256]{1,0:T(8,128)S(1)}, u32[]{:S(2)}, u32[]{:S(2)}) collective-permute-start(f32[160,256]{1,0:T(8,128)S(1)} %get-tuple-element.57), channel_id=1, source_target_pairs={{0,16},{1,17},{2,18},{3,19},{4,20},{5,21},{6,22},{7,23},{8,24},{9,... | collective-permute-start | bytes 491528 | tf_op jit(solution)/shard_map/ppermute | solution.py:330
  32.6 2.9 %collective-permute-done.2 = f32[384,256]{1,0:T(8,128)S(1)} collective-permute-done((f32[384,256]{1,0:T(8,128)S(1)}, f32[384,256]{1,0:T(8,128)S(1)}, u32[]{:S(2)}, u32[]{:S(2)}) %collective-permute-start.2) | collective-permute-done | bytes 393248 | tf_op jit(solution)/shard_map/ppermute | solution.py:330
  35.6 4.2 %collective-permute-start.10 = (f32[160,256]{1,0:T(8,128)S(1)}, f32[160,256]{1,0:T(8,128)S(1)}, u32[]{:S(2)}, u32[]{:S(2)}) collective-permute-start(f32[160,256]{1,0:T(8,128)S(1)} %get-tuple-element.53), channel_id=1, source_target_pairs={{0,24},{1,25},{2,26},{3,27},{4,28},{5,29},{6,30},{7,31},{8,16},{9,... | collective-permute-start | bytes 491528 | tf_op jit(solution)/shard_map/ppermute | solution.py:330
  39.7 5.4 %collective-permute-done.4 = f32[384,256]{1,0:T(8,128)S(1)} collective-permute-done((f32[384,256]{1,0:T(8,128)S(1)}, f32[384,256]{1,0:T(8,128)S(1)}, u32[]{:S(2)}, u32[]{:S(2)}) %collective-permute-start.4) | collective-permute-done | bytes 393248 | tf_op jit(solution)/shard_map/ppermute | solution.py:330
  45.1 0.1 add_add_fusion
  45.3 2.7 %collective-permute-start.12 = (f32[96,256]{1,0:T(8,128)S(1)}, f32[96,256]{1,0:T(8,128)S(1)}, u32[]{:S(2)}, u32[]{:S(2)}) collective-permute-start(f32[96,256]{1,0:T(8,128)S(1)} %get-tuple-element.61), channel_id=1, source_target_pairs={{0,16},{1,17},{2,18},{3,19},{4,20},{5,21},{6,22},{7,23},{8,24},{9,... | collective-permute-start | bytes 294920 | tf_op jit(solution)/shard_map/ppermute | solution.py:330
  47.9 1.3 %collective-permute-start.13 = (f32[96,256]{1,0:T(8,128)S(1)}, f32[96,256]{1,0:T(8,128)S(1)}, u32[]{:S(2)}, u32[]{:S(2)}) collective-permute-start(f32[96,256]{1,0:T(8,128)S(1)} %get-tuple-element.58), channel_id=1, source_target_pairs={{0,24},{1,25},{2,26},{3,27},{4,28},{5,29},{6,30},{7,31},{8,16},{9,... | collective-permute-start | bytes 294920 | tf_op jit(solution)/shard_map/ppermute | solution.py:330
  49.3 0.3 collective-permute-start.11
  49.6 1.7 %collective-permute-start.16 = (f32[160,256]{1,0:T(8,128)S(1)}, f32[160,256]{1,0:T(8,128)S(1)}, u32[]{:S(2)}, u32[]{:S(2)}) collective-permute-start(f32[160,256]{1,0:T(8,128)S(1)} %add_add_fusion.2), channel_id=1, source_target_pairs={{0,6},{1,7},{2,4},{3,5},{4,2},{5,3},{6,0},{7,1},{8,14},{9,15},{10,... | collective-permute-start | bytes 491528 | tf_op jit(solution)/shard_map/ppermute | solution.py:330
  51.3 0.9 collective-permute-start.15
  52.2 2.0 %collective-permute-done.12 = f32[96,256]{1,0:T(8,128)S(1)} collective-permute-done((f32[96,256]{1,0:T(8,128)S(1)}, f32[96,256]{1,0:T(8,128)S(1)}, u32[]{:S(2)}, u32[]{:S(2)}) %collective-permute-start.12) | collective-permute-done | bytes 98336 | tf_op jit(solution)/shard_map/ppermute | solution.py:330
  54.2 2.1 %collective-permute-start.14 = (f32[160,256]{1,0:T(8,128)S(1)}, f32[160,256]{1,0:T(8,128)S(1)}, u32[]{:S(2)}, u32[]{:S(2)}) collective-permute-start(f32[160,256]{1,0:T(8,128)S(1)} %add_add_fusion.2), channel_id=1, source_target_pairs={{0,2},{1,3},{2,0},{3,1},{4,6},{5,7},{6,4},{7,5},{8,10},{9,11},{10,... | collective-permute-start | bytes 491528 | tf_op jit(solution)/shard_map/ppermute | solution.py:330
  56.3 0.6 collective-permute-done.16
  56.9 1.7 %collective-permute-done.15 = f32[160,256]{1,0:T(8,128)S(1)} collective-permute-done((f32[160,256]{1,0:T(8,128)S(1)}, f32[160,256]{1,0:T(8,128)S(1)}, u32[]{:S(2)}, u32[]{:S(2)}) %collective-permute-start.15) | collective-permute-done | bytes 163872 | tf_op jit(solution)/shard_map/ppermute | solution.py:330
  58.6 1.0 %collective-permute-done.14 = f32[160,256]{1,0:T(8,128)S(1)} collective-permute-done((f32[160,256]{1,0:T(8,128)S(1)}, f32[160,256]{1,0:T(8,128)S(1)}, u32[]{:S(2)}, u32[]{:S(2)}) %collective-permute-start.14) | collective-permute-done | bytes 163872 | tf_op jit(solution)/shard_map/ppermute | solution.py:330
  59.7 4.2 %collective-permute-start.19 = (f32[128,256]{1,0:T(8,128)S(1)}, f32[128,256]{1,0:T(8,128)S(1)}, u32[]{:S(2)}, u32[]{:S(2)}) collective-permute-start(f32[128,256]{1,0:T(8,128)S(1)} %pad_maximum_fusion.3), channel_id=1, source_target_pairs={{0,24},{1,25},{2,26},{3,27},{4,28},{5,29},{6,30},{7,31},{8,16},{9,... | collective-permute-start | bytes 393224 | tf_op jit(solution)/shard_map/ppermute | solution.py:330
  63.9 0.6 collective-permute-start.17
  64.6 3.7 %collective-permute-done.19 = f32[128,256]{1,0:T(8,128)S(1)} collective-permute-done((f32[128,256]{1,0:T(8,128)S(1)}, f32[128,256]{1,0:T(8,128)S(1)}, u32[]{:S(2)}, u32[]{:S(2)}) %collective-permute-start.19) | collective-permute-done | bytes 131104 | tf_op jit(solution)/shard_map/ppermute | solution.py:330
  68.3 5.8 %collective-permute-done.18 = f32[128,256]{1,0:T(8,128)S(1)} collective-permute-done((f32[128,256]{1,0:T(8,128)S(1)}, f32[128,256]{1,0:T(8,128)S(1)}, u32[]{:S(2)}, u32[]{:S(2)}) %collective-permute-start.18) | collective-permute-done | bytes 131104 | tf_op jit(solution)/shard_map/ppermute | solution.py:330
  74.2 0.1 collective-permute-start.21
  74.3 0.1 collective-permute-start.20
  74.4 0.9 collective-permute-start.25
  75.3 1.8 %collective-permute-start.24 = (f32[384,256]{1,0:T(8,128)S(1)}, f32[384,256]{1,0:T(8,128)S(1)}, u32[]{:S(2)}, u32[]{:S(2)}) collective-permute-start(f32[384,256]{1,0:T(8,128)S(1)} %pad_maximum_fusion.1.refs_0_), channel_id=1, source_target_pairs={{0,4},{1,5},{2,6},{3,7},{4,0},{5,1},{6,2},{7,3},{8,12},{9,13},{10,... | collective-permute-start | bytes 1179656 | tf_op jit(solution)/shard_map/ppermute | solution.py:330
  77.1 0.8 collective-permute-start.23
  77.9 1.3 %collective-permute-done.21 = f32[128,256]{1,0:T(8,128)S(1)} collective-permute-done((f32[128,256]{1,0:T(8,128)S(1)}, f32[128,256]{1,0:T(8,128)S(1)}, u32[]{:S(2)}, u32[]{:S(2)}) %collective-permute-start.21) | collective-permute-done | bytes 131104 | tf_op jit(solution)/shard_map/ppermute | solution.py:330
  79.3 0.7 collective-permute-start.26
  80.0 10.9 %factor.1 = (f32[256,256]{1,0:T(8,128)}, bf16[512,256]{1,0:T(8,128)(2,1)S(1)}) custom-call(f32[128,256]{1,0:T(8,128)S(1)} %pad_maximum_fusion.4.kept, f32[128,256]{1,0:T(8,128)S(1)} %collective-permute-done.20.got), custom_call_target="tpu_custom_call" | custom-call | flops 10000000000 | bytes 524288 | tf_op jit(solution)/shard_map/factor/pallas_call | solution.py:228
  90.9 1.5 %collective-permute-done.26 = f32[256,256]{1,0:T(8,128)S(1)} collective-permute-done((f32[256,256]{1,0:T(8,128)S(1)}, f32[256,256]{1,0:T(8,128)S(1)}, u32[]{:S(2)}, u32[]{:S(2)}) %collective-permute-start.26) | collective-permute-done | bytes 262176 | tf_op jit(solution)/shard_map/ppermute | solution.py:330
  92.4 1.9 %basis.1 = bf16[2048,256]{1,0:T(8,128)(2,1)} custom-call(f32[2048,256]{1,0:T(8,128)S(1)} %copy-done, bf16[512,256]{1,0:T(8,128)(2,1)S(1)} %get-tuple-element.73.inverse), custom_call_target="tpu_custom_call" | custom-call | flops 805306368 | bytes 3145728 | tf_op jit(solution)/shard_map/basis/pallas_call | solution.py:261
  94.3 0.1 collective-permute-start.30
  94.4 0.6 collective-permute-done.24.refs_2_
  95.0 0.1 collective-permute-done.23.refs_1_
  95.1 0.5 collective-permute-start.28
  95.7 1.9 %project.2.refs_0_ = f32[256,4096]{1,0:T(8,128)} custom-call(bf16[512,256]{1,0:T(8,128)(2,1)S(1)} %get-tuple-element.73.inverse, f32[384,256]{1,0:T(8,128)S(1)} %pad_maximum_fusion.1.refs_0_, f32[384,256]{1,0:T(8,128)S(1)} %collective-permute-done.23.refs_1_, f32[384,256]{1,0:T(8,128)S(1)} %collective-permute-done.24.refs_2_, ...), custom_call_target="tpu_custom_call" | custom-call | flops 805306368 | bytes 4194304 | tf_op jit(solution)/shard_map/project/pallas_call | solution.py:307
  97.6 0.4 collective-permute-done.29.refs_4_
  98.0 1.9 %project.3 = f32[256,4096]{1,0:T(8,128)} custom-call(bf16[512,256]{1,0:T(8,128)(2,1)S(1)} %get-tuple-element.73.inverse, f32[256,4096]{1,0:T(8,128)} %project.2.refs_0_, f32[384,256]{1,0:T(8,128)S(1)} %collective-permute-done.22.refs_1_, f32[384,256]{1,0:T(8,128)S(1)} %collective-permute-done.27.refs_2_, ...), custom_call_target="tpu_custom_call", output_to_operand_aliasing={{}: (1, {})} | custom-call | flops 805306368 | bytes 4194304 | tf_op jit(solution)/shard_map/project/pallas_call | solution.py:307
  (45 shorter events, 0.5 us)
Async XLA Ops:
  20.8 1.9 %collective-permute-start.1 = (f32[384,256]{1,0:T(8,128)S(1)}, f32[384,256]{1,0:T(8,128)S(1)}, u32[]{:S(2)}, u32[]{:S(2)}) collective-permute-start(f32[384,256]{1,0:T(8,128)S(1)} %get-tuple-element.44), channel_id=1, source_target_pairs={{0,1},{1,0},{2,3},{3,2},{4,5},{5,4},{6,7},{7,6},{8,9},{9,8},{10,11... | collective-permute-start | bytes 1179656 | tf_op jit(solution)/shard_map/ppermute | solution.py:330
  21.4 4.3 %collective-permute-start.3 = (f32[384,256]{1,0:T(8,128)S(1)}, f32[384,256]{1,0:T(8,128)S(1)}, u32[]{:S(2)}, u32[]{:S(2)}) collective-permute-start(f32[384,256]{1,0:T(8,128)S(1)} %get-tuple-element.45), channel_id=1, source_target_pairs={{0,1},{1,0},{2,3},{3,2},{4,5},{5,4},{6,7},{7,6},{8,9},{9,8},{10,11... | collective-permute-start | bytes 1179656 | tf_op jit(solution)/shard_map/ppermute | solution.py:330
  21.4 8.6 %collective-permute-start = (f32[384,256]{1,0:T(8,128)S(1)}, f32[384,256]{1,0:T(8,128)S(1)}, u32[]{:S(2)}, u32[]{:S(2)}) collective-permute-start(f32[384,256]{1,0:T(8,128)S(1)} %get-tuple-element.43), channel_id=1, source_target_pairs={{0,1},{1,0},{2,3},{3,2},{4,5},{5,4},{6,7},{7,6},{8,9},{9,8},{10,11... | collective-permute-start | bytes 1179656 | tf_op jit(solution)/shard_map/ppermute | solution.py:330
  21.9 5.5 %collective-permute-start.5 = (f32[384,256]{1,0:T(8,128)S(1)}, f32[384,256]{1,0:T(8,128)S(1)}, u32[]{:S(2)}, u32[]{:S(2)}) collective-permute-start(f32[384,256]{1,0:T(8,128)S(1)} %get-tuple-element.48), channel_id=1, source_target_pairs={{0,1},{1,0},{2,3},{3,2},{4,5},{5,4},{6,7},{7,6},{8,9},{9,8},{10,11... | collective-permute-start | bytes 1179656 | tf_op jit(solution)/shard_map/ppermute | solution.py:330
  21.9 6.4 %collective-permute-start.7 = (f32[640,256]{1,0:T(8,128)S(1)}, f32[640,256]{1,0:T(8,128)S(1)}, u32[]{:S(2)}, u32[]{:S(2)}) collective-permute-start(f32[640,256]{1,0:T(8,128)S(1)} %get-tuple-element.52), channel_id=1, source_target_pairs={{0,1},{1,0},{2,3},{3,2},{4,5},{5,4},{6,7},{7,6},{8,9},{9,8},{10,11... | collective-permute-start | bytes 1966088 | tf_op jit(solution)/shard_map/ppermute | solution.py:330
  22.8 12.8 %collective-permute-start.2 = (f32[384,256]{1,0:T(8,128)S(1)}, f32[384,256]{1,0:T(8,128)S(1)}, u32[]{:S(2)}, u32[]{:S(2)}) collective-permute-start(f32[384,256]{1,0:T(8,128)S(1)} %slice_add_fusion.2), channel_id=1, source_target_pairs={{0,2},{1,3},{2,0},{3,1},{4,6},{5,7},{6,4},{7,5},{8,10},{9,11},{10,... | collective-permute-start | bytes 1179656 | tf_op jit(solution)/shard_map/ppermute | solution.py:330
  25.7 19.4 %collective-permute-start.4 = (f32[384,256]{1,0:T(8,128)S(1)}, f32[384,256]{1,0:T(8,128)S(1)}, u32[]{:S(2)}, u32[]{:S(2)}) collective-permute-start(f32[384,256]{1,0:T(8,128)S(1)} %slice_add_fusion.1), channel_id=1, source_target_pairs={{0,4},{1,5},{2,6},{3,7},{4,0},{5,1},{6,2},{7,3},{8,12},{9,13},{10,... | collective-permute-start | bytes 1179656 | tf_op jit(solution)/shard_map/ppermute | solution.py:330
  27.4 17.7 %collective-permute-start.6 = (f32[384,256]{1,0:T(8,128)S(1)}, f32[384,256]{1,0:T(8,128)S(1)}, u32[]{:S(2)}, u32[]{:S(2)}) collective-permute-start(f32[384,256]{1,0:T(8,128)S(1)} %slice_add_fusion), channel_id=1, source_target_pairs={{0,6},{1,7},{2,4},{3,5},{4,2},{5,3},{6,0},{7,1},{8,14},{9,15},{10,... | collective-permute-start | bytes 1179656 | tf_op jit(solution)/shard_map/ppermute | solution.py:330
  28.4 20.9 %collective-permute-start.8 = (f32[160,256]{1,0:T(8,128)S(1)}, f32[160,256]{1,0:T(8,128)S(1)}, u32[]{:S(2)}, u32[]{:S(2)}) collective-permute-start(f32[160,256]{1,0:T(8,128)S(1)} %get-tuple-element.56), channel_id=1, source_target_pairs={{0,8},{1,9},{2,10},{3,11},{4,12},{5,13},{6,14},{7,15},{8,0},{9,1},... | collective-permute-start | bytes 491528 | tf_op jit(solution)/shard_map/ppermute | solution.py:330
  30.1 19.2 %collective-permute-start.9 = (f32[160,256]{1,0:T(8,128)S(1)}, f32[160,256]{1,0:T(8,128)S(1)}, u32[]{:S(2)}, u32[]{:S(2)}) collective-permute-start(f32[160,256]{1,0:T(8,128)S(1)} %get-tuple-element.57), channel_id=1, source_target_pairs={{0,16},{1,17},{2,18},{3,19},{4,20},{5,21},{6,22},{7,23},{8,24},{9,... | collective-permute-start | bytes 491528 | tf_op jit(solution)/shard_map/ppermute | solution.py:330
  35.6 13.7 %collective-permute-start.10 = (f32[160,256]{1,0:T(8,128)S(1)}, f32[160,256]{1,0:T(8,128)S(1)}, u32[]{:S(2)}, u32[]{:S(2)}) collective-permute-start(f32[160,256]{1,0:T(8,128)S(1)} %get-tuple-element.53), channel_id=1, source_target_pairs={{0,24},{1,25},{2,26},{3,27},{4,28},{5,29},{6,30},{7,31},{8,16},{9,... | collective-permute-start | bytes 491528 | tf_op jit(solution)/shard_map/ppermute | solution.py:330
  45.3 9.0 %collective-permute-start.12 = (f32[96,256]{1,0:T(8,128)S(1)}, f32[96,256]{1,0:T(8,128)S(1)}, u32[]{:S(2)}, u32[]{:S(2)}) collective-permute-start(f32[96,256]{1,0:T(8,128)S(1)} %get-tuple-element.61), channel_id=1, source_target_pairs={{0,16},{1,17},{2,18},{3,19},{4,20},{5,21},{6,22},{7,23},{8,24},{9,... | collective-permute-start | bytes 294920 | tf_op jit(solution)/shard_map/ppermute | solution.py:330
  47.9 8.4 %collective-permute-start.13 = (f32[96,256]{1,0:T(8,128)S(1)}, f32[96,256]{1,0:T(8,128)S(1)}, u32[]{:S(2)}, u32[]{:S(2)}) collective-permute-start(f32[96,256]{1,0:T(8,128)S(1)} %get-tuple-element.58), channel_id=1, source_target_pairs={{0,24},{1,25},{2,26},{3,27},{4,28},{5,29},{6,30},{7,31},{8,16},{9,... | collective-permute-start | bytes 294920 | tf_op jit(solution)/shard_map/ppermute | solution.py:330
  49.3 7.0 %collective-permute-start.11 = (f32[96,256]{1,0:T(8,128)S(1)}, f32[96,256]{1,0:T(8,128)S(1)}, u32[]{:S(2)}, u32[]{:S(2)}) collective-permute-start(f32[96,256]{1,0:T(8,128)S(1)} %get-tuple-element.60), channel_id=1, source_target_pairs={{0,8},{1,9},{2,10},{3,11},{4,12},{5,13},{6,14},{7,15},{8,0},{9,1},... | collective-permute-start | bytes 294920 | tf_op jit(solution)/shard_map/ppermute | solution.py:330
  49.6 7.3 %collective-permute-start.16 = (f32[160,256]{1,0:T(8,128)S(1)}, f32[160,256]{1,0:T(8,128)S(1)}, u32[]{:S(2)}, u32[]{:S(2)}) collective-permute-start(f32[160,256]{1,0:T(8,128)S(1)} %add_add_fusion.2), channel_id=1, source_target_pairs={{0,6},{1,7},{2,4},{3,5},{4,2},{5,3},{6,0},{7,1},{8,14},{9,15},{10,... | collective-permute-start | bytes 491528 | tf_op jit(solution)/shard_map/ppermute | solution.py:330
  51.3 7.3 %collective-permute-start.15 = (f32[160,256]{1,0:T(8,128)S(1)}, f32[160,256]{1,0:T(8,128)S(1)}, u32[]{:S(2)}, u32[]{:S(2)}) collective-permute-start(f32[160,256]{1,0:T(8,128)S(1)} %add_add_fusion.2), channel_id=1, source_target_pairs={{0,4},{1,5},{2,6},{3,7},{4,0},{5,1},{6,2},{7,3},{8,12},{9,13},{10,... | collective-permute-start | bytes 491528 | tf_op jit(solution)/shard_map/ppermute | solution.py:330
  54.2 5.4 %collective-permute-start.14 = (f32[160,256]{1,0:T(8,128)S(1)}, f32[160,256]{1,0:T(8,128)S(1)}, u32[]{:S(2)}, u32[]{:S(2)}) collective-permute-start(f32[160,256]{1,0:T(8,128)S(1)} %add_add_fusion.2), channel_id=1, source_target_pairs={{0,2},{1,3},{2,0},{3,1},{4,6},{5,7},{6,4},{7,5},{8,10},{9,11},{10,... | collective-permute-start | bytes 491528 | tf_op jit(solution)/shard_map/ppermute | solution.py:330
  59.7 8.6 %collective-permute-start.19 = (f32[128,256]{1,0:T(8,128)S(1)}, f32[128,256]{1,0:T(8,128)S(1)}, u32[]{:S(2)}, u32[]{:S(2)}) collective-permute-start(f32[128,256]{1,0:T(8,128)S(1)} %pad_maximum_fusion.3), channel_id=1, source_target_pairs={{0,24},{1,25},{2,26},{3,27},{4,28},{5,29},{6,30},{7,31},{8,16},{9,... | collective-permute-start | bytes 393224 | tf_op jit(solution)/shard_map/ppermute | solution.py:330
  63.9 10.2 %collective-permute-start.18 = (f32[128,256]{1,0:T(8,128)S(1)}, f32[128,256]{1,0:T(8,128)S(1)}, u32[]{:S(2)}, u32[]{:S(2)}) collective-permute-start(f32[128,256]{1,0:T(8,128)S(1)} %pad_maximum_fusion.3), channel_id=1, source_target_pairs={{0,16},{1,17},{2,18},{3,19},{4,20},{5,21},{6,22},{7,23},{8,24},{9,... | collective-permute-start | bytes 393224 | tf_op jit(solution)/shard_map/ppermute | solution.py:330
  63.9 10.2 %collective-permute-start.17 = (f32[128,256]{1,0:T(8,128)S(1)}, f32[128,256]{1,0:T(8,128)S(1)}, u32[]{:S(2)}, u32[]{:S(2)}) collective-permute-start(f32[128,256]{1,0:T(8,128)S(1)} %pad_maximum_fusion.3), channel_id=1, source_target_pairs={{0,8},{1,9},{2,10},{3,11},{4,12},{5,13},{6,14},{7,15},{8,0},{9,1},... | collective-permute-start | bytes 393224 | tf_op jit(solution)/shard_map/ppermute | solution.py:330
  74.2 5.0 %collective-permute-start.21 = (f32[128,256]{1,0:T(8,128)S(1)}, f32[128,256]{1,0:T(8,128)S(1)}, u32[]{:S(2)}, u32[]{:S(2)}) collective-permute-start(f32[128,256]{1,0:T(8,128)S(1)} %slice.119), channel_id=1, source_target_pairs={{0,8},{1,9},{2,10},{3,11},{4,12},{5,13},{6,14},{7,15},{8,0},{9,1},... | collective-permute-start | bytes 393224 | tf_op jit(solution)/shard_map/ppermute | solution.py:330
  74.3 5.0 %collective-permute-start.20 = (f32[128,256]{1,0:T(8,128)S(1)}, f32[128,256]{1,0:T(8,128)S(1)}, u32[]{:S(2)}, u32[]{:S(2)}) collective-permute-start(f32[128,256]{1,0:T(8,128)S(1)} %pad_maximum_fusion.4.kept), channel_id=1, source_target_pairs={{0,1},{1,0},{2,3},{3,2},{4,5},{5,4},{6,7},{7,6},{8,9},{9,8},{10,11... | collective-permute-start | bytes 393224 | tf_op jit(solution)/shard_map/ppermute | solution.py:330
  74.4 20.0 %collective-permute-start.25 = (f32[384,256]{1,0:T(8,128)S(1)}, f32[384,256]{1,0:T(8,128)S(1)}, u32[]{:S(2)}, u32[]{:S(2)}) collective-permute-start(f32[384,256]{1,0:T(8,128)S(1)} %pad_maximum_fusion.1.refs_0_), channel_id=1, source_target_pairs={{0,6},{1,7},{2,4},{3,5},{4,2},{5,3},{6,0},{7,1},{8,14},{9,15},{10,... | collective-permute-start | bytes 1179656 | tf_op jit(solution)/shard_map/ppermute | solution.py:330
  75.3 19.7 %collective-permute-start.24 = (f32[384,256]{1,0:T(8,128)S(1)}, f32[384,256]{1,0:T(8,128)S(1)}, u32[]{:S(2)}, u32[]{:S(2)}) collective-permute-start(f32[384,256]{1,0:T(8,128)S(1)} %pad_maximum_fusion.1.refs_0_), channel_id=1, source_target_pairs={{0,4},{1,5},{2,6},{3,7},{4,0},{5,1},{6,2},{7,3},{8,12},{9,13},{10,... | collective-permute-start | bytes 1179656 | tf_op jit(solution)/shard_map/ppermute | solution.py:330
  77.1 18.1 %collective-permute-start.23 = (f32[384,256]{1,0:T(8,128)S(1)}, f32[384,256]{1,0:T(8,128)S(1)}, u32[]{:S(2)}, u32[]{:S(2)}) collective-permute-start(f32[384,256]{1,0:T(8,128)S(1)} %pad_maximum_fusion.1.refs_0_), channel_id=1, source_target_pairs={{0,2},{1,3},{2,0},{3,1},{4,6},{5,7},{6,4},{7,5},{8,10},{9,11},{10,... | collective-permute-start | bytes 1179656 | tf_op jit(solution)/shard_map/ppermute | solution.py:330
  79.3 13.2 %copy-start = (f32[2048,256]{1,0:T(8,128)S(1)}, f32[2048,256]{1,0:T(8,128)}, u32[]{:S(2)}) copy-start(f32[2048,256]{1,0:T(8,128)} %get-tuple-element.74.sketch) | copy-start | bytes 6291460
  79.3 13.1 %collective-permute-start.26 = (f32[256,256]{1,0:T(8,128)S(1)}, f32[256,256]{1,0:T(8,128)S(1)}, u32[]{:S(2)}, u32[]{:S(2)}) collective-permute-start(f32[256,256]{1,0:T(8,128)S(1)} %pad_maximum_fusion.2), channel_id=1, source_target_pairs={{0,16},{1,17},{2,18},{3,19},{4,20},{5,21},{6,22},{7,23},{8,24},{9,... | collective-permute-start | bytes 786440 | tf_op jit(solution)/shard_map/ppermute | solution.py:330
  80.0 12.4 %collective-permute-start.22 = (f32[384,256]{1,0:T(8,128)S(1)}, f32[384,256]{1,0:T(8,128)S(1)}, u32[]{:S(2)}, u32[]{:S(2)}) collective-permute-start(f32[384,256]{1,0:T(8,128)S(1)} %pad_maximum_fusion.1.refs_0_), channel_id=1, source_target_pairs={{0,1},{1,0},{2,3},{3,2},{4,5},{5,4},{6,7},{7,6},{8,9},{9,8},{10,11... | collective-permute-start | bytes 1179656 | tf_op jit(solution)/shard_map/ppermute | solution.py:330
  94.3 3.7 %collective-permute-start.30 = (f32[512,256]{1,0:T(8,128)S(1)}, f32[512,256]{1,0:T(8,128)S(1)}, u32[]{:S(2)}, u32[]{:S(2)}) collective-permute-start(f32[512,256]{1,0:T(8,128)S(1)} %pad_maximum_fusion.refs_4_), channel_id=1, source_target_pairs={{0,1},{1,0},{2,3},{3,2},{4,5},{5,4},{6,7},{7,6},{8,9},{9,8},{10,11... | collective-permute-start | bytes 1572872 | tf_op jit(solution)/shard_map/ppermute | solution.py:330
  95.1 2.4 %collective-permute-start.27 = (f32[384,256]{1,0:T(8,128)S(1)}, f32[384,256]{1,0:T(8,128)S(1)}, u32[]{:S(2)}, u32[]{:S(2)}) collective-permute-start(f32[384,256]{1,0:T(8,128)S(1)} %collective-permute-done.23.refs_1_), channel_id=1, source_target_pairs={{0,1},{1,0},{2,3},{3,2},{4,5},{5,4},{6,7},{7,6},{8,9},{9,8},{10,11... | collective-permute-start | bytes 1179656 | tf_op jit(solution)/shard_map/ppermute | solution.py:330
  95.1 2.4 %collective-permute-start.28 = (f32[384,256]{1,0:T(8,128)S(1)}, f32[384,256]{1,0:T(8,128)S(1)}, u32[]{:S(2)}, u32[]{:S(2)}) collective-permute-start(f32[384,256]{1,0:T(8,128)S(1)} %collective-permute-done.24.refs_2_), channel_id=1, source_target_pairs={{0,1},{1,0},{2,3},{3,2},{4,5},{5,4},{6,7},{7,6},{8,9},{9,8},{10,11... | collective-permute-start | bytes 1179656 | tf_op jit(solution)/shard_map/ppermute | solution.py:330
  95.7 2.3 %collective-permute-start.29 = (f32[384,256]{1,0:T(8,128)S(1)}, f32[384,256]{1,0:T(8,128)S(1)}, u32[]{:S(2)}, u32[]{:S(2)}) collective-permute-start(f32[384,256]{1,0:T(8,128)S(1)} %collective-permute-done.25.refs_3_), channel_id=1, source_target_pairs={{0,1},{1,0},{2,3},{3,2},{4,5},{5,4},{6,7},{7,6},{8,9},{9,8},{10,11... | collective-permute-start | bytes 1179656 | tf_op jit(solution)/shard_map/ppermute | solution.py:330

commit v12 on v11

--- a/solution.py
+++ b/solution.py
@@ -31,7 +31,6 @@
 
 
 PLANE = 4
-FRONT_BLOCKS = (0, 1, 2, 4, 6, 8)
 
 
 def place():
@@ -51,22 +50,28 @@
     rows, d = e.shape
     k = rounded_t.shape[0]
     n = sem.shape[0] - 1
+    block = rows // n
     signs_copy = pltpu.make_async_copy(signs, s32, sem.at[n])
     signs_copy.start()
 
-    starts = [rows * i // 8 for i in FRONT_BLOCKS]
-    blocks = [pl.ds(a, b - a) for a, b in zip(starts, starts[1:])]
-    copies = [pltpu.make_async_copy(e.at[at], e_kept.at[at], sem.at[i]) for i, at in enumerate(blocks)]
-    for copy in copies:
-        copy.start()
+    def rows_copy(i):
+        at = pl.ds(pl.multiple_of(i * block, block), block)
+        return pltpu.make_async_copy(e.at[at], e_kept.at[at], sem.at[i])
+
+    for i in range(n):
+        rows_copy(i).start()
     signs_copy.wait()
     s16[...] = s32[...].astype(jnp.bfloat16)
 
-    for copy, at in zip(copies, blocks):
-        copy.wait()
+    def step(i, carry):
+        rows_copy(i).wait()
+        at = pl.ds(pl.multiple_of(i * block, block), block)
         sk = dot(e_kept[at, :], s16[...]) * in_scale
         sketch[at, :] = sk
         rounded_t[:, at] = sk.astype(jnp.bfloat16).T
+        return carry
+
+    lax.fori_loop(0, n, step, 0)
     outs = [pltpu.make_async_copy(sketch, sketch_out, out_sem.at[0])]
     outs[0].start()
     high, low = split(sketch[...])
@@ -109,7 +114,7 @@
 def front_call(e, signs, rows_all, line):
     rows, d = e.shape
     k = signs.shape[1]
-    copies = len(FRONT_BLOCKS) - 1
+    copies = 4
     rows1, rows2 = row_classes(k, line)
     width = d // (4 * PLANE)
     classes = [(2 * PLANE * rows1, width), (2 * PLANE * rows2 + k // 2, width)]
@@ -364,16 +369,14 @@
         a1 = kept1[0] + with_pair(sent1[0])
         parts2 = in_turn(*[a + b for a, b in zip(parts_of(kept2, line), parts_of(got2, line))])
         from_line = [over_line[g](parts2[g]) for g in range(1, line)]
-        mine, near, *far = parts_of(sum(from_plane, a1), line)
+        parts1 = in_turn(*parts_of(sum(from_plane, a1), line))
         a2 = sum(from_line, parts2[0])
-        mine, *far = in_turn(mine, *far)
-        from_line = [over_line[g](a) for g, a in enumerate(far, 2)]
+        from_line = [over_line[g](parts1[g]) for g in range(1, line)]
         a2 = in_turn(a2)
         whole2 = [over_plane[g](a2) for g in range(1, PLANE)]
-        from_line = [over_line[1](in_turn(near)), *from_line]
         a2 = (a2 + whole2[0]) + (whole2[1] + whole2[2])
         n2 = a2.shape[0] - k // 2 // line
-        a1 = in_turn(join(sum(from_line, mine), a2[n2:]))
+        a1 = in_turn(join(sum(from_line, parts1[0]), a2[n2:]))
         gathered = [a1] + [over_line[g](a1) for g in range(1, line)]
         n1 = a1.shape[0] - k // 2 // line
         a1 = in_turn(join(*[a[:n1] for a in gathered]))

time: 100 us -> 94 us (0.940)
  Pallas kernels: 36.7 us -> 32.3 us
  waiting for transfers between devices: 27.4 us -> 25.7 us
    pallas_call x1, Pallas kernels: 20.2 us -> 15.9 us  [front_call(): pl.pallas_call(functools.partial(front_kernel, 1.0 / math.sqrt(d), 1.0 /...]
    ppermute x31, waiting for transfers between devices: 27.4 us -> 25.7 us  [over(): return lambda a: lax.ppermute(a, AXES, pairs)]
  transfers between devices with their start and end apart: 31 -> 31, of which waited for: 14 -> 14; matrix products, arithmetic and copies ran while one was open for 1% -> 1% of each run, Pallas kernels for 15% -> 16%
where the time goes in v12:
time: 94 us; the launch traced here: 93.9 us
  starting transfers between devices  34.1 us (36%)
  Pallas kernels  32.3 us (34%)
  waiting for transfers between devices  25.7 us (27%)
  between operations  1.05 us (1%)
    ppermute x31, starting transfers between devices, over(): return lambda a: lax.ppermute(a, AXES, pairs)  34.1 us
    ppermute x31, waiting for transfers between devices, over(): return lambda a: lax.ppermute(a, AXES, pairs)  25.7 us
    pallas_call x1, Pallas kernels, front_call(): pl.pallas_call(functools.partial(front_kernel, 1.0 / math.sqrt(d), 1.0 /...  15.9 us
    pallas_call x1, Pallas kernels, factor_call(): pl.pallas_call(functools.partial(factor_kernel, line), in_specs=[VMEM_SPE...  10.9 us
    pallas_call x2, Pallas kernels, project_call(): pl.pallas_call(functools.partial(project_kernel, line, is_own), in_specs=...  3.76 us
  transfers between devices with their start and end apart: 31, of which 14 were waited for; matrix products, arithmetic and copies ran while one was open for 1% of the time, Pallas kernels for 16%

profile of v12, /device:TPU:0, one launch (start us, length us, event | category | flops | bytes accessed | tf_op | source)
XLA Modules:
  0.0 93.9 jit_solution(10148012829484874429)
XLA Ops:
  0.6 15.9 %front.1 = (f32[2048,256]{1,0:T(8,128)}, f32[640,256]{1,0:T(8,128)S(1)}, f32[1536,256]{1,0:T(8,128)S(1)}, f32[640,256]{1,0:T(8,128)S(1)}, f32[384,256]{1,0:T(8,1...) custom-call(bf16[2048,4096]{1,0:T(8,128)(2,1)} %e.1, s32[4096,256]{1,0:T(8,128)} %signs.1), custom_call_target="tpu_custom_call" | custom-call | flops 8589934592 | bytes 20971520 | tf_op jit(solution)/shard_map/front/pallas_call | solution.py:122
  16.5 0.5 collective-permute-start.1
  17.0 0.1 collective-permute-start.3
  17.1 0.4 collective-permute-start
  17.5 0.1 collective-permute-start.5
  17.6 0.4 collective-permute-start.7
  18.0 0.3 collective-permute-done.1
  18.4 2.9 %collective-permute-start.2 = (f32[384,256]{1,0:T(8,128)S(1)}, f32[384,256]{1,0:T(8,128)S(1)}, u32[]{:S(2)}, u32[]{:S(2)}) collective-permute-start(f32[384,256]{1,0:T(8,128)S(1)} %slice_add_fusion.2), channel_id=1, source_target_pairs={{0,2},{1,3},{2,0},{3,1},{4,6},{5,7},{6,4},{7,5},{8,10},{9,11},{10,... | collective-permute-start | bytes 1179656 | tf_op jit(solution)/shard_map/ppermute | solution.py:335
  21.3 0.1 slice_add_fusion.1
  21.4 1.6 %collective-permute-start.4 = (f32[384,256]{1,0:T(8,128)S(1)}, f32[384,256]{1,0:T(8,128)S(1)}, u32[]{:S(2)}, u32[]{:S(2)}) collective-permute-start(f32[384,256]{1,0:T(8,128)S(1)} %slice_add_fusion.1), channel_id=1, source_target_pairs={{0,4},{1,5},{2,6},{3,7},{4,0},{5,1},{6,2},{7,3},{8,12},{9,13},{10,... | collective-permute-start | bytes 1179656 | tf_op jit(solution)/shard_map/ppermute | solution.py:335
  23.1 0.9 collective-permute-start.6
  24.0 0.1 slice_add_fusion.3
  24.1 1.6 %collective-permute-start.11 = (f32[160,256]{1,0:T(8,128)S(1)}, f32[160,256]{1,0:T(8,128)S(1)}, u32[]{:S(2)}, u32[]{:S(2)}) collective-permute-start(f32[160,256]{1,0:T(8,128)S(1)} %get-tuple-element.59), channel_id=1, source_target_pairs={{0,8},{1,9},{2,10},{3,11},{4,12},{5,13},{6,14},{7,15},{8,0},{9,1},... | collective-permute-start | bytes 491528 | tf_op jit(solution)/shard_map/ppermute | solution.py:335
  25.7 2.6 %collective-permute-start.12 = (f32[160,256]{1,0:T(8,128)S(1)}, f32[160,256]{1,0:T(8,128)S(1)}, u32[]{:S(2)}, u32[]{:S(2)}) collective-permute-start(f32[160,256]{1,0:T(8,128)S(1)} %get-tuple-element.60), channel_id=1, source_target_pairs={{0,16},{1,17},{2,18},{3,19},{4,20},{5,21},{6,22},{7,23},{8,24},{9,... | collective-permute-start | bytes 491528 | tf_op jit(solution)/shard_map/ppermute | solution.py:335
  28.3 2.9 %collective-permute-done.2 = f32[384,256]{1,0:T(8,128)S(1)} collective-permute-done((f32[384,256]{1,0:T(8,128)S(1)}, f32[384,256]{1,0:T(8,128)S(1)}, u32[]{:S(2)}, u32[]{:S(2)}) %collective-permute-start.2) | collective-permute-done | bytes 393248 | tf_op jit(solution)/shard_map/ppermute | solution.py:335
  31.2 4.2 %collective-permute-start.13 = (f32[160,256]{1,0:T(8,128)S(1)}, f32[160,256]{1,0:T(8,128)S(1)}, u32[]{:S(2)}, u32[]{:S(2)}) collective-permute-start(f32[160,256]{1,0:T(8,128)S(1)} %get-tuple-element.53), channel_id=1, source_target_pairs={{0,24},{1,25},{2,26},{3,27},{4,28},{5,29},{6,30},{7,31},{8,16},{9,... | collective-permute-start | bytes 491528 | tf_op jit(solution)/shard_map/ppermute | solution.py:335
  35.4 5.4 %collective-permute-done.4 = f32[384,256]{1,0:T(8,128)S(1)} collective-permute-done((f32[384,256]{1,0:T(8,128)S(1)}, f32[384,256]{1,0:T(8,128)S(1)}, u32[]{:S(2)}, u32[]{:S(2)}) %collective-permute-start.4) | collective-permute-done | bytes 393248 | tf_op jit(solution)/shard_map/ppermute | solution.py:335
  40.8 0.1 add_add_fusion
  40.9 1.6 %collective-permute-start.8 = (f32[96,256]{1,0:T(8,128)S(1)}, f32[96,256]{1,0:T(8,128)S(1)}, u32[]{:S(2)}, u32[]{:S(2)}) collective-permute-start(f32[96,256]{1,0:T(8,128)S(1)} %get-tuple-element.55), channel_id=1, source_target_pairs={{0,8},{1,9},{2,10},{3,11},{4,12},{5,13},{6,14},{7,15},{8,0},{9,1},... | collective-permute-start | bytes 294920 | tf_op jit(solution)/shard_map/ppermute | solution.py:335
  42.6 2.6 %collective-permute-start.9 = (f32[96,256]{1,0:T(8,128)S(1)}, f32[96,256]{1,0:T(8,128)S(1)}, u32[]{:S(2)}, u32[]{:S(2)}) collective-permute-start(f32[96,256]{1,0:T(8,128)S(1)} %get-tuple-element.56), channel_id=1, source_target_pairs={{0,16},{1,17},{2,18},{3,19},{4,20},{5,21},{6,22},{7,23},{8,24},{9,... | collective-permute-start | bytes 294920 | tf_op jit(solution)/shard_map/ppermute | solution.py:335
  45.2 0.2 collective-permute-start.10
  45.5 1.7 %collective-permute-start.16 = (f32[160,256]{1,0:T(8,128)S(1)}, f32[160,256]{1,0:T(8,128)S(1)}, u32[]{:S(2)}, u32[]{:S(2)}) collective-permute-start(f32[160,256]{1,0:T(8,128)S(1)} %add_add_fusion.2), channel_id=1, source_target_pairs={{0,6},{1,7},{2,4},{3,5},{4,2},{5,3},{6,0},{7,1},{8,14},{9,15},{10,... | collective-permute-start | bytes 491528 | tf_op jit(solution)/shard_map/ppermute | solution.py:335
  47.2 0.9 collective-permute-start.15
  48.1 0.9 collective-permute-start.14
  49.0 3.1 %collective-permute-done.9 = f32[96,256]{1,0:T(8,128)S(1)} collective-permute-done((f32[96,256]{1,0:T(8,128)S(1)}, f32[96,256]{1,0:T(8,128)S(1)}, u32[]{:S(2)}, u32[]{:S(2)}) %collective-permute-start.9) | collective-permute-done | bytes 98336 | tf_op jit(solution)/shard_map/ppermute | solution.py:335
  52.2 0.4 collective-permute-done.16
  52.6 1.7 %collective-permute-done.15 = f32[160,256]{1,0:T(8,128)S(1)} collective-permute-done((f32[160,256]{1,0:T(8,128)S(1)}, f32[160,256]{1,0:T(8,128)S(1)}, u32[]{:S(2)}, u32[]{:S(2)}) %collective-permute-start.15) | collective-permute-done | bytes 163872 | tf_op jit(solution)/shard_map/ppermute | solution.py:335
  54.2 0.1 collective-permute-done.14
  54.4 3.6 %collective-permute-start.19 = (f32[128,256]{1,0:T(8,128)S(1)}, f32[128,256]{1,0:T(8,128)S(1)}, u32[]{:S(2)}, u32[]{:S(2)}) collective-permute-start(f32[128,256]{1,0:T(8,128)S(1)} %pad_maximum_fusion.3), channel_id=1, source_target_pairs={{0,24},{1,25},{2,26},{3,27},{4,28},{5,29},{6,30},{7,31},{8,16},{9,... | collective-permute-start | bytes 393224 | tf_op jit(solution)/shard_map/ppermute | solution.py:335
  58.0 0.9 collective-permute-start.17
  58.9 3.5 %collective-permute-done.19 = f32[128,256]{1,0:T(8,128)S(1)} collective-permute-done((f32[128,256]{1,0:T(8,128)S(1)}, f32[128,256]{1,0:T(8,128)S(1)}, u32[]{:S(2)}, u32[]{:S(2)}) %collective-permute-start.19) | collective-permute-done | bytes 131104 | tf_op jit(solution)/shard_map/ppermute | solution.py:335
  62.4 4.8 %collective-permute-done.18 = f32[128,256]{1,0:T(8,128)S(1)} collective-permute-done((f32[128,256]{1,0:T(8,128)S(1)}, f32[128,256]{1,0:T(8,128)S(1)}, u32[]{:S(2)}, u32[]{:S(2)}) %collective-permute-start.18) | collective-permute-done | bytes 131104 | tf_op jit(solution)/shard_map/ppermute | solution.py:335
  67.3 0.3 collective-permute-start.21
  67.7 1.4 %collective-permute-start.25 = (f32[384,256]{1,0:T(8,128)S(1)}, f32[384,256]{1,0:T(8,128)S(1)}, u32[]{:S(2)}, u32[]{:S(2)}) collective-permute-start(f32[384,256]{1,0:T(8,128)S(1)} %pad_maximum_fusion.1.refs_0_), channel_id=1, source_target_pairs={{0,6},{1,7},{2,4},{3,5},{4,2},{5,3},{6,0},{7,1},{8,14},{9,15},{10,... | collective-permute-start | bytes 1179656 | tf_op jit(solution)/shard_map/ppermute | solution.py:335
  69.1 1.7 %collective-permute-start.24 = (f32[384,256]{1,0:T(8,128)S(1)}, f32[384,256]{1,0:T(8,128)S(1)}, u32[]{:S(2)}, u32[]{:S(2)}) collective-permute-start(f32[384,256]{1,0:T(8,128)S(1)} %pad_maximum_fusion.1.refs_0_), channel_id=1, source_target_pairs={{0,4},{1,5},{2,6},{3,7},{4,0},{5,1},{6,2},{7,3},{8,12},{9,13},{10,... | collective-permute-start | bytes 1179656 | tf_op jit(solution)/shard_map/ppermute | solution.py:335
  70.8 0.3 collective-permute-start.23
  71.2 1.2 %collective-permute-done.21 = f32[128,256]{1,0:T(8,128)S(1)} collective-permute-done((f32[128,256]{1,0:T(8,128)S(1)}, f32[128,256]{1,0:T(8,128)S(1)}, u32[]{:S(2)}, u32[]{:S(2)}) %collective-permute-start.21) | collective-permute-done | bytes 131104 | tf_op jit(solution)/shard_map/ppermute | solution.py:335
  72.4 1.8 %collective-permute-start.26 = (f32[256,256]{1,0:T(8,128)S(1)}, f32[256,256]{1,0:T(8,128)S(1)}, u32[]{:S(2)}, u32[]{:S(2)}) collective-permute-start(f32[256,256]{1,0:T(8,128)S(1)} %pad_maximum_fusion.2), channel_id=1, source_target_pairs={{0,16},{1,17},{2,18},{3,19},{4,20},{5,21},{6,22},{7,23},{8,24},{9,... | collective-permute-start | bytes 786440 | tf_op jit(solution)/shard_map/ppermute | solution.py:335
  74.2 10.9 %factor.1 = (f32[256,256]{1,0:T(8,128)}, bf16[512,256]{1,0:T(8,128)(2,1)S(1)}) custom-call(f32[128,256]{1,0:T(8,128)S(1)} %pad_maximum_fusion.4.kept, f32[128,256]{1,0:T(8,128)S(1)} %collective-permute-done.20.got), custom_call_target="tpu_custom_call" | custom-call | flops 10000000000 | bytes 524288 | tf_op jit(solution)/shard_map/factor/pallas_call | solution.py:233
  85.1 1.0 %collective-permute-done.26 = f32[256,256]{1,0:T(8,128)S(1)} collective-permute-done((f32[256,256]{1,0:T(8,128)S(1)}, f32[256,256]{1,0:T(8,128)S(1)}, u32[]{:S(2)}, u32[]{:S(2)}) %collective-permute-start.26) | collective-permute-done | bytes 262176 | tf_op jit(solution)/shard_map/ppermute | solution.py:335
  86.2 1.9 %basis.1 = bf16[2048,256]{1,0:T(8,128)(2,1)} custom-call(f32[2048,256]{1,0:T(8,128)S(1)} %copy-done, bf16[512,256]{1,0:T(8,128)(2,1)S(1)} %get-tuple-element.73.inverse), custom_call_target="tpu_custom_call" | custom-call | flops 805306368 | bytes 3145728 | tf_op jit(solution)/shard_map/basis/pallas_call | solution.py:266
  88.0 0.1 collective-permute-start.30
  88.1 0.4 collective-permute-done.24.refs_2_
  88.5 0.5 collective-permute-done.23.refs_1_
  89.0 0.5 collective-permute-start.28
  89.5 1.9 %project.2.refs_0_ = f32[256,4096]{1,0:T(8,128)} custom-call(bf16[512,256]{1,0:T(8,128)(2,1)S(1)} %get-tuple-element.73.inverse, f32[384,256]{1,0:T(8,128)S(1)} %pad_maximum_fusion.1.refs_0_, f32[384,256]{1,0:T(8,128)S(1)} %collective-permute-done.23.refs_1_, f32[384,256]{1,0:T(8,128)S(1)} %collective-permute-done.24.refs_2_, ...), custom_call_target="tpu_custom_call" | custom-call | flops 805306368 | bytes 4194304 | tf_op jit(solution)/shard_map/project/pallas_call | solution.py:312
  91.4 0.4 collective-permute-done.29.refs_4_
  91.8 1.9 %project.3 = f32[256,4096]{1,0:T(8,128)} custom-call(bf16[512,256]{1,0:T(8,128)(2,1)S(1)} %get-tuple-element.73.inverse, f32[256,4096]{1,0:T(8,128)} %project.2.refs_0_, f32[384,256]{1,0:T(8,128)S(1)} %collective-permute-done.22.refs_1_, f32[384,256]{1,0:T(8,128)S(1)} %collective-permute-done.27.refs_2_, ...), custom_call_target="tpu_custom_call", output_to_operand_aliasing={{}: (1, {})} | custom-call | flops 805306368 | bytes 4194304 | tf_op jit(solution)/shard_map/project/pallas_call | solution.py:312
  (45 shorter events, 0.5 us)
Async XLA Ops:
  16.5 1.9 %collective-permute-start.1 = (f32[384,256]{1,0:T(8,128)S(1)}, f32[384,256]{1,0:T(8,128)S(1)}, u32[]{:S(2)}, u32[]{:S(2)}) collective-permute-start(f32[384,256]{1,0:T(8,128)S(1)} %get-tuple-element.44), channel_id=1, source_target_pairs={{0,1},{1,0},{2,3},{3,2},{4,5},{5,4},{6,7},{7,6},{8,9},{9,8},{10,11... | collective-permute-start | bytes 1179656 | tf_op jit(solution)/shard_map/ppermute | solution.py:335
  17.0 4.3 %collective-permute-start.3 = (f32[384,256]{1,0:T(8,128)S(1)}, f32[384,256]{1,0:T(8,128)S(1)}, u32[]{:S(2)}, u32[]{:S(2)}) collective-permute-start(f32[384,256]{1,0:T(8,128)S(1)} %get-tuple-element.45), channel_id=1, source_target_pairs={{0,1},{1,0},{2,3},{3,2},{4,5},{5,4},{6,7},{7,6},{8,9},{9,8},{10,11... | collective-permute-start | bytes 1179656 | tf_op jit(solution)/shard_map/ppermute | solution.py:335
  17.1 8.6 %collective-permute-start = (f32[384,256]{1,0:T(8,128)S(1)}, f32[384,256]{1,0:T(8,128)S(1)}, u32[]{:S(2)}, u32[]{:S(2)}) collective-permute-start(f32[384,256]{1,0:T(8,128)S(1)} %get-tuple-element.43), channel_id=1, source_target_pairs={{0,1},{1,0},{2,3},{3,2},{4,5},{5,4},{6,7},{7,6},{8,9},{9,8},{10,11... | collective-permute-start | bytes 1179656 | tf_op jit(solution)/shard_map/ppermute | solution.py:335
  17.5 5.5 %collective-permute-start.5 = (f32[384,256]{1,0:T(8,128)S(1)}, f32[384,256]{1,0:T(8,128)S(1)}, u32[]{:S(2)}, u32[]{:S(2)}) collective-permute-start(f32[384,256]{1,0:T(8,128)S(1)} %get-tuple-element.48), channel_id=1, source_target_pairs={{0,1},{1,0},{2,3},{3,2},{4,5},{5,4},{6,7},{7,6},{8,9},{9,8},{10,11... | collective-permute-start | bytes 1179656 | tf_op jit(solution)/shard_map/ppermute | solution.py:335
  17.6 6.4 %collective-permute-start.7 = (f32[640,256]{1,0:T(8,128)S(1)}, f32[640,256]{1,0:T(8,128)S(1)}, u32[]{:S(2)}, u32[]{:S(2)}) collective-permute-start(f32[640,256]{1,0:T(8,128)S(1)} %get-tuple-element.52), channel_id=1, source_target_pairs={{0,1},{1,0},{2,3},{3,2},{4,5},{5,4},{6,7},{7,6},{8,9},{9,8},{10,11... | collective-permute-start | bytes 1966088 | tf_op jit(solution)/shard_map/ppermute | solution.py:335
  18.4 12.8 %collective-permute-start.2 = (f32[384,256]{1,0:T(8,128)S(1)}, f32[384,256]{1,0:T(8,128)S(1)}, u32[]{:S(2)}, u32[]{:S(2)}) collective-permute-start(f32[384,256]{1,0:T(8,128)S(1)} %slice_add_fusion.2), channel_id=1, source_target_pairs={{0,2},{1,3},{2,0},{3,1},{4,6},{5,7},{6,4},{7,5},{8,10},{9,11},{10,... | collective-permute-start | bytes 1179656 | tf_op jit(solution)/shard_map/ppermute | solution.py:335
  21.4 19.4 %collective-permute-start.4 = (f32[384,256]{1,0:T(8,128)S(1)}, f32[384,256]{1,0:T(8,128)S(1)}, u32[]{:S(2)}, u32[]{:S(2)}) collective-permute-start(f32[384,256]{1,0:T(8,128)S(1)} %slice_add_fusion.1), channel_id=1, source_target_pairs={{0,4},{1,5},{2,6},{3,7},{4,0},{5,1},{6,2},{7,3},{8,12},{9,13},{10,... | collective-permute-start | bytes 1179656 | tf_op jit(solution)/shard_map/ppermute | solution.py:335
  23.1 17.7 %collective-permute-start.6 = (f32[384,256]{1,0:T(8,128)S(1)}, f32[384,256]{1,0:T(8,128)S(1)}, u32[]{:S(2)}, u32[]{:S(2)}) collective-permute-start(f32[384,256]{1,0:T(8,128)S(1)} %slice_add_fusion), channel_id=1, source_target_pairs={{0,6},{1,7},{2,4},{3,5},{4,2},{5,3},{6,0},{7,1},{8,14},{9,15},{10,... | collective-permute-start | bytes 1179656 | tf_op jit(solution)/shard_map/ppermute | solution.py:335
  24.1 21.1 %collective-permute-start.11 = (f32[160,256]{1,0:T(8,128)S(1)}, f32[160,256]{1,0:T(8,128)S(1)}, u32[]{:S(2)}, u32[]{:S(2)}) collective-permute-start(f32[160,256]{1,0:T(8,128)S(1)} %get-tuple-element.59), channel_id=1, source_target_pairs={{0,8},{1,9},{2,10},{3,11},{4,12},{5,13},{6,14},{7,15},{8,0},{9,1},... | collective-permute-start | bytes 491528 | tf_op jit(solution)/shard_map/ppermute | solution.py:335
  25.7 19.7 %collective-permute-start.12 = (f32[160,256]{1,0:T(8,128)S(1)}, f32[160,256]{1,0:T(8,128)S(1)}, u32[]{:S(2)}, u32[]{:S(2)}) collective-permute-start(f32[160,256]{1,0:T(8,128)S(1)} %get-tuple-element.60), channel_id=1, source_target_pairs={{0,16},{1,17},{2,18},{3,19},{4,20},{5,21},{6,22},{7,23},{8,24},{9,... | collective-permute-start | bytes 491528 | tf_op jit(solution)/shard_map/ppermute | solution.py:335
  31.2 14.2 %collective-permute-start.13 = (f32[160,256]{1,0:T(8,128)S(1)}, f32[160,256]{1,0:T(8,128)S(1)}, u32[]{:S(2)}, u32[]{:S(2)}) collective-permute-start(f32[160,256]{1,0:T(8,128)S(1)} %get-tuple-element.53), channel_id=1, source_target_pairs={{0,24},{1,25},{2,26},{3,27},{4,28},{5,29},{6,30},{7,31},{8,16},{9,... | collective-permute-start | bytes 491528 | tf_op jit(solution)/shard_map/ppermute | solution.py:335
  40.9 7.2 %collective-permute-start.8 = (f32[96,256]{1,0:T(8,128)S(1)}, f32[96,256]{1,0:T(8,128)S(1)}, u32[]{:S(2)}, u32[]{:S(2)}) collective-permute-start(f32[96,256]{1,0:T(8,128)S(1)} %get-tuple-element.55), channel_id=1, source_target_pairs={{0,8},{1,9},{2,10},{3,11},{4,12},{5,13},{6,14},{7,15},{8,0},{9,1},... | collective-permute-start | bytes 294920 | tf_op jit(solution)/shard_map/ppermute | solution.py:335
  42.6 9.5 %collective-permute-start.9 = (f32[96,256]{1,0:T(8,128)S(1)}, f32[96,256]{1,0:T(8,128)S(1)}, u32[]{:S(2)}, u32[]{:S(2)}) collective-permute-start(f32[96,256]{1,0:T(8,128)S(1)} %get-tuple-element.56), channel_id=1, source_target_pairs={{0,16},{1,17},{2,18},{3,19},{4,20},{5,21},{6,22},{7,23},{8,24},{9,... | collective-permute-start | bytes 294920 | tf_op jit(solution)/shard_map/ppermute | solution.py:335
  45.2 7.0 %collective-permute-start.10 = (f32[96,256]{1,0:T(8,128)S(1)}, f32[96,256]{1,0:T(8,128)S(1)}, u32[]{:S(2)}, u32[]{:S(2)}) collective-permute-start(f32[96,256]{1,0:T(8,128)S(1)} %get-tuple-element.57), channel_id=1, source_target_pairs={{0,24},{1,25},{2,26},{3,27},{4,28},{5,29},{6,30},{7,31},{8,16},{9,... | collective-permute-start | bytes 294920 | tf_op jit(solution)/shard_map/ppermute | solution.py:335
  45.5 7.1 %collective-permute-start.16 = (f32[160,256]{1,0:T(8,128)S(1)}, f32[160,256]{1,0:T(8,128)S(1)}, u32[]{:S(2)}, u32[]{:S(2)}) collective-permute-start(f32[160,256]{1,0:T(8,128)S(1)} %add_add_fusion.2), channel_id=1, source_target_pairs={{0,6},{1,7},{2,4},{3,5},{4,2},{5,3},{6,0},{7,1},{8,14},{9,15},{10,... | collective-permute-start | bytes 491528 | tf_op jit(solution)/shard_map/ppermute | solution.py:335
  47.2 7.0 %collective-permute-start.15 = (f32[160,256]{1,0:T(8,128)S(1)}, f32[160,256]{1,0:T(8,128)S(1)}, u32[]{:S(2)}, u32[]{:S(2)}) collective-permute-start(f32[160,256]{1,0:T(8,128)S(1)} %add_add_fusion.2), channel_id=1, source_target_pairs={{0,4},{1,5},{2,6},{3,7},{4,0},{5,1},{6,2},{7,3},{8,12},{9,13},{10,... | collective-permute-start | bytes 491528 | tf_op jit(solution)/shard_map/ppermute | solution.py:335
  48.1 6.3 %collective-permute-start.14 = (f32[160,256]{1,0:T(8,128)S(1)}, f32[160,256]{1,0:T(8,128)S(1)}, u32[]{:S(2)}, u32[]{:S(2)}) collective-permute-start(f32[160,256]{1,0:T(8,128)S(1)} %add_add_fusion.2), channel_id=1, source_target_pairs={{0,2},{1,3},{2,0},{3,1},{4,6},{5,7},{6,4},{7,5},{8,10},{9,11},{10,... | collective-permute-start | bytes 491528 | tf_op jit(solution)/shard_map/ppermute | solution.py:335
  54.4 8.0 %collective-permute-start.19 = (f32[128,256]{1,0:T(8,128)S(1)}, f32[128,256]{1,0:T(8,128)S(1)}, u32[]{:S(2)}, u32[]{:S(2)}) collective-permute-start(f32[128,256]{1,0:T(8,128)S(1)} %pad_maximum_fusion.3), channel_id=1, source_target_pairs={{0,24},{1,25},{2,26},{3,27},{4,28},{5,29},{6,30},{7,31},{8,16},{9,... | collective-permute-start | bytes 393224 | tf_op jit(solution)/shard_map/ppermute | solution.py:335
  58.0 9.2 %collective-permute-start.18 = (f32[128,256]{1,0:T(8,128)S(1)}, f32[128,256]{1,0:T(8,128)S(1)}, u32[]{:S(2)}, u32[]{:S(2)}) collective-permute-start(f32[128,256]{1,0:T(8,128)S(1)} %pad_maximum_fusion.3), channel_id=1, source_target_pairs={{0,16},{1,17},{2,18},{3,19},{4,20},{5,21},{6,22},{7,23},{8,24},{9,... | collective-permute-start | bytes 393224 | tf_op jit(solution)/shard_map/ppermute | solution.py:335
  58.0 9.2 %collective-permute-start.17 = (f32[128,256]{1,0:T(8,128)S(1)}, f32[128,256]{1,0:T(8,128)S(1)}, u32[]{:S(2)}, u32[]{:S(2)}) collective-permute-start(f32[128,256]{1,0:T(8,128)S(1)} %pad_maximum_fusion.3), channel_id=1, source_target_pairs={{0,8},{1,9},{2,10},{3,11},{4,12},{5,13},{6,14},{7,15},{8,0},{9,1},... | collective-permute-start | bytes 393224 | tf_op jit(solution)/shard_map/ppermute | solution.py:335
  67.3 5.0 %collective-permute-start.21 = (f32[128,256]{1,0:T(8,128)S(1)}, f32[128,256]{1,0:T(8,128)S(1)}, u32[]{:S(2)}, u32[]{:S(2)}) collective-permute-start(f32[128,256]{1,0:T(8,128)S(1)} %slice.119), channel_id=1, source_target_pairs={{0,8},{1,9},{2,10},{3,11},{4,12},{5,13},{6,14},{7,15},{8,0},{9,1},... | collective-permute-start | bytes 393224 | tf_op jit(solution)/shard_map/ppermute | solution.py:335
  67.7 4.7 %collective-permute-start.20 = (f32[128,256]{1,0:T(8,128)S(1)}, f32[128,256]{1,0:T(8,128)S(1)}, u32[]{:S(2)}, u32[]{:S(2)}) collective-permute-start(f32[128,256]{1,0:T(8,128)S(1)} %pad_maximum_fusion.4.kept), channel_id=1, source_target_pairs={{0,1},{1,0},{2,3},{3,2},{4,5},{5,4},{6,7},{7,6},{8,9},{9,8},{10,11... | collective-permute-start | bytes 393224 | tf_op jit(solution)/shard_map/ppermute | solution.py:335
  67.7 20.4 %collective-permute-start.25 = (f32[384,256]{1,0:T(8,128)S(1)}, f32[384,256]{1,0:T(8,128)S(1)}, u32[]{:S(2)}, u32[]{:S(2)}) collective-permute-start(f32[384,256]{1,0:T(8,128)S(1)} %pad_maximum_fusion.1.refs_0_), channel_id=1, source_target_pairs={{0,6},{1,7},{2,4},{3,5},{4,2},{5,3},{6,0},{7,1},{8,14},{9,15},{10,... | collective-permute-start | bytes 1179656 | tf_op jit(solution)/shard_map/ppermute | solution.py:335
  69.1 19.4 %collective-permute-start.24 = (f32[384,256]{1,0:T(8,128)S(1)}, f32[384,256]{1,0:T(8,128)S(1)}, u32[]{:S(2)}, u32[]{:S(2)}) collective-permute-start(f32[384,256]{1,0:T(8,128)S(1)} %pad_maximum_fusion.1.refs_0_), channel_id=1, source_target_pairs={{0,4},{1,5},{2,6},{3,7},{4,0},{5,1},{6,2},{7,3},{8,12},{9,13},{10,... | collective-permute-start | bytes 1179656 | tf_op jit(solution)/shard_map/ppermute | solution.py:335
  70.8 18.1 %collective-permute-start.23 = (f32[384,256]{1,0:T(8,128)S(1)}, f32[384,256]{1,0:T(8,128)S(1)}, u32[]{:S(2)}, u32[]{:S(2)}) collective-permute-start(f32[384,256]{1,0:T(8,128)S(1)} %pad_maximum_fusion.1.refs_0_), channel_id=1, source_target_pairs={{0,2},{1,3},{2,0},{3,1},{4,6},{5,7},{6,4},{7,5},{8,10},{9,11},{10,... | collective-permute-start | bytes 1179656 | tf_op jit(solution)/shard_map/ppermute | solution.py:335
  72.4 13.8 %copy-start = (f32[2048,256]{1,0:T(8,128)S(1)}, f32[2048,256]{1,0:T(8,128)}, u32[]{:S(2)}) copy-start(f32[2048,256]{1,0:T(8,128)} %get-tuple-element.74.sketch) | copy-start | bytes 6291460
  72.4 13.7 %collective-permute-start.26 = (f32[256,256]{1,0:T(8,128)S(1)}, f32[256,256]{1,0:T(8,128)S(1)}, u32[]{:S(2)}, u32[]{:S(2)}) collective-permute-start(f32[256,256]{1,0:T(8,128)S(1)} %pad_maximum_fusion.2), channel_id=1, source_target_pairs={{0,16},{1,17},{2,18},{3,19},{4,20},{5,21},{6,22},{7,23},{8,24},{9,... | collective-permute-start | bytes 786440 | tf_op jit(solution)/shard_map/ppermute | solution.py:335
  74.2 11.9 %collective-permute-start.22 = (f32[384,256]{1,0:T(8,128)S(1)}, f32[384,256]{1,0:T(8,128)S(1)}, u32[]{:S(2)}, u32[]{:S(2)}) collective-permute-start(f32[384,256]{1,0:T(8,128)S(1)} %pad_maximum_fusion.1.refs_0_), channel_id=1, source_target_pairs={{0,1},{1,0},{2,3},{3,2},{4,5},{5,4},{6,7},{7,6},{8,9},{9,8},{10,11... | collective-permute-start | bytes 1179656 | tf_op jit(solution)/shard_map/ppermute | solution.py:335
  88.0 3.8 %collective-permute-start.30 = (f32[512,256]{1,0:T(8,128)S(1)}, f32[512,256]{1,0:T(8,128)S(1)}, u32[]{:S(2)}, u32[]{:S(2)}) collective-permute-start(f32[512,256]{1,0:T(8,128)S(1)} %pad_maximum_fusion.refs_4_), channel_id=1, source_target_pairs={{0,1},{1,0},{2,3},{3,2},{4,5},{5,4},{6,7},{7,6},{8,9},{9,8},{10,11... | collective-permute-start | bytes 1572872 | tf_op jit(solution)/shard_map/ppermute | solution.py:335
  89.0 2.4 %collective-permute-start.27 = (f32[384,256]{1,0:T(8,128)S(1)}, f32[384,256]{1,0:T(8,128)S(1)}, u32[]{:S(2)}, u32[]{:S(2)}) collective-permute-start(f32[384,256]{1,0:T(8,128)S(1)} %collective-permute-done.23.refs_1_), channel_id=1, source_target_pairs={{0,1},{1,0},{2,3},{3,2},{4,5},{5,4},{6,7},{7,6},{8,9},{9,8},{10,11... | collective-permute-start | bytes 1179656 | tf_op jit(solution)/shard_map/ppermute | solution.py:335
  89.0 2.4 %collective-permute-start.28 = (f32[384,256]{1,0:T(8,128)S(1)}, f32[384,256]{1,0:T(8,128)S(1)}, u32[]{:S(2)}, u32[]{:S(2)}) collective-permute-start(f32[384,256]{1,0:T(8,128)S(1)} %collective-permute-done.24.refs_2_), channel_id=1, source_target_pairs={{0,1},{1,0},{2,3},{3,2},{4,5},{5,4},{6,7},{7,6},{8,9},{9,8},{10,11... | collective-permute-start | bytes 1179656 | tf_op jit(solution)/shard_map/ppermute | solution.py:335
  89.5 2.3 %collective-permute-start.29 = (f32[384,256]{1,0:T(8,128)S(1)}, f32[384,256]{1,0:T(8,128)S(1)}, u32[]{:S(2)}, u32[]{:S(2)}) collective-permute-start(f32[384,256]{1,0:T(8,128)S(1)} %collective-permute-done.25.refs_3_), channel_id=1, source_target_pairs={{0,1},{1,0},{2,3},{3,2},{4,5},{5,4},{6,7},{7,6},{8,9},{9,8},{10,11... | collective-permute-start | bytes 1179656 | tf_op jit(solution)/shard_map/ppermute | solution.py:335
